TPU v7x, 128 devices: a whole 4x4x4 slice. The times are simulated.
128 devices in a mesh: pool: 16 (over z, y), grp: 8 (over x, core).
Axes of the slice: x: 4, y: 4, z: 4, core: 2. Of those that a mesh axis runs over, the one named last changes fastest.
Arguments:
- embeddings: bfloat16 [131072, 1024], P(('pool', 'grp')), may hold values from -6 to 6
- members: int32 [256, 512], replicated, may hold values from 0 to 131071, as said below
- valid: int32 [256], replicated, may hold values from 128 to 512, as said below
- block_cluster: int32 [256], replicated, may hold values from 0 to 255, as said below
Outputs:
- duplicate_score: float32 [131072], P(('pool', 'grp'))
Inputs may be any that keep to these rules, and one draw needn't show every extreme that they name: `members`: every pool row is held by at most one live slot. Device d (pool-major index) owns blocks d * 2 to d * 2 + 1; of the rows held by one device's live slots, at most 8 lie in any one row shard (rows s * 1024 to s * 1024 + 1023, the rows of device s), the counts from two shards differ by at most one, and in every draw the live rows of some device come exactly 8 from every shard. Dead slots hold arbitrary row numbers. `valid`: in every draw all 2 blocks of some device are full. `block_cluster`: Nondecreasing; equal values form runs of blocks inside one cluster group of 16 blocks, each value is the index of its run's first block, the first block of each group starts a new cluster, and the last block forms a cluster of its own.
All inputs are finite; a program needn't handle non-finite values.
Results may differ from a plain program's by a relative error of at most 0.0014.
Values may be sent and summed in bfloat16 or wider, within the bound.
No kernel may reach another device: no remote copies, remote signals or barrier semaphores. Data moves between devices by JAX's collectives and lax.ppermute only.
A program may use at most 64 MiB of HBM per device.

v0:
```python
import jax
import jax.numpy as jnp
from jax import lax
from jax.sharding import PartitionSpec as P

EPS = 1e-06


def unit_rows(values):
    wide = values.astype(jnp.float32)
    return (wide * lax.rsqrt(jnp.sum(wide * wide, axis=1, keepdims=True) + EPS)).astype(
        jnp.bfloat16
    )


def tile_best(current, query_rows, key_rows, key_count, same_block):
    column = jnp.arange(query_rows.shape[0], dtype=jnp.int32)
    sims = lax.dot_general(
        query_rows, key_rows, (((1,), (1,)), ((), ())), preferred_element_type=jnp.float32
    )
    keep = (column[None, :] < key_count) & (
        jnp.logical_not(same_block) | (column[None, :] < column[:, None])
    )
    return jnp.maximum(current, jnp.max(jnp.where(keep, sims, 0.0), axis=1))


def body(embeddings, members, valid, block_cluster):
    rows_dev, feature_width = embeddings.shape
    block_len = members.shape[1]
    devices = lax.axis_size(("pool", "grp"))
    group_size = lax.axis_size("grp")
    per_device = members.shape[0] // devices
    slots = per_device * block_len
    capacity = slots // devices
    device_index = lax.axis_index(("pool", "grp"))
    group_index = lax.axis_index("grp")
    unit = unit_rows(embeddings)
    column = jnp.arange(block_len, dtype=jnp.int32)
    live_all = (column[None, :] < valid[:, None]).reshape(devices, slots)
    slot_rows = members.reshape(devices, slots)
    mine = live_all & (slot_rows // rows_dev == device_index)
    rank = jnp.cumsum(mine.astype(jnp.int32), axis=1) - 1
    places = jnp.arange(capacity, dtype=jnp.int32)
    hits = mine[:, :, None] & (rank[:, :, None] == places[None, None, :])
    local_rows = slot_rows - device_index * rows_dev
    table = jnp.sum(jnp.where(hits, local_rows[:, :, None], 0), axis=1).reshape(-1)
    filled = jnp.any(hits, axis=1).reshape(-1)
    outgoing = jnp.where(
        filled[:, None], jnp.take(unit, table, axis=0), jnp.zeros((), jnp.bfloat16)
    )
    incoming = lax.all_to_all(outgoing, ("pool", "grp"), split_axis=0, concat_axis=0, tiled=True)
    own_rows = lax.dynamic_slice_in_dim(slot_rows, device_index, 1, 0)[0]
    own_live = lax.dynamic_slice_in_dim(live_all, device_index, 1, 0)[0]
    source = own_rows // rows_dev
    source_hits = (source[:, None] == jnp.arange(devices, dtype=jnp.int32)[None, :]) & own_live[
        :, None
    ]
    running_count = jnp.cumsum(source_hits.astype(jnp.int32), axis=0)
    seen = jnp.sum(jnp.where(source_hits, running_count, 0), axis=1) - 1
    position = jnp.where(own_live, source * capacity + seen, 0)
    own = jnp.where(
        own_live[:, None], jnp.take(incoming, position, axis=0), jnp.zeros((), jnp.bfloat16)
    )
    group_blocks = per_device * group_size
    group_first = device_index // group_size * group_blocks
    clusters = lax.dynamic_slice_in_dim(block_cluster, group_first, group_blocks)
    counts = lax.dynamic_slice_in_dim(valid, group_first, group_blocks)
    my_first = group_index * per_device
    own_blocks = own.reshape(per_device, block_len, feature_width)
    carried = jnp.zeros((per_device, block_len), jnp.float32)
    piece = lax.all_gather(own, "grp", axis=0, tiled=True)
    piece_blocks = piece.shape[0] // block_len
    key_rows = piece.reshape(piece_blocks, block_len, feature_width)
    updated = []
    for local_block in range(per_device):
        query_block = my_first + local_block
        query_rows = own_blocks[local_block]

        def inner(offset, running):
            key_block = offset
            usable = (clusters[key_block] == clusters[query_block]) & (key_block <= query_block)

            def work(current):
                return tile_best(
                    current,
                    query_rows,
                    key_rows[offset],
                    counts[key_block],
                    key_block == query_block,
                )

            return lax.cond(usable, work, lambda current: current, running)

        updated.append(lax.fori_loop(0, piece_blocks, inner, carried[local_block]))
    best = jnp.stack(updated)
    values = best.reshape(-1)
    outbound = (
        jnp.zeros((devices * capacity + 1,), jnp.float32)
        .at[jnp.where(own_live, position, devices * capacity)]
        .set(values)
    )
    returned = lax.all_to_all(
        outbound[: devices * capacity], ("pool", "grp"), split_axis=0, concat_axis=0, tiled=True
    )
    scores = (
        jnp.zeros((rows_dev + 1,), jnp.float32).at[jnp.where(filled, table, rows_dev)].set(returned)
    )
    return scores[:rows_dev]


def solution(mesh):
    in_specs = (P(("pool", "grp"), None), P(), P(), P())
    out_specs = P(("pool", "grp"))
    return jax.shard_map(body, mesh=mesh, in_specs=in_specs, out_specs=out_specs, check_vma=False)
```

profile of v0, /device:TPU:1, one launch (start us, length us, event | category | flops | bytes accessed | tf_op | source)
XLA Modules:
  0.0 363.6 jit_solution(11302233174775088126)
XLA Ops:
  6.5 1.1 reshape.320
  7.6 1.2 reshape.319
  10.5 0.9 copy.42
  11.4 1.6 fusion.36
  13.1 2.3 fusion.17
  15.4 2.3 select_reduce_fusion
  18.3 1.1 copy-done.2
  19.8 5.4 %gather_fusion = bf16[1024,1024]{1,0:T(8,128)(2,1)} fusion(bf16[1024,1024]{1,0:T(8,128)(2,1)S(1)} %fusion.15, s32[1024]{0:T(1024)S(1)} %fusion.55), kind=kCustom, calls=%fused_computation.clone | custom fusion | bytes 4198400 | tf_op jit(solution)/shard_map/jit(_take)/gather | solution.py:49
  25.2 3.1 fusion.18
  28.3 11.5 %all-to-all-start = ((bf16[128,8,1024]{2,1,0:T(8,128)(2,1)}), bf16[128,8,1024]{2,1,0:T(8,128)(2,1)S(1)}, u32[]{:S(2)}, u32[]{:S(2)}) async-start(bf16[128,8,1024]{2,1,0:T(8,128)(2,1)} %fusion.18), calls=%async_computation | async-start | bytes 4194304 | tf_op jit(solution)/shard_map/all_to_all | solution.py:51
  41.4 28.9 %all-to-all-done = bf16[128,8,1024]{2,1,0:T(8,128)(2,1)S(1)} async-done(((bf16[128,8,1024]{2,1,0:T(8,128)(2,1)}), bf16[128,8,1024]{2,1,0:T(8,128)(2,1)S(1)}, u32[]{:S(2)}, u32[]{:S(2)}) %all-to-all-start) | async-done | bytes 2097184 | tf_op jit(solution)/shard_map/all_to_all | solution.py:51
  70.3 5.4 %gather_fusion.1 = bf16[1024,1024]{1,0:T(8,128)(2,1)} fusion(bf16[1024,1024]{1,0:T(8,128)(2,1)S(1)} %bitcast.81, s32[1024]{0:T(1024)S(1)} %get-tuple-element.456), kind=kCustom, calls=%fused_computation.1.clone | custom fusion | bytes 4198400 | tf_op jit(solution)/shard_map/jit(_take)/gather | solution.py:62
  75.6 3.1 select_select_fusion
  80.4 1.5 fusion.61
  81.8 78.0 %all-gather.2.cloned.1.call-done = bf16[8192,1024]{1,0:T(8,128)(2,1)} async-done(((bf16[1024,1024]{1,0:T(8,128)(2,1)}), bf16[8192,1024]{1,0:T(8,128)(2,1)}) %all-gather.2.cloned.1.call-update) | async-done | bytes 16777232 | tf_op jit(solution)/shard_map/all_gather | solution.py:71
  159.8 40.4 %while.37 = (s32[]{:T(128)}, f32[512]{0:T(512)S(1)}, s32[16]{0:T(128)S(1)}, s32[1]{0:T(128)}, s32[]{:T(128)}, /*index=5*/s32[16]{0:T(128)S(1)}, bf16[16,512,1024...) while((s32[]{:T(128)}, f32[512]{0:T(512)S(1)}, s32[16]{0:T(128)S(1)}, s32[1]{0:T(128)}, s32[]{:T(128)}, ...), condition=%wide.region_17.19_spmd, body=%wide.region_13.18_spmd.sunk | while | flops 538182144 | bytes 2106629 | solution.py:94
  166.0 3.6 conditional.5
  167.3 2.3 fusion.8
  171.7 3.6 conditional.5
  173.0 2.3 fusion.8
  177.4 0.7 dynamic_slice.92
  200.3 32.2 %while.36 = (s32[]{:T(128)}, f32[512]{0:T(512)S(1)}, s32[16]{0:T(128)S(1)}, s32[1]{0:T(128)}, s32[]{:T(128)}, /*index=5*/s32[16]{0:T(128)S(1)}, bf16[16,512,1024...) while((s32[]{:T(128)}, f32[512]{0:T(512)S(1)}, s32[16]{0:T(128)S(1)}, s32[1]{0:T(128)}, s32[]{:T(128)}, ...), condition=%wide.region_12.14_spmd, body=%wide.region_8.13_spmd.sunk | while | flops 538182144 | bytes 2106629 | solution.py:94
  205.7 3.4 conditional.4
  205.7 0.7 dynamic_slice.50
  206.4 0.7 iota_compare_fusion.1
  207.1 2.0 fusion.1
  232.6 4.3 %scatter_custom_fusion = f32[1025]{0:T(1024)S(1)} fusion(s32[1024]{0:T(1024)S(1)} %bitcast.97, f32[1024]{0:T(1024)S(1)} %bitcast.96, f32[]{:T(128)} %constant.159.clone.1), kind=kCustom, calls=%fused_computation.110 | custom fusion | bytes 4104 | tf_op jit(solution)/shard_map/scatter | solution.py:100
  236.9 0.7 all_to_all.19
  237.6 103.2 %all-to-all-start.1 = ((f32[128,8,1]{1,2,0:T(1,128)}), f32[128,8,1]{1,2,0:T(1,128)S(1)}, u32[]{:S(2)}, u32[]{:S(2)}) async-start(f32[128,8,1]{1,2,0:T(1,128)} %bitcast.26), calls=%async_computation.1 | async-start | bytes 131072 | tf_op jit(solution)/shard_map/all_to_all | solution.py:102
  340.9 9.6 %all-to-all-done.1 = f32[128,8,1]{1,2,0:T(1,128)S(1)} async-done(((f32[128,8,1]{1,2,0:T(1,128)}), f32[128,8,1]{1,2,0:T(1,128)S(1)}, u32[]{:S(2)}, u32[]{:S(2)}) %all-to-all-start.1) | async-done | bytes 4128 | tf_op jit(solution)/shard_map/all_to_all | solution.py:102
  351.0 0.8 reduce.6
  351.9 4.3 %scatter_custom_fusion.1 = f32[1025]{0:T(1024)S(1)} fusion(s32[1024]{0:T(1024)S(1)} %bitcast.95, f32[1024]{0:T(1024)S(1)} %reshape.354, f32[]{:T(128)} %constant.159.clone.1), kind=kCustom, calls=%fused_computation.108 | custom fusion | bytes 4104 | tf_op jit(solution)/shard_map/scatter | solution.py:106
  (135 shorter events, 29.2 us)
Async XLA Ops:
  6.5 2.6 copy-start.4
  11.4 6.4 %copy-start.1 = (bf16[1024,1024]{1,0:T(8,128)(2,1)S(1)}, bf16[1024,1024]{1,0:T(8,128)(2,1)}, u32[]{:S(2)}) copy-start(bf16[1024,1024]{1,0:T(8,128)(2,1)} %param.14) | copy-start | bytes 6291460
  17.7 1.6 copy-start.2
  28.3 42.0 %all-to-all-start = ((bf16[128,8,1024]{2,1,0:T(8,128)(2,1)}), bf16[128,8,1024]{2,1,0:T(8,128)(2,1)S(1)}, u32[]{:S(2)}, u32[]{:S(2)}) async-start(bf16[128,8,1024]{2,1,0:T(8,128)(2,1)} %fusion.18), calls=%async_computation | async-start | bytes 4194304 | tf_op jit(solution)/shard_map/all_to_all | solution.py:51
  39.8 120.1 %all-gather.2.cloned.1.call-start = ((), (), s32[]{:S(2)}) async-start(), calls=%async_computation.2 | async-start | bytes 18874368 | tf_op jit(solution)/shard_map/all_gather | solution.py:71
  78.8 0.7 copy-start.5
  78.8 1.6 copy-start
  159.8 40.5 %copy-start.3 = (bf16[512,1024]{1,0:T(8,128)(2,1)S(1)}, bf16[512,1024]{1,0:T(8,128)(2,1)}, u32[]{:S(2)}) copy-start(bf16[512,1024]{1,0:T(8,128)(2,1)} %get-tuple-element.592) | copy-start | bytes 3145732
  237.6 112.8 %all-to-all-start.1 = ((f32[128,8,1]{1,2,0:T(1,128)}), f32[128,8,1]{1,2,0:T(1,128)S(1)}, u32[]{:S(2)}, u32[]{:S(2)}) async-start(f32[128,8,1]{1,2,0:T(1,128)} %bitcast.26), calls=%async_computation.1 | async-start | bytes 131072 | tf_op jit(solution)/shard_map/all_to_all | solution.py:102
Sparse Core Ops, SparseCore 0:
  78.9 80.8 all-gather.1
where the time goes:
time: 367 us; the launch traced here: 364 us
  waiting for transfers between devices  116 us (32%)
  starting transfers between devices  115 us (31%)
  local copies, waits for them, and re-layouts  52 us (14%)
  loops' own time  42.3 us (12%)
  other arithmetic  17.6 us (5%)
  between operations  13.8 us (4%)
  matrix products  6.6 us (2%)
    all_to_all x1, starting transfers between devices, body(): lax.all_to_all(outbound[:devices * capacity], ('pool', 'grp'), split_axis...  103 us
    all_gather x1, waiting for transfers between devices, body(): piece = lax.all_gather(own, 'grp', axis=0, tiled=True)  78 us
    another operation x2, loops' own time, body(): updated.append(lax.fori_loop(0, piece_blocks, inner, carried[local_block]))  41.8 us
    all_to_all x1, waiting for transfers between devices, body(): lax.all_to_all(outgoing, ('pool', 'grp'), split_axis=0, concat_axis=0, ti...  28.9 us
    dynamic_slice x32, local copies, waits for them, and re-layouts, inner(): clusters[key_block] == clusters[query_block]  19.9 us
    all_to_all x1, starting transfers between devices, body(): lax.all_to_all(outgoing, ('pool', 'grp'), split_axis=0, concat_axis=0, ti...  11.5 us
    all_to_all x1, waiting for transfers between devices, body(): lax.all_to_all(outbound[:devices * capacity], ('pool', 'grp'), split_axis...  9.59 us
  transfers between devices with their start and end apart: 3, of which 3 were waited for; matrix products, arithmetic and copies ran while one was open for 1% of the time, Pallas kernels for 0%

commit v1 on v0

v1 whole, which is shorter than its diff:
```python
import jax
import jax.numpy as jnp
from jax import lax
from jax.experimental import pallas as pl
from jax.experimental.pallas import tpu as pltpu
from jax.sharding import PartitionSpec as P

EPS = 1e-06
F32 = jnp.float32
BF16 = jnp.bfloat16
I32 = jnp.int32
CHUNKS = 2
NT = (((1,), (1,)), ((), ()))
PARAMS = pltpu.CompilerParams(vmem_limit_bytes=50 * 1024 * 1024)


def iota(shape, dim):
    return lax.broadcasted_iota(I32, shape, dim)


def normal_rows(rows):
    return (rows * lax.rsqrt(jnp.sum(rows * rows, axis=1, keepdims=True) + EPS)).astype(BF16)


def picked_rows(table, emb_ref, first, count, pools):
    width = emb_ref.shape[0]
    wanted = []
    for k in range(first, first + count):
        hit = table[:, k : k + 1] == iota((table.shape[0], width), 1)
        wanted.append(jnp.where(hit, 1.0, 0.0).reshape(pools, -1, width))
    choice = jnp.concatenate(wanted, axis=1).reshape(-1, width).astype(BF16)
    return normal_rows(jnp.dot(choice, emb_ref[...], preferred_element_type=F32))


def table_kernel(
    pools, group, places, members_ref, valid_ref, emb_ref, table_ref, out_ref, found_ref
):
    rows_dev = emb_ref.shape[0]
    device = lax.axis_index("pool") * group + lax.axis_index("grp")
    blocks, block_len = members_ref.shape
    devices = blocks // 2
    before = jnp.where(
        iota((block_len, block_len), 0) < iota((block_len, block_len), 1), 1.0, 0.0
    ).astype(BF16)
    at = iota((blocks, blocks), 1) == iota((blocks, blocks), 0)
    live = jnp.sum(jnp.where(at, valid_ref[...], 0), axis=1, keepdims=True)
    local = members_ref[...] - device * rows_dev
    mine = (local >= 0) & (local < rows_dev) & (iota((blocks, block_len), 1) < live)
    ones = jnp.where(mine, 1.0, 0.0)
    counts = jnp.broadcast_to(jnp.sum(ones, axis=1, keepdims=True), (blocks, 128))
    counts = jnp.where(iota((blocks, 128), 0) % 2 == 1, pltpu.roll(counts, 1, 0), 0.0)
    rank = jnp.dot(ones.astype(BF16), before, preferred_element_type=F32) + counts[:, :1]
    rank = jnp.where(mine, rank, -1.0)
    value = (local + 1).astype(F32)
    lane = iota((blocks, 128), 1)
    found = jnp.zeros((blocks, 128), F32)
    for k in range(places):
        entry = jnp.sum(jnp.where(rank == k, value, 0.0), axis=1, keepdims=True)
        found = jnp.where(lane == k, entry, found)
    found_ref[...] = found
    pair = found_ref[pl.ds(0, devices, stride=2), :] + found_ref[pl.ds(1, devices, stride=2), :]
    table = pair.astype(I32) - 1
    table_ref[...] = table
    out_ref[...] = picked_rows(table, emb_ref, 0, places // CHUNKS, pools)


def rows_kernel(pools, first, count, table_ref, emb_ref, out_ref):
    out_ref[...] = picked_rows(table_ref[...], emb_ref, first, count, pools)


def meta_kernel(group, places, members_ref, valid_ref, cluster_ref, out_ref):
    blocks, block_len = members_ref.shape
    sources = blocks // 2
    slots = 2 * block_len
    pool = lax.axis_index("pool")
    width = group * places
    before = jnp.where(iota((slots, slots), 0) < iota((slots, slots), 1), 1.0, 0.0).astype(BF16)
    slot = iota((1, slots), 1)
    kind = iota((2 * width, slots), 0)
    kind_place = kind % width // group
    kind_owner = kind % group
    kind_value = jnp.where(kind < width, slot // 32, slot % 32 + 1)
    found = jnp.zeros((sources, 2 * width), F32)
    block_lane = iota((1, blocks), 1)
    lane = iota((1, width), 1)
    first_cluster = jnp.zeros((1, width), I32)
    second_cluster = jnp.zeros((1, width), I32)
    for owner in range(group):
        block = (pool * group + owner) * 2
        halves, lives = [], []
        for half in range(2):
            halves.append(members_ref[pl.ds(block + half, 1), :])
            at = block_lane == block + half
            lives.append(jnp.sum(jnp.where(at, valid_ref[...], 0), axis=1, keepdims=True))
            cluster = jnp.sum(jnp.where(at, cluster_ref[...], 0), axis=1, keepdims=True)
            if half == 0:
                first_cluster = jnp.where(lane % group == owner, cluster, first_cluster)
            else:
                second_cluster = jnp.where(lane % group == owner, cluster, second_cluster)
        rows = jnp.concatenate(halves, axis=1)
        end = jnp.where(slot < block_len, lives[0], block_len + lives[1])
        origin = jnp.where(slot < end, rows // slots, -1)
        match = iota((sources, slots), 0) == origin
        ones = jnp.where(match, 1.0, 0.0).astype(BF16)
        ranks = jnp.dot(ones, before, preferred_element_type=F32)
        rank = jnp.sum(jnp.where(match, ranks, 0.0), axis=0, keepdims=True).astype(I32)
        weight = jnp.where((kind_owner == owner) & (kind_place == rank), kind_value, 0)
        found = found + lax.dot_general(
            ones, weight.astype(F32).astype(BF16), NT, preferred_element_type=F32
        )
    found = found.astype(I32)
    place = found[:, :width] * 32 + found[:, width:] - 1
    filled = found[:, width:] > 0
    position = jnp.where(filled, place + lane % group * slots, -1)
    cluster = jnp.where(place < block_len, first_cluster, second_cluster)
    out_ref[:, :width] = position
    out_ref[:, width:] = jnp.where(filled, cluster, -1)


def columns(row):
    return jnp.transpose(jnp.broadcast_to(row, (128, row.shape[1])))


def block_pair(left, right, sims_ref, left_meta, right_meta, row_ref, row_at, col_ref, col_at):
    left_pos, left_cluster = left_meta
    right_pos, right_cluster = right_meta
    sims_ref[...] = lax.dot_general(left, right, NT, preferred_element_type=F32)
    count, across = sims_ref.shape
    step = 128
    col = [jnp.zeros((8, 128), F32) for _ in range(across // 128)]
    for top in range(0, count, step):
        pos = left_pos[row_at + top : row_at + top + step, :]
        cluster = left_cluster[row_at + top : row_at + top + step, :]
        best = row_ref[row_at + top : row_at + top + step, :]
        for part in range(across // 128):
            lanes = slice(part * 128, part * 128 + 128)
            sims = sims_ref[top : top + step, lanes]
            sims = jnp.where(cluster == right_cluster[:, lanes], sims, 0.0)
            earlier = right_pos[:, lanes] < pos
            best = jnp.maximum(best, jnp.where(earlier, sims, 0.0))
            if col_ref is not None:
                later = jnp.where(earlier, 0.0, sims)
                col[part] = jnp.maximum(col[part], jnp.max(later.reshape(-1, 8, 128), axis=0))
        row_ref[row_at + top : row_at + top + step, :] = best
    if col_ref is not None:
        for part in range(across // 128):
            lanes = pl.ds(col_at + part * 128, 128)
            col_ref[:, lanes] = jnp.maximum(col_ref[:, lanes], col[part])


def place_meta(meta_ref, index, dead, pos_ref, cluster_ref):
    pos_ref[...] = columns(meta_ref[0, pl.ds(index, 1), :])
    cluster = meta_ref[1, pl.ds(index, 1), :]
    cluster_ref[...] = columns(jnp.where(cluster < 0, dead, cluster))


def row_result(row_ref):
    return jnp.max(jnp.transpose(row_ref[...]), axis=0, keepdims=True)


def col_result(col_ref):
    return jnp.max(col_ref[...], axis=0, keepdims=True)


def near_kernel(
    own0, own1, sib0, sib1, meta_ref, out_ref, sims, own_pos, own_cluster, own_row, own_col, sib_col
):
    index = lax.axis_index("grp")
    core = index % 2
    half = own0.shape[0]
    own, sib = (own0, own1), (sib0, sib1)
    place_meta(meta_ref, index, -2, own_pos, own_cluster)
    for ref in (own_row, own_col, sib_col):
        ref[...] = jnp.zeros(ref.shape, F32)
    left = (own_pos, own_cluster)
    for a, b in ((0, 0), (0, 1), (1, 1)):
        lanes = pl.ds(b * half, half)
        right = (meta_ref[0, pl.ds(index, 1), lanes], meta_ref[1, pl.ds(index, 1), lanes])
        block_pair(
            own[a][...], own[b][...], sims.at[(a + b) % 2], left, right, own_row, a * half,
            None if a == b else own_col, b * half,
        )
    other = index + 1 - 2 * core

    def with_sibling(flip):
        for a in range(2):
            b = a ^ flip
            lanes = pl.ds(b * half, half)
            right = (meta_ref[0, pl.ds(other, 1), lanes], meta_ref[1, pl.ds(other, 1), lanes])
            block_pair(
                own[a][...], sib[b][...], sims.at[a], left, right, own_row, a * half, sib_col, b * half
            )

    pl.when(core == 0)(lambda: with_sibling(0))
    pl.when(core == 1)(lambda: with_sibling(1))
    out_ref[0:1, :] = jnp.maximum(row_result(own_row), col_result(own_col))
    out_ref[1:2, :] = col_result(sib_col)


def far_kernel(
    pools, group, own0, own1, sib0, sib1, low0, low1, lows0, lows1, high0, high1, meta_ref, near_ref,
    out_ref, held, sems, sims, pos, clusters, rows, high_col, every,
):
    index = lax.axis_index("grp")
    chip = index // 2
    core = index % 2
    sources = [high0, own0, own1, sib0, sib1, high1, low0, low1, lows0, lows1]
    copies = []
    for n, source in enumerate(sources):
        copy = pltpu.make_async_copy(source, held.at[n], sems.at[n])
        copy.start()
        copies.append(copy)
    half = own0.shape[0]
    below = (index + group - 2) % group
    above = (index + 2) % group
    other = index + 1 - 2 * core
    below_other = below + 1 - 2 * core
    for n, cls in enumerate((index, other, below, below_other)):
        place_meta(meta_ref, cls, -2, pos.at[n], clusters.at[n])
    rows[...] = jnp.zeros(rows.shape, F32)
    high_col[...] = jnp.zeros(high_col.shape, F32)

    def pair(n, a, b, flight):
        lanes = pl.ds(b * half, half)
        right = (meta_ref[0, pl.ds(above, 1), lanes], meta_ref[1, pl.ds(above, 1), lanes])
        left = (pos.at[n], clusters.at[n])
        place = (1, 3, 6, 8)[n] + a
        block_pair(
            held[place], held[0 if b == 0 else 5], sims.at[flight % 2], left, right, rows.at[n],
            a * half, high_col, b * half,
        )

    copies[0].wait()
    for n in range(4):
        copies[1 + n].wait()
        pair(n // 2, n % 2, 0, n)
    copies[5].wait()
    for n in range(4):
        pair(n // 2, n % 2, 1, n)
    for n in range(6, 10):
        copies[n].wait()

    def distant(flip):
        for n in range(4):
            pair(2 + n // 2, n % 2, n % 2 ^ flip, n)

    first = (chip == 1) | (chip == 2)
    pl.when(first)(lambda: distant(0))
    pl.when(jnp.logical_not(first))(lambda: distant(1))
    every[...] = jnp.zeros(every.shape, F32)
    every[pl.ds(index, 1), :] = jnp.maximum(near_ref[0:1, :], row_result(rows.at[0]))
    every[pl.ds(other, 1), :] = jnp.maximum(near_ref[1:2, :], row_result(rows.at[1]))
    every[pl.ds(below, 1), :] = row_result(rows.at[2])
    every[pl.ds(below_other, 1), :] = row_result(rows.at[3])
    every[pl.ds(above, 1), :] = col_result(high_col)
    width = half // pools
    for p in range(pools):
        for h in range(CHUNKS):
            out_ref[p * group : (p + 1) * group, h * width : (h + 1) * width] = every[
                :, h * half + p * width : h * half + (p + 1) * width
            ]


def score_kernel(pools, group, places, table_ref, returned_ref, out_ref):
    rows_dev = out_ref.shape[1]
    arrived = jnp.transpose(
        jnp.concatenate([returned_ref[...], jnp.zeros_like(returned_ref)], axis=1)
    )
    table = table_ref[...]
    row = iota((8, rows_dev), 1)
    total = jnp.zeros((8, rows_dev), F32)
    for p in range(pools):
        for k in range(places):
            value = jnp.max(
                arrived[k * group : (k + 1) * group, p * group : (p + 1) * group],
                axis=1,
                keepdims=True,
            )
            entry = table[p * group : (p + 1) * group, k : k + 1]
            total = jnp.where(entry == row, value, total)
    out_ref[...] = jnp.sum(total, axis=0, keepdims=True)


def body(embeddings, members, valid, block_cluster):
    rows_dev, feature = embeddings.shape
    pools = lax.axis_size("pool")
    group = lax.axis_size("grp")
    devices = pools * group
    places = rows_dev // devices
    half = rows_dev // CHUNKS
    sds = jax.ShapeDtypeStruct
    valid_row = valid.reshape(1, -1)
    cluster_row = block_cluster.reshape(1, -1)

    table, out0 = pl.pallas_call(
        lambda *refs: table_kernel(pools, group, places, *refs),
        out_shape=(sds((devices, 128), I32), sds((half, feature), BF16)),
        scratch_shapes=[pltpu.VMEM((2 * devices, 128), F32)],
        compiler_params=PARAMS,
        name="table",
    )(members, valid_row, embeddings)
    out1 = pl.pallas_call(
        lambda *refs: rows_kernel(pools, places // CHUNKS, places // CHUNKS, *refs),
        out_shape=sds((half, feature), BF16),
        compiler_params=PARAMS,
        name="rows",
    )(table, embeddings)
    meta = pl.pallas_call(
        lambda *refs: meta_kernel(group, places, *refs),
        out_shape=sds((devices, 2 * group * places), I32),
        compiler_params=PARAMS,
        name="meta",
    )(members, valid_row, cluster_row)
    meta = (
        meta.reshape(pools, group, 2, CHUNKS, half // pools)
        .transpose(2, 1, 3, 0, 4)
        .reshape(2, group, rows_dev)
    )

    def shift(rows, by):
        return lax.ppermute(rows, "grp", [(g, (g + by) % group) for g in range(group)])

    def swap(rows):
        return lax.ppermute(rows, "grp", [(g, g ^ 1) for g in range(group)])

    own, sib, low, lows, high = [], [], [], [], []
    for out in (out0, out1):
        rows = lax.all_to_all(out, "pool", split_axis=0, concat_axis=0, tiled=True)
        own.append(rows)
        low.append(shift(rows, 2))
        high.append(shift(rows, -2))
        sib.append(swap(rows))
        lows.append(swap(low[-1]))

    near = pl.pallas_call(
        near_kernel,
        out_shape=sds((2, rows_dev), F32),
        scratch_shapes=[
            pltpu.VMEM((2, half, half), F32),
            pltpu.VMEM((rows_dev, 128), I32),
            pltpu.VMEM((rows_dev, 128), I32),
            pltpu.VMEM((rows_dev, 128), F32),
            pltpu.VMEM((8, rows_dev), F32),
            pltpu.VMEM((8, rows_dev), F32),
        ],
        compiler_params=PARAMS,
        cost_estimate=pl.CostEstimate(
            flops=5 * 2 * half * half * feature, bytes_accessed=4 * half * feature * 2, transcendentals=0
        ),
        name="near",
    )(*own, *sib, meta)
    hbm = pl.BlockSpec(memory_space=pl.ANY)
    vmem = pl.BlockSpec(memory_space=pltpu.VMEM)
    best = pl.pallas_call(
        lambda *refs: far_kernel(pools, group, *refs),
        out_shape=sds((devices, group * places), F32),
        in_specs=[hbm] * 10 + [vmem] * 2,
        scratch_shapes=[
            pltpu.VMEM((10, half, feature), BF16),
            pltpu.SemaphoreType.DMA((10,)),
            pltpu.VMEM((2, half, half), F32),
            pltpu.VMEM((4, rows_dev, 128), I32),
            pltpu.VMEM((4, rows_dev, 128), I32),
            pltpu.VMEM((4, rows_dev, 128), F32),
            pltpu.VMEM((8, rows_dev), F32),
            pltpu.VMEM((group, rows_dev), F32),
        ],
        compiler_params=PARAMS,
        cost_estimate=pl.CostEstimate(
            flops=12 * 2 * half * half * feature, bytes_accessed=10 * half * feature * 2, transcendentals=0
        ),
        name="far",
    )(*own, *sib, *low, *lows, *high, meta, near)
    returned = lax.all_to_all(best, ("pool", "grp"), split_axis=0, concat_axis=0, tiled=True)
    scores = pl.pallas_call(
        lambda *refs: score_kernel(pools, group, places, *refs),
        out_shape=sds((1, rows_dev), F32),
        compiler_params=PARAMS,
        name="score",
    )(table, returned)
    return scores.reshape(rows_dev)


def solution(mesh):
    in_specs = (P(("pool", "grp"), None), P(), P(), P())
    out_specs = P(("pool", "grp"))
    return jax.shard_map(body, mesh=mesh, in_specs=in_specs, out_specs=out_specs, check_vma=False)
```

time: 367 us -> 131 us (0.36)
  starting transfers between devices: 115 us -> 23.3 us
  waiting for transfers between devices: 116 us -> 37.4 us
  local copies, waits for them, and re-layouts: 52 us -> 3.88 us
  loops' own time: 42.3 us -> 0 us
  blocking collectives: 0 us -> 39.9 us
  Pallas kernels: 0 us -> 26.3 us
  other arithmetic: 17.6 us -> 0 us
  between operations: 13.8 us -> 0.13 us
  matrix products: 6.6 us -> 0 us
    all_to_all x2 -> x1, starting transfers between devices: 115 us -> 3.65 us  [body(): rows = lax.all_to_all(out, 'pool', split_axis=0, concat_axis=0, tiled=True)]
    all_gather x1 -> x0, waiting for transfers between devices: 78 us -> none  [body(): piece = lax.all_gather(own, 'grp', axis=0, tiled=True)]
    another operation x34 -> x0, loops' own time: 42.3 us -> none  [the longest x2 41.8 us: body(): updated.append(lax.fori_loop(0, piece_blocks, inner, carried[local_block]))]
    all_to_all x0 -> x2, blocking collectives: none -> 39.9 us  [the longest x1 24.7 us: body(): rows = lax.all_to_all(out, 'pool', split_axis=0, concat_axis=0, tiled=True)]
    all_to_all x2 -> x1, waiting for transfers between devices: 38.4 us -> 11.5 us  [body(): rows = lax.all_to_all(out, 'pool', split_axis=0, concat_axis=0, tiled=True)]
    pallas_call x0 -> x6, Pallas kernels: none -> 26.3 us  [the longest x1 11.5 us: body(): pl.pallas_call(lambda *refs: far_kernel(pools, group, *refs), out_shape=s...]
    ppermute x0 -> x8, waiting for transfers between devices: none -> 25.9 us  [the longest x4 25.9 us: shift(): lax.ppermute(rows, 'grp', [(g, (g + by) % group) for g in range(group)])]
    dynamic_slice x40 -> x0, local copies, waits for them, and re-layouts: 22.7 us -> none  [the longest x32 19.9 us: inner(): clusters[key_block] == clusters[query_block]]
  transfers between devices with their start and end apart: 3 -> 9, of which waited for: 3 -> 4; matrix products, arithmetic and copies ran while one was open for 1% -> 0% of each run, Pallas kernels for 0% -> 7%
where the time goes in v1:
time: 131 us
  blocking collectives  39.9 us (30%)
  waiting for transfers between devices  37.4 us (29%)
  Pallas kernels  26.3 us (20%)
  starting transfers between devices  23.3 us (18%)
  local copies, waits for them, and re-layouts  3.88 us (3%)
    ppermute x4, waiting for transfers between devices, shift(): lax.ppermute(rows, 'grp', [(g, (g + by) % group) for g in range(group)])  25.9 us
    all_to_all x1, blocking collectives, body(): rows = lax.all_to_all(out, 'pool', split_axis=0, concat_axis=0, tiled=True)  24.7 us
    all_to_all x1, blocking collectives, body(): lax.all_to_all(best, ('pool', 'grp'), split_axis=0, concat_axis=0, tiled=...  15.3 us
    ppermute x4, starting transfers between devices, swap(): return lax.ppermute(rows, 'grp', [(g, g ^ 1) for g in range(group)])  14.4 us
    all_to_all x1, waiting for transfers between devices, body(): rows = lax.all_to_all(out, 'pool', split_axis=0, concat_axis=0, tiled=True)  11.5 us
    pallas_call x1, Pallas kernels, body(): pl.pallas_call(lambda *refs: far_kernel(pools, group, *refs), out_shape=s...  11.5 us
    pallas_call x1, Pallas kernels, body(): pl.pallas_call(near_kernel, out_shape=sds((2, rows_dev), F32), scratch_sh...  5.55 us
    ppermute x4, starting transfers between devices, shift(): lax.ppermute(rows, 'grp', [(g, (g + by) % group) for g in range(group)])  5.26 us
  transfers between devices with their start and end apart: 9, of which 4 were waited for; matrix products, arithmetic and copies ran while one was open for 0% of the time, Pallas kernels for 7%

profile of v1, /device:TPU:1, one launch (start us, length us, event | category | flops | bytes accessed | tf_op | source)
XLA Modules:
  0.0 131.0 jit_solution(8349082323648393912)
XLA Ops:
  0.0 1.6 %copy-done = bf16[1024,1024]{1,0:T(8,128)(2,1)S(1)} copy-done((bf16[1024,1024]{1,0:T(8,128)(2,1)S(1)}, bf16[1024,1024]{1,0:T(8,128)(2,1)}, u32[]{:S(2)}) %copy-start) | copy-done | bytes 2097176
  1.6 1.0 copy-done.2
  2.6 0.7 copy-done.5
  3.3 2.5 %table.1 = (s32[128,128]{1,0:T(8,128)S(1)}, bf16[512,1024]{1,0:T(8,128)(2,1)S(1)}) custom-call(s32[256,512]{1,0:T(8,128)S(1)} %copy-done.2, s32[1,256]{1,0:T(1,128)S(1)} %bitcast.30, bf16[1024,1024]{1,0:T(8,128)(2,1)S(1)} %copy-done), custom_call_target="tpu_custom_call" | custom-call | tf_op jit(solution)/shard_map/table/pallas_call | solution.py:295
  5.9 1.4 %rows.1 = bf16[512,1024]{1,0:T(8,128)(2,1)S(1)} custom-call(s32[128,128]{1,0:T(8,128)S(1)} %get-tuple-element.7.refs_0_, bf16[1024,1024]{1,0:T(8,128)(2,1)S(1)} %copy-done.1), custom_call_target="tpu_custom_call" | custom-call | tf_op jit(solution)/shard_map/rows/pallas_call | solution.py:302
  7.3 0.0 copy-start.3
  7.3 0.0 copy-start.6
  7.3 0.0 copy-start.7
  7.3 24.7 %all_to_all.33 = bf16[16,32,1024]{2,1,0:T(8,128)(2,1)S(1)} all-to-all(bf16[16,32,1024]{2,1,0:T(8,128)(2,1)S(1)} %bitcast.16), channel_id=1, replica_groups=mesh['pool'=16,'grp'=8] {'pool'}, dimensions={0} | all-to-all | bytes 2097152 | tf_op jit(solution)/shard_map/all_to_all | solution.py:328
  32.0 3.7 %all-to-all-start = ((bf16[16,32,1024]{2,1,0:T(8,128)(2,1)}), bf16[16,32,1024]{2,1,0:T(8,128)(2,1)S(1)}, u32[]{:S(2)}, u32[]{:S(2)}) async-start(bf16[16,32,1024]{2,1,0:T(8,128)(2,1)} %bitcast.27), calls=%async_computation | async-start | bytes 2097152 | tf_op jit(solution)/shard_map/all_to_all | solution.py:328
  35.7 1.3 collective-permute-start.3
  37.0 2.3 %collective-permute-start.1 = (bf16[512,1024]{1,0:T(8,128)(2,1)S(1)}, bf16[512,1024]{1,0:T(8,128)(2,1)}, u32[]{:S(2)}, u32[]{:S(2)}) collective-permute-start(bf16[512,1024]{1,0:T(8,128)(2,1)S(1)} %bitcast.18), channel_id=1, source_target_pairs={{0,1},{1,0},{2,3},{3,2},{4,5},{5,4},{6,7},{7,6},{8,9},{9,8},{10,11... | collective-permute-start | bytes 3145736 | tf_op jit(solution)/shard_map/ppermute | solution.py:324
  39.2 11.5 %all-to-all-done = bf16[16,32,1024]{2,1,0:T(8,128)(2,1)S(1)} async-done(((bf16[16,32,1024]{2,1,0:T(8,128)(2,1)}), bf16[16,32,1024]{2,1,0:T(8,128)(2,1)S(1)}, u32[]{:S(2)}, u32[]{:S(2)}) %all-to-all-start) | async-done | bytes 1048608 | tf_op jit(solution)/shard_map/all_to_all | solution.py:328
  50.7 1.2 collective-permute-start.2
  51.9 3.6 %collective-permute-start = (bf16[512,1024]{1,0:T(8,128)(2,1)S(1)}, bf16[512,1024]{1,0:T(8,128)(2,1)}, u32[]{:S(2)}, u32[]{:S(2)}) collective-permute-start(bf16[512,1024]{1,0:T(8,128)(2,1)S(1)} %bitcast.23), channel_id=1, source_target_pairs={{0,1},{1,0},{2,3},{3,2},{4,5},{5,4},{6,7},{7,6},{8,9},{9,8},{10,11... | collective-permute-start | bytes 3145736 | tf_op jit(solution)/shard_map/ppermute | solution.py:324
  55.5 1.5 %collective-permute-start.7 = (bf16[512,1024]{1,0:T(8,128)(2,1)S(1)}, bf16[512,1024]{1,0:T(8,128)(2,1)}, u32[]{:S(2)}, u32[]{:S(2)}) collective-permute-start(bf16[512,1024]{1,0:T(8,128)(2,1)S(1)} %bitcast.19), channel_id=1, source_target_pairs={{0,6},{1,7},{2,0},{3,1},{4,2},{5,3},{6,4},{7,5},{8,14},{9,15},{10,... | collective-permute-start | bytes 3145736 | tf_op jit(solution)/shard_map/ppermute | solution.py:321
  57.0 2.8 %collective-permute-done.3.refs_5_ = bf16[512,1024]{1,0:T(8,128)(2,1)} collective-permute-done((bf16[512,1024]{1,0:T(8,128)(2,1)S(1)}, bf16[512,1024]{1,0:T(8,128)(2,1)}, u32[]{:S(2)}, u32[]{:S(2)}) %collective-permute-start.3) | collective-permute-done | bytes 1048608 | tf_op jit(solution)/shard_map/ppermute | solution.py:321
  59.7 1.3 collective-permute-start.6
  61.0 0.0 collective-permute-done.1.sib1.refs_3_
  61.0 5.7 %collective-permute-start.5 = (bf16[512,1024]{1,0:T(8,128)(2,1)}, bf16[512,1024]{1,0:T(8,128)(2,1)}, u32[]{:S(2)}, u32[]{:S(2)}) collective-permute-start(bf16[512,1024]{1,0:T(8,128)(2,1)} %collective-permute-done.3.refs_5_), channel_id=1, source_target_pairs={{0,1},{1,0},{2,3},{3,2},{4,5},{5,4},{6,7},{7,6},{8,9},{9,8},{10,11... | collective-permute-start | bytes 3145736 | tf_op jit(solution)/shard_map/ppermute | solution.py:324
  66.7 15.5 %collective-permute-done.2.refs_4_ = bf16[512,1024]{1,0:T(8,128)(2,1)} collective-permute-done((bf16[512,1024]{1,0:T(8,128)(2,1)S(1)}, bf16[512,1024]{1,0:T(8,128)(2,1)}, u32[]{:S(2)}, u32[]{:S(2)}) %collective-permute-start.2) | collective-permute-done | bytes 1048608 | tf_op jit(solution)/shard_map/ppermute | solution.py:321
  82.2 2.9 %collective-permute-start.4 = (bf16[512,1024]{1,0:T(8,128)(2,1)}, bf16[512,1024]{1,0:T(8,128)(2,1)}, u32[]{:S(2)}, u32[]{:S(2)}) collective-permute-start(bf16[512,1024]{1,0:T(8,128)(2,1)} %collective-permute-done.2.refs_4_), channel_id=1, source_target_pairs={{0,1},{1,0},{2,3},{3,2},{4,5},{5,4},{6,7},{7,6},{8,9},{9,8},{10,11... | collective-permute-start | bytes 3145736 | tf_op jit(solution)/shard_map/ppermute | solution.py:324
  85.1 4.0 %meta.1 = s32[128,128]{1,0:T(8,128)S(1)} custom-call(s32[256,512]{1,0:T(8,128)S(1)} %copy-done.3, s32[1,256]{1,0:T(1,128)S(1)} %bitcast.31, s32[1,256]{1,0:T(1,128)S(1)} %bitcast.32), custom_call_target="tpu_custom_call" | custom-call | tf_op jit(solution)/shard_map/meta/pallas_call | solution.py:308
  89.1 0.2 reshape.23
  89.3 0.2 copy.9
  89.5 0.1 reshape.24.meta_ref.refs_10_
  89.7 5.6 %near.1.refs_11_ = f32[2,1024]{1,0:T(2,128)S(1)} custom-call(bf16[512,1024]{1,0:T(8,128)(2,1)S(1)} %bitcast.25, bf16[512,1024]{1,0:T(8,128)(2,1)S(1)} %bitcast.20, bf16[512,1024]{1,0:T(8,128)(2,1)} %collective-permute-done.sib0.refs_2_, bf16[512,1024]{1,0:T(8,128)(2,1)} %collective-permute-done.1.sib1.refs_3_, s32[2,8,1024]{2,1,0:T(8,128)S(1)} %reshape.24.meta_ref.refs_10_), custom_call_target="tpu_custom_call" | custom-call | flops 2684354560 | bytes 4194304 | tf_op jit(solution)/shard_map/near/pallas_call | solution.py:335
  95.2 0.0 collective-permute-done.7.refs_9_
  95.2 7.6 %collective-permute-done.6.refs_8_ = bf16[512,1024]{1,0:T(8,128)(2,1)} collective-permute-done((bf16[512,1024]{1,0:T(8,128)(2,1)S(1)}, bf16[512,1024]{1,0:T(8,128)(2,1)}, u32[]{:S(2)}, u32[]{:S(2)}) %collective-permute-start.6) | collective-permute-done | bytes 1048608 | tf_op jit(solution)/shard_map/ppermute | solution.py:321
  102.9 11.5 %far.1 = f32[128,64]{1,0:T(8,128)S(1)} custom-call(bf16[512,1024]{1,0:T(8,128)(2,1)S(1)} %bitcast.26, bf16[512,1024]{1,0:T(8,128)(2,1)S(1)} %bitcast.21, bf16[512,1024]{1,0:T(8,128)(2,1)} %collective-permute-done.sib0.refs_2_, bf16[512,1024]{1,0:T(8,128)(2,1)} %collective-permute-done.1.sib1.refs_3_, bf16[512,1024]{1,0:T(8,128)(2,1)} %collective-permute-done.2.refs_4_, ...), custom_call_target="tpu_custom_call" | custom-call | flops 6442450944 | bytes 10485760 | tf_op jit(solution)/shard_map/far/pallas_call | solution.py:354
  114.3 15.3 %all_to_all.34 = f32[128,1,64]{2,1,0:T(1,128)S(1)} all-to-all(f32[128,1,64]{2,1,0:T(1,128)S(1)} %bitcast.29), channel_id=1, replica_groups=mesh['pool'=16,'grp'=8] {'pool','grp'}, dimensions={0} | all-to-all | bytes 65536 | tf_op jit(solution)/shard_map/all_to_all | solution.py:374
  129.6 1.4 %score.1 = f32[1,1024]{1,0:T(1,128)} custom-call(s32[128,128]{1,0:T(8,128)S(1)} %get-tuple-element.7.refs_0_, f32[128,64]{1,0:T(8,128)S(1)} %bitcast.28), custom_call_target="tpu_custom_call" | custom-call | tf_op jit(solution)/shard_map/score/pallas_call | solution.py:375
  (13 shorter events, 0.0 us)
Async XLA Ops:
  0.0 1.6 %copy-start = (bf16[1024,1024]{1,0:T(8,128)(2,1)S(1)}, bf16[1024,1024]{1,0:T(8,128)(2,1)}, u32[]{:S(2)}) copy-start(bf16[1024,1024]{1,0:T(8,128)(2,1)} %refs_1_.1) | copy-start | bytes 6291460
  1.6 1.0 copy-start.2
  2.6 0.7 copy-start.5
  3.3 2.6 %copy-start.1 = (bf16[1024,1024]{1,0:T(8,128)(2,1)S(1)}, bf16[1024,1024]{1,0:T(8,128)(2,1)}, u32[]{:S(2)}) copy-start(bf16[1024,1024]{1,0:T(8,128)(2,1)} %refs_1_.1) | copy-start | bytes 6291460
  5.9 26.1 %copy-start.4 = (bf16[512,1024]{1,0:T(8,128)(2,1)}, bf16[512,1024]{1,0:T(8,128)(2,1)S(1)}, u32[]{:S(2)}) copy-start(bf16[512,1024]{1,0:T(8,128)(2,1)S(1)} %get-tuple-element.8) | copy-start | bytes 3145732
  7.3 77.8 %copy-start.3 = (s32[256,512]{1,0:T(8,128)S(1)}, s32[256,512]{1,0:T(8,128)}, u32[]{:S(2)}) copy-start(s32[256,512]{1,0:T(8,128)} %refs_0_.3) | copy-start | bytes 1572868
  7.3 77.8 %copy-start.6 = (s32[256]{0:T(256)S(1)}, s32[256]{0:T(256)}, u32[]{:S(2)}) copy-start(s32[256]{0:T(256)} %param.6) | copy-start | bytes 3076
  7.3 77.8 %copy-start.7 = (s32[256]{0:T(256)S(1)}, s32[256]{0:T(256)}, u32[]{:S(2)}) copy-start(s32[256]{0:T(256)} %param.7) | copy-start | bytes 3076
  32.0 18.7 %all-to-all-start = ((bf16[16,32,1024]{2,1,0:T(8,128)(2,1)}), bf16[16,32,1024]{2,1,0:T(8,128)(2,1)S(1)}, u32[]{:S(2)}, u32[]{:S(2)}) async-start(bf16[16,32,1024]{2,1,0:T(8,128)(2,1)} %bitcast.27), calls=%async_computation | async-start | bytes 2097152 | tf_op jit(solution)/shard_map/all_to_all | solution.py:328
  35.7 24.1 %collective-permute-start.3 = (bf16[512,1024]{1,0:T(8,128)(2,1)S(1)}, bf16[512,1024]{1,0:T(8,128)(2,1)}, u32[]{:S(2)}, u32[]{:S(2)}) collective-permute-start(bf16[512,1024]{1,0:T(8,128)(2,1)S(1)} %bitcast.17), channel_id=1, source_target_pairs={{0,2},{1,3},{2,4},{3,5},{4,6},{5,7},{6,0},{7,1},{8,10},{9,11},{10,... | collective-permute-start | bytes 3145736 | tf_op jit(solution)/shard_map/ppermute | solution.py:321
  37.0 24.0 %collective-permute-start.1 = (bf16[512,1024]{1,0:T(8,128)(2,1)S(1)}, bf16[512,1024]{1,0:T(8,128)(2,1)}, u32[]{:S(2)}, u32[]{:S(2)}) collective-permute-start(bf16[512,1024]{1,0:T(8,128)(2,1)S(1)} %bitcast.18), channel_id=1, source_target_pairs={{0,1},{1,0},{2,3},{3,2},{4,5},{5,4},{6,7},{7,6},{8,9},{9,8},{10,11... | collective-permute-start | bytes 3145736 | tf_op jit(solution)/shard_map/ppermute | solution.py:324
  50.7 31.5 %collective-permute-start.2 = (bf16[512,1024]{1,0:T(8,128)(2,1)S(1)}, bf16[512,1024]{1,0:T(8,128)(2,1)}, u32[]{:S(2)}, u32[]{:S(2)}) collective-permute-start(bf16[512,1024]{1,0:T(8,128)(2,1)S(1)} %bitcast.22), channel_id=1, source_target_pairs={{0,2},{1,3},{2,4},{3,5},{4,6},{5,7},{6,0},{7,1},{8,10},{9,11},{10,... | collective-permute-start | bytes 3145736 | tf_op jit(solution)/shard_map/ppermute | solution.py:321
  51.9 37.7 %collective-permute-start = (bf16[512,1024]{1,0:T(8,128)(2,1)S(1)}, bf16[512,1024]{1,0:T(8,128)(2,1)}, u32[]{:S(2)}, u32[]{:S(2)}) collective-permute-start(bf16[512,1024]{1,0:T(8,128)(2,1)S(1)} %bitcast.23), channel_id=1, source_target_pairs={{0,1},{1,0},{2,3},{3,2},{4,5},{5,4},{6,7},{7,6},{8,9},{9,8},{10,11... | collective-permute-start | bytes 3145736 | tf_op jit(solution)/shard_map/ppermute | solution.py:324
  55.5 39.7 %collective-permute-start.7 = (bf16[512,1024]{1,0:T(8,128)(2,1)S(1)}, bf16[512,1024]{1,0:T(8,128)(2,1)}, u32[]{:S(2)}, u32[]{:S(2)}) collective-permute-start(bf16[512,1024]{1,0:T(8,128)(2,1)S(1)} %bitcast.19), channel_id=1, source_target_pairs={{0,6},{1,7},{2,0},{3,1},{4,2},{5,3},{6,4},{7,5},{8,14},{9,15},{10,... | collective-permute-start | bytes 3145736 | tf_op jit(solution)/shard_map/ppermute | solution.py:321
  59.7 43.1 %collective-permute-start.6 = (bf16[512,1024]{1,0:T(8,128)(2,1)S(1)}, bf16[512,1024]{1,0:T(8,128)(2,1)}, u32[]{:S(2)}, u32[]{:S(2)}) collective-permute-start(bf16[512,1024]{1,0:T(8,128)(2,1)S(1)} %bitcast.24), channel_id=1, source_target_pairs={{0,6},{1,7},{2,0},{3,1},{4,2},{5,3},{6,4},{7,5},{8,14},{9,15},{10,... | collective-permute-start | bytes 3145736 | tf_op jit(solution)/shard_map/ppermute | solution.py:321
  61.0 41.9 %collective-permute-start.5 = (bf16[512,1024]{1,0:T(8,128)(2,1)}, bf16[512,1024]{1,0:T(8,128)(2,1)}, u32[]{:S(2)}, u32[]{:S(2)}) collective-permute-start(bf16[512,1024]{1,0:T(8,128)(2,1)} %collective-permute-done.3.refs_5_), channel_id=1, source_target_pairs={{0,1},{1,0},{2,3},{3,2},{4,5},{5,4},{6,7},{7,6},{8,9},{9,8},{10,11... | collective-permute-start | bytes 3145736 | tf_op jit(solution)/shard_map/ppermute | solution.py:324
  82.2 20.7 %collective-permute-start.4 = (bf16[512,1024]{1,0:T(8,128)(2,1)}, bf16[512,1024]{1,0:T(8,128)(2,1)}, u32[]{:S(2)}, u32[]{:S(2)}) collective-permute-start(bf16[512,1024]{1,0:T(8,128)(2,1)} %collective-permute-done.2.refs_4_), channel_id=1, source_target_pairs={{0,1},{1,0},{2,3},{3,2},{4,5},{5,4},{6,7},{7,6},{8,9},{9,8},{10,11... | collective-permute-start | bytes 3145736 | tf_op jit(solution)/shard_map/ppermute | solution.py:324

commit v2 on v1

v2 whole, which is shorter than its diff:
```python
import jax
import jax.numpy as jnp
from jax import lax
from jax.experimental import pallas as pl
from jax.experimental.pallas import tpu as pltpu
from jax.sharding import PartitionSpec as P

EPS = 1e-06
F32 = jnp.float32
BF16 = jnp.bfloat16
I32 = jnp.int32
QUARTER = 256
CODE = 8192
NT = (((1,), (1,)), ((), ()))
PARAMS = pltpu.CompilerParams(vmem_limit_bytes=24 * 1024 * 1024)


def iota(shape, dim):
    return lax.broadcasted_iota(I32, shape, dim)


def normal_rows(rows):
    return (rows * lax.rsqrt(jnp.sum(rows * rows, axis=1, keepdims=True) + EPS)).astype(BF16)


def picked_rows(table, emb, first, count, pools):
    width = emb.shape[0]
    wanted = []
    for k in range(first, first + count):
        hit = table[:, k : k + 1] == iota((table.shape[0], width), 1)
        wanted.append(jnp.where(hit, 1.0, 0.0).reshape(pools, -1, width))
    choice = jnp.concatenate(wanted, axis=1).reshape(-1, width).astype(BF16)
    return normal_rows(jnp.dot(choice, emb, preferred_element_type=F32))


def table_kernel(
    pools, group, places, last, members_hbm, valid_hbm, emb_hbm, table_ref, main_ref, last_ref,
    members_ref, valid_ref, emb_ref, found_ref, sems,
):
    copies = []
    for n, (source, target) in enumerate(
        ((members_hbm, members_ref), (valid_hbm, valid_ref), (emb_hbm, emb_ref))
    ):
        copies.append(pltpu.make_async_copy(source, target, sems.at[n]))
        copies[-1].start()
    rows_dev = emb_ref.shape[0]
    device = lax.axis_index("pool") * group + lax.axis_index("grp")
    blocks, block_len = members_ref.shape
    devices = blocks // 2
    before = jnp.where(
        iota((block_len, block_len), 0) < iota((block_len, block_len), 1), 1.0, 0.0
    ).astype(BF16)
    at = iota((blocks, blocks), 1) == iota((blocks, blocks), 0)
    copies[0].wait()
    copies[1].wait()
    live = jnp.sum(jnp.where(at, valid_ref[...], 0), axis=1, keepdims=True)
    local = members_ref[...] - device * rows_dev
    mine = (local >= 0) & (local < rows_dev) & (iota((blocks, block_len), 1) < live)
    ones = jnp.where(mine, 1.0, 0.0)
    counts = jnp.broadcast_to(jnp.sum(ones, axis=1, keepdims=True), (blocks, 128))
    counts = jnp.where(iota((blocks, 128), 0) % 2 == 1, pltpu.roll(counts, 1, 0), 0.0)
    rank = jnp.dot(ones.astype(BF16), before, preferred_element_type=F32) + counts[:, :1]
    rank = jnp.where(mine, rank, -1.0)
    value = (local + 1).astype(F32)
    lane = iota((blocks, 128), 1)
    found = jnp.zeros((blocks, 128), F32)
    for k in range(places):
        entry = jnp.sum(jnp.where(rank == k, value, 0.0), axis=1, keepdims=True)
        found = jnp.where(lane == k, entry, found)
    found_ref[...] = found
    pair = found_ref[pl.ds(0, devices, stride=2), :] + found_ref[pl.ds(1, devices, stride=2), :]
    table = pair.astype(I32) - 1
    table_ref[...] = table
    copies[2].wait()
    last_ref[...] = picked_rows(table, emb_ref[...], places - last, last, pools)
    main_ref[...] = picked_rows(table, emb_ref[...], 0, places - last, pools)


def columns(row):
    return jnp.transpose(jnp.broadcast_to(row, (128, row.shape[1])))


def relatives():
    group = lax.axis_size("grp")
    index = lax.axis_index("grp")
    flip = 1 - 2 * (index % 2)
    below = (index + group - 2) % group
    return index, index + flip, below, below + flip, (index + 2) % group


def meta_kernel(
    group, places, last, members_hbm, valid_hbm, cluster_hbm, out_ref, codes_ref,
    members_ref, valid_ref, cluster_ref, sems,
):
    blocks = valid_ref.shape[1]
    block_len = members_ref.shape[1]
    pool = lax.axis_index("pool")
    first_block = pl.multiple_of(pool * 2 * group, 2 * group)
    copies = []
    for n, (source, target) in enumerate(
        (
            (members_hbm.at[pl.ds(first_block, 2 * group), :], members_ref),
            (valid_hbm, valid_ref),
            (cluster_hbm, cluster_ref),
        )
    ):
        copies.append(pltpu.make_async_copy(source, target, sems.at[n]))
        copies[-1].start()
    sources = blocks // 2
    slots = 2 * block_len
    width = group * places
    before = jnp.where(iota((slots, slots), 0) < iota((slots, slots), 1), 1.0, 0.0).astype(BF16)
    slot = iota((1, slots), 1)
    kind = iota((2 * width, slots), 0)
    kind_place = kind % width // group
    kind_owner = kind % group
    kind_value = jnp.where(kind < width, slot // 32, slot % 32 + 1)
    found = jnp.zeros((sources, 2 * width), F32)
    block_lane = iota((1, blocks), 1)
    lane = iota((1, width), 1)
    first_cluster = jnp.zeros((1, width), I32)
    second_cluster = jnp.zeros((1, width), I32)
    for copy in copies:
        copy.wait()
    for owner in range(group):
        halves, lives = [], []
        for half in range(2):
            halves.append(members_ref[2 * owner + half : 2 * owner + half + 1, :])
            at = block_lane == first_block + 2 * owner + half
            lives.append(jnp.sum(jnp.where(at, valid_ref[...], 0), axis=1, keepdims=True))
            cluster = jnp.sum(jnp.where(at, cluster_ref[...], 0), axis=1, keepdims=True)
            if half == 0:
                first_cluster = jnp.where(lane % group == owner, cluster, first_cluster)
            else:
                second_cluster = jnp.where(lane % group == owner, cluster, second_cluster)
        rows = jnp.concatenate(halves, axis=1)
        end = jnp.where(slot < block_len, lives[0], block_len + lives[1])
        origin = jnp.where(slot < end, rows // slots, -1)
        match = iota((sources, slots), 0) == origin
        ones = jnp.where(match, 1.0, 0.0).astype(BF16)
        ranks = jnp.dot(ones, before, preferred_element_type=F32)
        rank = jnp.sum(jnp.where(match, ranks, 0.0), axis=0, keepdims=True).astype(I32)
        weight = jnp.where((kind_owner == owner) & (kind_place == rank), kind_value, 0)
        found = found + lax.dot_general(
            ones, weight.astype(F32).astype(BF16), NT, preferred_element_type=F32
        )
    found = found.astype(I32)
    place = found[:, :width] * 32 + found[:, width:] - 1
    filled = found[:, width:] > 0
    position = jnp.where(filled, place + lane % group * slots, -1)
    cluster = jnp.where(filled, jnp.where(place < block_len, first_cluster, second_cluster), -1)
    main = (places - last) * group
    rest = last * group
    pools = sources // group
    for n, values in enumerate((position, cluster)):
        for p in range(pools):
            own = values[p * group : (p + 1) * group, :]
            out_ref[n, :, p * main : (p + 1) * main] = own[:, :main]
            at = pools * main + p * rest
            out_ref[n, :, at : at + rest] = own[:, main:]
    for n, cls in enumerate(relatives()[:4]):
        pos = out_ref[0, pl.ds(cls, 1), :]
        cluster = out_ref[1, pl.ds(cls, 1), :]
        codes_ref[n, :, :] = columns(jnp.where(cluster < 0, -2 * CODE, cluster * CODE + pos))


def run(pieces, sims_ref):
    for n in range(len(pieces) + 1):
        if n < len(pieces):
            piece = pieces[n]
            sims_ref[n % 2, : piece["count"], :] = lax.dot_general(
                piece["left"](), piece["right"](), NT, preferred_element_type=F32
            )
        if n > 0:
            take_maxima(sims_ref.at[(n - 1) % 2], **pieces[n - 1])


def take_maxima(sims_ref, left, right, count, codes, rows, start, pos_row, cluster_row, col, col_start, same):
    step = 128
    right_pos, right_cluster = pos_row(), cluster_row()
    parts = QUARTER // 128
    best_col = [jnp.zeros((8, 128), F32) for _ in range(parts)]
    for top in range(0, count, step):
        code = codes[start + top : start + top + step, :]
        pos = code & (CODE - 1)
        cluster = code >> 13
        best = rows[start + top : start + top + step, :]
        for part in range(parts):
            lanes = slice(part * 128, part * 128 + 128)
            sims = sims_ref[top : top + step, lanes]
            sims = jnp.where(cluster == right_cluster[:, lanes], sims, 0.0)
            earlier = right_pos[:, lanes] < pos
            best = jnp.maximum(best, jnp.where(earlier, sims, 0.0))
            if top < same:
                later = jnp.where(earlier, 0.0, sims)
                best_col[part] = jnp.maximum(
                    best_col[part], jnp.max(later.reshape(-1, 8, 128), axis=0)
                )
        rows[start + top : start + top + step, :] = best
    if same > 0:
        for part in range(parts):
            lanes = slice(col_start + part * 128, col_start + part * 128 + 128)
            col[:, lanes] = jnp.maximum(col[:, lanes], best_col[part])


def row_result(row_ref):
    return jnp.max(jnp.transpose(row_ref[...]), axis=0, keepdims=True)


def col_result(col_ref):
    return jnp.max(col_ref[...], axis=0, keepdims=True)


OWN, SIB, LOW, LOWS, HIGH = range(5)


class Tiles:
    def __init__(self, meta, codes, rows, cols, parts):
        self.meta, self.codes, self.rows, self.cols, self.parts = meta, codes, rows, cols, parts
        self.relatives = relatives()
        for ref in (rows, cols):
            ref[...] = jnp.zeros(ref.shape, F32)

    def load(self, cls, quarter, count=1):
        ref, at = self.parts[cls, quarter]
        if len(ref.shape) == 3:
            return ref[:, at : at + QUARTER // ref.shape[0], :].reshape(-1, ref.shape[2])
        return ref[at : at + count * QUARTER, :]

    def piece(self, left, quarter, count, right, right_quarter, same=None):
        lanes = slice(right_quarter * QUARTER, (right_quarter + 1) * QUARTER)
        cls = self.relatives[right]
        return dict(
            left=lambda: self.load(left, quarter, count),
            right=lambda: self.load(right, right_quarter),
            count=count * QUARTER,
            codes=self.codes.at[left],
            rows=self.rows.at[left],
            start=quarter * QUARTER,
            pos_row=lambda: self.meta[0, pl.ds(cls, 1), lanes],
            cluster_row=lambda: self.meta[1, pl.ds(cls, 1), lanes],
            col=self.cols.at[right],
            col_start=right_quarter * QUARTER,
            same=count * QUARTER if same is None else same,
        )

    def matched(self, flip, left, right, pairs):
        return [
            self.piece(left, a, 1, right, b) for a, b in pairs if (a + b) % 2 == flip
        ]

    def finish(self, before, out):
        for cls in range(5):
            best = col_result(self.cols.at[cls])
            if cls < HIGH:
                best = jnp.maximum(best, row_result(self.rows.at[cls]))
            if before is not None:
                best = jnp.maximum(best, before[cls : cls + 1, :])
            out[cls : cls + 1, :] = best


def either(flag, work):
    pl.when(flag)(lambda: work(1))
    pl.when(jnp.logical_not(flag))(lambda: work(0))


def second_core():
    return lax.axis_index("grp") % 2 == 1


def outer_chip():
    chip = lax.axis_index("grp") // 2
    return (chip == 0) | (chip == 3)


def quarters(*groups):
    parts = {}
    for cls, refs in groups:
        for quarter, ref, at in refs:
            parts[cls, quarter] = (ref, at)
    return parts


def whole(ref):
    return [(q, ref, q * QUARTER) for q in range(3)]


def near_kernel(own0, sib0, meta, codes, out, sims, rows, cols):
    tiles = Tiles(meta, codes, rows, cols, quarters((OWN, whole(own0)), (SIB, whole(sib0))))
    run([tiles.piece(OWN, 0, b + 1, OWN, b, same=b * QUARTER) for b in range(3)], sims)
    pairs = [(a, b) for b in range(3) for a in range(3)]
    either(second_core(), lambda flip: run(tiles.matched(flip, OWN, SIB, pairs), sims))
    tiles.finish(None, out)


def middle_kernel(
    own0, sib0, arrived, sib3, lows3, low0, low1, lows0, lows1, high0, high1, meta, codes, before,
    out, sims, rows, cols,
):
    tiles = Tiles(
        meta, codes, rows, cols,
        quarters(
            (OWN, whole(own0) + [(3, arrived, 0)]),
            (SIB, whole(sib0) + [(3, sib3, 0)]),
            (LOW, [(0, low0, 0), (1, low1, 0), (3, arrived, 16)]),
            (LOWS, [(0, lows0, 0), (1, lows1, 0), (3, lows3, 0)]),
            (HIGH, [(0, high0, 0), (1, high1, 0), (3, arrived, 32)]),
        ),
    )
    pieces = [tiles.piece(OWN, 0, 3, OWN, 3), tiles.piece(OWN, 3, 1, OWN, 3, same=0)]
    for b in (0, 1, 3):
        for cls in (OWN, SIB):
            pieces.append(tiles.piece(cls, 0, 3, HIGH, b))
            pieces.append(tiles.piece(cls, 3, 1, HIGH, b))
    run(pieces, sims)
    pairs = [(a, b) for b in range(4) for a in range(4) if 3 in (a, b)]
    either(second_core(), lambda flip: run(tiles.matched(flip, OWN, SIB, pairs), sims))
    pairs = [(a, b) for b in (0, 1, 3) for a in (0, 1, 3)]
    either(
        outer_chip(),
        lambda flip: run(
            tiles.matched(flip, LOW, HIGH, pairs) + tiles.matched(flip, LOWS, HIGH, pairs), sims
        ),
    )
    tiles.finish(before, out)


def late_kernel(
    own0, sib0, arrived, sib3, lows3, low0, low1, low2, lows0, lows1, high0, high1, high2, meta,
    codes, before, out, sims, rows, cols,
):
    tiles = Tiles(
        meta, codes, rows, cols,
        quarters(
            (OWN, whole(own0) + [(3, arrived, 0)]),
            (SIB, whole(sib0) + [(3, sib3, 0)]),
            (LOW, [(0, low0, 0), (1, low1, 0), (2, low2, 0), (3, arrived, 16)]),
            (LOWS, [(0, lows0, 0), (1, lows1, 0), (3, lows3, 0)]),
            (HIGH, [(0, high0, 0), (1, high1, 0), (2, high2, 0), (3, arrived, 32)]),
        ),
    )
    pieces = []
    for cls in (OWN, SIB):
        pieces.append(tiles.piece(cls, 0, 3, HIGH, 2))
        pieces.append(tiles.piece(cls, 3, 1, HIGH, 2))
    run(pieces, sims)
    pairs = [(a, b) for b in range(4) for a in range(4) if 2 in (a, b)]
    others = [(a, 2) for a in (0, 1, 3)]
    either(
        outer_chip(),
        lambda flip: run(
            tiles.matched(flip, LOW, HIGH, pairs) + tiles.matched(flip, LOWS, HIGH, others), sims
        ),
    )
    tiles.finish(before, out)


def last_kernel(
    pools, group, main, rest, arrived, lows2, high0, high1, high2, meta, codes, before,
    out, sims, rows, cols, best, every,
):
    tiles = Tiles(
        meta, codes, rows, cols,
        quarters(
            (LOWS, [(2, lows2, 0)]),
            (HIGH, [(0, high0, 0), (1, high1, 0), (2, high2, 0), (3, arrived, 32)]),
        ),
    )
    pairs = [(2, b) for b in range(4)]
    either(outer_chip(), lambda flip: run(tiles.matched(flip, LOWS, HIGH, pairs), sims))
    best[...] = before[...]
    span = slice(2 * QUARTER, 3 * QUARTER)
    found = jnp.max(jnp.transpose(rows[LOWS, span, :]), axis=0, keepdims=True)
    best[LOWS : LOWS + 1, span] = jnp.maximum(best[LOWS : LOWS + 1, span], found)
    best[HIGH : HIGH + 1, :] = jnp.maximum(best[HIGH : HIGH + 1, :], col_result(cols.at[HIGH]))
    every[...] = jnp.zeros(every.shape, F32)
    for cls, place in enumerate(tiles.relatives):
        every[pl.ds(place, 1), :] = best[cls : cls + 1, :]
    for p in range(pools):
        rows_out = slice(p * group, (p + 1) * group)
        out[rows_out, :main] = every[:, p * main : (p + 1) * main]
        at = pools * main + p * rest
        out[rows_out, main:] = every[:, at : at + rest]


def score_kernel(pools, group, places, table_ref, returned_ref, out_ref):
    rows_dev = out_ref.shape[1]
    arrived = jnp.transpose(
        jnp.concatenate([returned_ref[...], jnp.zeros_like(returned_ref)], axis=1)
    )
    table = table_ref[...]
    row = iota((8, rows_dev), 1)
    total = jnp.zeros((8, rows_dev), F32)
    for p in range(pools):
        for k in range(places):
            value = jnp.max(
                arrived[k * group : (k + 1) * group, p * group : (p + 1) * group],
                axis=1,
                keepdims=True,
            )
            entry = table[p * group : (p + 1) * group, k : k + 1]
            total = jnp.where(entry == row, value, total)
    out_ref[...] = jnp.sum(total, axis=0, keepdims=True)


def body(embeddings, members, valid, block_cluster):
    rows_dev, feature = embeddings.shape
    pools = lax.axis_size("pool")
    group = lax.axis_size("grp")
    devices = pools * group
    places = rows_dev // devices
    last = places // 4
    sds = jax.ShapeDtypeStruct
    hbm = pl.BlockSpec(memory_space=pltpu.HBM)
    valid_row = valid.reshape(1, -1)
    cluster_row = block_cluster.reshape(1, -1)
    blocks, block_len = members.shape

    table, main, rest = pl.pallas_call(
        lambda *refs: table_kernel(pools, group, places, last, *refs),
        out_shape=(
            sds((devices, 128), I32),
            sds((3 * QUARTER, feature), BF16),
            sds((QUARTER, feature), BF16),
        ),
        in_specs=[hbm] * 3,
        scratch_shapes=[
            pltpu.VMEM((blocks, block_len), I32),
            pltpu.VMEM((1, blocks), I32),
            pltpu.VMEM((rows_dev, feature), BF16),
            pltpu.VMEM((blocks, 128), F32),
            pltpu.SemaphoreType.DMA((3,)),
        ],
        compiler_params=PARAMS,
        cost_estimate=cost(rows_dev * rows_dev * feature),
        name="table",
    )(members, valid_row, embeddings)
    meta, codes = pl.pallas_call(
        lambda *refs: meta_kernel(group, places, last, *refs),
        out_shape=(sds((2, group, rows_dev), I32), sds((4, rows_dev, 128), I32)),
        in_specs=[hbm] * 3,
        scratch_shapes=[
            pltpu.VMEM((2 * group, block_len), I32),
            pltpu.VMEM((1, blocks), I32),
            pltpu.VMEM((1, blocks), I32),
            pltpu.SemaphoreType.DMA((3,)),
        ],
        compiler_params=PARAMS,
        cost_estimate=cost(2 * rows_dev**3),
        name="meta",
    )(members, valid_row, cluster_row)

    def shift(rows, by):
        return lax.ppermute(rows, "grp", [(g, (g + by) % group) for g in range(group)])

    def swap(rows):
        return lax.ppermute(rows, "grp", [(g, g ^ 1) for g in range(group)])

    def to_pools(rows):
        return lax.all_to_all(rows, "pool", split_axis=0, concat_axis=0, tiled=True)

    low_rest, high_rest = shift(rest, 2), shift(rest, -2)
    own0 = to_pools(main.reshape(pools, -1, feature)).reshape(-1, feature)
    sent = [part.reshape(pools, -1, feature) for part in (rest, low_rest, high_rest)]
    arrived = to_pools(jnp.concatenate(sent, axis=1))
    low, lows, high = [], [], []
    for q in range(3):
        part = own0[q * QUARTER : (q + 1) * QUARTER]
        low.append(shift(part, 2))
        high.append(shift(part, -2))
        lows.append(swap(low[-1]))
    sib0 = swap(own0)
    width = QUARTER // pools
    sib3 = swap(arrived[:, :width].reshape(-1, feature))
    lows3 = swap(arrived[:, width : 2 * width].reshape(-1, feature))

    def tiles(kernel, name, squares, operands, out_shape=(8, rows_dev), more=()):
        return pl.pallas_call(
            kernel,
            out_shape=sds(out_shape, F32),
            scratch_shapes=[
                pltpu.VMEM((2, 3 * QUARTER, QUARTER), F32),
                pltpu.VMEM((4, rows_dev, 128), F32),
                pltpu.VMEM((5, 8, rows_dev), F32),
                *more,
            ],
            compiler_params=PARAMS,
            cost_estimate=cost(squares * QUARTER * QUARTER * feature),
            name=name,
        )(*operands)

    near = tiles(near_kernel, "near", 11, (own0, sib0, meta, codes))
    middle = tiles(
        middle_kernel, "middle", 42,
        (own0, sib0, arrived, sib3, lows3, *low[:2], *lows[:2], *high[:2], meta, codes, near),
    )
    late = tiles(
        late_kernel, "late", 14,
        (own0, sib0, arrived, sib3, lows3, *low, *lows[:2], *high, meta, codes, middle),
    )
    best = tiles(
        lambda *refs: last_kernel(pools, group, group * (places - last), group * last, *refs),
        "last", 2, (arrived, lows[2], *high, meta, codes, late),
        out_shape=(devices, group * places),
        more=(pltpu.VMEM((8, rows_dev), F32), pltpu.VMEM((group, rows_dev), F32)),
    )
    returned = lax.all_to_all(best, ("pool", "grp"), split_axis=0, concat_axis=0, tiled=True)
    scores = pl.pallas_call(
        lambda *refs: score_kernel(pools, group, places, *refs),
        out_shape=sds((1, rows_dev), F32),
        compiler_params=PARAMS,
        name="score",
    )(table, returned)
    return scores.reshape(rows_dev)


def cost(products):
    return pl.CostEstimate(flops=2 * products, bytes_accessed=0, transcendentals=0)


def solution(mesh):
    in_specs = (P(("pool", "grp"), None), P(), P(), P())
    out_specs = P(("pool", "grp"))
    return jax.shard_map(body, mesh=mesh, in_specs=in_specs, out_specs=out_specs, check_vma=False)
```

time: 131 us -> 128 us (0.977)
  blocking collectives: 39.9 us -> 20.6 us
  Pallas kernels: 26.3 us -> 32.4 us
  starting transfers between devices: 23.3 us -> 28.8 us
  local copies, waits for them, and re-layouts: 3.88 us -> 5.58 us
  waiting for transfers between devices: 37.4 us -> 38.9 us
  other arithmetic: 0 us -> 1.33 us
    all_to_all x1 -> x0, blocking collectives: 24.7 us -> none  [body(): rows = lax.all_to_all(out, 'pool', split_axis=0, concat_axis=0, tiled=True)]
    all_to_all x1 -> x2, waiting for transfers between devices: 11.5 us -> 21.6 us  [to_pools(): return lax.all_to_all(rows, 'pool', split_axis=0, concat_axis=0, tiled=True)]
    ppermute x4 -> x6, starting transfers between devices: 14.4 us -> 4.8 us  [swap(): return lax.ppermute(rows, 'grp', [(g, g ^ 1) for g in range(group)])]
    all_to_all x1 -> x2, starting transfers between devices: 3.65 us -> 13.2 us  [to_pools(): return lax.all_to_all(rows, 'pool', split_axis=0, concat_axis=0, tiled=True)]
    ppermute x4 -> x8, waiting for transfers between devices: 25.9 us -> 17.3 us  [shift(): lax.ppermute(rows, 'grp', [(g, (g + by) % group) for g in range(group)])]
    pallas_call x5 -> x6, Pallas kernels: 25 us -> 31 us  [the longest x4 21.2 us: tiles(): pl.pallas_call(kernel, out_shape=sds(out_shape, F32), scratch_shapes=[plt...]
    ppermute x4 -> x8, starting transfers between devices: 5.26 us -> 10.8 us  [shift(): lax.ppermute(rows, 'grp', [(g, (g + by) % group) for g in range(group)])]
    all_to_all x1, blocking collectives: 15.3 us -> 20.6 us  [body(): lax.all_to_all(best, ('pool', 'grp'), split_axis=0, concat_axis=0, tiled=...]
  transfers between devices with their start and end apart: 9 -> 16, of which waited for: 4 -> 5; matrix products, arithmetic and copies ran while one was open for 0% -> 2% of each run, Pallas kernels for 7% -> 19%
where the time goes in v2:
time: 128 us
  waiting for transfers between devices  38.9 us (30%)
  Pallas kernels  32.4 us (25%)
  starting transfers between devices  28.8 us (22%)
  blocking collectives  20.6 us (16%)
  local copies, waits for them, and re-layouts  5.58 us (4%)
  other arithmetic  1.33 us (1%)
    all_to_all x2, waiting for transfers between devices, to_pools(): return lax.all_to_all(rows, 'pool', split_axis=0, concat_axis=0, tiled=True)  21.6 us
    pallas_call x4, Pallas kernels, tiles(): pl.pallas_call(kernel, out_shape=sds(out_shape, F32), scratch_shapes=[plt...  21.2 us
    all_to_all x1, blocking collectives, body(): lax.all_to_all(best, ('pool', 'grp'), split_axis=0, concat_axis=0, tiled=...  20.6 us
    ppermute x8, waiting for transfers between devices, shift(): lax.ppermute(rows, 'grp', [(g, (g + by) % group) for g in range(group)])  17.3 us
    all_to_all x2, starting transfers between devices, to_pools(): return lax.all_to_all(rows, 'pool', split_axis=0, concat_axis=0, tiled=True)  13.2 us
    ppermute x8, starting transfers between devices, shift(): lax.ppermute(rows, 'grp', [(g, (g + by) % group) for g in range(group)])  10.8 us
    pallas_call x1, Pallas kernels, body(): pl.pallas_call(lambda *refs: table_kernel(pools, group, places, last, *re...  4.93 us
    pallas_call x1, Pallas kernels, body(): pl.pallas_call(lambda *refs: meta_kernel(group, places, last, *refs), out...  4.84 us
  transfers between devices with their start and end apart: 16, of which 5 were waited for; matrix products, arithmetic and copies ran while one was open for 2% of the time, Pallas kernels for 19%

profile of v2, /device:TPU:1, one launch (start us, length us, event | category | flops | bytes accessed | tf_op | source)
XLA Modules:
  0.0 127.7 jit_solution(14748808169001577164)
XLA Ops:
  0.0 1.6 %copy-done = bf16[1024,1024]{1,0:T(8,128)(2,1)S(1)} copy-done((bf16[1024,1024]{1,0:T(8,128)(2,1)S(1)}, bf16[1024,1024]{1,0:T(8,128)(2,1)}, u32[]{:S(2)}) %copy-start) | copy-done | bytes 2097176
  1.6 1.0 copy-done.1
  2.6 0.7 copy-done.3
  3.3 4.9 %table.1 = (s32[128,128]{1,0:T(8,128)S(1)}, bf16[768,1024]{1,0:T(8,128)(2,1)}, bf16[256,1024]{1,0:T(8,128)(2,1)S(1)}) custom-call(s32[256,512]{1,0:T(8,128)S(1)} %copy-done.1, s32[1,256]{1,0:T(1,128)S(1)} %bitcast.22, bf16[1024,1024]{1,0:T(8,128)(2,1)S(1)} %copy-done), custom_call_target="tpu_custom_call" | custom-call | flops 2147483648 | tf_op jit(solution)/shard_map/table/pallas_call | solution.py:419
  8.3 8.6 %all-to-all-start.1 = ((bf16[16,48,1024]{2,1,0:T(8,128)(2,1)}), bf16[16,48,1024]{2,1,0:T(8,128)(2,1)S(1)}, u32[]{:S(2)}, u32[]{:S(2)}) async-start(bf16[16,48,1024]{2,1,0:T(8,128)(2,1)} %bitcast.4), calls=%async_computation.1 | async-start | bytes 3145728 | tf_op jit(solution)/shard_map/all_to_all | solution.py:460
  16.9 1.3 %collective-permute-start = (bf16[256,1024]{1,0:T(8,128)(2,1)S(1)}, bf16[256,1024]{1,0:T(8,128)(2,1)S(1)}, u32[]{:S(2)}, u32[]{:S(2)}) collective-permute-start(bf16[256,1024]{1,0:T(8,128)(2,1)S(1)} %get-tuple-element.11), channel_id=1, source_target_pairs={{0,2},{1,3},{2,4},{3,5},{4,6},{5,7},{6,0},{7,1},{8,10},{9,11},{10,... | collective-permute-start | bytes 1572872 | tf_op jit(solution)/shard_map/ppermute | solution.py:454
  18.2 1.5 %collective-permute-start.1 = (bf16[256,1024]{1,0:T(8,128)(2,1)S(1)}, bf16[256,1024]{1,0:T(8,128)(2,1)S(1)}, u32[]{:S(2)}, u32[]{:S(2)}) collective-permute-start(bf16[256,1024]{1,0:T(8,128)(2,1)S(1)} %get-tuple-element.11), channel_id=1, source_target_pairs={{0,6},{1,7},{2,0},{3,1},{4,2},{5,3},{6,4},{7,5},{8,14},{9,15},{10,... | collective-permute-start | bytes 1572872 | tf_op jit(solution)/shard_map/ppermute | solution.py:454
  19.6 11.0 %collective-permute-done = bf16[256,1024]{1,0:T(8,128)(2,1)S(1)} collective-permute-done((bf16[256,1024]{1,0:T(8,128)(2,1)S(1)}, bf16[256,1024]{1,0:T(8,128)(2,1)S(1)}, u32[]{:S(2)}, u32[]{:S(2)}) %collective-permute-start) | collective-permute-done | bytes 524320 | tf_op jit(solution)/shard_map/ppermute | solution.py:454
  30.6 1.3 %pad_maximum_fusion = bf16[16,48,1024]{2,1,0:T(8,128)(2,1)} fusion(bf16[16,16,1024]{2,1,0:T(8,128)(2,1)S(1)} %bitcast.28, bf16[16,16,1024]{2,1,0:T(8,128)(2,1)S(1)} %bitcast.27, bf16[16,16,1024]{2,1,0:T(8,128)(2,1)S(1)} %bitcast.19), kind=kLoop, calls=%fused_computation | loop fusion | flops 4718592 | bytes 3145728 | tf_op jit(solution)/shard_map/concatenate | solution.py:465
  32.0 7.8 %all-to-all-done.1 = bf16[16,48,1024]{2,1,0:T(8,128)(2,1)S(1)} async-done(((bf16[16,48,1024]{2,1,0:T(8,128)(2,1)}), bf16[16,48,1024]{2,1,0:T(8,128)(2,1)S(1)}, u32[]{:S(2)}, u32[]{:S(2)}) %all-to-all-start.1) | async-done | bytes 1572896 | tf_op jit(solution)/shard_map/all_to_all | solution.py:460
  39.8 4.6 %all-to-all-start = ((bf16[16,48,1024]{2,1,0:T(8,128)(2,1)}), bf16[16,48,1024]{2,1,0:T(8,128)(2,1)S(1)}, u32[]{:S(2)}, u32[]{:S(2)}) async-start(bf16[16,48,1024]{2,1,0:T(8,128)(2,1)} %pad_maximum_fusion), calls=%async_computation | async-start | bytes 3145728 | tf_op jit(solution)/shard_map/all_to_all | solution.py:460
  44.3 1.8 %collective-permute-start.7 = (bf16[768,1024]{1,0:T(8,128)(2,1)S(1)}, bf16[768,1024]{1,0:T(8,128)(2,1)}, u32[]{:S(2)}, u32[]{:S(2)}) collective-permute-start(bf16[768,1024]{1,0:T(8,128)(2,1)S(1)} %bitcast.14), channel_id=1, source_target_pairs={{0,1},{1,0},{2,3},{3,2},{4,5},{5,4},{6,7},{7,6},{8,9},{9,8},{10,11... | collective-permute-start | bytes 4718600 | tf_op jit(solution)/shard_map/ppermute | solution.py:457
  46.1 1.2 fusion.1
  47.3 1.2 collective-permute-start.10
  48.5 1.2 collective-permute-start.11
  49.8 1.5 %collective-permute-start.4 = (bf16[256,1024]{1,0:T(8,128)(2,1)}, bf16[256,1024]{1,0:T(8,128)(2,1)}, u32[]{:S(2)}, u32[]{:S(2)}) collective-permute-start(bf16[256,1024]{1,0:T(8,128)(2,1)} %get-tuple-element.18), channel_id=1, source_target_pairs={{0,6},{1,7},{2,0},{3,1},{4,2},{5,3},{6,4},{7,5},{8,14},{9,15},{10,... | collective-permute-start | bytes 1572872 | tf_op jit(solution)/shard_map/ppermute | solution.py:454
  51.2 0.2 collective-permute-start.5
  51.5 13.8 %all-to-all-done.arrived.refs_0_ = bf16[16,48,1024]{2,1,0:T(8,128)(2,1)S(1)} async-done(((bf16[16,48,1024]{2,1,0:T(8,128)(2,1)}), bf16[16,48,1024]{2,1,0:T(8,128)(2,1)S(1)}, u32[]{:S(2)}, u32[]{:S(2)}) %all-to-all-start) | async-done | bytes 1572896 | tf_op jit(solution)/shard_map/all_to_all | solution.py:460
  65.3 1.0 copy-done.6
  66.3 1.2 collective-permute-start.2
  67.5 6.1 %collective-permute-done.11.low1 = bf16[256,1024]{1,0:T(8,128)(2,1)} collective-permute-done((bf16[256,1024]{1,0:T(8,128)(2,1)}, bf16[256,1024]{1,0:T(8,128)(2,1)}, u32[]{:S(2)}, u32[]{:S(2)}) %collective-permute-start.11) | collective-permute-done | bytes 524320 | tf_op jit(solution)/shard_map/ppermute | solution.py:454
  73.6 1.2 collective-permute-start.8
  74.8 0.8 collective-permute-start.12
  75.8 4.8 %meta.1 = (s32[2,8,1024]{2,1,0:T(8,128)S(1)}, s32[4,1024,128]{2,1,0:T(8,128)S(1)}) custom-call(s32[256,512]{1,0:T(8,128)S(1)} %copy-done.2, s32[1,256]{1,0:T(1,128)S(1)} %bitcast.23, s32[1,256]{1,0:T(1,128)S(1)} %bitcast.24), custom_call_target="tpu_custom_call" | custom-call | flops 4294967296 | tf_op jit(solution)/shard_map/meta/pallas_call | solution.py:438
  80.6 4.1 %near.1.before = f32[8,1024]{1,0:T(8,128)S(1)} custom-call(bf16[768,1024]{1,0:T(8,128)(2,1)S(1)} %bitcast.16, bf16[768,1024]{1,0:T(8,128)(2,1)} %collective-permute-done.7.sib0, s32[2,8,1024]{2,1,0:T(8,128)S(1)} %get-tuple-element.13.meta.refs_5_, s32[4,1024,128]{2,1,0:T(8,128)S(1)} %get-tuple-element.14.codes.refs_6_), custom_call_target="tpu_custom_call" | custom-call | flops 1476395008 | tf_op jit(solution)/shard_map/near/pallas_call | solution.py:478
  84.7 2.7 %collective-permute-start.6 = (bf16[256,1024]{1,0:T(8,128)(2,1)S(1)}, bf16[256,1024]{1,0:T(8,128)(2,1)S(1)}, u32[]{:S(2)}, u32[]{:S(2)}) collective-permute-start(bf16[256,1024]{1,0:T(8,128)(2,1)S(1)} %copy-done.6), channel_id=1, source_target_pairs={{0,6},{1,7},{2,0},{3,1},{4,2},{5,3},{6,4},{7,5},{8,14},{9,15},{10,... | collective-permute-start | bytes 1572872 | tf_op jit(solution)/shard_map/ppermute | solution.py:454
  87.4 0.9 collective-permute-start.3
  88.3 9.5 %middle.1.before = f32[8,1024]{1,0:T(8,128)S(1)} custom-call(bf16[768,1024]{1,0:T(8,128)(2,1)S(1)} %bitcast.17, bf16[768,1024]{1,0:T(8,128)(2,1)} %collective-permute-done.7.sib0, bf16[16,48,1024]{2,1,0:T(8,128)(2,1)S(1)} %all-to-all-done.arrived.refs_0_, bf16[256,1024]{1,0:T(8,128)(2,1)S(1)} %collective-permute-done.8.sib3, ...), custom_call_target="tpu_custom_call" | custom-call | flops 5637144576 | tf_op jit(solution)/shard_map/middle/pallas_call | solution.py:478
  98.0 5.7 %late.1.refs_7_ = f32[8,1024]{1,0:T(8,128)S(1)} custom-call(bf16[768,1024]{1,0:T(8,128)(2,1)S(1)} %bitcast.18, bf16[768,1024]{1,0:T(8,128)(2,1)} %collective-permute-done.7.sib0, bf16[16,48,1024]{2,1,0:T(8,128)(2,1)S(1)} %all-to-all-done.arrived.refs_0_, bf16[256,1024]{1,0:T(8,128)(2,1)S(1)} %collective-permute-done.8.sib3, ...), custom_call_target="tpu_custom_call" | custom-call | flops 1879048192 | tf_op jit(solution)/shard_map/late/pallas_call | solution.py:478
  103.7 2.0 %last.1 = f32[128,64]{1,0:T(8,128)S(1)} custom-call(bf16[16,48,1024]{2,1,0:T(8,128)(2,1)S(1)} %all-to-all-done.arrived.refs_0_, bf16[256,1024]{1,0:T(8,128)(2,1)S(1)} %collective-permute-done.3.refs_1_, bf16[256,1024]{1,0:T(8,128)(2,1)} %collective-permute-done.4.high0.refs_2_, bf16[256,1024]{1,0:T(8,128)(2,1)} %collective-permute-done.5.high1.refs_3_, ...), custom_call_target="tpu_custom_call" | custom-call | flops 268435456 | tf_op jit(solution)/shard_map/last/pallas_call | solution.py:478
  105.7 20.6 %all_to_all.21 = f32[128,1,64]{2,1,0:T(1,128)S(1)} all-to-all(f32[128,1,64]{2,1,0:T(1,128)S(1)} %bitcast.20), channel_id=1, replica_groups=mesh['pool'=16,'grp'=8] {'pool','grp'}, dimensions={0} | all-to-all | bytes 65536 | tf_op jit(solution)/shard_map/all_to_all | solution.py:507
  126.3 1.4 %score.1 = f32[1,1024]{1,0:T(1,128)} custom-call(s32[128,128]{1,0:T(8,128)S(1)} %get-tuple-element.10.refs_0_, f32[128,64]{1,0:T(8,128)S(1)} %bitcast.21), custom_call_target="tpu_custom_call" | custom-call | tf_op jit(solution)/shard_map/score/pallas_call | solution.py:508
  (25 shorter events, 0.4 us)
Async XLA Ops:
  0.0 1.6 %copy-start = (bf16[1024,1024]{1,0:T(8,128)(2,1)S(1)}, bf16[1024,1024]{1,0:T(8,128)(2,1)}, u32[]{:S(2)}) copy-start(bf16[1024,1024]{1,0:T(8,128)(2,1)} %refs_2_.1) | copy-start | bytes 6291460
  1.6 1.0 copy-start.1
  2.6 0.7 copy-start.3
  8.3 31.5 %all-to-all-start.1 = ((bf16[16,48,1024]{2,1,0:T(8,128)(2,1)}), bf16[16,48,1024]{2,1,0:T(8,128)(2,1)S(1)}, u32[]{:S(2)}, u32[]{:S(2)}) async-start(bf16[16,48,1024]{2,1,0:T(8,128)(2,1)} %bitcast.4), calls=%async_computation.1 | async-start | bytes 3145728 | tf_op jit(solution)/shard_map/all_to_all | solution.py:460
  16.9 13.8 %collective-permute-start = (bf16[256,1024]{1,0:T(8,128)(2,1)S(1)}, bf16[256,1024]{1,0:T(8,128)(2,1)S(1)}, u32[]{:S(2)}, u32[]{:S(2)}) collective-permute-start(bf16[256,1024]{1,0:T(8,128)(2,1)S(1)} %get-tuple-element.11), channel_id=1, source_target_pairs={{0,2},{1,3},{2,4},{3,5},{4,6},{5,7},{6,0},{7,1},{8,10},{9,11},{10,... | collective-permute-start | bytes 1572872 | tf_op jit(solution)/shard_map/ppermute | solution.py:454
  18.2 12.5 %collective-permute-start.1 = (bf16[256,1024]{1,0:T(8,128)(2,1)S(1)}, bf16[256,1024]{1,0:T(8,128)(2,1)S(1)}, u32[]{:S(2)}, u32[]{:S(2)}) collective-permute-start(bf16[256,1024]{1,0:T(8,128)(2,1)S(1)} %get-tuple-element.11), channel_id=1, source_target_pairs={{0,6},{1,7},{2,0},{3,1},{4,2},{5,3},{6,4},{7,5},{8,14},{9,15},{10,... | collective-permute-start | bytes 1572872 | tf_op jit(solution)/shard_map/ppermute | solution.py:454
  39.8 25.5 %all-to-all-start = ((bf16[16,48,1024]{2,1,0:T(8,128)(2,1)}), bf16[16,48,1024]{2,1,0:T(8,128)(2,1)S(1)}, u32[]{:S(2)}, u32[]{:S(2)}) async-start(bf16[16,48,1024]{2,1,0:T(8,128)(2,1)} %pad_maximum_fusion), calls=%async_computation | async-start | bytes 3145728 | tf_op jit(solution)/shard_map/all_to_all | solution.py:460
  44.3 31.3 %collective-permute-start.7 = (bf16[768,1024]{1,0:T(8,128)(2,1)S(1)}, bf16[768,1024]{1,0:T(8,128)(2,1)}, u32[]{:S(2)}, u32[]{:S(2)}) collective-permute-start(bf16[768,1024]{1,0:T(8,128)(2,1)S(1)} %bitcast.14), channel_id=1, source_target_pairs={{0,1},{1,0},{2,3},{3,2},{4,5},{5,4},{6,7},{7,6},{8,9},{9,8},{10,11... | collective-permute-start | bytes 4718600 | tf_op jit(solution)/shard_map/ppermute | solution.py:457
  47.3 28.4 %copy-start.4 = (s32[256]{0:T(256)S(1)}, s32[256]{0:T(256)}, u32[]{:S(2)}) copy-start(s32[256]{0:T(256)} %param.6) | copy-start | bytes 3076
  47.3 28.4 %copy-start.5 = (s32[256]{0:T(256)S(1)}, s32[256]{0:T(256)}, u32[]{:S(2)}) copy-start(s32[256]{0:T(256)} %param.7) | copy-start | bytes 3076
  47.3 18.0 %collective-permute-start.10 = (bf16[256,1024]{1,0:T(8,128)(2,1)}, bf16[256,1024]{1,0:T(8,128)(2,1)}, u32[]{:S(2)}, u32[]{:S(2)}) collective-permute-start(bf16[256,1024]{1,0:T(8,128)(2,1)} %get-tuple-element.18), channel_id=1, source_target_pairs={{0,2},{1,3},{2,4},{3,5},{4,6},{5,7},{6,0},{7,1},{8,10},{9,11},{10,... | collective-permute-start | bytes 1572872 | tf_op jit(solution)/shard_map/ppermute | solution.py:454
  48.5 25.1 %collective-permute-start.11 = (bf16[256,1024]{1,0:T(8,128)(2,1)}, bf16[256,1024]{1,0:T(8,128)(2,1)}, u32[]{:S(2)}, u32[]{:S(2)}) collective-permute-start(bf16[256,1024]{1,0:T(8,128)(2,1)} %get-tuple-element.17), channel_id=1, source_target_pairs={{0,2},{1,3},{2,4},{3,5},{4,6},{5,7},{6,0},{7,1},{8,10},{9,11},{10,... | collective-permute-start | bytes 1572872 | tf_op jit(solution)/shard_map/ppermute | solution.py:454
  49.8 25.1 %collective-permute-start.4 = (bf16[256,1024]{1,0:T(8,128)(2,1)}, bf16[256,1024]{1,0:T(8,128)(2,1)}, u32[]{:S(2)}, u32[]{:S(2)}) collective-permute-start(bf16[256,1024]{1,0:T(8,128)(2,1)} %get-tuple-element.18), channel_id=1, source_target_pairs={{0,6},{1,7},{2,0},{3,1},{4,2},{5,3},{6,4},{7,5},{8,14},{9,15},{10,... | collective-permute-start | bytes 1572872 | tf_op jit(solution)/shard_map/ppermute | solution.py:454
  51.2 23.6 %collective-permute-start.5 = (bf16[256,1024]{1,0:T(8,128)(2,1)}, bf16[256,1024]{1,0:T(8,128)(2,1)}, u32[]{:S(2)}, u32[]{:S(2)}) collective-permute-start(bf16[256,1024]{1,0:T(8,128)(2,1)} %get-tuple-element.17), channel_id=1, source_target_pairs={{0,6},{1,7},{2,0},{3,1},{4,2},{5,3},{6,4},{7,5},{8,14},{9,15},{10,... | collective-permute-start | bytes 1572872 | tf_op jit(solution)/shard_map/ppermute | solution.py:454
  65.2 1.0 copy-start.6
  65.2 10.5 %copy-start.2 = (s32[256,512]{1,0:T(8,128)S(1)}, s32[256,512]{1,0:T(8,128)}, u32[]{:S(2)}) copy-start(s32[256,512]{1,0:T(8,128)} %refs_0_.3) | copy-start | bytes 1572868
  66.3 18.4 %collective-permute-start.2 = (bf16[256,1024]{1,0:T(8,128)(2,1)S(1)}, bf16[256,1024]{1,0:T(8,128)(2,1)S(1)}, u32[]{:S(2)}, u32[]{:S(2)}) collective-permute-start(bf16[256,1024]{1,0:T(8,128)(2,1)S(1)} %copy-done.6), channel_id=1, source_target_pairs={{0,2},{1,3},{2,4},{3,5},{4,6},{5,7},{6,0},{7,1},{8,10},{9,11},{10,... | collective-permute-start | bytes 1572872 | tf_op jit(solution)/shard_map/ppermute | solution.py:454
  73.6 13.7 %collective-permute-start.8 = (bf16[256,1024]{1,0:T(8,128)(2,1)S(1)}, bf16[256,1024]{1,0:T(8,128)(2,1)S(1)}, u32[]{:S(2)}, u32[]{:S(2)}) collective-permute-start(bf16[256,1024]{1,0:T(8,128)(2,1)S(1)} %bitcast.26), channel_id=1, source_target_pairs={{0,1},{1,0},{2,3},{3,2},{4,5},{5,4},{6,7},{7,6},{8,9},{9,8},{10,11... | collective-permute-start | bytes 1572872 | tf_op jit(solution)/shard_map/ppermute | solution.py:457
  74.8 13.5 %collective-permute-start.9 = (bf16[256,1024]{1,0:T(8,128)(2,1)S(1)}, bf16[256,1024]{1,0:T(8,128)(2,1)S(1)}, u32[]{:S(2)}, u32[]{:S(2)}) collective-permute-start(bf16[256,1024]{1,0:T(8,128)(2,1)S(1)} %bitcast.25), channel_id=1, source_target_pairs={{0,1},{1,0},{2,3},{3,2},{4,5},{5,4},{6,7},{7,6},{8,9},{9,8},{10,11... | collective-permute-start | bytes 1572872 | tf_op jit(solution)/shard_map/ppermute | solution.py:457
  74.8 13.5 %collective-permute-start.12 = (bf16[256,1024]{1,0:T(8,128)(2,1)}, bf16[256,1024]{1,0:T(8,128)(2,1)S(1)}, u32[]{:S(2)}, u32[]{:S(2)}) collective-permute-start(bf16[256,1024]{1,0:T(8,128)(2,1)} %collective-permute-done.10.low0), channel_id=1, source_target_pairs={{0,1},{1,0},{2,3},{3,2},{4,5},{5,4},{6,7},{7,6},{8,9},{9,8},{10,11... | collective-permute-start | bytes 1572872 | tf_op jit(solution)/shard_map/ppermute | solution.py:457
  75.7 12.7 %collective-permute-start.13 = (bf16[256,1024]{1,0:T(8,128)(2,1)}, bf16[256,1024]{1,0:T(8,128)(2,1)S(1)}, u32[]{:S(2)}, u32[]{:S(2)}) collective-permute-start(bf16[256,1024]{1,0:T(8,128)(2,1)} %collective-permute-done.11.low1), channel_id=1, source_target_pairs={{0,1},{1,0},{2,3},{3,2},{4,5},{5,4},{6,7},{7,6},{8,9},{9,8},{10,11... | collective-permute-start | bytes 1572872 | tf_op jit(solution)/shard_map/ppermute | solution.py:457
  84.7 13.3 %collective-permute-start.6 = (bf16[256,1024]{1,0:T(8,128)(2,1)S(1)}, bf16[256,1024]{1,0:T(8,128)(2,1)S(1)}, u32[]{:S(2)}, u32[]{:S(2)}) collective-permute-start(bf16[256,1024]{1,0:T(8,128)(2,1)S(1)} %copy-done.6), channel_id=1, source_target_pairs={{0,6},{1,7},{2,0},{3,1},{4,2},{5,3},{6,4},{7,5},{8,14},{9,15},{10,... | collective-permute-start | bytes 1572872 | tf_op jit(solution)/shard_map/ppermute | solution.py:454
  87.4 16.3 %collective-permute-start.3 = (bf16[256,1024]{1,0:T(8,128)(2,1)S(1)}, bf16[256,1024]{1,0:T(8,128)(2,1)S(1)}, u32[]{:S(2)}, u32[]{:S(2)}) collective-permute-start(bf16[256,1024]{1,0:T(8,128)(2,1)S(1)} %collective-permute-done.2.low2), channel_id=1, source_target_pairs={{0,1},{1,0},{2,3},{3,2},{4,5},{5,4},{6,7},{7,6},{8,9},{9,8},{10,11... | collective-permute-start | bytes 1572872 | tf_op jit(solution)/shard_map/ppermute | solution.py:457

commit v3 on v2

--- a/solution.py
+++ b/solution.py
@@ -12,7 +12,8 @@
 QUARTER = 256
 CODE = 8192
 NT = (((1,), (1,)), ((), ()))
-PARAMS = pltpu.CompilerParams(vmem_limit_bytes=24 * 1024 * 1024)
+PARAMS = pltpu.CompilerParams(vmem_limit_bytes=20 * 1024 * 1024)
+TABLE_PARAMS = pltpu.CompilerParams(vmem_limit_bytes=62 * 1024 * 1024)
 
 
 def iota(shape, dim):
@@ -34,7 +35,7 @@
 
 
 def table_kernel(
-    pools, group, places, last, members_hbm, valid_hbm, emb_hbm, table_ref, main_ref, last_ref,
+    pools, group, places, last, members_hbm, valid_hbm, emb_hbm, table_ref, main_ref,
     members_ref, valid_ref, emb_ref, found_ref, sems,
 ):
     copies = []
@@ -72,12 +73,12 @@
     table = pair.astype(I32) - 1
     table_ref[...] = table
     copies[2].wait()
-    last_ref[...] = picked_rows(table, emb_ref[...], places - last, last, pools)
     main_ref[...] = picked_rows(table, emb_ref[...], 0, places - last, pools)
 
 
-def columns(row):
-    return jnp.transpose(jnp.broadcast_to(row, (128, row.shape[1])))
+def rest_kernel(pools, places, last, table_ref, emb_ref, after, out):
+    del after
+    out[...] = picked_rows(table_ref[...], emb_ref[...], places - last, last, pools)
 
 
 def relatives():
@@ -90,7 +91,7 @@
 
 def meta_kernel(
     group, places, last, members_hbm, valid_hbm, cluster_hbm, out_ref, codes_ref,
-    members_ref, valid_ref, cluster_ref, sems,
+    members_ref, valid_ref, cluster_ref, packed_ref, sems,
 ):
     blocks = valid_ref.shape[1]
     block_len = members_ref.shape[1]
@@ -158,10 +159,12 @@
             out_ref[n, :, p * main : (p + 1) * main] = own[:, :main]
             at = pools * main + p * rest
             out_ref[n, :, at : at + rest] = own[:, main:]
+    packed_ref[...] = jnp.zeros(packed_ref.shape, I32)
     for n, cls in enumerate(relatives()[:4]):
         pos = out_ref[0, pl.ds(cls, 1), :]
         cluster = out_ref[1, pl.ds(cls, 1), :]
-        codes_ref[n, :, :] = columns(jnp.where(cluster < 0, -2 * CODE, cluster * CODE + pos))
+        packed_ref[n : n + 1, :] = jnp.where(cluster < 0, -2 * CODE, cluster * CODE + pos)
+    codes_ref[...] = jnp.transpose(packed_ref[...])
 
 
 def run(pieces, sims_ref):
@@ -175,13 +178,14 @@
             take_maxima(sims_ref.at[(n - 1) % 2], **pieces[n - 1])
 
 
-def take_maxima(sims_ref, left, right, count, codes, rows, start, pos_row, cluster_row, col, col_start, same):
+def take_maxima(sims_ref, left, right, count, codes, cls, rows, start, pos_row, cluster_row, col, col_start, same):
     step = 128
     right_pos, right_cluster = pos_row(), cluster_row()
     parts = QUARTER // 128
     best_col = [jnp.zeros((8, 128), F32) for _ in range(parts)]
     for top in range(0, count, step):
-        code = codes[start + top : start + top + step, :]
+        code = codes[start + top : start + top + step, cls : cls + 1]
+        code = jnp.broadcast_to(code, (step, 128))
         pos = code & (CODE - 1)
         cluster = code >> 13
         best = rows[start + top : start + top + step, :]
@@ -214,31 +218,53 @@
 OWN, SIB, LOW, LOWS, HIGH = range(5)
 
 
+class Fetch:
+    def __init__(self, sources, held, sems):
+        self.held, self.copies = dict(), dict()
+        for n, source in enumerate(sources):
+            copy = pltpu.make_async_copy(source, held[n], sems.at[n])
+            copy.start()
+            self.held[n], self.copies[n] = held[n], copy
+
+    def get(self, n):
+        copy = self.copies.pop(n, None)
+        if copy is not None:
+            copy.wait()
+        return self.held[n]
+
+    def all(self):
+        for n in list(self.copies):
+            self.get(n)
+
+
 class Tiles:
-    def __init__(self, meta, codes, rows, cols, parts):
-        self.meta, self.codes, self.rows, self.cols, self.parts = meta, codes, rows, cols, parts
+    def __init__(self, fetch, meta, codes, rows, cols, parts):
+        self.fetch, self.parts = fetch, parts
+        self.meta, self.codes, self.rows, self.cols = meta, codes, rows, cols
         self.relatives = relatives()
         for ref in (rows, cols):
             ref[...] = jnp.zeros(ref.shape, F32)
 
     def load(self, cls, quarter, count=1):
-        ref, at = self.parts[cls, quarter]
+        number, at = self.parts[cls, quarter]
+        ref = self.fetch.get(number)
         if len(ref.shape) == 3:
             return ref[:, at : at + QUARTER // ref.shape[0], :].reshape(-1, ref.shape[2])
         return ref[at : at + count * QUARTER, :]
 
     def piece(self, left, quarter, count, right, right_quarter, same=None):
         lanes = slice(right_quarter * QUARTER, (right_quarter + 1) * QUARTER)
-        cls = self.relatives[right]
+        place = self.relatives[right]
         return dict(
             left=lambda: self.load(left, quarter, count),
             right=lambda: self.load(right, right_quarter),
             count=count * QUARTER,
-            codes=self.codes.at[left],
+            codes=self.codes,
+            cls=left,
             rows=self.rows.at[left],
             start=quarter * QUARTER,
-            pos_row=lambda: self.meta[0, pl.ds(cls, 1), lanes],
-            cluster_row=lambda: self.meta[1, pl.ds(cls, 1), lanes],
+            pos_row=lambda: self.meta[0, pl.ds(place, 1), lanes],
+            cluster_row=lambda: self.meta[1, pl.ds(place, 1), lanes],
             col=self.cols.at[right],
             col_start=right_quarter * QUARTER,
             same=count * QUARTER if same is None else same,
@@ -273,46 +299,68 @@
     return (chip == 0) | (chip == 3)
 
 
-def quarters(*groups):
-    parts = {}
-    for cls, refs in groups:
-        for quarter, ref, at in refs:
-            parts[cls, quarter] = (ref, at)
-    return parts
-
-
-def whole(ref):
-    return [(q, ref, q * QUARTER) for q in range(3)]
-
-
-def near_kernel(own0, sib0, meta, codes, out, sims, rows, cols):
-    tiles = Tiles(meta, codes, rows, cols, quarters((OWN, whole(own0)), (SIB, whole(sib0))))
+def parts_of(**groups):
+    names = dict(own=OWN, sib=SIB, low=LOW, lows=LOWS, high=HIGH)
+    return {(names[name], q): part for name, parts in groups.items() for q, part in parts.items()}
+
+
+def whole(n):
+    return {q: (n, q * QUARTER) for q in range(3)}
+
+
+def halves(n):
+    return {q: (n, q * QUARTER) for q in range(2)}
+
+
+def join_kernel(pools, rest, low_rest, high_rest, out):
+    width = QUARTER // pools
+    for n, part in enumerate((rest, low_rest, high_rest)):
+        out[:, n * width : (n + 1) * width, :] = part[...].reshape(pools, width, -1)
+
+
+def cut_kernel(arrived, after, out):
+    del after
+    out[...] = arrived[:, : out.shape[1], :]
+
+
+def follow_kernel(rows, after, out):
+    del after
+    out[...] = rows[...]
+
+
+def near_kernel(own0, sib0, meta, codes, out, sims, rows, cols, sems, *held):
+    fetch = Fetch((own0, sib0), held, sems)
+    tiles = Tiles(fetch, meta, codes, rows, cols, parts_of(own=whole(0), sib=whole(1)))
     run([tiles.piece(OWN, 0, b + 1, OWN, b, same=b * QUARTER) for b in range(3)], sims)
+    fetch.all()
     pairs = [(a, b) for b in range(3) for a in range(3)]
     either(second_core(), lambda flip: run(tiles.matched(flip, OWN, SIB, pairs), sims))
     tiles.finish(None, out)
 
 
 def middle_kernel(
-    own0, sib0, arrived, sib3, lows3, low0, low1, lows0, lows1, high0, high1, meta, codes, before,
-    out, sims, rows, cols,
+    own0, arrived, high01, sib0, swapped, low01, lows01, meta, codes, before, out,
+    sims, rows, cols, sems, *held,
 ):
+    fetch = Fetch((own0, arrived, high01, sib0, swapped, low01, lows01), held, sems)
+    width = arrived.shape[1] // 3
     tiles = Tiles(
-        meta, codes, rows, cols,
-        quarters(
-            (OWN, whole(own0) + [(3, arrived, 0)]),
-            (SIB, whole(sib0) + [(3, sib3, 0)]),
-            (LOW, [(0, low0, 0), (1, low1, 0), (3, arrived, 16)]),
-            (LOWS, [(0, lows0, 0), (1, lows1, 0), (3, lows3, 0)]),
-            (HIGH, [(0, high0, 0), (1, high1, 0), (3, arrived, 32)]),
+        fetch, meta, codes, rows, cols,
+        parts_of(
+            own={**whole(0), 3: (1, 0)},
+            sib={**whole(3), 3: (4, 0)},
+            low={**halves(5), 3: (1, width)},
+            lows={**halves(6), 3: (4, width)},
+            high={**halves(2), 3: (1, 2 * width)},
         ),
     )
     pieces = [tiles.piece(OWN, 0, 3, OWN, 3), tiles.piece(OWN, 3, 1, OWN, 3, same=0)]
-    for b in (0, 1, 3):
-        for cls in (OWN, SIB):
+    for cls in (OWN, SIB):
+        for b in (3, 0, 1):
             pieces.append(tiles.piece(cls, 0, 3, HIGH, b))
             pieces.append(tiles.piece(cls, 3, 1, HIGH, b))
     run(pieces, sims)
+    fetch.all()
     pairs = [(a, b) for b in range(4) for a in range(4) if 3 in (a, b)]
     either(second_core(), lambda flip: run(tiles.matched(flip, OWN, SIB, pairs), sims))
     pairs = [(a, b) for b in (0, 1, 3) for a in (0, 1, 3)]
@@ -326,24 +374,28 @@
 
 
 def late_kernel(
-    own0, sib0, arrived, sib3, lows3, low0, low1, low2, lows0, lows1, high0, high1, high2, meta,
-    codes, before, out, sims, rows, cols,
+    own0, high2, sib0, arrived, swapped, low2, low01, lows01, high01, meta, codes, before, out,
+    sims, rows, cols, sems, *held,
 ):
+    fetch = Fetch((own0, high2, sib0, arrived, swapped, low2, low01, lows01, high01), held, sems)
+    width = arrived.shape[1] // 3
     tiles = Tiles(
-        meta, codes, rows, cols,
-        quarters(
-            (OWN, whole(own0) + [(3, arrived, 0)]),
-            (SIB, whole(sib0) + [(3, sib3, 0)]),
-            (LOW, [(0, low0, 0), (1, low1, 0), (2, low2, 0), (3, arrived, 16)]),
-            (LOWS, [(0, lows0, 0), (1, lows1, 0), (3, lows3, 0)]),
-            (HIGH, [(0, high0, 0), (1, high1, 0), (2, high2, 0), (3, arrived, 32)]),
+        fetch, meta, codes, rows, cols,
+        parts_of(
+            own={**whole(0), 3: (3, 0)},
+            sib={**whole(2), 3: (4, 0)},
+            low={**halves(6), 2: (5, 0), 3: (3, width)},
+            lows={**halves(7), 3: (4, width)},
+            high={**halves(8), 2: (1, 0), 3: (3, 2 * width)},
         ),
     )
     pieces = []
     for cls in (OWN, SIB):
         pieces.append(tiles.piece(cls, 0, 3, HIGH, 2))
+    for cls in (OWN, SIB):
         pieces.append(tiles.piece(cls, 3, 1, HIGH, 2))
     run(pieces, sims)
+    fetch.all()
     pairs = [(a, b) for b in range(4) for a in range(4) if 2 in (a, b)]
     others = [(a, 2) for a in (0, 1, 3)]
     either(
@@ -356,16 +408,16 @@
 
 
 def last_kernel(
-    pools, group, main, rest, arrived, lows2, high0, high1, high2, meta, codes, before,
-    out, sims, rows, cols, best, every,
+    pools, group, main, rest, lows2, high01, high2, arrived, meta, codes, before, out,
+    sims, rows, cols, best, every, sems, *held,
 ):
+    fetch = Fetch((lows2, high01, high2, arrived), held, sems)
+    width = arrived.shape[1] // 3
     tiles = Tiles(
-        meta, codes, rows, cols,
-        quarters(
-            (LOWS, [(2, lows2, 0)]),
-            (HIGH, [(0, high0, 0), (1, high1, 0), (2, high2, 0), (3, arrived, 32)]),
-        ),
-    )
+        fetch, meta, codes, rows, cols,
+        parts_of(lows={2: (0, 0)}, high={**halves(1), 2: (2, 0), 3: (3, 2 * width)}),
+    )
+    fetch.all()
     pairs = [(2, b) for b in range(4)]
     either(outer_chip(), lambda flip: run(tiles.matched(flip, LOWS, HIGH, pairs), sims))
     best[...] = before[...]
@@ -416,12 +468,11 @@
     cluster_row = block_cluster.reshape(1, -1)
     blocks, block_len = members.shape
 
-    table, main, rest = pl.pallas_call(
+    table, main = pl.pallas_call(
         lambda *refs: table_kernel(pools, group, places, last, *refs),
         out_shape=(
             sds((devices, 128), I32),
             sds((3 * QUARTER, feature), BF16),
-            sds((QUARTER, feature), BF16),
         ),
         in_specs=[hbm] * 3,
         scratch_shapes=[
@@ -431,18 +482,19 @@
             pltpu.VMEM((blocks, 128), F32),
             pltpu.SemaphoreType.DMA((3,)),
         ],
-        compiler_params=PARAMS,
+        compiler_params=TABLE_PARAMS,
         cost_estimate=cost(rows_dev * rows_dev * feature),
         name="table",
     )(members, valid_row, embeddings)
     meta, codes = pl.pallas_call(
         lambda *refs: meta_kernel(group, places, last, *refs),
-        out_shape=(sds((2, group, rows_dev), I32), sds((4, rows_dev, 128), I32)),
+        out_shape=(sds((2, group, rows_dev), I32), sds((rows_dev, 128), I32)),
         in_specs=[hbm] * 3,
         scratch_shapes=[
             pltpu.VMEM((2 * group, block_len), I32),
             pltpu.VMEM((1, blocks), I32),
             pltpu.VMEM((1, blocks), I32),
+            pltpu.VMEM((128, rows_dev), I32),
             pltpu.SemaphoreType.DMA((3,)),
         ],
         compiler_params=PARAMS,
@@ -459,49 +511,76 @@
     def to_pools(rows):
         return lax.all_to_all(rows, "pool", split_axis=0, concat_axis=0, tiled=True)
 
+    vmem = pl.BlockSpec(memory_space=pltpu.VMEM)
+    rest = pl.pallas_call(
+        lambda *refs: rest_kernel(pools, places, last, *refs),
+        out_shape=sds((QUARTER, feature), BF16),
+        in_specs=[vmem, vmem, hbm],
+        compiler_params=PARAMS,
+        name="rest",
+    )(table, embeddings, meta)
     low_rest, high_rest = shift(rest, 2), shift(rest, -2)
     own0 = to_pools(main.reshape(pools, -1, feature)).reshape(-1, feature)
-    sent = [part.reshape(pools, -1, feature) for part in (rest, low_rest, high_rest)]
-    arrived = to_pools(jnp.concatenate(sent, axis=1))
-    low, lows, high = [], [], []
-    for q in range(3):
-        part = own0[q * QUARTER : (q + 1) * QUARTER]
-        low.append(shift(part, 2))
-        high.append(shift(part, -2))
-        lows.append(swap(low[-1]))
+    sent = pl.pallas_call(
+        lambda *refs: join_kernel(pools, *refs),
+        out_shape=sds((pools, 3 * QUARTER // pools, feature), BF16),
+        compiler_params=PARAMS,
+        name="join",
+    )(rest, low_rest, high_rest)
+    arrived = to_pools(sent)
+    early = own0[: 2 * QUARTER]
+    low01, high01 = shift(early, 2), shift(early, -2)
     sib0 = swap(own0)
-    width = QUARTER // pools
-    sib3 = swap(arrived[:, :width].reshape(-1, feature))
-    lows3 = swap(arrived[:, width : 2 * width].reshape(-1, feature))
-
-    def tiles(kernel, name, squares, operands, out_shape=(8, rows_dev), more=()):
+
+    def tiles(kernel, name, squares, operands, small, out_shape=sds((8, rows_dev), F32), more=()):
         return pl.pallas_call(
             kernel,
-            out_shape=sds(out_shape, F32),
+            out_shape=out_shape,
+            in_specs=[hbm] * len(operands) + [vmem] * len(small),
             scratch_shapes=[
                 pltpu.VMEM((2, 3 * QUARTER, QUARTER), F32),
                 pltpu.VMEM((4, rows_dev, 128), F32),
                 pltpu.VMEM((5, 8, rows_dev), F32),
                 *more,
+                pltpu.SemaphoreType.DMA((len(operands),)),
+                *[pltpu.VMEM(operand.shape, BF16) for operand in operands],
             ],
             compiler_params=PARAMS,
             cost_estimate=cost(squares * QUARTER * QUARTER * feature),
             name=name,
-        )(*operands)
-
-    near = tiles(near_kernel, "near", 11, (own0, sib0, meta, codes))
+        )(*operands, *small)
+
+    near = tiles(near_kernel, "near", 11, (own0, sib0), (meta, codes))
+    tail = own0[2 * QUARTER :]
+    low2, high2 = shift(tail, 2), shift(tail, -2)
+    crossing = pl.pallas_call(
+        cut_kernel,
+        out_shape=sds((pools, 2 * QUARTER // pools, feature), BF16),
+        in_specs=[vmem, hbm],
+        compiler_params=PARAMS,
+        name="cut",
+    )(arrived, near)
+    swapped = swap(crossing)
+    low01 = pl.pallas_call(
+        follow_kernel,
+        out_shape=sds(low01.shape, BF16),
+        in_specs=[vmem, hbm],
+        compiler_params=PARAMS,
+        name="follow",
+    )(low01, near)
+    lows01 = swap(low01)
     middle = tiles(
         middle_kernel, "middle", 42,
-        (own0, sib0, arrived, sib3, lows3, *low[:2], *lows[:2], *high[:2], meta, codes, near),
+        (own0, arrived, high01, sib0, swapped, low01, lows01), (meta, codes, near),
     )
     late = tiles(
         late_kernel, "late", 14,
-        (own0, sib0, arrived, sib3, lows3, *low, *lows[:2], *high, meta, codes, middle),
+        (own0, high2, sib0, arrived, swapped, low2, low01, lows01, high01), (meta, codes, middle),
     )
     best = tiles(
         lambda *refs: last_kernel(pools, group, group * (places - last), group * last, *refs),
-        "last", 2, (arrived, lows[2], *high, meta, codes, late),
-        out_shape=(devices, group * places),
+        "last", 2, (swap(low2), high01, high2, arrived), (meta, codes, late),
+        out_shape=sds((devices, group * places), F32),
         more=(pltpu.VMEM((8, rows_dev), F32), pltpu.VMEM((group, rows_dev), F32)),
     )
     returned = lax.all_to_all(best, ("pool", "grp"), split_axis=0, concat_axis=0, tiled=True)

time: 128 us -> 126 us (0.984)
  waiting for transfers between devices: 38.9 us -> 46.5 us
  blocking collectives: 20.6 us -> 16 us
  starting transfers between devices: 28.8 us -> 25.4 us
  local copies, waits for them, and re-layouts: 5.58 us -> 2.3 us
  Pallas kernels: 32.4 us -> 35 us
  other arithmetic: 1.33 us -> 0 us
    all_to_all x2, waiting for transfers between devices: 21.6 us -> 34.4 us  [to_pools(): return lax.all_to_all(rows, 'pool', split_axis=0, concat_axis=0, tiled=True)]
    ppermute x8 -> x6, waiting for transfers between devices: 17.3 us -> 12.1 us  [shift(): lax.ppermute(rows, 'grp', [(g, (g + by) % group) for g in range(group)])]
    all_to_all x1, blocking collectives: 20.6 us -> 16 us  [body(): lax.all_to_all(best, ('pool', 'grp'), split_axis=0, concat_axis=0, tiled=...]
    unnamed x14 -> x18, local copies, waits for them, and re-layouts: 4.28 us -> 1.18 us
    pallas_call x4 -> x8, Pallas kernels: 21.2 us -> 23.9 us  [the longest x4 21.6 us: tiles(): pl.pallas_call(kernel, out_shape=out_shape, in_specs=[hbm] * len(operands...]
    ppermute x8 -> x6, starting transfers between devices: 10.8 us -> 8.17 us  [shift(): lax.ppermute(rows, 'grp', [(g, (g + by) % group) for g in range(group)])]
    concatenate x1 -> x0, other arithmetic: 1.33 us -> none  [body(): arrived = to_pools(jnp.concatenate(sent, axis=1))]
    ppermute x6 -> x4, starting transfers between devices: 4.8 us -> 4.82 us  [swap(): return lax.ppermute(rows, 'grp', [(g, g ^ 1) for g in range(group)])]
  transfers between devices with their start and end apart: 16 -> 12, of which waited for: 5 -> 3; matrix products, arithmetic and copies ran while one was open for 2% -> 1% of each run, Pallas kernels for 19% -> 21%
where the time goes in v3:
time: 126 us; the launch traced here: 125 us
  waiting for transfers between devices  46.5 us (37%)
  Pallas kernels  35 us (28%)
  starting transfers between devices  25.4 us (20%)
  blocking collectives  16 us (13%)
  local copies, waits for them, and re-layouts  2.3 us (2%)
    all_to_all x2, waiting for transfers between devices, to_pools(): return lax.all_to_all(rows, 'pool', split_axis=0, concat_axis=0, tiled=True)  34.4 us
    pallas_call x4, Pallas kernels, tiles(): pl.pallas_call(kernel, out_shape=out_shape, in_specs=[hbm] * len(operands...  21.6 us
    all_to_all x1, blocking collectives, body(): lax.all_to_all(best, ('pool', 'grp'), split_axis=0, concat_axis=0, tiled=...  16 us
    all_to_all x2, starting transfers between devices, to_pools(): return lax.all_to_all(rows, 'pool', split_axis=0, concat_axis=0, tiled=True)  12.4 us
    ppermute x6, waiting for transfers between devices, shift(): lax.ppermute(rows, 'grp', [(g, (g + by) % group) for g in range(group)])  12.1 us
    ppermute x6, starting transfers between devices, shift(): lax.ppermute(rows, 'grp', [(g, (g + by) % group) for g in range(group)])  8.17 us
    pallas_call x1, Pallas kernels, body(): pl.pallas_call(lambda *refs: table_kernel(pools, group, places, last, *re...  5.18 us
    ppermute x4, starting transfers between devices, swap(): return lax.ppermute(rows, 'grp', [(g, g ^ 1) for g in range(group)])  4.82 us
  transfers between devices with their start and end apart: 12, of which 3 were waited for; matrix products, arithmetic and copies ran while one was open for 1% of the time, Pallas kernels for 21%

profile of v3, /device:TPU:1, one launch (start us, length us, event | category | flops | bytes accessed | tf_op | source)
XLA Modules:
  0.0 125.4 jit_solution(17213405198359085313)
XLA Ops:
  0.0 5.2 %table.1 = (s32[128,128]{1,0:T(8,128)}, bf16[768,1024]{1,0:T(8,128)(2,1)}) custom-call(s32[256,512]{1,0:T(8,128)} %refs_0_.3, s32[1,256]{1,0:T(1,128)} %bitcast.17, bf16[1024,1024]{1,0:T(8,128)(2,1)} %refs_1_.1), custom_call_target="tpu_custom_call" | custom-call | flops 2147483648 | tf_op jit(solution)/shard_map/table/pallas_call | solution.py:471
  5.2 0.0 copy-start.6
  5.2 0.0 copy-start.7
  5.2 0.0 copy-start.8
  5.2 8.7 %all-to-all-start = ((bf16[16,48,1024]{2,1,0:T(8,128)(2,1)}), bf16[16,48,1024]{2,1,0:T(8,128)(2,1)S(1)}, u32[]{:S(2)}, u32[]{:S(2)}) async-start(bf16[16,48,1024]{2,1,0:T(8,128)(2,1)} %bitcast.20), calls=%async_computation | async-start | bytes 3145728 | tf_op jit(solution)/shard_map/all_to_all | solution.py:512
  14.0 4.4 %meta.1 = (s32[2,8,1024]{2,1,0:T(8,128)S(1)}, s32[1024,128]{1,0:T(8,128)S(1)}) custom-call(s32[256,512]{1,0:T(8,128)S(1)} %copy-done.6, s32[1,256]{1,0:T(1,128)S(1)} %bitcast.18, s32[1,256]{1,0:T(1,128)S(1)} %bitcast.19), custom_call_target="tpu_custom_call" | custom-call | flops 4294967296 | tf_op jit(solution)/shard_map/meta/pallas_call | solution.py:489
  18.5 0.9 rest.1.refs_0_
  19.4 1.3 %collective-permute-start.4 = (bf16[256,1024]{1,0:T(8,128)(2,1)S(1)}, bf16[256,1024]{1,0:T(8,128)(2,1)S(1)}, u32[]{:S(2)}, u32[]{:S(2)}) collective-permute-start(bf16[256,1024]{1,0:T(8,128)(2,1)S(1)} %rest.1.refs_0_), channel_id=1, source_target_pairs={{0,2},{1,3},{2,4},{3,5},{4,6},{5,7},{6,0},{7,1},{8,10},{9,11},{10,... | collective-permute-start | bytes 1572872 | tf_op jit(solution)/shard_map/ppermute | solution.py:506
  20.7 1.5 %collective-permute-start.5 = (bf16[256,1024]{1,0:T(8,128)(2,1)S(1)}, bf16[256,1024]{1,0:T(8,128)(2,1)S(1)}, u32[]{:S(2)}, u32[]{:S(2)}) collective-permute-start(bf16[256,1024]{1,0:T(8,128)(2,1)S(1)} %rest.1.refs_0_), channel_id=1, source_target_pairs={{0,6},{1,7},{2,0},{3,1},{4,2},{5,3},{6,4},{7,5},{8,14},{9,15},{10,... | collective-permute-start | bytes 1572872 | tf_op jit(solution)/shard_map/ppermute | solution.py:506
  22.1 14.7 %all-to-all-done = bf16[16,48,1024]{2,1,0:T(8,128)(2,1)S(1)} async-done(((bf16[16,48,1024]{2,1,0:T(8,128)(2,1)}), bf16[16,48,1024]{2,1,0:T(8,128)(2,1)S(1)}, u32[]{:S(2)}, u32[]{:S(2)}) %all-to-all-start) | async-done | bytes 1572896 | tf_op jit(solution)/shard_map/all_to_all | solution.py:512
  36.8 2.5 %collective-permute-start.6 = (bf16[768,1024]{1,0:T(8,128)(2,1)S(1)}, bf16[768,1024]{1,0:T(8,128)(2,1)}, u32[]{:S(2)}, u32[]{:S(2)}) collective-permute-start(bf16[768,1024]{1,0:T(8,128)(2,1)S(1)} %bitcast.9), channel_id=1, source_target_pairs={{0,1},{1,0},{2,3},{3,2},{4,5},{5,4},{6,7},{7,6},{8,9},{9,8},{10,11... | collective-permute-start | bytes 4718600 | tf_op jit(solution)/shard_map/ppermute | solution.py:509
  39.4 0.1 join.1
  39.5 1.1 copy-done
  40.6 3.7 %all-to-all-start.1 = ((bf16[16,48,1024]{2,1,0:T(8,128)(2,1)}), bf16[16,48,1024]{2,1,0:T(8,128)(2,1)S(1)}, u32[]{:S(2)}, u32[]{:S(2)}) async-start(bf16[16,48,1024]{2,1,0:T(8,128)(2,1)} %copy-done), calls=%async_computation.1 | async-start | bytes 3145728 | tf_op jit(solution)/shard_map/all_to_all | solution.py:512
  44.4 1.1 slice.9
  45.5 1.2 collective-permute-start.8
  46.7 1.5 %collective-permute-start.2 = (bf16[512,1024]{1,0:T(8,128)(2,1)}, bf16[512,1024]{1,0:T(8,128)(2,1)}, u32[]{:S(2)}, u32[]{:S(2)}) collective-permute-start(bf16[512,1024]{1,0:T(8,128)(2,1)} %slice.9), channel_id=1, source_target_pairs={{0,6},{1,7},{2,0},{3,1},{4,2},{5,3},{6,4},{7,5},{8,14},{9,15},{10,... | collective-permute-start | bytes 3145736 | tf_op jit(solution)/shard_map/ppermute | solution.py:506
  48.1 3.3 %near.1.after.before = f32[8,1024]{1,0:T(8,128)S(1)} custom-call(bf16[768,1024]{1,0:T(8,128)(2,1)S(1)} %bitcast.11, bf16[768,1024]{1,0:T(8,128)(2,1)} %collective-permute-done.6.sib0, s32[2,8,1024]{2,1,0:T(8,128)S(1)} %get-tuple-element.11.refs_2_.meta.refs_4_, s32[1024,128]{1,0:T(8,128)S(1)} %copy-done.3), custom_call_target="tpu_custom_call" | custom-call | flops 1476395008 | tf_op jit(solution)/shard_map/near/pallas_call | solution.py:536
  51.4 19.7 %all-to-all-done.1.arrived.refs_3_ = bf16[16,48,1024]{2,1,0:T(8,128)(2,1)S(1)} async-done(((bf16[16,48,1024]{2,1,0:T(8,128)(2,1)}), bf16[16,48,1024]{2,1,0:T(8,128)(2,1)S(1)}, u32[]{:S(2)}, u32[]{:S(2)}) %all-to-all-start.1) | async-done | bytes 1572896 | tf_op jit(solution)/shard_map/all_to_all | solution.py:512
  71.1 0.1 cut.1
  71.2 0.9 collective-permute-start.7
  72.0 1.3 %follow.1.low01 = bf16[512,1024]{1,0:T(8,128)(2,1)S(1)} custom-call(bf16[512,1024]{1,0:T(8,128)(2,1)} %collective-permute-done.8.rows, f32[8,1024]{1,0:T(8,128)S(1)} %near.1.after.before), custom_call_target="tpu_custom_call" | custom-call | tf_op jit(solution)/shard_map/follow/pallas_call | solution.py:564
  73.3 0.6 collective-permute-start.9
  74.0 0.8 collective-permute-start
  74.8 1.9 %collective-permute-start.3 = (bf16[256,1024]{1,0:T(8,128)(2,1)S(1)}, bf16[256,1024]{1,0:T(8,128)(2,1)S(1)}, u32[]{:S(2)}, u32[]{:S(2)}) collective-permute-start(bf16[256,1024]{1,0:T(8,128)(2,1)S(1)} %slice.8), channel_id=1, source_target_pairs={{0,6},{1,7},{2,0},{3,1},{4,2},{5,3},{6,4},{7,5},{8,14},{9,15},{10,... | collective-permute-start | bytes 1572872 | tf_op jit(solution)/shard_map/ppermute | solution.py:506
  76.7 12.1 %collective-permute-done.low2 = bf16[256,1024]{1,0:T(8,128)(2,1)S(1)} collective-permute-done((bf16[256,1024]{1,0:T(8,128)(2,1)S(1)}, bf16[256,1024]{1,0:T(8,128)(2,1)S(1)}, u32[]{:S(2)}, u32[]{:S(2)}) %collective-permute-start) | collective-permute-done | bytes 524320 | tf_op jit(solution)/shard_map/ppermute | solution.py:506
  88.8 0.8 collective-permute-start.1
  89.6 10.5 %middle.1.before = f32[8,1024]{1,0:T(8,128)S(1)} custom-call(bf16[768,1024]{1,0:T(8,128)(2,1)S(1)} %bitcast.13, bf16[16,48,1024]{2,1,0:T(8,128)(2,1)S(1)} %all-to-all-done.1.arrived.refs_3_, bf16[512,1024]{1,0:T(8,128)(2,1)} %collective-permute-done.2.high01.refs_1_, bf16[768,1024]{1,0:T(8,128)(2,1)} %collective-permute-done.6.sib0, ...), custom_call_target="tpu_custom_call" | custom-call | flops 5637144576 | tf_op jit(solution)/shard_map/middle/pallas_call | solution.py:536
  100.1 5.8 %late.1.refs_6_ = f32[8,1024]{1,0:T(8,128)S(1)} custom-call(bf16[768,1024]{1,0:T(8,128)(2,1)S(1)} %bitcast.14, bf16[256,1024]{1,0:T(8,128)(2,1)S(1)} %collective-permute-done.3.high2.refs_2_, bf16[768,1024]{1,0:T(8,128)(2,1)} %collective-permute-done.6.sib0, bf16[16,48,1024]{2,1,0:T(8,128)(2,1)S(1)} %all-to-all-done.1.arrived.refs_3_, ...), custom_call_target="tpu_custom_call" | custom-call | flops 1879048192 | tf_op jit(solution)/shard_map/late/pallas_call | solution.py:536
  105.9 2.1 %last.1 = f32[128,64]{1,0:T(8,128)S(1)} custom-call(bf16[256,1024]{1,0:T(8,128)(2,1)S(1)} %collective-permute-done.1.refs_0_, bf16[512,1024]{1,0:T(8,128)(2,1)} %collective-permute-done.2.high01.refs_1_, bf16[256,1024]{1,0:T(8,128)(2,1)S(1)} %collective-permute-done.3.high2.refs_2_, bf16[16,48,1024]{2,1,0:T(8,128)(2,1)S(1)} %all-to-all-done.1.arrived.refs_3_, ...), custom_call_target="tpu_custom_call" | custom-call | flops 268435456 | tf_op jit(solution)/shard_map/last/pallas_call | solution.py:536
  108.0 16.0 %all_to_all.21 = f32[128,1,64]{2,1,0:T(1,128)S(1)} all-to-all(f32[128,1,64]{2,1,0:T(1,128)S(1)} %bitcast.15), channel_id=1, replica_groups=mesh['pool'=16,'grp'=8] {'pool','grp'}, dimensions={0} | all-to-all | bytes 65536 | tf_op jit(solution)/shard_map/all_to_all | solution.py:586
  124.0 1.4 %score.1 = f32[1,1024]{1,0:T(1,128)} custom-call(s32[128,128]{1,0:T(8,128)S(1)} %copy-done.5, f32[128,64]{1,0:T(8,128)S(1)} %bitcast.16), custom_call_target="tpu_custom_call" | custom-call | tf_op jit(solution)/shard_map/score/pallas_call | solution.py:587
  (24 shorter events, 0.1 us)
Async XLA Ops:
  5.2 8.8 %copy-start.6 = (s32[256,512]{1,0:T(8,128)S(1)}, s32[256,512]{1,0:T(8,128)}, u32[]{:S(2)}) copy-start(s32[256,512]{1,0:T(8,128)} %refs_0_.3) | copy-start | bytes 1572868
  5.2 8.8 %copy-start.7 = (s32[256]{0:T(256)S(1)}, s32[256]{0:T(256)}, u32[]{:S(2)}) copy-start(s32[256]{0:T(256)} %param.6) | copy-start | bytes 3076
  5.2 8.8 %copy-start.8 = (s32[256]{0:T(256)S(1)}, s32[256]{0:T(256)}, u32[]{:S(2)}) copy-start(s32[256]{0:T(256)} %param.7) | copy-start | bytes 3076
  5.2 31.6 %all-to-all-start = ((bf16[16,48,1024]{2,1,0:T(8,128)(2,1)}), bf16[16,48,1024]{2,1,0:T(8,128)(2,1)S(1)}, u32[]{:S(2)}, u32[]{:S(2)}) async-start(bf16[16,48,1024]{2,1,0:T(8,128)(2,1)} %bitcast.20), calls=%async_computation | async-start | bytes 3145728 | tf_op jit(solution)/shard_map/all_to_all | solution.py:512
  14.0 4.5 %copy-start.1 = (bf16[1024,1024]{1,0:T(8,128)(2,1)S(1)}, bf16[1024,1024]{1,0:T(8,128)(2,1)}, u32[]{:S(2)}) copy-start(bf16[1024,1024]{1,0:T(8,128)(2,1)} %refs_1_.1) | copy-start | bytes 6291460
  14.0 4.5 %copy-start.5 = (s32[128,128]{1,0:T(8,128)S(1)}, s32[128,128]{1,0:T(8,128)}, u32[]{:S(2)}) copy-start(s32[128,128]{1,0:T(8,128)} %get-tuple-element.9.refs_0_) | copy-start | bytes 196612
  18.5 2.2 %copy-start.2 = (s32[1024,128]{1,0:T(8,128)}, s32[1024,128]{1,0:T(8,128)S(1)}, u32[]{:S(2)}) copy-start(s32[1024,128]{1,0:T(8,128)S(1)} %get-tuple-element.12.codes.refs_5_) | copy-start | bytes 1572868
  19.4 20.0 %collective-permute-start.4 = (bf16[256,1024]{1,0:T(8,128)(2,1)S(1)}, bf16[256,1024]{1,0:T(8,128)(2,1)S(1)}, u32[]{:S(2)}, u32[]{:S(2)}) collective-permute-start(bf16[256,1024]{1,0:T(8,128)(2,1)S(1)} %rest.1.refs_0_), channel_id=1, source_target_pairs={{0,2},{1,3},{2,4},{3,5},{4,6},{5,7},{6,0},{7,1},{8,10},{9,11},{10,... | collective-permute-start | bytes 1572872 | tf_op jit(solution)/shard_map/ppermute | solution.py:506
  20.7 18.7 %collective-permute-start.5 = (bf16[256,1024]{1,0:T(8,128)(2,1)S(1)}, bf16[256,1024]{1,0:T(8,128)(2,1)S(1)}, u32[]{:S(2)}, u32[]{:S(2)}) collective-permute-start(bf16[256,1024]{1,0:T(8,128)(2,1)S(1)} %rest.1.refs_0_), channel_id=1, source_target_pairs={{0,6},{1,7},{2,0},{3,1},{4,2},{5,3},{6,4},{7,5},{8,14},{9,15},{10,... | collective-permute-start | bytes 1572872 | tf_op jit(solution)/shard_map/ppermute | solution.py:506
  36.8 11.3 %collective-permute-start.6 = (bf16[768,1024]{1,0:T(8,128)(2,1)S(1)}, bf16[768,1024]{1,0:T(8,128)(2,1)}, u32[]{:S(2)}, u32[]{:S(2)}) collective-permute-start(bf16[768,1024]{1,0:T(8,128)(2,1)S(1)} %bitcast.9), channel_id=1, source_target_pairs={{0,1},{1,0},{2,3},{3,2},{4,5},{5,4},{6,7},{7,6},{8,9},{9,8},{10,11... | collective-permute-start | bytes 4718600 | tf_op jit(solution)/shard_map/ppermute | solution.py:509
  39.5 1.1 copy-start
  40.6 30.4 %all-to-all-start.1 = ((bf16[16,48,1024]{2,1,0:T(8,128)(2,1)}), bf16[16,48,1024]{2,1,0:T(8,128)(2,1)S(1)}, u32[]{:S(2)}, u32[]{:S(2)}) async-start(bf16[16,48,1024]{2,1,0:T(8,128)(2,1)} %copy-done), calls=%async_computation.1 | async-start | bytes 3145728 | tf_op jit(solution)/shard_map/all_to_all | solution.py:512
  44.4 3.8 %copy-start.3 = (s32[1024,128]{1,0:T(8,128)S(1)}, s32[1024,128]{1,0:T(8,128)}, u32[]{:S(2)}) copy-start(s32[1024,128]{1,0:T(8,128)} %copy-done.2) | copy-start | bytes 1572868
  45.5 26.6 %collective-permute-start.8 = (bf16[512,1024]{1,0:T(8,128)(2,1)}, bf16[512,1024]{1,0:T(8,128)(2,1)}, u32[]{:S(2)}, u32[]{:S(2)}) collective-permute-start(bf16[512,1024]{1,0:T(8,128)(2,1)} %slice.9), channel_id=1, source_target_pairs={{0,2},{1,3},{2,4},{3,5},{4,6},{5,7},{6,0},{7,1},{8,10},{9,11},{10,... | collective-permute-start | bytes 3145736 | tf_op jit(solution)/shard_map/ppermute | solution.py:506
  46.7 42.9 %collective-permute-start.2 = (bf16[512,1024]{1,0:T(8,128)(2,1)}, bf16[512,1024]{1,0:T(8,128)(2,1)}, u32[]{:S(2)}, u32[]{:S(2)}) collective-permute-start(bf16[512,1024]{1,0:T(8,128)(2,1)} %slice.9), channel_id=1, source_target_pairs={{0,6},{1,7},{2,0},{3,1},{4,2},{5,3},{6,4},{7,5},{8,14},{9,15},{10,... | collective-permute-start | bytes 3145736 | tf_op jit(solution)/shard_map/ppermute | solution.py:506
  71.1 18.5 %copy-start.4 = (s32[1024,128]{1,0:T(8,128)S(1)}, s32[1024,128]{1,0:T(8,128)}, u32[]{:S(2)}) copy-start(s32[1024,128]{1,0:T(8,128)} %copy-done.2) | copy-start | bytes 1572868
  71.2 18.4 %collective-permute-start.7 = (bf16[16,32,1024]{2,1,0:T(8,128)(2,1)S(1)}, bf16[16,32,1024]{2,1,0:T(8,128)(2,1)S(1)}, u32[]{:S(2)}, u32[]{:S(2)}) collective-permute-start(bf16[16,32,1024]{2,1,0:T(8,128)(2,1)S(1)} %cut.1), channel_id=1, source_target_pairs={{0,1},{1,0},{2,3},{3,2},{4,5},{5,4},{6,7},{7,6},{8,9},{9,8},{10,11... | collective-permute-start | bytes 3145736 | tf_op jit(solution)/shard_map/ppermute | solution.py:509
  73.3 16.3 %collective-permute-start.9 = (bf16[512,1024]{1,0:T(8,128)(2,1)S(1)}, bf16[512,1024]{1,0:T(8,128)(2,1)S(1)}, u32[]{:S(2)}, u32[]{:S(2)}) collective-permute-start(bf16[512,1024]{1,0:T(8,128)(2,1)S(1)} %follow.1.low01), channel_id=1, source_target_pairs={{0,1},{1,0},{2,3},{3,2},{4,5},{5,4},{6,7},{7,6},{8,9},{9,8},{10,11... | collective-permute-start | bytes 3145736 | tf_op jit(solution)/shard_map/ppermute | solution.py:509
  74.0 14.8 %collective-permute-start = (bf16[256,1024]{1,0:T(8,128)(2,1)S(1)}, bf16[256,1024]{1,0:T(8,128)(2,1)S(1)}, u32[]{:S(2)}, u32[]{:S(2)}) collective-permute-start(bf16[256,1024]{1,0:T(8,128)(2,1)S(1)} %slice.8), channel_id=1, source_target_pairs={{0,2},{1,3},{2,4},{3,5},{4,6},{5,7},{6,0},{7,1},{8,10},{9,11},{10,... | collective-permute-start | bytes 1572872 | tf_op jit(solution)/shard_map/ppermute | solution.py:506
  74.8 25.3 %collective-permute-start.3 = (bf16[256,1024]{1,0:T(8,128)(2,1)S(1)}, bf16[256,1024]{1,0:T(8,128)(2,1)S(1)}, u32[]{:S(2)}, u32[]{:S(2)}) collective-permute-start(bf16[256,1024]{1,0:T(8,128)(2,1)S(1)} %slice.8), channel_id=1, source_target_pairs={{0,6},{1,7},{2,0},{3,1},{4,2},{5,3},{6,4},{7,5},{8,14},{9,15},{10,... | collective-permute-start | bytes 1572872 | tf_op jit(solution)/shard_map/ppermute | solution.py:506
  88.8 17.1 %collective-permute-start.1 = (bf16[256,1024]{1,0:T(8,128)(2,1)S(1)}, bf16[256,1024]{1,0:T(8,128)(2,1)S(1)}, u32[]{:S(2)}, u32[]{:S(2)}) collective-permute-start(bf16[256,1024]{1,0:T(8,128)(2,1)S(1)} %collective-permute-done.low2), channel_id=1, source_target_pairs={{0,1},{1,0},{2,3},{3,2},{4,5},{5,4},{6,7},{7,6},{8,9},{9,8},{10,11... | collective-permute-start | bytes 1572872 | tf_op jit(solution)/shard_map/ppermute | solution.py:509

commit v4 on v3

--- a/solution.py
+++ b/solution.py
@@ -308,10 +308,6 @@
     return {q: (n, q * QUARTER) for q in range(3)}
 
 
-def halves(n):
-    return {q: (n, q * QUARTER) for q in range(2)}
-
-
 def join_kernel(pools, rest, low_rest, high_rest, out):
     width = QUARTER // pools
     for n, part in enumerate((rest, low_rest, high_rest)):
@@ -323,8 +319,8 @@
     out[...] = arrived[:, : out.shape[1], :]
 
 
-def follow_kernel(rows, after, out):
-    del after
+def follow_kernel(rows, after, also_after, out):
+    del after, also_after
     out[...] = rows[...]
 
 
@@ -338,66 +334,56 @@
     tiles.finish(None, out)
 
 
-def middle_kernel(
-    own0, arrived, high01, sib0, swapped, low01, lows01, meta, codes, before, out,
-    sims, rows, cols, sems, *held,
+def early_kernel(
+    own0, arrived, sib0, swapped, meta, codes, before, out, sims, rows, cols, sems, *held
 ):
-    fetch = Fetch((own0, arrived, high01, sib0, swapped, low01, lows01), held, sems)
+    fetch = Fetch((own0, arrived, sib0, swapped), held, sems)
     width = arrived.shape[1] // 3
     tiles = Tiles(
         fetch, meta, codes, rows, cols,
         parts_of(
             own={**whole(0), 3: (1, 0)},
-            sib={**whole(3), 3: (4, 0)},
-            low={**halves(5), 3: (1, width)},
-            lows={**halves(6), 3: (4, width)},
-            high={**halves(2), 3: (1, 2 * width)},
+            sib={**whole(2), 3: (3, 0)},
+            low={3: (1, width)},
+            lows={3: (3, width)},
+            high={3: (1, 2 * width)},
         ),
     )
     pieces = [tiles.piece(OWN, 0, 3, OWN, 3), tiles.piece(OWN, 3, 1, OWN, 3, same=0)]
     for cls in (OWN, SIB):
-        for b in (3, 0, 1):
-            pieces.append(tiles.piece(cls, 0, 3, HIGH, b))
-            pieces.append(tiles.piece(cls, 3, 1, HIGH, b))
+        pieces.append(tiles.piece(cls, 0, 3, HIGH, 3))
+        pieces.append(tiles.piece(cls, 3, 1, HIGH, 3))
     run(pieces, sims)
     fetch.all()
     pairs = [(a, b) for b in range(4) for a in range(4) if 3 in (a, b)]
     either(second_core(), lambda flip: run(tiles.matched(flip, OWN, SIB, pairs), sims))
-    pairs = [(a, b) for b in (0, 1, 3) for a in (0, 1, 3)]
-    either(
-        outer_chip(),
-        lambda flip: run(
-            tiles.matched(flip, LOW, HIGH, pairs) + tiles.matched(flip, LOWS, HIGH, pairs), sims
-        ),
-    )
+    both = [tiles.piece(cls, 3, 1, HIGH, 3) for cls in (LOW, LOWS)]
+    pl.when(jnp.logical_not(outer_chip()))(lambda: run(both, sims))
     tiles.finish(before, out)
 
 
 def late_kernel(
-    own0, high2, sib0, arrived, swapped, low2, low01, lows01, high01, meta, codes, before, out,
+    own0, high0, sib0, arrived, swapped, low0, meta, codes, before, out,
     sims, rows, cols, sems, *held,
 ):
-    fetch = Fetch((own0, high2, sib0, arrived, swapped, low2, low01, lows01, high01), held, sems)
+    fetch = Fetch((own0, high0, sib0, arrived, swapped, low0), held, sems)
     width = arrived.shape[1] // 3
     tiles = Tiles(
         fetch, meta, codes, rows, cols,
         parts_of(
             own={**whole(0), 3: (3, 0)},
             sib={**whole(2), 3: (4, 0)},
-            low={**halves(6), 2: (5, 0), 3: (3, width)},
-            lows={**halves(7), 3: (4, width)},
-            high={**halves(8), 2: (1, 0), 3: (3, 2 * width)},
+            low={**whole(5), 3: (3, width)},
+            lows={3: (4, width)},
+            high={**whole(1), 3: (3, 2 * width)},
         ),
     )
-    pieces = []
-    for cls in (OWN, SIB):
-        pieces.append(tiles.piece(cls, 0, 3, HIGH, 2))
-    for cls in (OWN, SIB):
-        pieces.append(tiles.piece(cls, 3, 1, HIGH, 2))
+    pieces = [tiles.piece(cls, 0, 3, HIGH, b) for cls in (OWN, SIB) for b in range(3)]
+    pieces += [tiles.piece(cls, 3, 1, HIGH, b) for cls in (OWN, SIB) for b in range(3)]
     run(pieces, sims)
     fetch.all()
-    pairs = [(a, b) for b in range(4) for a in range(4) if 2 in (a, b)]
-    others = [(a, 2) for a in (0, 1, 3)]
+    pairs = [(a, b) for b in range(4) for a in range(4) if (a, b) != (3, 3)]
+    others = [(3, b) for b in range(3)]
     either(
         outer_chip(),
         lambda flip: run(
@@ -408,22 +394,20 @@
 
 
 def last_kernel(
-    pools, group, main, rest, lows2, high01, high2, arrived, meta, codes, before, out,
+    pools, group, main, rest, lows0, high0, arrived, meta, codes, before, out,
     sims, rows, cols, best, every, sems, *held,
 ):
-    fetch = Fetch((lows2, high01, high2, arrived), held, sems)
+    fetch = Fetch((lows0, high0, arrived), held, sems)
     width = arrived.shape[1] // 3
     tiles = Tiles(
         fetch, meta, codes, rows, cols,
-        parts_of(lows={2: (0, 0)}, high={**halves(1), 2: (2, 0), 3: (3, 2 * width)}),
+        parts_of(lows=whole(0), high={**whole(1), 3: (2, 2 * width)}),
     )
     fetch.all()
-    pairs = [(2, b) for b in range(4)]
+    pairs = [(a, b) for b in range(4) for a in range(3)]
     either(outer_chip(), lambda flip: run(tiles.matched(flip, LOWS, HIGH, pairs), sims))
     best[...] = before[...]
-    span = slice(2 * QUARTER, 3 * QUARTER)
-    found = jnp.max(jnp.transpose(rows[LOWS, span, :]), axis=0, keepdims=True)
-    best[LOWS : LOWS + 1, span] = jnp.maximum(best[LOWS : LOWS + 1, span], found)
+    best[LOWS : LOWS + 1, :] = jnp.maximum(best[LOWS : LOWS + 1, :], row_result(rows.at[LOWS]))
     best[HIGH : HIGH + 1, :] = jnp.maximum(best[HIGH : HIGH + 1, :], col_result(cols.at[HIGH]))
     every[...] = jnp.zeros(every.shape, F32)
     for cls, place in enumerate(tiles.relatives):
@@ -528,8 +512,7 @@
         name="join",
     )(rest, low_rest, high_rest)
     arrived = to_pools(sent)
-    early = own0[: 2 * QUARTER]
-    low01, high01 = shift(early, 2), shift(early, -2)
+    low0, high0 = shift(own0, 2), shift(own0, -2)
     sib0 = swap(own0)
 
     def tiles(kernel, name, squares, operands, small, out_shape=sds((8, rows_dev), F32), more=()):
@@ -551,8 +534,6 @@
         )(*operands, *small)
 
     near = tiles(near_kernel, "near", 11, (own0, sib0), (meta, codes))
-    tail = own0[2 * QUARTER :]
-    low2, high2 = shift(tail, 2), shift(tail, -2)
     crossing = pl.pallas_call(
         cut_kernel,
         out_shape=sds((pools, 2 * QUARTER // pools, feature), BF16),
@@ -561,25 +542,24 @@
         name="cut",
     )(arrived, near)
     swapped = swap(crossing)
-    low01 = pl.pallas_call(
-        follow_kernel,
-        out_shape=sds(low01.shape, BF16),
-        in_specs=[vmem, hbm],
-        compiler_params=PARAMS,
-        name="follow",
-    )(low01, near)
-    lows01 = swap(low01)
-    middle = tiles(
-        middle_kernel, "middle", 42,
-        (own0, arrived, high01, sib0, swapped, low01, lows01), (meta, codes, near),
+    early = tiles(
+        early_kernel, "early", 16, (own0, arrived, sib0, swapped), (meta, codes, near)
+    )
+    lows0 = swap(
+        pl.pallas_call(
+            follow_kernel,
+            out_shape=sds(low0.shape, BF16),
+            in_specs=[vmem, hbm, hbm],
+            compiler_params=PARAMS,
+            name="follow",
+        )(low0, high0, early)
     )
     late = tiles(
-        late_kernel, "late", 14,
-        (own0, high2, sib0, arrived, swapped, low2, low01, lows01, high01), (meta, codes, middle),
+        late_kernel, "late", 32, (own0, high0, sib0, arrived, swapped, low0), (meta, codes, early)
     )
     best = tiles(
         lambda *refs: last_kernel(pools, group, group * (places - last), group * last, *refs),
-        "last", 2, (swap(low2), high01, high2, arrived), (meta, codes, late),
+        "last", 6, (lows0, high0, arrived), (meta, codes, late),
         out_shape=sds((devices, group * places), F32),
         more=(pltpu.VMEM((8, rows_dev), F32), pltpu.VMEM((group, rows_dev), F32)),
     )

time: 126 us -> 117 us (0.929)
  waiting for transfers between devices: 46.5 us -> 37.1 us
  Pallas kernels: 35 us -> 37.5 us
    ppermute x6 -> x4, waiting for transfers between devices: 12.1 us -> 5.9 us  [shift(): lax.ppermute(rows, 'grp', [(g, (g + by) % group) for g in range(group)])]
    all_to_all x2, waiting for transfers between devices: 34.4 us -> 28.9 us  [to_pools(): return lax.all_to_all(rows, 'pool', split_axis=0, concat_axis=0, tiled=True)]
    ppermute x6 -> x4, starting transfers between devices: 8.17 us -> 5.1 us  [shift(): lax.ppermute(rows, 'grp', [(g, (g + by) % group) for g in range(group)])]
    ppermute x4 -> x3, starting transfers between devices: 4.82 us -> 7.46 us  [swap(): return lax.ppermute(rows, 'grp', [(g, g ^ 1) for g in range(group)])]
    ppermute x4 -> x3, waiting for transfers between devices: 0.01 us -> 2.29 us  [swap(): return lax.ppermute(rows, 'grp', [(g, g ^ 1) for g in range(group)])]
  transfers between devices with their start and end apart: 12 -> 9, of which waited for: 3 -> 5; matrix products, arithmetic and copies ran while one was open for 1% -> 0% of each run, Pallas kernels for 21% -> 24%
where the time goes in v4:
time: 117 us
  Pallas kernels  37.5 us (32%)
  waiting for transfers between devices  37.1 us (32%)
  starting transfers between devices  25 us (21%)
  blocking collectives  15.8 us (14%)
    all_to_all x2, waiting for transfers between devices, to_pools(): return lax.all_to_all(rows, 'pool', split_axis=0, concat_axis=0, tiled=True)  28.9 us
    pallas_call x4, Pallas kernels, tiles(): pl.pallas_call(kernel, out_shape=out_shape, in_specs=[hbm] * len(operands...  22.8 us
    all_to_all x1, blocking collectives, body(): lax.all_to_all(best, ('pool', 'grp'), split_axis=0, concat_axis=0, tiled=...  15.8 us
    all_to_all x2, starting transfers between devices, to_pools(): return lax.all_to_all(rows, 'pool', split_axis=0, concat_axis=0, tiled=True)  12.5 us
    ppermute x3, starting transfers between devices, swap(): return lax.ppermute(rows, 'grp', [(g, g ^ 1) for g in range(group)])  7.46 us
    ppermute x4, waiting for transfers between devices, shift(): lax.ppermute(rows, 'grp', [(g, (g + by) % group) for g in range(group)])  5.9 us
    pallas_call x1, Pallas kernels, body(): pl.pallas_call(lambda *refs: table_kernel(pools, group, places, last, *re...  5.16 us
    ppermute x4, starting transfers between devices, shift(): lax.ppermute(rows, 'grp', [(g, (g + by) % group) for g in range(group)])  5.1 us
  transfers between devices with their start and end apart: 9, of which 5 were waited for; matrix products, arithmetic and copies ran while one was open for 0% of the time, Pallas kernels for 24%

profile of v4, /device:TPU:1, one launch (start us, length us, event | category | flops | bytes accessed | tf_op | source)
XLA Modules:
  0.0 116.7 jit_solution(8024237242255344652)
XLA Ops:
  0.0 5.2 %table.1 = (s32[128,128]{1,0:T(8,128)}, bf16[768,1024]{1,0:T(8,128)(2,1)}) custom-call(s32[256,512]{1,0:T(8,128)} %refs_0_.3, s32[1,256]{1,0:T(1,128)} %bitcast.11, bf16[1024,1024]{1,0:T(8,128)(2,1)} %refs_1_.1), custom_call_target="tpu_custom_call" | custom-call | flops 2147483648 | tf_op jit(solution)/shard_map/table/pallas_call | solution.py:455
  5.2 0.0 copy-start.5
  5.2 0.0 copy-start.6
  5.2 0.0 copy-start.7
  5.2 8.8 %all-to-all-start = ((bf16[16,48,1024]{2,1,0:T(8,128)(2,1)}), bf16[16,48,1024]{2,1,0:T(8,128)(2,1)}, u32[]{:S(2)}, u32[]{:S(2)}) async-start(bf16[16,48,1024]{2,1,0:T(8,128)(2,1)} %bitcast.14), calls=%async_computation | async-start | bytes 3145728 | tf_op jit(solution)/shard_map/all_to_all | solution.py:496
  14.0 0.0 copy-start
  14.0 4.5 %meta.1 = (s32[2,8,1024]{2,1,0:T(8,128)S(1)}, s32[1024,128]{1,0:T(8,128)S(1)}) custom-call(s32[256,512]{1,0:T(8,128)S(1)} %copy-done.5, s32[1,256]{1,0:T(1,128)S(1)} %bitcast.12, s32[1,256]{1,0:T(1,128)S(1)} %bitcast.13), custom_call_target="tpu_custom_call" | custom-call | flops 4294967296 | tf_op jit(solution)/shard_map/meta/pallas_call | solution.py:473
  18.5 0.9 rest.1.refs_0_
  19.4 2.5 %collective-permute-start.3 = (bf16[256,1024]{1,0:T(8,128)(2,1)S(1)}, bf16[256,1024]{1,0:T(8,128)(2,1)S(1)}, u32[]{:S(2)}, u32[]{:S(2)}) collective-permute-start(bf16[256,1024]{1,0:T(8,128)(2,1)S(1)} %rest.1.refs_0_), channel_id=1, source_target_pairs={{0,6},{1,7},{2,0},{3,1},{4,2},{5,3},{6,4},{7,5},{8,14},{9,15},{10,... | collective-permute-start | bytes 1572872 | tf_op jit(solution)/shard_map/ppermute | solution.py:490
  22.0 15.0 %all-to-all-done = bf16[16,48,1024]{2,1,0:T(8,128)(2,1)} async-done(((bf16[16,48,1024]{2,1,0:T(8,128)(2,1)}), bf16[16,48,1024]{2,1,0:T(8,128)(2,1)}, u32[]{:S(2)}, u32[]{:S(2)}) %all-to-all-start) | async-done | bytes 1572896 | tf_op jit(solution)/shard_map/all_to_all | solution.py:496
  36.9 2.5 %collective-permute-start.4 = (bf16[768,1024]{1,0:T(8,128)(2,1)}, bf16[768,1024]{1,0:T(8,128)(2,1)}, u32[]{:S(2)}, u32[]{:S(2)}) collective-permute-start(bf16[768,1024]{1,0:T(8,128)(2,1)} %bitcast.2.own0), channel_id=1, source_target_pairs={{0,1},{1,0},{2,3},{3,2},{4,5},{5,4},{6,7},{7,6},{8,9},{9,8},{10,11... | collective-permute-start | bytes 4718600 | tf_op jit(solution)/shard_map/ppermute | solution.py:493
  39.5 0.0 collective-permute-done.2.refs_1_
  39.5 1.3 %join.1 = bf16[16,48,1024]{2,1,0:T(8,128)(2,1)} custom-call(bf16[256,1024]{1,0:T(8,128)(2,1)S(1)} %rest.1.refs_0_, bf16[256,1024]{1,0:T(8,128)(2,1)S(1)} %collective-permute-done.2.refs_1_, bf16[256,1024]{1,0:T(8,128)(2,1)S(1)} %collective-permute-done.3.refs_2_), custom_call_target="tpu_custom_call" | custom-call | tf_op jit(solution)/shard_map/join/pallas_call | solution.py:508
  40.8 3.7 %all-to-all-start.1 = ((bf16[16,48,1024]{2,1,0:T(8,128)(2,1)}), bf16[16,48,1024]{2,1,0:T(8,128)(2,1)S(1)}, u32[]{:S(2)}, u32[]{:S(2)}) async-start(bf16[16,48,1024]{2,1,0:T(8,128)(2,1)} %join.1), calls=%async_computation.1 | async-start | bytes 3145728 | tf_op jit(solution)/shard_map/all_to_all | solution.py:496
  44.5 2.5 %collective-permute-start.1 = (bf16[768,1024]{1,0:T(8,128)(2,1)}, bf16[768,1024]{1,0:T(8,128)(2,1)S(1)}, u32[]{:S(2)}, u32[]{:S(2)}) collective-permute-start(bf16[768,1024]{1,0:T(8,128)(2,1)} %bitcast.2.own0), channel_id=1, source_target_pairs={{0,6},{1,7},{2,0},{3,1},{4,2},{5,3},{6,4},{7,5},{8,14},{9,15},{10,... | collective-permute-start | bytes 4718600 | tf_op jit(solution)/shard_map/ppermute | solution.py:490
  47.0 0.0 collective-permute-start
  47.0 0.0 collective-permute-done.4.sib0
  47.1 1.0 copy-done.2
  48.1 4.2 %near.1.after.before = f32[8,1024]{1,0:T(8,128)S(1)} custom-call(bf16[768,1024]{1,0:T(8,128)(2,1)} %bitcast.2.own0, bf16[768,1024]{1,0:T(8,128)(2,1)} %collective-permute-done.4.sib0, s32[2,8,1024]{2,1,0:T(8,128)S(1)} %get-tuple-element.11.refs_2_.meta.refs_3_, s32[1024,128]{1,0:T(8,128)S(1)} %copy-done.2), custom_call_target="tpu_custom_call" | custom-call | flops 1476395008 | tf_op jit(solution)/shard_map/near/pallas_call | solution.py:519
  52.3 13.9 %all-to-all-done.1.arrived.refs_2_ = bf16[16,48,1024]{2,1,0:T(8,128)(2,1)S(1)} async-done(((bf16[16,48,1024]{2,1,0:T(8,128)(2,1)}), bf16[16,48,1024]{2,1,0:T(8,128)(2,1)S(1)}, u32[]{:S(2)}, u32[]{:S(2)}) %all-to-all-start.1) | async-done | bytes 1572896 | tf_op jit(solution)/shard_map/all_to_all | solution.py:496
  66.2 0.1 cut.1
  66.3 3.5 %collective-permute-start.5 = (bf16[16,32,1024]{2,1,0:T(8,128)(2,1)S(1)}, bf16[16,32,1024]{2,1,0:T(8,128)(2,1)S(1)}, u32[]{:S(2)}, u32[]{:S(2)}) collective-permute-start(bf16[16,32,1024]{2,1,0:T(8,128)(2,1)S(1)} %cut.1), channel_id=1, source_target_pairs={{0,1},{1,0},{2,3},{3,2},{4,5},{5,4},{6,7},{7,6},{8,9},{9,8},{10,11... | collective-permute-start | bytes 3145736 | tf_op jit(solution)/shard_map/ppermute | solution.py:493
  69.8 2.3 %collective-permute-done.5.swapped = bf16[16,32,1024]{2,1,0:T(8,128)(2,1)S(1)} collective-permute-done((bf16[16,32,1024]{2,1,0:T(8,128)(2,1)S(1)}, bf16[16,32,1024]{2,1,0:T(8,128)(2,1)S(1)}, u32[]{:S(2)}, u32[]{:S(2)}) %collective-permute-start.5) | collective-permute-done | bytes 1048608 | tf_op jit(solution)/shard_map/ppermute | solution.py:493
  72.1 6.3 %early.1.also_after.before = f32[8,1024]{1,0:T(8,128)S(1)} custom-call(bf16[768,1024]{1,0:T(8,128)(2,1)} %bitcast.2.own0, bf16[16,48,1024]{2,1,0:T(8,128)(2,1)S(1)} %all-to-all-done.1.arrived.refs_2_, bf16[768,1024]{1,0:T(8,128)(2,1)} %collective-permute-done.4.sib0, bf16[16,32,1024]{2,1,0:T(8,128)(2,1)S(1)} %collective-permute-done.5.swapped, ...), custom_call_target="tpu_custom_call" | custom-call | flops 2147483648 | tf_op jit(solution)/shard_map/early/pallas_call | solution.py:519
  78.4 2.8 %collective-permute-done.1.after.high0.refs_1_ = bf16[768,1024]{1,0:T(8,128)(2,1)S(1)} collective-permute-done((bf16[768,1024]{1,0:T(8,128)(2,1)}, bf16[768,1024]{1,0:T(8,128)(2,1)S(1)}, u32[]{:S(2)}, u32[]{:S(2)}) %collective-permute-start.1) | collective-permute-done | bytes 1572896 | tf_op jit(solution)/shard_map/ppermute | solution.py:490
  81.2 3.1 %collective-permute-done.rows.low0 = bf16[768,1024]{1,0:T(8,128)(2,1)} collective-permute-done((bf16[768,1024]{1,0:T(8,128)(2,1)}, bf16[768,1024]{1,0:T(8,128)(2,1)}, u32[]{:S(2)}, u32[]{:S(2)}) %collective-permute-start) | collective-permute-done | bytes 1572896 | tf_op jit(solution)/shard_map/ppermute | solution.py:490
  84.3 1.5 %follow.1 = bf16[768,1024]{1,0:T(8,128)(2,1)S(1)} custom-call(bf16[768,1024]{1,0:T(8,128)(2,1)} %collective-permute-done.rows.low0, bf16[768,1024]{1,0:T(8,128)(2,1)S(1)} %collective-permute-done.1.after.high0.refs_1_, f32[8,1024]{1,0:T(8,128)S(1)} %early.1.also_after.before), custom_call_target="tpu_custom_call" | custom-call | tf_op jit(solution)/shard_map/follow/pallas_call | solution.py:549
  85.8 1.4 %collective-permute-start.6 = (bf16[768,1024]{1,0:T(8,128)(2,1)S(1)}, bf16[768,1024]{1,0:T(8,128)(2,1)S(1)}, u32[]{:S(2)}, u32[]{:S(2)}) collective-permute-start(bf16[768,1024]{1,0:T(8,128)(2,1)S(1)} %follow.1), channel_id=1, source_target_pairs={{0,1},{1,0},{2,3},{3,2},{4,5},{5,4},{6,7},{7,6},{8,9},{9,8},{10,11... | collective-permute-start | bytes 4718600 | tf_op jit(solution)/shard_map/ppermute | solution.py:493
  87.2 10.3 %late.1.refs_5_ = f32[8,1024]{1,0:T(8,128)S(1)} custom-call(bf16[768,1024]{1,0:T(8,128)(2,1)} %bitcast.2.own0, bf16[768,1024]{1,0:T(8,128)(2,1)S(1)} %collective-permute-done.1.after.high0.refs_1_, bf16[768,1024]{1,0:T(8,128)(2,1)} %collective-permute-done.4.sib0, bf16[16,48,1024]{2,1,0:T(8,128)(2,1)S(1)} %all-to-all-done.1.arrived.refs_2_, ...), custom_call_target="tpu_custom_call" | custom-call | flops 4294967296 | tf_op jit(solution)/shard_map/late/pallas_call | solution.py:519
  97.5 2.0 %last.1 = f32[128,64]{1,0:T(8,128)S(1)} custom-call(bf16[768,1024]{1,0:T(8,128)(2,1)S(1)} %collective-permute-done.6.refs_0_, bf16[768,1024]{1,0:T(8,128)(2,1)S(1)} %collective-permute-done.1.after.high0.refs_1_, bf16[16,48,1024]{2,1,0:T(8,128)(2,1)S(1)} %all-to-all-done.1.arrived.refs_2_, s32[2,8,1024]{2,1,0:T(8,128)S(1)} %get-tuple-element.11.refs_2_.meta.refs_3_, ...), custom_call_target="tpu_custom_call" | custom-call | flops 805306368 | tf_op jit(solution)/shard_map/last/pallas_call | solution.py:519
  99.5 15.8 %all_to_all.21 = f32[128,1,64]{2,1,0:T(1,128)S(1)} all-to-all(f32[128,1,64]{2,1,0:T(1,128)S(1)} %bitcast.9), channel_id=1, replica_groups=mesh['pool'=16,'grp'=8] {'pool','grp'}, dimensions={0} | all-to-all | bytes 65536 | tf_op jit(solution)/shard_map/all_to_all | solution.py:566
  115.3 1.4 %score.1 = f32[1,1024]{1,0:T(1,128)} custom-call(s32[128,128]{1,0:T(8,128)S(1)} %copy-done.4, f32[128,64]{1,0:T(8,128)S(1)} %bitcast.10), custom_call_target="tpu_custom_call" | custom-call | tf_op jit(solution)/shard_map/score/pallas_call | solution.py:567
  (14 shorter events, 0.0 us)
Async XLA Ops:
  5.2 8.8 %copy-start.5 = (s32[256,512]{1,0:T(8,128)S(1)}, s32[256,512]{1,0:T(8,128)}, u32[]{:S(2)}) copy-start(s32[256,512]{1,0:T(8,128)} %refs_0_.3) | copy-start | bytes 1572868
  5.2 8.8 %copy-start.6 = (s32[256]{0:T(256)S(1)}, s32[256]{0:T(256)}, u32[]{:S(2)}) copy-start(s32[256]{0:T(256)} %param.6) | copy-start | bytes 3076
  5.2 8.8 %copy-start.7 = (s32[256]{0:T(256)S(1)}, s32[256]{0:T(256)}, u32[]{:S(2)}) copy-start(s32[256]{0:T(256)} %param.7) | copy-start | bytes 3076
  5.2 31.7 %all-to-all-start = ((bf16[16,48,1024]{2,1,0:T(8,128)(2,1)}), bf16[16,48,1024]{2,1,0:T(8,128)(2,1)}, u32[]{:S(2)}, u32[]{:S(2)}) async-start(bf16[16,48,1024]{2,1,0:T(8,128)(2,1)} %bitcast.14), calls=%async_computation | async-start | bytes 3145728 | tf_op jit(solution)/shard_map/all_to_all | solution.py:496
  14.0 4.5 %copy-start = (bf16[1024,1024]{1,0:T(8,128)(2,1)S(1)}, bf16[1024,1024]{1,0:T(8,128)(2,1)}, u32[]{:S(2)}) copy-start(bf16[1024,1024]{1,0:T(8,128)(2,1)} %refs_1_.1) | copy-start | bytes 6291460
  14.0 4.5 %copy-start.4 = (s32[128,128]{1,0:T(8,128)S(1)}, s32[128,128]{1,0:T(8,128)}, u32[]{:S(2)}) copy-start(s32[128,128]{1,0:T(8,128)} %get-tuple-element.9.refs_0_) | copy-start | bytes 196612
  18.5 0.9 copy-start.1
  19.4 20.1 %collective-permute-start.3 = (bf16[256,1024]{1,0:T(8,128)(2,1)S(1)}, bf16[256,1024]{1,0:T(8,128)(2,1)S(1)}, u32[]{:S(2)}, u32[]{:S(2)}) collective-permute-start(bf16[256,1024]{1,0:T(8,128)(2,1)S(1)} %rest.1.refs_0_), channel_id=1, source_target_pairs={{0,6},{1,7},{2,0},{3,1},{4,2},{5,3},{6,4},{7,5},{8,14},{9,15},{10,... | collective-permute-start | bytes 1572872 | tf_op jit(solution)/shard_map/ppermute | solution.py:490
  22.0 17.5 %collective-permute-start.2 = (bf16[256,1024]{1,0:T(8,128)(2,1)S(1)}, bf16[256,1024]{1,0:T(8,128)(2,1)S(1)}, u32[]{:S(2)}, u32[]{:S(2)}) collective-permute-start(bf16[256,1024]{1,0:T(8,128)(2,1)S(1)} %rest.1.refs_0_), channel_id=1, source_target_pairs={{0,2},{1,3},{2,4},{3,5},{4,6},{5,7},{6,0},{7,1},{8,10},{9,11},{10,... | collective-permute-start | bytes 1572872 | tf_op jit(solution)/shard_map/ppermute | solution.py:490
  36.9 10.1 %collective-permute-start.4 = (bf16[768,1024]{1,0:T(8,128)(2,1)}, bf16[768,1024]{1,0:T(8,128)(2,1)}, u32[]{:S(2)}, u32[]{:S(2)}) collective-permute-start(bf16[768,1024]{1,0:T(8,128)(2,1)} %bitcast.2.own0), channel_id=1, source_target_pairs={{0,1},{1,0},{2,3},{3,2},{4,5},{5,4},{6,7},{7,6},{8,9},{9,8},{10,11... | collective-permute-start | bytes 4718600 | tf_op jit(solution)/shard_map/ppermute | solution.py:493
  40.8 25.4 %all-to-all-start.1 = ((bf16[16,48,1024]{2,1,0:T(8,128)(2,1)}), bf16[16,48,1024]{2,1,0:T(8,128)(2,1)S(1)}, u32[]{:S(2)}, u32[]{:S(2)}) async-start(bf16[16,48,1024]{2,1,0:T(8,128)(2,1)} %join.1), calls=%async_computation.1 | async-start | bytes 3145728 | tf_op jit(solution)/shard_map/all_to_all | solution.py:496
  44.5 36.7 %collective-permute-start.1 = (bf16[768,1024]{1,0:T(8,128)(2,1)}, bf16[768,1024]{1,0:T(8,128)(2,1)S(1)}, u32[]{:S(2)}, u32[]{:S(2)}) collective-permute-start(bf16[768,1024]{1,0:T(8,128)(2,1)} %bitcast.2.own0), channel_id=1, source_target_pairs={{0,6},{1,7},{2,0},{3,1},{4,2},{5,3},{6,4},{7,5},{8,14},{9,15},{10,... | collective-permute-start | bytes 4718600 | tf_op jit(solution)/shard_map/ppermute | solution.py:490
  47.0 37.2 %collective-permute-start = (bf16[768,1024]{1,0:T(8,128)(2,1)}, bf16[768,1024]{1,0:T(8,128)(2,1)}, u32[]{:S(2)}, u32[]{:S(2)}) collective-permute-start(bf16[768,1024]{1,0:T(8,128)(2,1)} %bitcast.2.own0), channel_id=1, source_target_pairs={{0,2},{1,3},{2,4},{3,5},{4,6},{5,7},{6,0},{7,1},{8,10},{9,11},{10,... | collective-permute-start | bytes 4718600 | tf_op jit(solution)/shard_map/ppermute | solution.py:490
  47.0 1.0 copy-start.2
  66.2 5.9 %copy-start.3 = (s32[1024,128]{1,0:T(8,128)S(1)}, s32[1024,128]{1,0:T(8,128)}, u32[]{:S(2)}) copy-start(s32[1024,128]{1,0:T(8,128)} %copy-done.1) | copy-start | bytes 1572868
  66.3 5.8 %collective-permute-start.5 = (bf16[16,32,1024]{2,1,0:T(8,128)(2,1)S(1)}, bf16[16,32,1024]{2,1,0:T(8,128)(2,1)S(1)}, u32[]{:S(2)}, u32[]{:S(2)}) collective-permute-start(bf16[16,32,1024]{2,1,0:T(8,128)(2,1)S(1)} %cut.1), channel_id=1, source_target_pairs={{0,1},{1,0},{2,3},{3,2},{4,5},{5,4},{6,7},{7,6},{8,9},{9,8},{10,11... | collective-permute-start | bytes 3145736 | tf_op jit(solution)/shard_map/ppermute | solution.py:493
  85.8 11.7 %collective-permute-start.6 = (bf16[768,1024]{1,0:T(8,128)(2,1)S(1)}, bf16[768,1024]{1,0:T(8,128)(2,1)S(1)}, u32[]{:S(2)}, u32[]{:S(2)}) collective-permute-start(bf16[768,1024]{1,0:T(8,128)(2,1)S(1)} %follow.1), channel_id=1, source_target_pairs={{0,1},{1,0},{2,3},{3,2},{4,5},{5,4},{6,7},{7,6},{8,9},{9,8},{10,11... | collective-permute-start | bytes 4718600 | tf_op jit(solution)/shard_map/ppermute | solution.py:493

commit v5 on v4

--- a/solution.py
+++ b/solution.py
@@ -167,8 +167,10 @@
     codes_ref[...] = jnp.transpose(packed_ref[...])
 
 
-def run(pieces, sims_ref):
+def run(pieces, sims_ref, fetch=None):
     for n in range(len(pieces) + 1):
+        if n == 1 and fetch is not None:
+            fetch.rest()
         if n < len(pieces):
             piece = pieces[n]
             sims_ref[n % 2, : piece["count"], :] = lax.dot_general(
@@ -219,21 +221,27 @@
 
 
 class Fetch:
-    def __init__(self, sources, held, sems):
-        self.held, self.copies = dict(), dict()
+    def __init__(self, sources, held, sems, first):
+        self.copies, self.held, self.waited = [], held, set()
         for n, source in enumerate(sources):
-            copy = pltpu.make_async_copy(source, held[n], sems.at[n])
+            self.copies.append(pltpu.make_async_copy(source, held[n], sems.at[n]))
+        for copy in self.copies[:first]:
             copy.start()
-            self.held[n], self.copies[n] = held[n], copy
+        self.late = self.copies[first:]
 
     def get(self, n):
-        copy = self.copies.pop(n, None)
-        if copy is not None:
-            copy.wait()
+        if n not in self.waited:
+            self.copies[n].wait()
+            self.waited.add(n)
         return self.held[n]
 
+    def rest(self):
+        for copy in self.late:
+            copy.start()
+        self.late = []
+
     def all(self):
-        for n in list(self.copies):
+        for n in range(len(self.copies)):
             self.get(n)
 
 
@@ -314,59 +322,42 @@
         out[:, n * width : (n + 1) * width, :] = part[...].reshape(pools, width, -1)
 
 
-def cut_kernel(arrived, after, out):
-    del after
-    out[...] = arrived[:, : out.shape[1], :]
-
-
 def follow_kernel(rows, after, also_after, out):
-    del after, also_after
-    out[...] = rows[...]
-
-
-def near_kernel(own0, sib0, meta, codes, out, sims, rows, cols, sems, *held):
-    fetch = Fetch((own0, sib0), held, sems)
-    tiles = Tiles(fetch, meta, codes, rows, cols, parts_of(own=whole(0), sib=whole(1)))
-    run([tiles.piece(OWN, 0, b + 1, OWN, b, same=b * QUARTER) for b in range(3)], sims)
-    fetch.all()
-    pairs = [(a, b) for b in range(3) for a in range(3)]
-    either(second_core(), lambda flip: run(tiles.matched(flip, OWN, SIB, pairs), sims))
-    tiles.finish(None, out)
-
-
-def early_kernel(
-    own0, arrived, sib0, swapped, meta, codes, before, out, sims, rows, cols, sems, *held
-):
-    fetch = Fetch((own0, arrived, sib0, swapped), held, sems)
+    del rows, after, also_after, out
+
+
+def early_kernel(own0, sib0, arrived, swapped, meta, codes, out, sims, rows, cols, sems, *held):
+    fetch = Fetch((own0, sib0, arrived, swapped), held, sems, 1)
     width = arrived.shape[1] // 3
     tiles = Tiles(
         fetch, meta, codes, rows, cols,
         parts_of(
-            own={**whole(0), 3: (1, 0)},
-            sib={**whole(2), 3: (3, 0)},
-            low={3: (1, width)},
+            own={**whole(0), 3: (2, 0)},
+            sib={**whole(1), 3: (3, 0)},
+            low={3: (2, width)},
             lows={3: (3, width)},
-            high={3: (1, 2 * width)},
+            high={3: (2, 2 * width)},
         ),
     )
-    pieces = [tiles.piece(OWN, 0, 3, OWN, 3), tiles.piece(OWN, 3, 1, OWN, 3, same=0)]
+    pieces = [tiles.piece(OWN, 0, b + 1, OWN, b, same=b * QUARTER) for b in range(3)]
+    pieces += [tiles.piece(OWN, 0, 3, OWN, 3), tiles.piece(OWN, 3, 1, OWN, 3, same=0)]
     for cls in (OWN, SIB):
         pieces.append(tiles.piece(cls, 0, 3, HIGH, 3))
         pieces.append(tiles.piece(cls, 3, 1, HIGH, 3))
-    run(pieces, sims)
+    run(pieces, sims, fetch)
     fetch.all()
-    pairs = [(a, b) for b in range(4) for a in range(4) if 3 in (a, b)]
+    pairs = [(a, b) for b in range(4) for a in range(4)]
     either(second_core(), lambda flip: run(tiles.matched(flip, OWN, SIB, pairs), sims))
     both = [tiles.piece(cls, 3, 1, HIGH, 3) for cls in (LOW, LOWS)]
     pl.when(jnp.logical_not(outer_chip()))(lambda: run(both, sims))
-    tiles.finish(before, out)
+    tiles.finish(None, out)
 
 
 def late_kernel(
     own0, high0, sib0, arrived, swapped, low0, meta, codes, before, out,
     sims, rows, cols, sems, *held,
 ):
-    fetch = Fetch((own0, high0, sib0, arrived, swapped, low0), held, sems)
+    fetch = Fetch((own0, high0, sib0, arrived, swapped, low0), held, sems, 2)
     width = arrived.shape[1] // 3
     tiles = Tiles(
         fetch, meta, codes, rows, cols,
@@ -380,7 +371,7 @@
     )
     pieces = [tiles.piece(cls, 0, 3, HIGH, b) for cls in (OWN, SIB) for b in range(3)]
     pieces += [tiles.piece(cls, 3, 1, HIGH, b) for cls in (OWN, SIB) for b in range(3)]
-    run(pieces, sims)
+    run(pieces, sims, fetch)
     fetch.all()
     pairs = [(a, b) for b in range(4) for a in range(4) if (a, b) != (3, 3)]
     others = [(3, b) for b in range(3)]
@@ -397,7 +388,7 @@
     pools, group, main, rest, lows0, high0, arrived, meta, codes, before, out,
     sims, rows, cols, best, every, sems, *held,
 ):
-    fetch = Fetch((lows0, high0, arrived), held, sems)
+    fetch = Fetch((lows0, high0, arrived), held, sems, 3)
     width = arrived.shape[1] // 3
     tiles = Tiles(
         fetch, meta, codes, rows, cols,
@@ -511,7 +502,7 @@
         compiler_params=PARAMS,
         name="join",
     )(rest, low_rest, high_rest)
-    arrived = to_pools(sent)
+    arrived = lax.cond(jnp.any(valid > 0), to_pools, jnp.zeros_like, sent)
     low0, high0 = shift(own0, 2), shift(own0, -2)
     sib0 = swap(own0)
 
@@ -533,27 +524,18 @@
             name=name,
         )(*operands, *small)
 
-    near = tiles(near_kernel, "near", 11, (own0, sib0), (meta, codes))
-    crossing = pl.pallas_call(
-        cut_kernel,
-        out_shape=sds((pools, 2 * QUARTER // pools, feature), BF16),
-        in_specs=[vmem, hbm],
+    swapped = swap(arrived[:, : 2 * QUARTER // pools])
+    early = tiles(early_kernel, "early", 27, (own0, sib0, arrived, swapped), (meta, codes))
+    low0 = pl.pallas_call(
+        follow_kernel,
+        out_shape=sds(low0.shape, BF16),
+        in_specs=[hbm] * 3,
+        out_specs=hbm,
+        input_output_aliases={0: 0},
         compiler_params=PARAMS,
-        name="cut",
-    )(arrived, near)
-    swapped = swap(crossing)
-    early = tiles(
-        early_kernel, "early", 16, (own0, arrived, sib0, swapped), (meta, codes, near)
-    )
-    lows0 = swap(
-        pl.pallas_call(
-            follow_kernel,
-            out_shape=sds(low0.shape, BF16),
-            in_specs=[vmem, hbm, hbm],
-            compiler_params=PARAMS,
-            name="follow",
-        )(low0, high0, early)
-    )
+        name="follow",
+    )(low0, high0, early)
+    lows0 = swap(low0)
     late = tiles(
         late_kernel, "late", 32, (own0, high0, sib0, arrived, swapped, low0), (meta, codes, early)
     )

time: 117 us -> 116 us (level)
  blocking collectives: 15.8 us -> 41.2 us
  waiting for transfers between devices: 37.1 us -> 17.3 us
  starting transfers between devices: 25 us -> 18.7 us
  Pallas kernels: 37.5 us -> 35.5 us
    all_to_all x0 -> x1, blocking collectives: none -> 26.8 us  [to_pools(): return lax.all_to_all(rows, 'pool', split_axis=0, concat_axis=0, tiled=True)]
    all_to_all x2 -> x1, waiting for transfers between devices: 28.9 us -> 15 us  [to_pools(): return lax.all_to_all(rows, 'pool', split_axis=0, concat_axis=0, tiled=True)]
    ppermute x4, waiting for transfers between devices: 5.9 us -> 0.01 us  [shift(): lax.ppermute(rows, 'grp', [(g, (g + by) % group) for g in range(group)])]
    all_to_all x2 -> x1, starting transfers between devices: 12.5 us -> 8.77 us  [to_pools(): return lax.all_to_all(rows, 'pool', split_axis=0, concat_axis=0, tiled=True)]
    ppermute x3, starting transfers between devices: 7.46 us -> 4.87 us  [swap(): return lax.ppermute(rows, 'grp', [(g, g ^ 1) for g in range(group)])]
    pallas_call x1, Pallas kernels: 1.51 us -> 0.01 us  [body(): pl.pallas_call(follow_kernel, out_shape=sds(low0.shape, BF16), in_specs=[...]
    all_to_all x1, blocking collectives: 15.8 us -> 14.4 us  [body(): lax.all_to_all(best, ('pool', 'grp'), split_axis=0, concat_axis=0, tiled=...]
    slice x0 -> x1, local copies, waits for them, and re-layouts: none -> 1.37 us  [body(): swapped = swap(arrived[:, :2 * QUARTER // pools])]
  transfers between devices with their start and end apart: 9 -> 8, of which waited for: 5 -> 2; matrix products, arithmetic and copies ran while one was open for 0% -> 2% of each run, Pallas kernels for 24% -> 22%
where the time goes in v5:
time: 116 us
  blocking collectives  41.2 us (36%)
  Pallas kernels  35.5 us (31%)
  starting transfers between devices  18.7 us (16%)
  waiting for transfers between devices  17.3 us (15%)
  local copies, waits for them, and re-layouts  1.41 us (1%)
    all_to_all x1, blocking collectives, to_pools(): return lax.all_to_all(rows, 'pool', split_axis=0, concat_axis=0, tiled=True)  26.8 us
    pallas_call x3, Pallas kernels, tiles(): pl.pallas_call(kernel, out_shape=out_shape, in_specs=[hbm] * len(operands...  22.3 us
    all_to_all x1, waiting for transfers between devices, to_pools(): return lax.all_to_all(rows, 'pool', split_axis=0, concat_axis=0, tiled=True)  15 us
    all_to_all x1, blocking collectives, body(): lax.all_to_all(best, ('pool', 'grp'), split_axis=0, concat_axis=0, tiled=...  14.4 us
    all_to_all x1, starting transfers between devices, to_pools(): return lax.all_to_all(rows, 'pool', split_axis=0, concat_axis=0, tiled=True)  8.77 us
    pallas_call x1, Pallas kernels, body(): pl.pallas_call(lambda *refs: table_kernel(pools, group, places, last, *re...  5.17 us
    ppermute x4, starting transfers between devices, shift(): lax.ppermute(rows, 'grp', [(g, (g + by) % group) for g in range(group)])  5.03 us
    ppermute x3, starting transfers between devices, swap(): return lax.ppermute(rows, 'grp', [(g, g ^ 1) for g in range(group)])  4.87 us
  transfers between devices with their start and end apart: 8, of which 2 were waited for; matrix products, arithmetic and copies ran while one was open for 2% of the time, Pallas kernels for 22%

profile of v5, /device:TPU:1, one launch (start us, length us, event | category | flops | bytes accessed | tf_op | source)
XLA Modules:
  0.0 115.6 jit_solution(1052787119471688635)
XLA Ops:
  0.0 5.2 %table.1 = (s32[128,128]{1,0:T(8,128)}, bf16[768,1024]{1,0:T(8,128)(2,1)}) custom-call(s32[256,512]{1,0:T(8,128)} %refs_0_.3, s32[1,256]{1,0:T(1,128)} %bitcast.12, bf16[1024,1024]{1,0:T(8,128)(2,1)} %refs_1_.1), custom_call_target="tpu_custom_call" | custom-call | flops 2147483648 | tf_op jit(solution)/shard_map/table/pallas_call | solution.py:446
  5.2 0.0 copy-start.4
  5.2 0.0 copy-start.5
  5.2 0.0 copy-start.6
  5.2 8.8 %all-to-all-start.1 = ((bf16[16,48,1024]{2,1,0:T(8,128)(2,1)}), bf16[16,48,1024]{2,1,0:T(8,128)(2,1)}, u32[]{:S(2)}, u32[]{:S(2)}) async-start(bf16[16,48,1024]{2,1,0:T(8,128)(2,1)} %bitcast.14), calls=%async_computation.1 | async-start | bytes 3145728 | tf_op jit(solution)/shard_map/all_to_all | solution.py:487
  14.0 0.0 copy-start
  14.0 4.4 %meta.1 = (s32[2,8,1024]{2,1,0:T(8,128)S(1)}, s32[1024,128]{1,0:T(8,128)S(1)}) custom-call(s32[256,512]{1,0:T(8,128)S(1)} %copy-done.4, s32[1,256]{1,0:T(1,128)S(1)} %bitcast.13, s32[1,256]{1,0:T(1,128)S(1)} %bitcast.11), custom_call_target="tpu_custom_call" | custom-call | flops 4294967296 | tf_op jit(solution)/shard_map/meta/pallas_call | solution.py:464
  18.5 0.9 rest.1.refs_0_
  19.4 2.5 %collective-permute-start.4 = (bf16[256,1024]{1,0:T(8,128)(2,1)S(1)}, bf16[256,1024]{1,0:T(8,128)(2,1)S(1)}, u32[]{:S(2)}, u32[]{:S(2)}) collective-permute-start(bf16[256,1024]{1,0:T(8,128)(2,1)S(1)} %rest.1.refs_0_), channel_id=1, source_target_pairs={{0,6},{1,7},{2,0},{3,1},{4,2},{5,3},{6,4},{7,5},{8,14},{9,15},{10,... | collective-permute-start | bytes 1572872 | tf_op jit(solution)/shard_map/ppermute | solution.py:481
  22.0 0.0 collective-permute-start.3
  22.0 15.0 %all-to-all-done.1 = bf16[16,48,1024]{2,1,0:T(8,128)(2,1)} async-done(((bf16[16,48,1024]{2,1,0:T(8,128)(2,1)}), bf16[16,48,1024]{2,1,0:T(8,128)(2,1)}, u32[]{:S(2)}, u32[]{:S(2)}) %all-to-all-start.1) | async-done | bytes 1572896 | tf_op jit(solution)/shard_map/all_to_all | solution.py:487
  36.9 2.5 %collective-permute-start.2 = (bf16[768,1024]{1,0:T(8,128)(2,1)}, bf16[768,1024]{1,0:T(8,128)(2,1)}, u32[]{:S(2)}, u32[]{:S(2)}) collective-permute-start(bf16[768,1024]{1,0:T(8,128)(2,1)} %bitcast.2.own0), channel_id=1, source_target_pairs={{0,1},{1,0},{2,3},{3,2},{4,5},{5,4},{6,7},{7,6},{8,9},{9,8},{10,11... | collective-permute-start | bytes 4718600 | tf_op jit(solution)/shard_map/ppermute | solution.py:484
  39.5 2.5 %collective-permute-start.1 = (bf16[768,1024]{1,0:T(8,128)(2,1)}, bf16[768,1024]{1,0:T(8,128)(2,1)S(1)}, u32[]{:S(2)}, u32[]{:S(2)}) collective-permute-start(bf16[768,1024]{1,0:T(8,128)(2,1)} %bitcast.2.own0), channel_id=1, source_target_pairs={{0,6},{1,7},{2,0},{3,1},{4,2},{5,3},{6,4},{7,5},{8,14},{9,15},{10,... | collective-permute-start | bytes 4718600 | tf_op jit(solution)/shard_map/ppermute | solution.py:481
  42.0 0.0 collective-permute-start
  42.0 0.6 compare_reduce_fusion
  43.2 0.0 collective-permute-done.4.refs_2_
  43.3 0.0 collective-permute-done.3.refs_1_
  43.3 1.3 %join.1 = bf16[16,48,1024]{2,1,0:T(8,128)(2,1)} custom-call(bf16[256,1024]{1,0:T(8,128)(2,1)S(1)} %rest.1.refs_0_, bf16[256,1024]{1,0:T(8,128)(2,1)S(1)} %collective-permute-done.3.refs_1_, bf16[256,1024]{1,0:T(8,128)(2,1)S(1)} %collective-permute-done.4.refs_2_), custom_call_target="tpu_custom_call" | custom-call | tf_op jit(solution)/shard_map/join/pallas_call | solution.py:499
  44.6 26.8 %conditional.1 = (bf16[16,48,1024]{2,1,0:T(8,128)(2,1)}) conditional(s32[]{:T(128)} %convert_element_type.3, () %tuple.11, bf16[16,48,1024]{2,1,0:T(8,128)(2,1)} %join.1), branch_computations={%region_1.0_spmd, %region_2.0_spmd} | conditional | bytes 3145736 | solution.py:505
  44.6 26.8 %all_to_all.20 = bf16[16,48,1024]{2,1,0:T(8,128)(2,1)} all-to-all(bf16[16,48,1024]{2,1,0:T(8,128)(2,1)} %param.1), channel_id=1, replica_groups=mesh['pool'=16,'grp'=8] {'pool'}, dimensions={0} | all-to-all | bytes 3145728 | tf_op jit(solution)/shard_map/cond/branch_1_fun/all_to_all | solution.py:487
  71.4 1.4 %slice.4 = bf16[16,32,1024]{2,1,0:T(8,128)(2,1)S(1)} slice(bf16[16,48,1024]{2,1,0:T(8,128)(2,1)} %get-tuple-element.17.arrived.refs_2_), slice={[0:16], [0:32], [0:1024]} | slice | bytes 2097152 | tf_op jit(solution)/shard_map/slice | solution.py:527
  72.8 1.7 %collective-permute-start.5 = (bf16[16,32,1024]{2,1,0:T(8,128)(2,1)S(1)}, bf16[16,32,1024]{2,1,0:T(8,128)(2,1)S(1)}, u32[]{:S(2)}, u32[]{:S(2)}) collective-permute-start(bf16[16,32,1024]{2,1,0:T(8,128)(2,1)S(1)} %slice.4), channel_id=1, source_target_pairs={{0,1},{1,0},{2,3},{3,2},{4,5},{5,4},{6,7},{7,6},{8,9},{9,8},{10,11... | collective-permute-start | bytes 3145736 | tf_op jit(solution)/shard_map/ppermute | solution.py:484
  74.4 2.3 %collective-permute-done.5.swapped = bf16[16,32,1024]{2,1,0:T(8,128)(2,1)S(1)} collective-permute-done((bf16[16,32,1024]{2,1,0:T(8,128)(2,1)S(1)}, bf16[16,32,1024]{2,1,0:T(8,128)(2,1)S(1)}, u32[]{:S(2)}, u32[]{:S(2)}) %collective-permute-start.5) | collective-permute-done | bytes 1048608 | tf_op jit(solution)/shard_map/ppermute | solution.py:484
  76.7 0.0 collective-permute-done.2.sib0
  76.7 8.6 %early.1.also_after.before = f32[8,1024]{1,0:T(8,128)S(1)} custom-call(bf16[768,1024]{1,0:T(8,128)(2,1)} %bitcast.2.own0, bf16[768,1024]{1,0:T(8,128)(2,1)} %collective-permute-done.2.sib0, bf16[16,48,1024]{2,1,0:T(8,128)(2,1)} %get-tuple-element.17.arrived.refs_2_, bf16[16,32,1024]{2,1,0:T(8,128)(2,1)S(1)} %collective-permute-done.5.swapped, ...), custom_call_target="tpu_custom_call" | custom-call | flops 3623878656 | tf_op jit(solution)/shard_map/early/pallas_call | solution.py:510
  85.3 0.0 collective-permute-done.rows
  85.3 0.7 collective-permute-start.6
  86.0 10.5 %late.1.refs_5_ = f32[8,1024]{1,0:T(8,128)S(1)} custom-call(bf16[768,1024]{1,0:T(8,128)(2,1)} %bitcast.2.own0, bf16[768,1024]{1,0:T(8,128)(2,1)S(1)} %collective-permute-done.1.after.high0.refs_1_, bf16[768,1024]{1,0:T(8,128)(2,1)} %collective-permute-done.2.sib0, bf16[16,48,1024]{2,1,0:T(8,128)(2,1)} %get-tuple-element.17.arrived.refs_2_, ...), custom_call_target="tpu_custom_call" | custom-call | flops 4294967296 | tf_op jit(solution)/shard_map/late/pallas_call | solution.py:510
  96.5 0.0 collective-permute-done.6.refs_0_
  96.5 3.3 %last.1 = f32[128,64]{1,0:T(8,128)S(1)} custom-call(bf16[768,1024]{1,0:T(8,128)(2,1)S(1)} %collective-permute-done.6.refs_0_, bf16[768,1024]{1,0:T(8,128)(2,1)S(1)} %collective-permute-done.1.after.high0.refs_1_, bf16[16,48,1024]{2,1,0:T(8,128)(2,1)} %get-tuple-element.17.arrived.refs_2_, s32[2,8,1024]{2,1,0:T(8,128)S(1)} %get-tuple-element.15.refs_2_.meta.refs_3_, ...), custom_call_target="tpu_custom_call" | custom-call | flops 805306368 | tf_op jit(solution)/shard_map/last/pallas_call | solution.py:510
  99.8 14.4 %all_to_all.21 = f32[128,1,64]{2,1,0:T(1,128)S(1)} all-to-all(f32[128,1,64]{2,1,0:T(1,128)S(1)} %bitcast.9), channel_id=1, replica_groups=mesh['pool'=16,'grp'=8] {'pool','grp'}, dimensions={0} | all-to-all | bytes 65536 | tf_op jit(solution)/shard_map/all_to_all | solution.py:548
  114.2 1.4 %score.1 = f32[1,1024]{1,0:T(1,128)} custom-call(s32[128,128]{1,0:T(8,128)S(1)} %copy-done.3, f32[128,64]{1,0:T(8,128)S(1)} %bitcast.10), custom_call_target="tpu_custom_call" | custom-call | tf_op jit(solution)/shard_map/score/pallas_call | solution.py:549
  (12 shorter events, 0.0 us)
Async XLA Ops:
  5.2 8.8 %copy-start.4 = (s32[256,512]{1,0:T(8,128)S(1)}, s32[256,512]{1,0:T(8,128)}, u32[]{:S(2)}) copy-start(s32[256,512]{1,0:T(8,128)} %refs_0_.3) | copy-start | bytes 1572868
  5.2 8.8 %copy-start.5 = (s32[256]{0:T(256)S(1)}, s32[256]{0:T(256)}, u32[]{:S(2)}) copy-start(s32[256]{0:T(256)} %param.9) | copy-start | bytes 3076
  5.2 8.8 %copy-start.6 = (s32[256]{0:T(256)S(1)}, s32[256]{0:T(256)}, u32[]{:S(2)}) copy-start(s32[256]{0:T(256)} %param.8) | copy-start | bytes 3076
  5.2 31.7 %all-to-all-start.1 = ((bf16[16,48,1024]{2,1,0:T(8,128)(2,1)}), bf16[16,48,1024]{2,1,0:T(8,128)(2,1)}, u32[]{:S(2)}, u32[]{:S(2)}) async-start(bf16[16,48,1024]{2,1,0:T(8,128)(2,1)} %bitcast.14), calls=%async_computation.1 | async-start | bytes 3145728 | tf_op jit(solution)/shard_map/all_to_all | solution.py:487
  14.0 4.5 %copy-start = (bf16[1024,1024]{1,0:T(8,128)(2,1)S(1)}, bf16[1024,1024]{1,0:T(8,128)(2,1)}, u32[]{:S(2)}) copy-start(bf16[1024,1024]{1,0:T(8,128)(2,1)} %refs_1_.1) | copy-start | bytes 6291460
  14.0 4.5 %copy-start.3 = (s32[128,128]{1,0:T(8,128)S(1)}, s32[128,128]{1,0:T(8,128)}, u32[]{:S(2)}) copy-start(s32[128,128]{1,0:T(8,128)} %get-tuple-element.13.refs_0_) | copy-start | bytes 196612
  18.5 0.9 copy-start.1
  19.4 23.8 %collective-permute-start.4 = (bf16[256,1024]{1,0:T(8,128)(2,1)S(1)}, bf16[256,1024]{1,0:T(8,128)(2,1)S(1)}, u32[]{:S(2)}, u32[]{:S(2)}) collective-permute-start(bf16[256,1024]{1,0:T(8,128)(2,1)S(1)} %rest.1.refs_0_), channel_id=1, source_target_pairs={{0,6},{1,7},{2,0},{3,1},{4,2},{5,3},{6,4},{7,5},{8,14},{9,15},{10,... | collective-permute-start | bytes 1572872 | tf_op jit(solution)/shard_map/ppermute | solution.py:481
  22.0 21.3 %collective-permute-start.3 = (bf16[256,1024]{1,0:T(8,128)(2,1)S(1)}, bf16[256,1024]{1,0:T(8,128)(2,1)S(1)}, u32[]{:S(2)}, u32[]{:S(2)}) collective-permute-start(bf16[256,1024]{1,0:T(8,128)(2,1)S(1)} %rest.1.refs_0_), channel_id=1, source_target_pairs={{0,2},{1,3},{2,4},{3,5},{4,6},{5,7},{6,0},{7,1},{8,10},{9,11},{10,... | collective-permute-start | bytes 1572872 | tf_op jit(solution)/shard_map/ppermute | solution.py:481
  36.9 39.8 %collective-permute-start.2 = (bf16[768,1024]{1,0:T(8,128)(2,1)}, bf16[768,1024]{1,0:T(8,128)(2,1)}, u32[]{:S(2)}, u32[]{:S(2)}) collective-permute-start(bf16[768,1024]{1,0:T(8,128)(2,1)} %bitcast.2.own0), channel_id=1, source_target_pairs={{0,1},{1,0},{2,3},{3,2},{4,5},{5,4},{6,7},{7,6},{8,9},{9,8},{10,11... | collective-permute-start | bytes 4718600 | tf_op jit(solution)/shard_map/ppermute | solution.py:484
  39.5 45.8 %collective-permute-start.1 = (bf16[768,1024]{1,0:T(8,128)(2,1)}, bf16[768,1024]{1,0:T(8,128)(2,1)S(1)}, u32[]{:S(2)}, u32[]{:S(2)}) collective-permute-start(bf16[768,1024]{1,0:T(8,128)(2,1)} %bitcast.2.own0), channel_id=1, source_target_pairs={{0,6},{1,7},{2,0},{3,1},{4,2},{5,3},{6,4},{7,5},{8,14},{9,15},{10,... | collective-permute-start | bytes 4718600 | tf_op jit(solution)/shard_map/ppermute | solution.py:481
  42.0 43.4 %collective-permute-start = (bf16[768,1024]{1,0:T(8,128)(2,1)}, bf16[768,1024]{1,0:T(8,128)(2,1)}, u32[]{:S(2)}, u32[]{:S(2)}) collective-permute-start(bf16[768,1024]{1,0:T(8,128)(2,1)} %bitcast.2.own0), channel_id=1, source_target_pairs={{0,2},{1,3},{2,4},{3,5},{4,6},{5,7},{6,0},{7,1},{8,10},{9,11},{10,... | collective-permute-start | bytes 4718600 | tf_op jit(solution)/shard_map/ppermute | solution.py:481
  71.4 5.3 %copy-start.2 = (s32[1024,128]{1,0:T(8,128)S(1)}, s32[1024,128]{1,0:T(8,128)}, u32[]{:S(2)}) copy-start(s32[1024,128]{1,0:T(8,128)} %copy-done.1) | copy-start | bytes 1572868
  72.8 3.9 %collective-permute-start.5 = (bf16[16,32,1024]{2,1,0:T(8,128)(2,1)S(1)}, bf16[16,32,1024]{2,1,0:T(8,128)(2,1)S(1)}, u32[]{:S(2)}, u32[]{:S(2)}) collective-permute-start(bf16[16,32,1024]{2,1,0:T(8,128)(2,1)S(1)} %slice.4), channel_id=1, source_target_pairs={{0,1},{1,0},{2,3},{3,2},{4,5},{5,4},{6,7},{7,6},{8,9},{9,8},{10,11... | collective-permute-start | bytes 3145736 | tf_op jit(solution)/shard_map/ppermute | solution.py:484
  85.3 11.2 %collective-permute-start.6 = (bf16[768,1024]{1,0:T(8,128)(2,1)}, bf16[768,1024]{1,0:T(8,128)(2,1)S(1)}, u32[]{:S(2)}, u32[]{:S(2)}) collective-permute-start(bf16[768,1024]{1,0:T(8,128)(2,1)} %follow.1.low0), channel_id=1, source_target_pairs={{0,1},{1,0},{2,3},{3,2},{4,5},{5,4},{6,7},{7,6},{8,9},{9,8},{10,11... | collective-permute-start | bytes 4718600 | tf_op jit(solution)/shard_map/ppermute | solution.py:484

commit v6 on v5

--- a/solution.py
+++ b/solution.py
@@ -1,3 +1,5 @@
+import functools
+
 import jax
 import jax.numpy as jnp
 from jax import lax
@@ -12,7 +14,7 @@
 QUARTER = 256
 CODE = 8192
 NT = (((1,), (1,)), ((), ()))
-PARAMS = pltpu.CompilerParams(vmem_limit_bytes=20 * 1024 * 1024)
+PARAMS = pltpu.CompilerParams(vmem_limit_bytes=24 * 1024 * 1024)
 TABLE_PARAMS = pltpu.CompilerParams(vmem_limit_bytes=62 * 1024 * 1024)
 
 
@@ -167,10 +169,10 @@
     codes_ref[...] = jnp.transpose(packed_ref[...])
 
 
-def run(pieces, sims_ref, fetch=None):
+def run(pieces, sims_ref, tiles=None):
     for n in range(len(pieces) + 1):
-        if n == 1 and fetch is not None:
-            fetch.rest()
+        if n == 1 and tiles is not None:
+            tiles.start_rest()
         if n < len(pieces):
             piece = pieces[n]
             sims_ref[n % 2, : piece["count"], :] = lax.dot_general(
@@ -220,45 +222,48 @@
 OWN, SIB, LOW, LOWS, HIGH = range(5)
 
 
-class Fetch:
-    def __init__(self, sources, held, sems, first):
-        self.copies, self.held, self.waited = [], held, set()
-        for n, source in enumerate(sources):
-            self.copies.append(pltpu.make_async_copy(source, held[n], sems.at[n]))
-        for copy in self.copies[:first]:
+class Tiles:
+    def __init__(self, moves, first, held, sems, meta, codes, rows, cols, row_classes, col_classes):
+        self.held, self.meta, self.codes, self.rows, self.cols = held, meta, codes, rows, cols
+        self.row_classes, self.col_classes = row_classes, col_classes
+        self.relatives = relatives()
+        self.copies = {}
+        per = held.shape[1] // 4
+        for n, (cls, ref, at) in enumerate(moves):
+            if at is None:
+                source, target = ref, held.at[cls, pl.ds(0, 3 * per)]
+            else:
+                source, target = ref.at[:, pl.ds(at, 16), :], held.at[cls, pl.ds(3 * per, per)]
+            self.copies[cls, at is not None] = pltpu.make_async_copy(source, target, sems.at[n])
+        self.later = list(self.copies.values())[first:]
+        for copy in list(self.copies.values())[:first]:
             copy.start()
-        self.late = self.copies[first:]
-
-    def get(self, n):
-        if n not in self.waited:
-            self.copies[n].wait()
-            self.waited.add(n)
-        return self.held[n]
-
-    def rest(self):
-        for copy in self.late:
+        for cls in row_classes:
+            rows[cls, :, :] = jnp.zeros(rows.shape[1:], F32)
+        for cls in col_classes:
+            cols[cls, :, :] = jnp.zeros(cols.shape[1:], F32)
+
+    def start_rest(self):
+        for copy in self.later:
             copy.start()
-        self.late = []
-
-    def all(self):
-        for n in range(len(self.copies)):
-            self.get(n)
-
-
-class Tiles:
-    def __init__(self, fetch, meta, codes, rows, cols, parts):
-        self.fetch, self.parts = fetch, parts
-        self.meta, self.codes, self.rows, self.cols = meta, codes, rows, cols
-        self.relatives = relatives()
-        for ref in (rows, cols):
-            ref[...] = jnp.zeros(ref.shape, F32)
+        self.later = []
+
+    def wait(self, cls, last):
+        copy = self.copies.pop((cls, last), None)
+        if copy is not None:
+            copy.wait()
+
+    def wait_all(self):
+        for cls, last in list(self.copies):
+            self.wait(cls, last)
 
     def load(self, cls, quarter, count=1):
-        number, at = self.parts[cls, quarter]
-        ref = self.fetch.get(number)
-        if len(ref.shape) == 3:
-            return ref[:, at : at + QUARTER // ref.shape[0], :].reshape(-1, ref.shape[2])
-        return ref[at : at + count * QUARTER, :]
+        if quarter < 3:
+            self.wait(cls, False)
+        if quarter + count > 3:
+            self.wait(cls, True)
+        per = self.held.shape[1] // 4
+        return self.held[cls, quarter * per : (quarter + count) * per].reshape(count * QUARTER, -1)
 
     def piece(self, left, quarter, count, right, right_quarter, same=None):
         lanes = slice(right_quarter * QUARTER, (right_quarter + 1) * QUARTER)
@@ -279,18 +284,21 @@
         )
 
     def matched(self, flip, left, right, pairs):
-        return [
-            self.piece(left, a, 1, right, b) for a, b in pairs if (a + b) % 2 == flip
-        ]
-
-    def finish(self, before, out):
-        for cls in range(5):
-            best = col_result(self.cols.at[cls])
-            if cls < HIGH:
-                best = jnp.maximum(best, row_result(self.rows.at[cls]))
-            if before is not None:
-                best = jnp.maximum(best, before[cls : cls + 1, :])
-            out[cls : cls + 1, :] = best
+        pieces = []
+        for b in range(4):
+            mine = [a for a in range(4) if (a, b) in pairs and (a // 2 + b // 2) % 2 == flip]
+            if mine:
+                assert mine == list(range(mine[0], mine[-1] + 1))
+                pieces.append(self.piece(left, mine[0], len(mine), right, b))
+        return pieces
+
+    def result(self, cls):
+        best = []
+        if cls in self.row_classes:
+            best.append(row_result(self.rows.at[cls]))
+        if cls in self.col_classes:
+            best.append(col_result(self.cols.at[cls]))
+        return functools.reduce(jnp.maximum, best)
 
 
 def either(flag, work):
@@ -307,13 +315,11 @@
     return (chip == 0) | (chip == 3)
 
 
-def parts_of(**groups):
-    names = dict(own=OWN, sib=SIB, low=LOW, lows=LOWS, high=HIGH)
-    return {(names[name], q): part for name, parts in groups.items() for q, part in parts.items()}
-
-
-def whole(n):
-    return {q: (n, q * QUARTER) for q in range(3)}
+ALL_PAIRS = [(a, b) for a in range(4) for b in range(4)]
+
+
+def follow_kernel(rows, after, also_after, out):
+    del rows, after, also_after, out
 
 
 def join_kernel(pools, rest, low_rest, high_rest, out):
@@ -322,87 +328,58 @@
         out[:, n * width : (n + 1) * width, :] = part[...].reshape(pools, width, -1)
 
 
-def follow_kernel(rows, after, also_after, out):
-    del rows, after, also_after, out
-
-
-def early_kernel(own0, sib0, arrived, swapped, meta, codes, out, sims, rows, cols, sems, *held):
-    fetch = Fetch((own0, sib0, arrived, swapped), held, sems, 1)
+def near_kernel(own0, sib0, meta, codes, out, sims, rows, cols, held, sems):
+    moves = [(OWN, own0, None), (SIB, sib0, None)]
+    tiles = Tiles(moves, 1, held, sems, meta, codes, rows, cols, (OWN,), (OWN, SIB))
+    run([tiles.piece(OWN, 0, b + 1, OWN, b, same=b * QUARTER) for b in range(3)], sims, tiles)
+    tiles.wait_all()
+    pairs = [(a, b) for a, b in ALL_PAIRS if 3 not in (a, b)]
+    either(second_core(), lambda flip: run(tiles.matched(flip, OWN, SIB, pairs), sims))
+    out[...] = jnp.zeros(out.shape, F32)
+    for cls in (OWN, SIB):
+        out[cls : cls + 1, :] = tiles.result(cls)
+
+
+def main_kernel(
+    own0, arrived, high0, sib0, swapped, low0, meta, codes, near, out, sims, rows, cols, held, sems
+):
     width = arrived.shape[1] // 3
+    moves = [
+        (OWN, own0, None), (OWN, arrived, 0), (HIGH, high0, None), (HIGH, arrived, 2 * width),
+        (SIB, sib0, None), (SIB, swapped, 0), (LOW, low0, None), (LOW, arrived, width),
+    ]
     tiles = Tiles(
-        fetch, meta, codes, rows, cols,
-        parts_of(
-            own={**whole(0), 3: (2, 0)},
-            sib={**whole(1), 3: (3, 0)},
-            low={3: (2, width)},
-            lows={3: (3, width)},
-            high={3: (2, 2 * width)},
-        ),
+        moves, 3, held, sems, meta, codes, rows, cols, (OWN, SIB, LOW), (OWN, SIB, HIGH)
     )
-    pieces = [tiles.piece(OWN, 0, b + 1, OWN, b, same=b * QUARTER) for b in range(3)]
-    pieces += [tiles.piece(OWN, 0, 3, OWN, 3), tiles.piece(OWN, 3, 1, OWN, 3, same=0)]
-    for cls in (OWN, SIB):
-        pieces.append(tiles.piece(cls, 0, 3, HIGH, 3))
-        pieces.append(tiles.piece(cls, 3, 1, HIGH, 3))
-    run(pieces, sims, fetch)
-    fetch.all()
-    pairs = [(a, b) for b in range(4) for a in range(4)]
+    pieces = [tiles.piece(OWN, 0, 4, OWN, 3, same=3 * QUARTER)]
+    pieces += [tiles.piece(cls, 0, 4, HIGH, b) for cls in (OWN, SIB) for b in range(4)]
+    run(pieces, sims, tiles)
+    tiles.wait_all()
+    pairs = [(a, b) for a, b in ALL_PAIRS if 3 in (a, b)]
     either(second_core(), lambda flip: run(tiles.matched(flip, OWN, SIB, pairs), sims))
-    both = [tiles.piece(cls, 3, 1, HIGH, 3) for cls in (LOW, LOWS)]
-    pl.when(jnp.logical_not(outer_chip()))(lambda: run(both, sims))
-    tiles.finish(None, out)
-
-
-def late_kernel(
-    own0, high0, sib0, arrived, swapped, low0, meta, codes, before, out,
-    sims, rows, cols, sems, *held,
+    either(outer_chip(), lambda flip: run(tiles.matched(flip, LOW, HIGH, ALL_PAIRS), sims))
+    for cls in (OWN, SIB, LOW, HIGH):
+        out[cls : cls + 1, :] = jnp.maximum(near[cls : cls + 1, :], tiles.result(cls))
+
+
+def last_kernel(
+    pools, group, main, rest, lows0, high0, swapped, arrived, meta, codes, before, out,
+    sims, rows, cols, held, sems, every,
 ):
-    fetch = Fetch((own0, high0, sib0, arrived, swapped, low0), held, sems, 2)
     width = arrived.shape[1] // 3
-    tiles = Tiles(
-        fetch, meta, codes, rows, cols,
-        parts_of(
-            own={**whole(0), 3: (3, 0)},
-            sib={**whole(2), 3: (4, 0)},
-            low={**whole(5), 3: (3, width)},
-            lows={3: (4, width)},
-            high={**whole(1), 3: (3, 2 * width)},
-        ),
-    )
-    pieces = [tiles.piece(cls, 0, 3, HIGH, b) for cls in (OWN, SIB) for b in range(3)]
-    pieces += [tiles.piece(cls, 3, 1, HIGH, b) for cls in (OWN, SIB) for b in range(3)]
-    run(pieces, sims, fetch)
-    fetch.all()
-    pairs = [(a, b) for b in range(4) for a in range(4) if (a, b) != (3, 3)]
-    others = [(3, b) for b in range(3)]
-    either(
-        outer_chip(),
-        lambda flip: run(
-            tiles.matched(flip, LOW, HIGH, pairs) + tiles.matched(flip, LOWS, HIGH, others), sims
-        ),
-    )
-    tiles.finish(before, out)
-
-
-def last_kernel(
-    pools, group, main, rest, lows0, high0, arrived, meta, codes, before, out,
-    sims, rows, cols, best, every, sems, *held,
-):
-    fetch = Fetch((lows0, high0, arrived), held, sems, 3)
-    width = arrived.shape[1] // 3
-    tiles = Tiles(
-        fetch, meta, codes, rows, cols,
-        parts_of(lows=whole(0), high={**whole(1), 3: (2, 2 * width)}),
-    )
-    fetch.all()
-    pairs = [(a, b) for b in range(4) for a in range(3)]
-    either(outer_chip(), lambda flip: run(tiles.matched(flip, LOWS, HIGH, pairs), sims))
-    best[...] = before[...]
-    best[LOWS : LOWS + 1, :] = jnp.maximum(best[LOWS : LOWS + 1, :], row_result(rows.at[LOWS]))
-    best[HIGH : HIGH + 1, :] = jnp.maximum(best[HIGH : HIGH + 1, :], col_result(cols.at[HIGH]))
+    moves = [
+        (LOWS, lows0, None), (HIGH, high0, None),
+        (LOWS, swapped, width), (HIGH, arrived, 2 * width),
+    ]
+    tiles = Tiles(moves, 4, held, sems, meta, codes, rows, cols, (LOWS,), (HIGH,))
+    tiles.wait_all()
+    either(outer_chip(), lambda flip: run(tiles.matched(flip, LOWS, HIGH, ALL_PAIRS), sims))
     every[...] = jnp.zeros(every.shape, F32)
     for cls, place in enumerate(tiles.relatives):
-        every[pl.ds(place, 1), :] = best[cls : cls + 1, :]
+        best = [] if cls == LOWS else [before[cls : cls + 1, :]]
+        if cls in (LOWS, HIGH):
+            best.append(tiles.result(cls))
+        every[pl.ds(place, 1), :] = functools.reduce(jnp.maximum, best)
     for p in range(pools):
         rows_out = slice(p * group, (p + 1) * group)
         out[rows_out, :main] = every[:, p * main : (p + 1) * main]
@@ -443,6 +420,7 @@
     cluster_row = block_cluster.reshape(1, -1)
     blocks, block_len = members.shape
 
+    some = jnp.any(valid > 0)
     table, main = pl.pallas_call(
         lambda *refs: table_kernel(pools, group, places, last, *refs),
         out_shape=(
@@ -502,48 +480,56 @@
         compiler_params=PARAMS,
         name="join",
     )(rest, low_rest, high_rest)
-    arrived = lax.cond(jnp.any(valid > 0), to_pools, jnp.zeros_like, sent)
-    low0, high0 = shift(own0, 2), shift(own0, -2)
-    sib0 = swap(own0)
-
-    def tiles(kernel, name, squares, operands, small, out_shape=sds((8, rows_dev), F32), more=()):
-        return pl.pallas_call(
-            kernel,
-            out_shape=out_shape,
-            in_specs=[hbm] * len(operands) + [vmem] * len(small),
-            scratch_shapes=[
-                pltpu.VMEM((2, 3 * QUARTER, QUARTER), F32),
-                pltpu.VMEM((4, rows_dev, 128), F32),
-                pltpu.VMEM((5, 8, rows_dev), F32),
-                *more,
-                pltpu.SemaphoreType.DMA((len(operands),)),
-                *[pltpu.VMEM(operand.shape, BF16) for operand in operands],
-            ],
-            compiler_params=PARAMS,
-            cost_estimate=cost(squares * QUARTER * QUARTER * feature),
-            name=name,
-        )(*operands, *small)
-
-    swapped = swap(arrived[:, : 2 * QUARTER // pools])
-    early = tiles(early_kernel, "early", 27, (own0, sib0, arrived, swapped), (meta, codes))
-    low0 = pl.pallas_call(
+    own0 = pl.pallas_call(
         follow_kernel,
-        out_shape=sds(low0.shape, BF16),
+        out_shape=sds(own0.shape, BF16),
         in_specs=[hbm] * 3,
         out_specs=hbm,
         input_output_aliases={0: 0},
         compiler_params=PARAMS,
         name="follow",
-    )(low0, high0, early)
-    lows0 = swap(low0)
-    late = tiles(
-        late_kernel, "late", 32, (own0, high0, sib0, arrived, swapped, low0), (meta, codes, early)
+    )(own0, sent, some.astype(I32).reshape(1, 1))
+    low0, high0 = shift(own0, 2), shift(own0, -2)
+    sib0 = swap(own0)
+
+    def tiles(kernel, name, squares, moves, operands, small, out_shape=(8, rows_dev), more=()):
+        return pl.pallas_call(
+            kernel,
+            out_shape=sds(out_shape, F32),
+            in_specs=[hbm] * len(operands) + [vmem] * len(small),
+            scratch_shapes=[
+                pltpu.VMEM((2, rows_dev, QUARTER), F32),
+                pltpu.VMEM((4, rows_dev, 128), F32),
+                pltpu.VMEM((5, 8, rows_dev), F32),
+                pltpu.VMEM((5, rows_dev // 16, 16, feature), BF16),
+                pltpu.SemaphoreType.DMA((moves,)),
+                *more,
+            ],
+            compiler_params=PARAMS,
+            cost_estimate=cost(squares * QUARTER * QUARTER * feature),
+            name=name,
+        )(*[operand.reshape(-1, *operand.shape[-2:]) if operand.ndim == 3 else
+            operand.reshape(-1, 16, feature) for operand in operands], *small)
+
+    def bring(sent, own0, sib0, meta, codes):
+        near = tiles(near_kernel, "near", 11, 2, (own0, sib0), (meta, codes))
+        return to_pools(sent), near
+
+    def bring_nothing(sent, own0, sib0, meta, codes):
+        return jnp.zeros_like(sent), jnp.zeros((8, rows_dev), F32)
+
+    arrived, near = lax.cond(
+        some, bring, bring_nothing, sent, own0, sib0, meta, codes
+    )
+    swapped = swap(arrived)
+    best = tiles(
+        main_kernel, "main", 49, 8, (own0, arrived, high0, sib0, swapped, low0), (meta, codes, near)
     )
     best = tiles(
         lambda *refs: last_kernel(pools, group, group * (places - last), group * last, *refs),
-        "last", 6, (lows0, high0, arrived), (meta, codes, late),
-        out_shape=sds((devices, group * places), F32),
-        more=(pltpu.VMEM((8, rows_dev), F32), pltpu.VMEM((group, rows_dev), F32)),
+        "last", 8, 4, (swap(low0), high0, swapped, arrived), (meta, codes, best),
+        out_shape=(devices, group * places),
+        more=(pltpu.VMEM((group, rows_dev), F32),),
     )
     returned = lax.all_to_all(best, ("pool", "grp"), split_axis=0, concat_axis=0, tiled=True)
     scores = pl.pallas_call(

time: 116 us -> 116 us (level)
  blocking collectives: 41.2 us -> 17.1 us
  waiting for transfers between devices: 17.3 us -> 34.9 us
  starting transfers between devices: 18.7 us -> 25.4 us
    all_to_all x1 -> x0, blocking collectives: 26.8 us -> none  [to_pools(): return lax.all_to_all(rows, 'pool', split_axis=0, concat_axis=0, tiled=True)]
    ppermute x4, waiting for transfers between devices: 0.01 us -> 13.7 us  [shift(): lax.ppermute(rows, 'grp', [(g, (g + by) % group) for g in range(group)])]
    all_to_all x1 -> x2, starting transfers between devices: 8.77 us -> 15.4 us  [to_pools(): return lax.all_to_all(rows, 'pool', split_axis=0, concat_axis=0, tiled=True)]
    all_to_all x1 -> x2, waiting for transfers between devices: 15 us -> 19.7 us  [to_pools(): return lax.all_to_all(rows, 'pool', split_axis=0, concat_axis=0, tiled=True)]
    all_to_all x1, blocking collectives: 14.4 us -> 17.1 us  [body(): lax.all_to_all(best, ('pool', 'grp'), split_axis=0, concat_axis=0, tiled=...]
    slice x1 -> x0, local copies, waits for them, and re-layouts: 1.37 us -> none  [body(): swapped = swap(arrived[:, :2 * QUARTER // pools])]
    pallas_call x1, Pallas kernels: 1.3 us -> 0.1 us  [body(): pl.pallas_call(lambda *refs: join_kernel(pools, *refs), out_shape=sds((po...]
  transfers between devices with their start and end apart: 8 -> 9, of which waited for: 2 -> 7; matrix products, arithmetic and copies ran while one was open for 2% -> 1% of each run, Pallas kernels for 22% -> 22%
where the time goes in v6:
time: 116 us; the launch traced here: 115 us
  Pallas kernels  35.8 us (31%)
  waiting for transfers between devices  34.9 us (30%)
  starting transfers between devices  25.4 us (22%)
  blocking collectives  17.1 us (15%)
    pallas_call x3, Pallas kernels, tiles(): pl.pallas_call(kernel, out_shape=sds(out_shape, F32), in_specs=[hbm] * le...  23 us
    all_to_all x2, waiting for transfers between devices, to_pools(): return lax.all_to_all(rows, 'pool', split_axis=0, concat_axis=0, tiled=True)  19.7 us
    all_to_all x1, blocking collectives, body(): lax.all_to_all(best, ('pool', 'grp'), split_axis=0, concat_axis=0, tiled=...  17.1 us
    all_to_all x2, starting transfers between devices, to_pools(): return lax.all_to_all(rows, 'pool', split_axis=0, concat_axis=0, tiled=True)  15.4 us
    ppermute x4, waiting for transfers between devices, shift(): lax.ppermute(rows, 'grp', [(g, (g + by) % group) for g in range(group)])  13.7 us
    pallas_call x1, Pallas kernels, body(): pl.pallas_call(lambda *refs: meta_kernel(group, places, last, *refs), out...  5.25 us
    ppermute x4, starting transfers between devices, shift(): lax.ppermute(rows, 'grp', [(g, (g + by) % group) for g in range(group)])  5.23 us
    pallas_call x1, Pallas kernels, body(): pl.pallas_call(lambda *refs: table_kernel(pools, group, places, last, *re...  5.16 us
  transfers between devices with their start and end apart: 9, of which 7 were waited for; matrix products, arithmetic and copies ran while one was open for 1% of the time, Pallas kernels for 22%

profile of v6, /device:TPU:1, one launch (start us, length us, event | category | flops | bytes accessed | tf_op | source)
XLA Modules:
  0.0 115.2 jit_solution(394573988246780946)
XLA Ops:
  0.0 5.2 %table.1 = (s32[128,128]{1,0:T(8,128)}, bf16[768,1024]{1,0:T(8,128)(2,1)}) custom-call(s32[256,512]{1,0:T(8,128)} %refs_0_.3, s32[1,256]{1,0:T(1,128)} %bitcast.24, bf16[1024,1024]{1,0:T(8,128)(2,1)} %refs_1_.1), custom_call_target="tpu_custom_call" | custom-call | flops 2147483648 | tf_op jit(solution)/shard_map/table/pallas_call | solution.py:424
  5.2 0.0 copy-start.2
  5.2 0.0 copy-start.3
  5.2 0.0 copy-start.4
  5.2 8.8 %all-to-all-start.1 = ((bf16[16,48,1024]{2,1,0:T(8,128)(2,1)}), bf16[16,48,1024]{2,1,0:T(8,128)(2,1)}, u32[]{:S(2)}, u32[]{:S(2)}) async-start(bf16[16,48,1024]{2,1,0:T(8,128)(2,1)} %bitcast.26), calls=%async_computation.1 | async-start | bytes 3145728 | tf_op jit(solution)/shard_map/all_to_all | solution.py:465
  14.0 0.0 copy-start
  14.0 5.2 %meta.1 = (s32[2,8,1024]{2,1,0:T(8,128)S(1)}, s32[1024,128]{1,0:T(8,128)}) custom-call(s32[256,512]{1,0:T(8,128)S(1)} %copy-done.2, s32[1,256]{1,0:T(1,128)S(1)} %bitcast.25, s32[1,256]{1,0:T(1,128)S(1)} %bitcast.23), custom_call_target="tpu_custom_call" | custom-call | flops 4294967296 | tf_op jit(solution)/shard_map/meta/pallas_call | solution.py:442
  19.3 0.9 rest.1.refs_0_
  20.2 2.5 %collective-permute-start.1 = (bf16[256,1024]{1,0:T(8,128)(2,1)S(1)}, bf16[256,1024]{1,0:T(8,128)(2,1)S(1)}, u32[]{:S(2)}, u32[]{:S(2)}) collective-permute-start(bf16[256,1024]{1,0:T(8,128)(2,1)S(1)} %rest.1.refs_0_), channel_id=1, source_target_pairs={{0,6},{1,7},{2,0},{3,1},{4,2},{5,3},{6,4},{7,5},{8,14},{9,15},{10,... | collective-permute-start | bytes 1572872 | tf_op jit(solution)/shard_map/ppermute | solution.py:459
  22.7 0.6 compare_reduce_fusion
  24.0 9.0 %collective-permute-done.1.refs_2_ = bf16[256,1024]{1,0:T(8,128)(2,1)S(1)} collective-permute-done((bf16[256,1024]{1,0:T(8,128)(2,1)S(1)}, bf16[256,1024]{1,0:T(8,128)(2,1)S(1)}, u32[]{:S(2)}, u32[]{:S(2)}) %collective-permute-start.1) | collective-permute-done | bytes 524320 | tf_op jit(solution)/shard_map/ppermute | solution.py:459
  33.0 3.1 %collective-permute-done.refs_1_ = bf16[256,1024]{1,0:T(8,128)(2,1)S(1)} collective-permute-done((bf16[256,1024]{1,0:T(8,128)(2,1)S(1)}, bf16[256,1024]{1,0:T(8,128)(2,1)S(1)}, u32[]{:S(2)}, u32[]{:S(2)}) %collective-permute-start) | collective-permute-done | bytes 524320 | tf_op jit(solution)/shard_map/ppermute | solution.py:459
  36.1 0.1 join.1.after
  36.2 0.7 all-to-all-done.1
  36.9 0.5 copy-done.5
  37.4 2.2 %collective-permute-start.5 = (bf16[768,1024]{1,0:T(8,128)(2,1)}, bf16[768,1024]{1,0:T(8,128)(2,1)}, u32[]{:S(2)}, u32[]{:S(2)}) collective-permute-start(bf16[768,1024]{1,0:T(8,128)(2,1)} %follow.1), channel_id=1, source_target_pairs={{0,1},{1,0},{2,3},{3,2},{4,5},{5,4},{6,7},{7,6},{8,9},{9,8},{10,11... | collective-permute-start | bytes 4718600 | tf_op jit(solution)/shard_map/ppermute | solution.py:462
  39.6 1.1 collective-permute-start.2
  40.7 1.6 %collective-permute-start.4 = (bf16[768,1024]{1,0:T(8,128)(2,1)}, bf16[768,1024]{1,0:T(8,128)(2,1)S(1)}, u32[]{:S(2)}, u32[]{:S(2)}) collective-permute-start(bf16[768,1024]{1,0:T(8,128)(2,1)} %follow.1), channel_id=1, source_target_pairs={{0,6},{1,7},{2,0},{3,1},{4,2},{5,3},{6,4},{7,5},{8,14},{9,15},{10,... | collective-permute-start | bytes 4718600 | tf_op jit(solution)/shard_map/ppermute | solution.py:459
  42.2 0.7 collective-permute-done.5
  42.9 30.7 %conditional.1 = (bf16[16,48,1024]{2,1,0:T(8,128)(2,1)}, f32[8,1024]{1,0:T(8,128)S(1)}) conditional(s32[]{:T(128)} %convert_element_type.4, () %tuple.13, (bf16[16,48,1024]{2,1,0:T(8,128)(2,1)}, bf16[768,1024]{1,0:T(8,128)(2,1)}, bf16[768,1024]{1,0:T(8,128)(2,1)}, s32[2,8,1024]{2,1,0:T(8,128)S(1)}, s32[1024,128]{1,0:T(8,128)}) %tuple.17), branch_computations={%region_1.0_spmd, %region_2.0_spmd} | conditional | flops 1476395008 | bytes 4718640 | solution.py:521
  42.9 6.7 %all-to-all-start = ((bf16[16,48,1024]{2,1,0:T(8,128)(2,1)}), bf16[16,48,1024]{2,1,0:T(8,128)(2,1)}, u32[]{:S(2)}, u32[]{:S(2)}) async-start(bf16[16,48,1024]{2,1,0:T(8,128)(2,1)} %get-tuple-element.15), calls=%async_computation | async-start | bytes 3145728 | tf_op jit(solution)/shard_map/cond/branch_1_fun/all_to_all | solution.py:465
  49.6 5.0 %near.1 = f32[8,1024]{1,0:T(8,128)S(1)} custom-call(bf16[48,16,1024]{2,1,0:T(8,128)(2,1)} %bitcast.own0, bf16[48,16,1024]{2,1,0:T(8,128)(2,1)} %bitcast.1.sib0, s32[2,8,1024]{2,1,0:T(8,128)S(1)} %get-tuple-element.18.meta, s32[1024,128]{1,0:T(8,128)} %get-tuple-element.19.codes), custom_call_target="tpu_custom_call" | custom-call | flops 1476395008 | tf_op jit(solution)/shard_map/cond/branch_1_fun/near/pallas_call | solution.py:496
  54.6 19.0 %all-to-all-done = bf16[16,48,1024]{2,1,0:T(8,128)(2,1)} async-done(((bf16[16,48,1024]{2,1,0:T(8,128)(2,1)}), bf16[16,48,1024]{2,1,0:T(8,128)(2,1)}, u32[]{:S(2)}, u32[]{:S(2)}) %all-to-all-start) | async-done | bytes 1572896 | tf_op jit(solution)/shard_map/cond/branch_1_fun/all_to_all | solution.py:465
  73.6 1.8 %collective-permute-start.6 = (bf16[16,48,1024]{2,1,0:T(8,128)(2,1)}, bf16[16,48,1024]{2,1,0:T(8,128)(2,1)S(1)}, u32[]{:S(2)}, u32[]{:S(2)}) collective-permute-start(bf16[16,48,1024]{2,1,0:T(8,128)(2,1)} %get-tuple-element.30.arrived.refs_3_), channel_id=1, source_target_pairs={{0,1},{1,0},{2,3},{3,2},{4,5},{5,4},{6,7},{7,6},{8,9},{9,8},{10,11... | collective-permute-start | bytes 4718600 | tf_op jit(solution)/shard_map/ppermute | solution.py:462
  75.4 1.6 %collective-permute-done.2 = bf16[768,1024]{1,0:T(8,128)(2,1)S(1)} collective-permute-done((bf16[768,1024]{1,0:T(8,128)(2,1)}, bf16[768,1024]{1,0:T(8,128)(2,1)S(1)}, u32[]{:S(2)}, u32[]{:S(2)}) %collective-permute-start.2) | collective-permute-done | bytes 1572896 | tf_op jit(solution)/shard_map/ppermute | solution.py:459
  77.0 0.8 collective-permute-start.3
  77.8 0.8 collective-permute-done.6.swapped.refs_2_
  78.6 14.7 %main.1.refs_6_ = f32[8,1024]{1,0:T(8,128)S(1)} custom-call(bf16[48,16,1024]{2,1,0:T(8,128)(2,1)} %bitcast.9.own0, bf16[16,48,1024]{2,1,0:T(8,128)(2,1)} %get-tuple-element.30.arrived.refs_3_, bf16[48,16,1024]{2,1,0:T(8,128)(2,1)S(1)} %bitcast.17, bf16[48,16,1024]{2,1,0:T(8,128)(2,1)} %bitcast.10.sib0, ...), custom_call_target="tpu_custom_call" | custom-call | flops 6576668672 | tf_op jit(solution)/shard_map/main/pallas_call | solution.py:496
  93.3 0.0 collective-permute-done.3
  93.3 3.3 %last.1 = f32[128,64]{1,0:T(8,128)S(1)} custom-call(bf16[48,16,1024]{2,1,0:T(8,128)(2,1)S(1)} %bitcast.19, bf16[48,16,1024]{2,1,0:T(8,128)(2,1)S(1)} %bitcast.18, bf16[16,48,1024]{2,1,0:T(8,128)(2,1)S(1)} %collective-permute-done.6.swapped.refs_2_, bf16[16,48,1024]{2,1,0:T(8,128)(2,1)} %get-tuple-element.30.arrived.refs_3_, ...), custom_call_target="tpu_custom_call" | custom-call | flops 1073741824 | tf_op jit(solution)/shard_map/last/pallas_call | solution.py:496
  96.7 17.1 %all_to_all.20 = f32[128,1,64]{2,1,0:T(1,128)S(1)} all-to-all(f32[128,1,64]{2,1,0:T(1,128)S(1)} %bitcast.20), channel_id=1, replica_groups=mesh['pool'=16,'grp'=8] {'pool','grp'}, dimensions={0} | all-to-all | bytes 65536 | tf_op jit(solution)/shard_map/all_to_all | solution.py:534
  113.8 1.4 %score.1 = f32[1,1024]{1,0:T(1,128)} custom-call(s32[128,128]{1,0:T(8,128)S(1)} %copy-done.1, f32[128,64]{1,0:T(8,128)S(1)} %bitcast.21), custom_call_target="tpu_custom_call" | custom-call | tf_op jit(solution)/shard_map/score/pallas_call | solution.py:535
  (12 shorter events, 0.0 us)
Async XLA Ops:
  5.2 8.8 %copy-start.2 = (s32[256,512]{1,0:T(8,128)S(1)}, s32[256,512]{1,0:T(8,128)}, u32[]{:S(2)}) copy-start(s32[256,512]{1,0:T(8,128)} %refs_0_.3) | copy-start | bytes 1572868
  5.2 8.8 %copy-start.3 = (s32[256]{0:T(256)S(1)}, s32[256]{0:T(256)}, u32[]{:S(2)}) copy-start(s32[256]{0:T(256)} %param.9) | copy-start | bytes 3076
  5.2 8.8 %copy-start.4 = (s32[256]{0:T(256)S(1)}, s32[256]{0:T(256)}, u32[]{:S(2)}) copy-start(s32[256]{0:T(256)} %param.8) | copy-start | bytes 3076
  5.2 31.7 %all-to-all-start.1 = ((bf16[16,48,1024]{2,1,0:T(8,128)(2,1)}), bf16[16,48,1024]{2,1,0:T(8,128)(2,1)}, u32[]{:S(2)}, u32[]{:S(2)}) async-start(bf16[16,48,1024]{2,1,0:T(8,128)(2,1)} %bitcast.26), calls=%async_computation.1 | async-start | bytes 3145728 | tf_op jit(solution)/shard_map/all_to_all | solution.py:465
  14.0 5.3 %copy-start = (bf16[1024,1024]{1,0:T(8,128)(2,1)S(1)}, bf16[1024,1024]{1,0:T(8,128)(2,1)}, u32[]{:S(2)}) copy-start(bf16[1024,1024]{1,0:T(8,128)(2,1)} %refs_1_.1) | copy-start | bytes 6291460
  14.0 5.3 %copy-start.1 = (s32[128,128]{1,0:T(8,128)S(1)}, s32[128,128]{1,0:T(8,128)}, u32[]{:S(2)}) copy-start(s32[128,128]{1,0:T(8,128)} %get-tuple-element.26.refs_0_) | copy-start | bytes 196612
  20.2 12.8 %collective-permute-start.1 = (bf16[256,1024]{1,0:T(8,128)(2,1)S(1)}, bf16[256,1024]{1,0:T(8,128)(2,1)S(1)}, u32[]{:S(2)}, u32[]{:S(2)}) collective-permute-start(bf16[256,1024]{1,0:T(8,128)(2,1)S(1)} %rest.1.refs_0_), channel_id=1, source_target_pairs={{0,6},{1,7},{2,0},{3,1},{4,2},{5,3},{6,4},{7,5},{8,14},{9,15},{10,... | collective-permute-start | bytes 1572872 | tf_op jit(solution)/shard_map/ppermute | solution.py:459
  22.7 13.4 %collective-permute-start = (bf16[256,1024]{1,0:T(8,128)(2,1)S(1)}, bf16[256,1024]{1,0:T(8,128)(2,1)S(1)}, u32[]{:S(2)}, u32[]{:S(2)}) collective-permute-start(bf16[256,1024]{1,0:T(8,128)(2,1)S(1)} %rest.1.refs_0_), channel_id=1, source_target_pairs={{0,2},{1,3},{2,4},{3,5},{4,6},{5,7},{6,0},{7,1},{8,10},{9,11},{10,... | collective-permute-start | bytes 1572872 | tf_op jit(solution)/shard_map/ppermute | solution.py:459
  36.2 1.2 %copy-start.5 = (bf16[16,48,1024]{2,1,0:T(8,128)(2,1)}, bf16[16,48,1024]{2,1,0:T(8,128)(2,1)S(1)}, u32[]{:S(2)}) copy-start(bf16[16,48,1024]{2,1,0:T(8,128)(2,1)S(1)} %join.1.after) | copy-start | bytes 4718596
  37.4 5.5 %collective-permute-start.5 = (bf16[768,1024]{1,0:T(8,128)(2,1)}, bf16[768,1024]{1,0:T(8,128)(2,1)}, u32[]{:S(2)}, u32[]{:S(2)}) collective-permute-start(bf16[768,1024]{1,0:T(8,128)(2,1)} %follow.1), channel_id=1, source_target_pairs={{0,1},{1,0},{2,3},{3,2},{4,5},{5,4},{6,7},{7,6},{8,9},{9,8},{10,11... | collective-permute-start | bytes 4718600 | tf_op jit(solution)/shard_map/ppermute | solution.py:462
  39.6 37.4 %collective-permute-start.2 = (bf16[768,1024]{1,0:T(8,128)(2,1)}, bf16[768,1024]{1,0:T(8,128)(2,1)S(1)}, u32[]{:S(2)}, u32[]{:S(2)}) collective-permute-start(bf16[768,1024]{1,0:T(8,128)(2,1)} %follow.1), channel_id=1, source_target_pairs={{0,2},{1,3},{2,4},{3,5},{4,6},{5,7},{6,0},{7,1},{8,10},{9,11},{10,... | collective-permute-start | bytes 4718600 | tf_op jit(solution)/shard_map/ppermute | solution.py:459
  40.7 37.1 %collective-permute-start.4 = (bf16[768,1024]{1,0:T(8,128)(2,1)}, bf16[768,1024]{1,0:T(8,128)(2,1)S(1)}, u32[]{:S(2)}, u32[]{:S(2)}) collective-permute-start(bf16[768,1024]{1,0:T(8,128)(2,1)} %follow.1), channel_id=1, source_target_pairs={{0,6},{1,7},{2,0},{3,1},{4,2},{5,3},{6,4},{7,5},{8,14},{9,15},{10,... | collective-permute-start | bytes 4718600 | tf_op jit(solution)/shard_map/ppermute | solution.py:459
  42.9 30.7 %all-to-all-start = ((bf16[16,48,1024]{2,1,0:T(8,128)(2,1)}), bf16[16,48,1024]{2,1,0:T(8,128)(2,1)}, u32[]{:S(2)}, u32[]{:S(2)}) async-start(bf16[16,48,1024]{2,1,0:T(8,128)(2,1)} %get-tuple-element.15), calls=%async_computation | async-start | bytes 3145728 | tf_op jit(solution)/shard_map/cond/branch_1_fun/all_to_all | solution.py:465
  73.6 5.0 %collective-permute-start.6 = (bf16[16,48,1024]{2,1,0:T(8,128)(2,1)}, bf16[16,48,1024]{2,1,0:T(8,128)(2,1)S(1)}, u32[]{:S(2)}, u32[]{:S(2)}) collective-permute-start(bf16[16,48,1024]{2,1,0:T(8,128)(2,1)} %get-tuple-element.30.arrived.refs_3_), channel_id=1, source_target_pairs={{0,1},{1,0},{2,3},{3,2},{4,5},{5,4},{6,7},{7,6},{8,9},{9,8},{10,11... | collective-permute-start | bytes 4718600 | tf_op jit(solution)/shard_map/ppermute | solution.py:462
  77.0 16.3 %collective-permute-start.3 = (bf16[768,1024]{1,0:T(8,128)(2,1)S(1)}, bf16[768,1024]{1,0:T(8,128)(2,1)S(1)}, u32[]{:S(2)}, u32[]{:S(2)}) collective-permute-start(bf16[768,1024]{1,0:T(8,128)(2,1)S(1)} %collective-permute-done.2), channel_id=1, source_target_pairs={{0,1},{1,0},{2,3},{3,2},{4,5},{5,4},{6,7},{7,6},{8,9},{9,8},{10,11... | collective-permute-start | bytes 4718600 | tf_op jit(solution)/shard_map/ppermute | solution.py:462
  78.6 14.7 %copy-start.6 = (s32[1024,128]{1,0:T(8,128)S(1)}, s32[1024,128]{1,0:T(8,128)}, u32[]{:S(2)}) copy-start(s32[1024,128]{1,0:T(8,128)} %get-tuple-element.29.codes.refs_5_) | copy-start | bytes 1572868

commit v7 on v6

--- a/solution.py
+++ b/solution.py
@@ -229,14 +229,16 @@
         self.relatives = relatives()
         self.copies = {}
         per = held.shape[1] // 4
-        for n, (cls, ref, at) in enumerate(moves):
-            if at is None:
-                source, target = ref, held.at[cls, pl.ds(0, 3 * per)]
-            else:
-                source, target = ref.at[:, pl.ds(at, 16), :], held.at[cls, pl.ds(3 * per, per)]
-            self.copies[cls, at is not None] = pltpu.make_async_copy(source, target, sems.at[n])
-        self.later = list(self.copies.values())[first:]
-        for copy in list(self.copies.values())[:first]:
+        started = []
+        for n, (cls, ref, at, quarter, count) in enumerate(moves):
+            source = ref if at is None else ref.at[:, pl.ds(at, 16), :]
+            target = held.at[cls, pl.ds(quarter * per, count * per)]
+            started.append(pltpu.make_async_copy(source, target, sems.at[n]))
+            for q in range(quarter, quarter + count):
+                self.copies[cls, q] = started[-1]
+        self.later = started[first:]
+        self.waited = []
+        for copy in started[:first]:
             copy.start()
         for cls in row_classes:
             rows[cls, :, :] = jnp.zeros(rows.shape[1:], F32)
@@ -248,20 +250,19 @@
             copy.start()
         self.later = []
 
-    def wait(self, cls, last):
-        copy = self.copies.pop((cls, last), None)
-        if copy is not None:
+    def wait(self, cls, quarter):
+        copy = self.copies.pop((cls, quarter), None)
+        if copy is not None and not any(copy is other for other in self.waited):
             copy.wait()
+            self.waited.append(copy)
 
     def wait_all(self):
-        for cls, last in list(self.copies):
-            self.wait(cls, last)
+        for cls, quarter in list(self.copies):
+            self.wait(cls, quarter)
 
     def load(self, cls, quarter, count=1):
-        if quarter < 3:
-            self.wait(cls, False)
-        if quarter + count > 3:
-            self.wait(cls, True)
+        for q in range(quarter, quarter + count):
+            self.wait(cls, q)
         per = self.held.shape[1] // 4
         return self.held[cls, quarter * per : (quarter + count) * per].reshape(count * QUARTER, -1)
 
@@ -329,7 +330,7 @@
 
 
 def near_kernel(own0, sib0, meta, codes, out, sims, rows, cols, held, sems):
-    moves = [(OWN, own0, None), (SIB, sib0, None)]
+    moves = [(OWN, own0, None, 0, 3), (SIB, sib0, None, 0, 3)]
     tiles = Tiles(moves, 1, held, sems, meta, codes, rows, cols, (OWN,), (OWN, SIB))
     run([tiles.piece(OWN, 0, b + 1, OWN, b, same=b * QUARTER) for b in range(3)], sims, tiles)
     tiles.wait_all()
@@ -340,38 +341,58 @@
         out[cls : cls + 1, :] = tiles.result(cls)
 
 
-def main_kernel(
-    own0, arrived, high0, sib0, swapped, low0, meta, codes, near, out, sims, rows, cols, held, sems
+def middle_kernel(
+    own0, arrived, high01, sib0, meta, codes, near, out, sims, rows, cols, held, sems
 ):
     width = arrived.shape[1] // 3
     moves = [
-        (OWN, own0, None), (OWN, arrived, 0), (HIGH, high0, None), (HIGH, arrived, 2 * width),
-        (SIB, sib0, None), (SIB, swapped, 0), (LOW, low0, None), (LOW, arrived, width),
+        (OWN, own0, None, 0, 3), (OWN, arrived, 0, 3, 1), (HIGH, high01, None, 0, 2),
+        (HIGH, arrived, 2 * width, 3, 1), (SIB, sib0, None, 0, 3),
+    ]
+    tiles = Tiles(moves, 2, held, sems, meta, codes, rows, cols, (OWN, SIB), (OWN, HIGH))
+    pieces = [tiles.piece(OWN, 0, 4, OWN, 3, same=3 * QUARTER)]
+    pieces += [tiles.piece(OWN, 0, 4, HIGH, b) for b in (0, 1, 3)]
+    pieces += [tiles.piece(SIB, 0, 3, HIGH, b) for b in (0, 1, 3)]
+    run(pieces, sims, tiles)
+    out[...] = near[...]
+    for cls in (OWN, SIB, HIGH):
+        out[cls : cls + 1, :] = jnp.maximum(near[cls : cls + 1, :], tiles.result(cls))
+
+
+def main_kernel(
+    own0, arrived, high2, sib0, swapped, low0, high01, meta, codes, before, out,
+    sims, rows, cols, held, sems,
+):
+    width = arrived.shape[1] // 3
+    moves = [
+        (HIGH, high2, None, 2, 1), (OWN, own0, None, 0, 3), (OWN, arrived, 0, 3, 1),
+        (SIB, sib0, None, 0, 3), (SIB, swapped, 0, 3, 1), (HIGH, high01, None, 0, 2),
+        (HIGH, arrived, 2 * width, 3, 1), (LOW, low0, None, 0, 3), (LOW, arrived, width, 3, 1),
     ]
     tiles = Tiles(
-        moves, 3, held, sems, meta, codes, rows, cols, (OWN, SIB, LOW), (OWN, SIB, HIGH)
+        moves, 3, held, sems, meta, codes, rows, cols, (OWN, SIB, LOW), (SIB, HIGH)
     )
-    pieces = [tiles.piece(OWN, 0, 4, OWN, 3, same=3 * QUARTER)]
-    pieces += [tiles.piece(cls, 0, 4, HIGH, b) for cls in (OWN, SIB) for b in range(4)]
+    pieces = [tiles.piece(OWN, 0, 4, HIGH, 2), tiles.piece(SIB, 0, 4, HIGH, 2)]
+    pieces += [tiles.piece(SIB, 3, 1, HIGH, b) for b in (0, 1, 3)]
     run(pieces, sims, tiles)
-    tiles.wait_all()
     pairs = [(a, b) for a, b in ALL_PAIRS if 3 in (a, b)]
     either(second_core(), lambda flip: run(tiles.matched(flip, OWN, SIB, pairs), sims))
+    tiles.wait_all()
     either(outer_chip(), lambda flip: run(tiles.matched(flip, LOW, HIGH, ALL_PAIRS), sims))
     for cls in (OWN, SIB, LOW, HIGH):
-        out[cls : cls + 1, :] = jnp.maximum(near[cls : cls + 1, :], tiles.result(cls))
+        out[cls : cls + 1, :] = jnp.maximum(before[cls : cls + 1, :], tiles.result(cls))
 
 
 def last_kernel(
-    pools, group, main, rest, lows0, high0, swapped, arrived, meta, codes, before, out,
+    pools, group, main, rest, lows0, high01, high2, swapped, arrived, meta, codes, before, out,
     sims, rows, cols, held, sems, every,
 ):
     width = arrived.shape[1] // 3
     moves = [
-        (LOWS, lows0, None), (HIGH, high0, None),
-        (LOWS, swapped, width), (HIGH, arrived, 2 * width),
+        (LOWS, lows0, None, 0, 3), (LOWS, swapped, width, 3, 1), (HIGH, high01, None, 0, 2),
+        (HIGH, high2, None, 2, 1), (HIGH, arrived, 2 * width, 3, 1),
     ]
-    tiles = Tiles(moves, 4, held, sems, meta, codes, rows, cols, (LOWS,), (HIGH,))
+    tiles = Tiles(moves, 5, held, sems, meta, codes, rows, cols, (LOWS,), (HIGH,))
     tiles.wait_all()
     either(outer_chip(), lambda flip: run(tiles.matched(flip, LOWS, HIGH, ALL_PAIRS), sims))
     every[...] = jnp.zeros(every.shape, F32)
@@ -461,6 +482,17 @@
     def swap(rows):
         return lax.ppermute(rows, "grp", [(g, g ^ 1) for g in range(group)])
 
+    def follow(rows, after, also_after):
+        return pl.pallas_call(
+            follow_kernel,
+            out_shape=sds(rows.shape, BF16),
+            in_specs=[hbm] * 3,
+            out_specs=hbm,
+            input_output_aliases={0: 0},
+            compiler_params=PARAMS,
+            name="follow",
+        )(rows, after, also_after)
+
     def to_pools(rows):
         return lax.all_to_all(rows, "pool", split_axis=0, concat_axis=0, tiled=True)
 
@@ -480,16 +512,9 @@
         compiler_params=PARAMS,
         name="join",
     )(rest, low_rest, high_rest)
-    own0 = pl.pallas_call(
-        follow_kernel,
-        out_shape=sds(own0.shape, BF16),
-        in_specs=[hbm] * 3,
-        out_specs=hbm,
-        input_output_aliases={0: 0},
-        compiler_params=PARAMS,
-        name="follow",
-    )(own0, sent, some.astype(I32).reshape(1, 1))
-    low0, high0 = shift(own0, 2), shift(own0, -2)
+    own0 = follow(own0, sent, some.astype(I32).reshape(1, 1))
+    low0, high01 = shift(own0, 2), shift(own0[: 2 * QUARTER], -2)
+    high2 = shift(own0[2 * QUARTER :], -2)
     sib0 = swap(own0)
 
     def tiles(kernel, name, squares, moves, operands, small, out_shape=(8, rows_dev), more=()):
@@ -522,12 +547,17 @@
         some, bring, bring_nothing, sent, own0, sib0, meta, codes
     )
     swapped = swap(arrived)
+    middle = tiles(
+        middle_kernel, "middle", 25, 5, (own0, arrived, high01, sib0), (meta, codes, near)
+    )
+    low0 = follow(low0, middle, high2)
     best = tiles(
-        main_kernel, "main", 49, 8, (own0, arrived, high0, sib0, swapped, low0), (meta, codes, near)
+        main_kernel, "main", 23, 9, (own0, arrived, high2, sib0, swapped, low0, high01),
+        (meta, codes, middle),
     )
     best = tiles(
         lambda *refs: last_kernel(pools, group, group * (places - last), group * last, *refs),
-        "last", 8, 4, (swap(low0), high0, swapped, arrived), (meta, codes, best),
+        "last", 8, 5, (swap(low0), high01, high2, swapped, arrived), (meta, codes, best),
         out_shape=(devices, group * places),
         more=(pltpu.VMEM((group, rows_dev), F32),),
     )

time: 116 us -> 115 us (level)
  waiting for transfers between devices: 34.9 us -> 30 us
  blocking collectives: 17.1 us -> 12.3 us
  local copies, waits for them, and re-layouts: 0.51 us -> 5.14 us
  Pallas kernels: 35.8 us -> 40 us
    all_to_all x1, blocking collectives: 17.1 us -> 12.3 us  [body(): lax.all_to_all(best, ('pool', 'grp'), split_axis=0, concat_axis=0, tiled=...]
    slice x0 -> x2, local copies, waits for them, and re-layouts: none -> 4.21 us  [the longest x1 2.3 us: body(): low0, high01 = (shift(own0, 2), shift(own0[:2 * QUARTER], -2))]
    pallas_call x3 -> x4, Pallas kernels: 23 us -> 27.2 us  [tiles(): pl.pallas_call(kernel, out_shape=sds(out_shape, F32), in_specs=[hbm] * le...]
    ppermute x4 -> x5, waiting for transfers between devices: 13.7 us -> 9.73 us  [shift(): lax.ppermute(rows, 'grp', [(g, (g + by) % group) for g in range(group)])]
    all_to_all x2, starting transfers between devices: 15.4 us -> 13.2 us  [to_pools(): return lax.all_to_all(rows, 'pool', split_axis=0, concat_axis=0, tiled=True)]
    ppermute x3, waiting for transfers between devices: 1.54 us -> 0.01 us  [swap(): return lax.ppermute(rows, 'grp', [(g, g ^ 1) for g in range(group)])]
    ppermute x4 -> x5, starting transfers between devices: 5.23 us -> 6.69 us  [shift(): lax.ppermute(rows, 'grp', [(g, (g + by) % group) for g in range(group)])]
  transfers between devices with their start and end apart: 9 -> 10, of which waited for: 7 -> 3; matrix products, arithmetic and copies ran while one was open for 1% -> 4% of each run, Pallas kernels for 22% -> 26%
where the time goes in v7:
time: 115 us
  Pallas kernels  40 us (35%)
  waiting for transfers between devices  30 us (26%)
  starting transfers between devices  25.5 us (22%)
  blocking collectives  12.3 us (11%)
  local copies, waits for them, and re-layouts  5.14 us (4%)
    pallas_call x4, Pallas kernels, tiles(): pl.pallas_call(kernel, out_shape=sds(out_shape, F32), in_specs=[hbm] * le...  27.2 us
    all_to_all x2, waiting for transfers between devices, to_pools(): return lax.all_to_all(rows, 'pool', split_axis=0, concat_axis=0, tiled=True)  20.2 us
    all_to_all x2, starting transfers between devices, to_pools(): return lax.all_to_all(rows, 'pool', split_axis=0, concat_axis=0, tiled=True)  13.2 us
    all_to_all x1, blocking collectives, body(): lax.all_to_all(best, ('pool', 'grp'), split_axis=0, concat_axis=0, tiled=...  12.3 us
    ppermute x5, waiting for transfers between devices, shift(): lax.ppermute(rows, 'grp', [(g, (g + by) % group) for g in range(group)])  9.73 us
    ppermute x5, starting transfers between devices, shift(): lax.ppermute(rows, 'grp', [(g, (g + by) % group) for g in range(group)])  6.69 us
    ppermute x3, starting transfers between devices, swap(): return lax.ppermute(rows, 'grp', [(g, g ^ 1) for g in range(group)])  5.63 us
    pallas_call x1, Pallas kernels, body(): pl.pallas_call(lambda *refs: meta_kernel(group, places, last, *refs), out...  5.26 us
  transfers between devices with their start and end apart: 10, of which 3 were waited for; matrix products, arithmetic and copies ran while one was open for 4% of the time, Pallas kernels for 26%

profile of v7, /device:TPU:1, one launch (start us, length us, event | category | flops | bytes accessed | tf_op | source)
XLA Modules:
  0.0 114.5 jit_solution(1643231379565044630)
XLA Ops:
  0.0 5.2 %table.1 = (s32[128,128]{1,0:T(8,128)}, bf16[768,1024]{1,0:T(8,128)(2,1)}) custom-call(s32[256,512]{1,0:T(8,128)} %refs_0_.3, s32[1,256]{1,0:T(1,128)} %bitcast.28, bf16[1024,1024]{1,0:T(8,128)(2,1)} %refs_1_.1), custom_call_target="tpu_custom_call" | custom-call | flops 2147483648 | tf_op jit(solution)/shard_map/table/pallas_call | solution.py:445
  5.2 0.0 copy-start.2
  5.2 0.0 copy-start.3
  5.2 0.0 copy-start.4
  5.2 8.8 %all-to-all-start.1 = ((bf16[16,48,1024]{2,1,0:T(8,128)(2,1)}), bf16[16,48,1024]{2,1,0:T(8,128)(2,1)}, u32[]{:S(2)}, u32[]{:S(2)}) async-start(bf16[16,48,1024]{2,1,0:T(8,128)(2,1)} %bitcast.30), calls=%async_computation.1 | async-start | bytes 3145728 | tf_op jit(solution)/shard_map/all_to_all | solution.py:497
  14.1 0.0 copy-start
  14.1 5.3 %meta.1 = (s32[2,8,1024]{2,1,0:T(8,128)S(1)}, s32[1024,128]{1,0:T(8,128)}) custom-call(s32[256,512]{1,0:T(8,128)S(1)} %copy-done.2, s32[1,256]{1,0:T(1,128)S(1)} %bitcast.29, s32[1,256]{1,0:T(1,128)S(1)} %bitcast.27), custom_call_target="tpu_custom_call" | custom-call | flops 4294967296 | tf_op jit(solution)/shard_map/meta/pallas_call | solution.py:463
  19.4 0.9 rest.1.refs_0_
  20.2 1.3 %collective-permute-start = (bf16[256,1024]{1,0:T(8,128)(2,1)S(1)}, bf16[256,1024]{1,0:T(8,128)(2,1)S(1)}, u32[]{:S(2)}, u32[]{:S(2)}) collective-permute-start(bf16[256,1024]{1,0:T(8,128)(2,1)S(1)} %rest.1.refs_0_), channel_id=1, source_target_pairs={{0,2},{1,3},{2,4},{3,5},{4,6},{5,7},{6,0},{7,1},{8,10},{9,11},{10,... | collective-permute-start | bytes 1572872 | tf_op jit(solution)/shard_map/ppermute | solution.py:480
  21.5 1.5 %collective-permute-start.1 = (bf16[256,1024]{1,0:T(8,128)(2,1)S(1)}, bf16[256,1024]{1,0:T(8,128)(2,1)S(1)}, u32[]{:S(2)}, u32[]{:S(2)}) collective-permute-start(bf16[256,1024]{1,0:T(8,128)(2,1)S(1)} %rest.1.refs_0_), channel_id=1, source_target_pairs={{0,6},{1,7},{2,0},{3,1},{4,2},{5,3},{6,4},{7,5},{8,14},{9,15},{10,... | collective-permute-start | bytes 1572872 | tf_op jit(solution)/shard_map/ppermute | solution.py:480
  23.0 0.6 compare_reduce_fusion
  24.3 9.7 %collective-permute-done.refs_1_ = bf16[256,1024]{1,0:T(8,128)(2,1)S(1)} collective-permute-done((bf16[256,1024]{1,0:T(8,128)(2,1)S(1)}, bf16[256,1024]{1,0:T(8,128)(2,1)S(1)}, u32[]{:S(2)}, u32[]{:S(2)}) %collective-permute-start) | collective-permute-done | bytes 524320 | tf_op jit(solution)/shard_map/ppermute | solution.py:480
  34.0 0.1 join.1.after
  34.1 2.9 %all-to-all-done.1 = bf16[16,48,1024]{2,1,0:T(8,128)(2,1)} async-done(((bf16[16,48,1024]{2,1,0:T(8,128)(2,1)}), bf16[16,48,1024]{2,1,0:T(8,128)(2,1)}, u32[]{:S(2)}, u32[]{:S(2)}) %all-to-all-start.1) | async-done | bytes 1572896 | tf_op jit(solution)/shard_map/all_to_all | solution.py:497
  37.0 2.5 %collective-permute-start.3 = (bf16[768,1024]{1,0:T(8,128)(2,1)}, bf16[768,1024]{1,0:T(8,128)(2,1)}, u32[]{:S(2)}, u32[]{:S(2)}) collective-permute-start(bf16[768,1024]{1,0:T(8,128)(2,1)} %follow.2), channel_id=1, source_target_pairs={{0,1},{1,0},{2,3},{3,2},{4,5},{5,4},{6,7},{7,6},{8,9},{9,8},{10,11... | collective-permute-start | bytes 4718600 | tf_op jit(solution)/shard_map/ppermute | solution.py:483
  39.5 1.2 %collective-permute-start.2 = (bf16[768,1024]{1,0:T(8,128)(2,1)}, bf16[768,1024]{1,0:T(8,128)(2,1)S(1)}, u32[]{:S(2)}, u32[]{:S(2)}) collective-permute-start(bf16[768,1024]{1,0:T(8,128)(2,1)} %follow.2), channel_id=1, source_target_pairs={{0,2},{1,3},{2,4},{3,5},{4,6},{5,7},{6,0},{7,1},{8,10},{9,11},{10,... | collective-permute-start | bytes 4718600 | tf_op jit(solution)/shard_map/ppermute | solution.py:480
  40.7 2.3 %slice.8 = bf16[512,1024]{1,0:T(8,128)(2,1)} slice(bf16[768,1024]{1,0:T(8,128)(2,1)} %follow.2), slice={[0:512], [0:1024]} | slice | bytes 2097152 | tf_op jit(solution)/shard_map/slice | solution.py:516
  43.0 1.5 %collective-permute-start.4 = (bf16[512,1024]{1,0:T(8,128)(2,1)}, bf16[512,1024]{1,0:T(8,128)(2,1)S(1)}, u32[]{:S(2)}, u32[]{:S(2)}) collective-permute-start(bf16[512,1024]{1,0:T(8,128)(2,1)} %slice.8), channel_id=1, source_target_pairs={{0,6},{1,7},{2,0},{3,1},{4,2},{5,3},{6,4},{7,5},{8,14},{9,15},{10,... | collective-permute-start | bytes 3145736 | tf_op jit(solution)/shard_map/ppermute | solution.py:480
  44.5 1.9 %slice.9 = bf16[256,1024]{1,0:T(8,128)(2,1)} slice(bf16[768,1024]{1,0:T(8,128)(2,1)} %follow.2), slice={[512:768], [0:1024]} | slice | bytes 1048576 | tf_op jit(solution)/shard_map/slice | solution.py:517
  46.4 1.3 %collective-permute-start.5 = (bf16[256,1024]{1,0:T(8,128)(2,1)}, bf16[256,1024]{1,0:T(8,128)(2,1)S(1)}, u32[]{:S(2)}, u32[]{:S(2)}) collective-permute-start(bf16[256,1024]{1,0:T(8,128)(2,1)} %slice.9), channel_id=1, source_target_pairs={{0,6},{1,7},{2,0},{3,1},{4,2},{5,3},{6,4},{7,5},{8,14},{9,15},{10,... | collective-permute-start | bytes 1572872 | tf_op jit(solution)/shard_map/ppermute | solution.py:480
  47.7 26.8 %conditional.1 = (bf16[16,48,1024]{2,1,0:T(8,128)(2,1)}, f32[8,1024]{1,0:T(8,128)S(1)}) conditional(s32[]{:T(128)} %convert_element_type.4, () %tuple.13, (bf16[16,48,1024]{2,1,0:T(8,128)(2,1)}, bf16[768,1024]{1,0:T(8,128)(2,1)}, bf16[768,1024]{1,0:T(8,128)(2,1)}, s32[2,8,1024]{2,1,0:T(8,128)S(1)}, s32[1024,128]{1,0:T(8,128)}) %tuple.17), branch_computations={%region_1.0_spmd, %region_2.0_spmd} | conditional | flops 1476395008 | bytes 4718640 | solution.py:546
  47.7 4.5 %all-to-all-start = ((bf16[16,48,1024]{2,1,0:T(8,128)(2,1)}), bf16[16,48,1024]{2,1,0:T(8,128)(2,1)}, u32[]{:S(2)}, u32[]{:S(2)}) async-start(bf16[16,48,1024]{2,1,0:T(8,128)(2,1)} %get-tuple-element.15), calls=%async_computation | async-start | bytes 3145728 | tf_op jit(solution)/shard_map/cond/branch_1_fun/all_to_all | solution.py:497
  52.1 5.0 %near.1 = f32[8,1024]{1,0:T(8,128)S(1)} custom-call(bf16[48,16,1024]{2,1,0:T(8,128)(2,1)} %bitcast.own0, bf16[48,16,1024]{2,1,0:T(8,128)(2,1)} %bitcast.1.sib0, s32[2,8,1024]{2,1,0:T(8,128)S(1)} %get-tuple-element.18.meta, s32[1024,128]{1,0:T(8,128)} %get-tuple-element.19.codes), custom_call_target="tpu_custom_call" | custom-call | flops 1476395008 | tf_op jit(solution)/shard_map/cond/branch_1_fun/near/pallas_call | solution.py:521
  57.1 17.4 %all-to-all-done = bf16[16,48,1024]{2,1,0:T(8,128)(2,1)} async-done(((bf16[16,48,1024]{2,1,0:T(8,128)(2,1)}), bf16[16,48,1024]{2,1,0:T(8,128)(2,1)}, u32[]{:S(2)}, u32[]{:S(2)}) %all-to-all-start) | async-done | bytes 1572896 | tf_op jit(solution)/shard_map/cond/branch_1_fun/all_to_all | solution.py:497
  74.5 3.0 %collective-permute-start.7 = (bf16[16,48,1024]{2,1,0:T(8,128)(2,1)}, bf16[16,48,1024]{2,1,0:T(8,128)(2,1)S(1)}, u32[]{:S(2)}, u32[]{:S(2)}) collective-permute-start(bf16[16,48,1024]{2,1,0:T(8,128)(2,1)} %get-tuple-element.30.arrived.refs_4_), channel_id=1, source_target_pairs={{0,1},{1,0},{2,3},{3,2},{4,5},{5,4},{6,7},{7,6},{8,9},{9,8},{10,11... | collective-permute-start | bytes 4718600 | tf_op jit(solution)/shard_map/ppermute | solution.py:483
  77.5 9.3 %middle.1.after.before = f32[8,1024]{1,0:T(8,128)S(1)} custom-call(bf16[48,16,1024]{2,1,0:T(8,128)(2,1)} %bitcast.7.own0, bf16[16,48,1024]{2,1,0:T(8,128)(2,1)} %get-tuple-element.30.arrived.refs_4_, bf16[32,16,1024]{2,1,0:T(8,128)(2,1)S(1)} %bitcast.22, bf16[48,16,1024]{2,1,0:T(8,128)(2,1)} %bitcast.9.sib0, ...), custom_call_target="tpu_custom_call" | custom-call | flops 3355443200 | tf_op jit(solution)/shard_map/middle/pallas_call | solution.py:521
  86.8 0.1 collective-permute-start.6
  86.9 0.9 copy-done.6
  87.8 9.6 %main.1.refs_7_ = f32[8,1024]{1,0:T(8,128)S(1)} custom-call(bf16[48,16,1024]{2,1,0:T(8,128)(2,1)} %bitcast.7.own0, bf16[16,48,1024]{2,1,0:T(8,128)(2,1)} %get-tuple-element.30.arrived.refs_4_, bf16[16,16,1024]{2,1,0:T(8,128)(2,1)S(1)} %bitcast.18, bf16[48,16,1024]{2,1,0:T(8,128)(2,1)} %bitcast.9.sib0, ...), custom_call_target="tpu_custom_call" | custom-call | flops 3087007744 | tf_op jit(solution)/shard_map/main/pallas_call | solution.py:521
  97.4 3.4 %last.1 = f32[128,64]{1,0:T(8,128)S(1)} custom-call(bf16[48,16,1024]{2,1,0:T(8,128)(2,1)S(1)} %bitcast.21, bf16[32,16,1024]{2,1,0:T(8,128)(2,1)S(1)} %bitcast.24, bf16[16,16,1024]{2,1,0:T(8,128)(2,1)S(1)} %bitcast.19, bf16[16,48,1024]{2,1,0:T(8,128)(2,1)S(1)} %collective-permute-done.7.swapped.refs_3_, ...), custom_call_target="tpu_custom_call" | custom-call | flops 1073741824 | tf_op jit(solution)/shard_map/last/pallas_call | solution.py:521
  100.8 12.3 %all_to_all.20 = f32[128,1,64]{2,1,0:T(1,128)S(1)} all-to-all(f32[128,1,64]{2,1,0:T(1,128)S(1)} %bitcast.25), channel_id=1, replica_groups=mesh['pool'=16,'grp'=8] {'pool','grp'}, dimensions={0} | all-to-all | bytes 65536 | tf_op jit(solution)/shard_map/all_to_all | solution.py:564
  113.1 1.4 %score.1 = f32[1,1024]{1,0:T(1,128)} custom-call(s32[128,128]{1,0:T(8,128)S(1)} %copy-done.1, f32[128,64]{1,0:T(8,128)S(1)} %bitcast.26), custom_call_target="tpu_custom_call" | custom-call | tf_op jit(solution)/shard_map/score/pallas_call | solution.py:565
  (18 shorter events, 0.0 us)
Async XLA Ops:
  5.2 8.8 %copy-start.2 = (s32[256,512]{1,0:T(8,128)S(1)}, s32[256,512]{1,0:T(8,128)}, u32[]{:S(2)}) copy-start(s32[256,512]{1,0:T(8,128)} %refs_0_.3) | copy-start | bytes 1572868
  5.2 8.8 %copy-start.3 = (s32[256]{0:T(256)S(1)}, s32[256]{0:T(256)}, u32[]{:S(2)}) copy-start(s32[256]{0:T(256)} %param.9) | copy-start | bytes 3076
  5.2 8.8 %copy-start.4 = (s32[256]{0:T(256)S(1)}, s32[256]{0:T(256)}, u32[]{:S(2)}) copy-start(s32[256]{0:T(256)} %param.8) | copy-start | bytes 3076
  5.2 31.7 %all-to-all-start.1 = ((bf16[16,48,1024]{2,1,0:T(8,128)(2,1)}), bf16[16,48,1024]{2,1,0:T(8,128)(2,1)}, u32[]{:S(2)}, u32[]{:S(2)}) async-start(bf16[16,48,1024]{2,1,0:T(8,128)(2,1)} %bitcast.30), calls=%async_computation.1 | async-start | bytes 3145728 | tf_op jit(solution)/shard_map/all_to_all | solution.py:497
  14.1 5.3 %copy-start = (bf16[1024,1024]{1,0:T(8,128)(2,1)S(1)}, bf16[1024,1024]{1,0:T(8,128)(2,1)}, u32[]{:S(2)}) copy-start(bf16[1024,1024]{1,0:T(8,128)(2,1)} %refs_1_.1) | copy-start | bytes 6291460
  14.1 5.3 %copy-start.1 = (s32[128,128]{1,0:T(8,128)S(1)}, s32[128,128]{1,0:T(8,128)}, u32[]{:S(2)}) copy-start(s32[128,128]{1,0:T(8,128)} %get-tuple-element.26.refs_0_) | copy-start | bytes 196612
  20.2 13.7 %collective-permute-start = (bf16[256,1024]{1,0:T(8,128)(2,1)S(1)}, bf16[256,1024]{1,0:T(8,128)(2,1)S(1)}, u32[]{:S(2)}, u32[]{:S(2)}) collective-permute-start(bf16[256,1024]{1,0:T(8,128)(2,1)S(1)} %rest.1.refs_0_), channel_id=1, source_target_pairs={{0,2},{1,3},{2,4},{3,5},{4,6},{5,7},{6,0},{7,1},{8,10},{9,11},{10,... | collective-permute-start | bytes 1572872 | tf_op jit(solution)/shard_map/ppermute | solution.py:480
  21.5 12.5 %collective-permute-start.1 = (bf16[256,1024]{1,0:T(8,128)(2,1)S(1)}, bf16[256,1024]{1,0:T(8,128)(2,1)S(1)}, u32[]{:S(2)}, u32[]{:S(2)}) collective-permute-start(bf16[256,1024]{1,0:T(8,128)(2,1)S(1)} %rest.1.refs_0_), channel_id=1, source_target_pairs={{0,6},{1,7},{2,0},{3,1},{4,2},{5,3},{6,4},{7,5},{8,14},{9,15},{10,... | collective-permute-start | bytes 1572872 | tf_op jit(solution)/shard_map/ppermute | solution.py:480
  34.1 2.9 %copy-start.5 = (bf16[16,48,1024]{2,1,0:T(8,128)(2,1)}, bf16[16,48,1024]{2,1,0:T(8,128)(2,1)S(1)}, u32[]{:S(2)}) copy-start(bf16[16,48,1024]{2,1,0:T(8,128)(2,1)S(1)} %join.1.after) | copy-start | bytes 4718596
  37.0 10.7 %collective-permute-start.3 = (bf16[768,1024]{1,0:T(8,128)(2,1)}, bf16[768,1024]{1,0:T(8,128)(2,1)}, u32[]{:S(2)}, u32[]{:S(2)}) collective-permute-start(bf16[768,1024]{1,0:T(8,128)(2,1)} %follow.2), channel_id=1, source_target_pairs={{0,1},{1,0},{2,3},{3,2},{4,5},{5,4},{6,7},{7,6},{8,9},{9,8},{10,11... | collective-permute-start | bytes 4718600 | tf_op jit(solution)/shard_map/ppermute | solution.py:483
  39.5 47.3 %collective-permute-start.2 = (bf16[768,1024]{1,0:T(8,128)(2,1)}, bf16[768,1024]{1,0:T(8,128)(2,1)S(1)}, u32[]{:S(2)}, u32[]{:S(2)}) collective-permute-start(bf16[768,1024]{1,0:T(8,128)(2,1)} %follow.2), channel_id=1, source_target_pairs={{0,2},{1,3},{2,4},{3,5},{4,6},{5,7},{6,0},{7,1},{8,10},{9,11},{10,... | collective-permute-start | bytes 4718600 | tf_op jit(solution)/shard_map/ppermute | solution.py:480
  43.0 34.5 %collective-permute-start.4 = (bf16[512,1024]{1,0:T(8,128)(2,1)}, bf16[512,1024]{1,0:T(8,128)(2,1)S(1)}, u32[]{:S(2)}, u32[]{:S(2)}) collective-permute-start(bf16[512,1024]{1,0:T(8,128)(2,1)} %slice.8), channel_id=1, source_target_pairs={{0,6},{1,7},{2,0},{3,1},{4,2},{5,3},{6,4},{7,5},{8,14},{9,15},{10,... | collective-permute-start | bytes 3145736 | tf_op jit(solution)/shard_map/ppermute | solution.py:480
  46.4 40.4 %collective-permute-start.5 = (bf16[256,1024]{1,0:T(8,128)(2,1)}, bf16[256,1024]{1,0:T(8,128)(2,1)S(1)}, u32[]{:S(2)}, u32[]{:S(2)}) collective-permute-start(bf16[256,1024]{1,0:T(8,128)(2,1)} %slice.9), channel_id=1, source_target_pairs={{0,6},{1,7},{2,0},{3,1},{4,2},{5,3},{6,4},{7,5},{8,14},{9,15},{10,... | collective-permute-start | bytes 1572872 | tf_op jit(solution)/shard_map/ppermute | solution.py:480
  47.7 26.8 %all-to-all-start = ((bf16[16,48,1024]{2,1,0:T(8,128)(2,1)}), bf16[16,48,1024]{2,1,0:T(8,128)(2,1)}, u32[]{:S(2)}, u32[]{:S(2)}) async-start(bf16[16,48,1024]{2,1,0:T(8,128)(2,1)} %get-tuple-element.15), calls=%async_computation | async-start | bytes 3145728 | tf_op jit(solution)/shard_map/cond/branch_1_fun/all_to_all | solution.py:497
  74.5 12.4 %collective-permute-start.7 = (bf16[16,48,1024]{2,1,0:T(8,128)(2,1)}, bf16[16,48,1024]{2,1,0:T(8,128)(2,1)S(1)}, u32[]{:S(2)}, u32[]{:S(2)}) collective-permute-start(bf16[16,48,1024]{2,1,0:T(8,128)(2,1)} %get-tuple-element.30.arrived.refs_4_), channel_id=1, source_target_pairs={{0,1},{1,0},{2,3},{3,2},{4,5},{5,4},{6,7},{7,6},{8,9},{9,8},{10,11... | collective-permute-start | bytes 4718600 | tf_op jit(solution)/shard_map/ppermute | solution.py:483
  86.8 1.0 copy-start.6
  86.8 10.6 %collective-permute-start.6 = (bf16[768,1024]{1,0:T(8,128)(2,1)S(1)}, bf16[768,1024]{1,0:T(8,128)(2,1)S(1)}, u32[]{:S(2)}, u32[]{:S(2)}) collective-permute-start(bf16[768,1024]{1,0:T(8,128)(2,1)S(1)} %follow.3), channel_id=1, source_target_pairs={{0,1},{1,0},{2,3},{3,2},{4,5},{5,4},{6,7},{7,6},{8,9},{9,8},{10,11... | collective-permute-start | bytes 4718600 | tf_op jit(solution)/shard_map/ppermute | solution.py:483

commit v8 on v7

--- a/solution.py
+++ b/solution.py
@@ -14,7 +14,7 @@
 QUARTER = 256
 CODE = 8192
 NT = (((1,), (1,)), ((), ()))
-PARAMS = pltpu.CompilerParams(vmem_limit_bytes=24 * 1024 * 1024)
+PARAMS = pltpu.CompilerParams(vmem_limit_bytes=12 * 1024 * 1024)
 TABLE_PARAMS = pltpu.CompilerParams(vmem_limit_bytes=62 * 1024 * 1024)
 
 
@@ -169,10 +169,8 @@
     codes_ref[...] = jnp.transpose(packed_ref[...])
 
 
-def run(pieces, sims_ref, tiles=None):
+def run(pieces, sims_ref):
     for n in range(len(pieces) + 1):
-        if n == 1 and tiles is not None:
-            tiles.start_rest()
         if n < len(pieces):
             piece = pieces[n]
             sims_ref[n % 2, : piece["count"], :] = lax.dot_general(
@@ -223,48 +221,24 @@
 
 
 class Tiles:
-    def __init__(self, moves, first, held, sems, meta, codes, rows, cols, row_classes, col_classes):
-        self.held, self.meta, self.codes, self.rows, self.cols = held, meta, codes, rows, cols
+    def __init__(self, parts, meta, codes, rows, cols, row_classes, col_classes):
+        self.meta, self.codes, self.rows, self.cols = meta, codes, rows, cols
         self.row_classes, self.col_classes = row_classes, col_classes
         self.relatives = relatives()
-        self.copies = {}
-        per = held.shape[1] // 4
-        started = []
-        for n, (cls, ref, at, quarter, count) in enumerate(moves):
-            source = ref if at is None else ref.at[:, pl.ds(at, 16), :]
-            target = held.at[cls, pl.ds(quarter * per, count * per)]
-            started.append(pltpu.make_async_copy(source, target, sems.at[n]))
+        self.parts = {}
+        for cls, ref, at, quarter, count in parts:
             for q in range(quarter, quarter + count):
-                self.copies[cls, q] = started[-1]
-        self.later = started[first:]
-        self.waited = []
-        for copy in started[:first]:
-            copy.start()
+                self.parts[cls, q] = (ref, at if len(ref.shape) == 3 else (q - quarter) * QUARTER)
         for cls in row_classes:
             rows[cls, :, :] = jnp.zeros(rows.shape[1:], F32)
         for cls in col_classes:
             cols[cls, :, :] = jnp.zeros(cols.shape[1:], F32)
 
-    def start_rest(self):
-        for copy in self.later:
-            copy.start()
-        self.later = []
-
-    def wait(self, cls, quarter):
-        copy = self.copies.pop((cls, quarter), None)
-        if copy is not None and not any(copy is other for other in self.waited):
-            copy.wait()
-            self.waited.append(copy)
-
-    def wait_all(self):
-        for cls, quarter in list(self.copies):
-            self.wait(cls, quarter)
-
     def load(self, cls, quarter, count=1):
-        for q in range(quarter, quarter + count):
-            self.wait(cls, q)
-        per = self.held.shape[1] // 4
-        return self.held[cls, quarter * per : (quarter + count) * per].reshape(count * QUARTER, -1)
+        ref, at = self.parts[cls, quarter]
+        if len(ref.shape) == 3:
+            return ref[:, at : at + QUARTER // ref.shape[0], :].reshape(QUARTER, -1)
+        return ref[at : at + count * QUARTER, :]
 
     def piece(self, left, quarter, count, right, right_quarter, same=None):
         lanes = slice(right_quarter * QUARTER, (right_quarter + 1) * QUARTER)
@@ -288,9 +262,10 @@
         pieces = []
         for b in range(4):
             mine = [a for a in range(4) if (a, b) in pairs and (a // 2 + b // 2) % 2 == flip]
-            if mine:
-                assert mine == list(range(mine[0], mine[-1] + 1))
-                pieces.append(self.piece(left, mine[0], len(mine), right, b))
+            if mine == [0, 1] and self.parts[left, 0][0] is self.parts[left, 1][0]:
+                pieces.append(self.piece(left, 0, 2, right, b))
+            else:
+                pieces += [self.piece(left, a, 1, right, b) for a in mine]
         return pieces
 
     def result(self, cls):
@@ -323,17 +298,30 @@
     del rows, after, also_after, out
 
 
+def split_kernel(rows, after, also_after, out, first, third, sems):
+    del after, also_after, out
+    parts = ((first, 0, 2), (third, 2, 1))
+    copies = [
+        pltpu.make_async_copy(rows.at[pl.ds(at * QUARTER, n * QUARTER), :], part, sems.at[i])
+        for i, (part, at, n) in enumerate(parts)
+    ]
+    for copy in copies:
+        copy.start()
+    for copy in copies:
+        copy.wait()
+
+
 def join_kernel(pools, rest, low_rest, high_rest, out):
     width = QUARTER // pools
     for n, part in enumerate((rest, low_rest, high_rest)):
         out[:, n * width : (n + 1) * width, :] = part[...].reshape(pools, width, -1)
 
 
-def near_kernel(own0, sib0, meta, codes, out, sims, rows, cols, held, sems):
+def near_kernel(own0, sib0, meta, codes, out, sims, rows, cols):
     moves = [(OWN, own0, None, 0, 3), (SIB, sib0, None, 0, 3)]
-    tiles = Tiles(moves, 1, held, sems, meta, codes, rows, cols, (OWN,), (OWN, SIB))
-    run([tiles.piece(OWN, 0, b + 1, OWN, b, same=b * QUARTER) for b in range(3)], sims, tiles)
-    tiles.wait_all()
+    tiles = Tiles(
+        moves, meta, codes, rows, cols, (OWN,), (OWN, SIB))
+    run([tiles.piece(OWN, 0, b + 1, OWN, b, same=b * QUARTER) for b in range(3)], sims)
     pairs = [(a, b) for a, b in ALL_PAIRS if 3 not in (a, b)]
     either(second_core(), lambda flip: run(tiles.matched(flip, OWN, SIB, pairs), sims))
     out[...] = jnp.zeros(out.shape, F32)
@@ -342,18 +330,20 @@
 
 
 def middle_kernel(
-    own0, arrived, high01, sib0, meta, codes, near, out, sims, rows, cols, held, sems
+    own0, arrived, high01, sib0, meta, codes, near, out, sims, rows, cols
 ):
     width = arrived.shape[1] // 3
     moves = [
         (OWN, own0, None, 0, 3), (OWN, arrived, 0, 3, 1), (HIGH, high01, None, 0, 2),
         (HIGH, arrived, 2 * width, 3, 1), (SIB, sib0, None, 0, 3),
     ]
-    tiles = Tiles(moves, 2, held, sems, meta, codes, rows, cols, (OWN, SIB), (OWN, HIGH))
-    pieces = [tiles.piece(OWN, 0, 4, OWN, 3, same=3 * QUARTER)]
-    pieces += [tiles.piece(OWN, 0, 4, HIGH, b) for b in (0, 1, 3)]
+    tiles = Tiles(
+        moves, meta, codes, rows, cols, (OWN, SIB), (OWN, HIGH))
+    pieces = [tiles.piece(OWN, 0, 3, OWN, 3), tiles.piece(OWN, 3, 1, OWN, 3, same=0)]
+    for b in (0, 1, 3):
+        pieces += [tiles.piece(OWN, 0, 3, HIGH, b), tiles.piece(OWN, 3, 1, HIGH, b)]
     pieces += [tiles.piece(SIB, 0, 3, HIGH, b) for b in (0, 1, 3)]
-    run(pieces, sims, tiles)
+    run(pieces, sims)
     out[...] = near[...]
     for cls in (OWN, SIB, HIGH):
         out[cls : cls + 1, :] = jnp.maximum(near[cls : cls + 1, :], tiles.result(cls))
@@ -361,7 +351,7 @@
 
 def main_kernel(
     own0, arrived, high2, sib0, swapped, low0, high01, meta, codes, before, out,
-    sims, rows, cols, held, sems,
+    sims, rows, cols,
 ):
     width = arrived.shape[1] // 3
     moves = [
@@ -370,14 +360,14 @@
         (HIGH, arrived, 2 * width, 3, 1), (LOW, low0, None, 0, 3), (LOW, arrived, width, 3, 1),
     ]
     tiles = Tiles(
-        moves, 3, held, sems, meta, codes, rows, cols, (OWN, SIB, LOW), (SIB, HIGH)
+        moves, meta, codes, rows, cols, (OWN, SIB, LOW), (SIB, HIGH)
     )
-    pieces = [tiles.piece(OWN, 0, 4, HIGH, 2), tiles.piece(SIB, 0, 4, HIGH, 2)]
-    pieces += [tiles.piece(SIB, 3, 1, HIGH, b) for b in (0, 1, 3)]
-    run(pieces, sims, tiles)
+    pieces = [tiles.piece(cls, 0, 3, HIGH, 2) for cls in (OWN, SIB)]
+    pieces += [tiles.piece(OWN, 3, 1, HIGH, 2)]
+    pieces += [tiles.piece(SIB, 3, 1, HIGH, b) for b in range(4)]
+    run(pieces, sims)
     pairs = [(a, b) for a, b in ALL_PAIRS if 3 in (a, b)]
     either(second_core(), lambda flip: run(tiles.matched(flip, OWN, SIB, pairs), sims))
-    tiles.wait_all()
     either(outer_chip(), lambda flip: run(tiles.matched(flip, LOW, HIGH, ALL_PAIRS), sims))
     for cls in (OWN, SIB, LOW, HIGH):
         out[cls : cls + 1, :] = jnp.maximum(before[cls : cls + 1, :], tiles.result(cls))
@@ -385,15 +375,15 @@
 
 def last_kernel(
     pools, group, main, rest, lows0, high01, high2, swapped, arrived, meta, codes, before, out,
-    sims, rows, cols, held, sems, every,
+    sims, rows, cols, every,
 ):
     width = arrived.shape[1] // 3
     moves = [
         (LOWS, lows0, None, 0, 3), (LOWS, swapped, width, 3, 1), (HIGH, high01, None, 0, 2),
         (HIGH, high2, None, 2, 1), (HIGH, arrived, 2 * width, 3, 1),
     ]
-    tiles = Tiles(moves, 5, held, sems, meta, codes, rows, cols, (LOWS,), (HIGH,))
-    tiles.wait_all()
+    tiles = Tiles(
+        moves, meta, codes, rows, cols, (LOWS,), (HIGH,))
     either(outer_chip(), lambda flip: run(tiles.matched(flip, LOWS, HIGH, ALL_PAIRS), sims))
     every[...] = jnp.zeros(every.shape, F32)
     for cls, place in enumerate(tiles.relatives):
@@ -512,32 +502,36 @@
         compiler_params=PARAMS,
         name="join",
     )(rest, low_rest, high_rest)
-    own0 = follow(own0, sent, some.astype(I32).reshape(1, 1))
-    low0, high01 = shift(own0, 2), shift(own0[: 2 * QUARTER], -2)
-    high2 = shift(own0[2 * QUARTER :], -2)
+    own0, own01, own2 = pl.pallas_call(
+        split_kernel,
+        out_shape=tuple(sds((n * QUARTER, feature), BF16) for n in (3, 2, 1)),
+        in_specs=[hbm] * 3,
+        out_specs=(hbm, hbm, hbm),
+        input_output_aliases={0: 0},
+        scratch_shapes=[pltpu.SemaphoreType.DMA((2,))],
+        compiler_params=PARAMS,
+        name="split",
+    )(own0, sent, some.astype(I32).reshape(1, 1))
+    low0, high01, high2 = shift(own0, 2), shift(own01, -2), shift(own2, -2)
     sib0 = swap(own0)
 
-    def tiles(kernel, name, squares, moves, operands, small, out_shape=(8, rows_dev), more=()):
+    def tiles(kernel, name, squares, operands, small, out_shape=(8, rows_dev), more=()):
         return pl.pallas_call(
             kernel,
             out_shape=sds(out_shape, F32),
-            in_specs=[hbm] * len(operands) + [vmem] * len(small),
             scratch_shapes=[
-                pltpu.VMEM((2, rows_dev, QUARTER), F32),
+                pltpu.VMEM((2, 3 * QUARTER, QUARTER), F32),
                 pltpu.VMEM((4, rows_dev, 128), F32),
                 pltpu.VMEM((5, 8, rows_dev), F32),
-                pltpu.VMEM((5, rows_dev // 16, 16, feature), BF16),
-                pltpu.SemaphoreType.DMA((moves,)),
                 *more,
             ],
             compiler_params=PARAMS,
             cost_estimate=cost(squares * QUARTER * QUARTER * feature),
             name=name,
-        )(*[operand.reshape(-1, *operand.shape[-2:]) if operand.ndim == 3 else
-            operand.reshape(-1, 16, feature) for operand in operands], *small)
+        )(*operands, *small)
 
     def bring(sent, own0, sib0, meta, codes):
-        near = tiles(near_kernel, "near", 11, 2, (own0, sib0), (meta, codes))
+        near = tiles(near_kernel, "near", 11, (own0, sib0), (meta, codes))
         return to_pools(sent), near
 
     def bring_nothing(sent, own0, sib0, meta, codes):
@@ -548,16 +542,16 @@
     )
     swapped = swap(arrived)
     middle = tiles(
-        middle_kernel, "middle", 25, 5, (own0, arrived, high01, sib0), (meta, codes, near)
+        middle_kernel, "middle", 25, (own0, arrived, high01, sib0), (meta, codes, near)
     )
     low0 = follow(low0, middle, high2)
     best = tiles(
-        main_kernel, "main", 23, 9, (own0, arrived, high2, sib0, swapped, low0, high01),
+        main_kernel, "main", 23, (own0, arrived, high2, sib0, swapped, low0, high01),
         (meta, codes, middle),
     )
     best = tiles(
         lambda *refs: last_kernel(pools, group, group * (places - last), group * last, *refs),
-        "last", 8, 5, (swap(low0), high01, high2, swapped, arrived), (meta, codes, best),
+        "last", 8, (swap(low0), high01, high2, swapped, arrived), (meta, codes, best),
         out_shape=(devices, group * places),
         more=(pltpu.VMEM((group, rows_dev), F32),),
     )

time: 115 us -> 158 us (1.37)
  Pallas kernels: 40 us -> 84 us
  local copies, waits for them, and re-layouts: 5.14 us -> 0.94 us
  blocking collectives: 12.3 us -> 15 us
    pallas_call x4 -> x5, Pallas kernels: 27.2 us -> 71.2 us  [the longest x1 48.8 us: body(): pl.pallas_call(split_kernel, out_shape=tuple((sds((n * QUARTER, feature),...]
    slice x2 -> x0, local copies, waits for them, and re-layouts: 4.21 us -> none  [the longest x1 2.3 us: body(): low0, high01 = (shift(own0, 2), shift(own0[:2 * QUARTER], -2))]
    all_to_all x1, blocking collectives: 12.3 us -> 15 us  [body(): lax.all_to_all(best, ('pool', 'grp'), split_axis=0, concat_axis=0, tiled=...]
    all_to_all x2, waiting for transfers between devices: 20.2 us -> 21.8 us  [to_pools(): return lax.all_to_all(rows, 'pool', split_axis=0, concat_axis=0, tiled=True)]
  transfers between devices with their start and end apart: 10 -> 10, of which waited for: 3 -> 3; matrix products, arithmetic and copies ran while one was open for 4% -> 0% of each run, Pallas kernels for 26% -> 16%
where the time goes in v8:
time: 158 us
  Pallas kernels  84 us (53%)
  waiting for transfers between devices  31.5 us (20%)
  starting transfers between devices  25 us (16%)
  blocking collectives  15 us (9%)
    pallas_call x1, Pallas kernels, body(): pl.pallas_call(split_kernel, out_shape=tuple((sds((n * QUARTER, feature),...  48.8 us
    pallas_call x4, Pallas kernels, tiles(): pl.pallas_call(kernel, out_shape=sds(out_shape, F32), scratch_shapes=[plt...  22.4 us
    all_to_all x2, waiting for transfers between devices, to_pools(): return lax.all_to_all(rows, 'pool', split_axis=0, concat_axis=0, tiled=True)  21.8 us
    all_to_all x1, blocking collectives, body(): lax.all_to_all(best, ('pool', 'grp'), split_axis=0, concat_axis=0, tiled=...  15 us
    all_to_all x2, starting transfers between devices, to_pools(): return lax.all_to_all(rows, 'pool', split_axis=0, concat_axis=0, tiled=True)  13.2 us
    ppermute x5, waiting for transfers between devices, shift(): lax.ppermute(rows, 'grp', [(g, (g + by) % group) for g in range(group)])  9.73 us
    ppermute x5, starting transfers between devices, shift(): lax.ppermute(rows, 'grp', [(g, (g + by) % group) for g in range(group)])  6.7 us
    pallas_call x1, Pallas kernels, body(): pl.pallas_call(lambda *refs: meta_kernel(group, places, last, *refs), out...  5.26 us
  transfers between devices with their start and end apart: 10, of which 3 were waited for; matrix products, arithmetic and copies ran while one was open for 0% of the time, Pallas kernels for 16%

profile of v8, /device:TPU:1, one launch (start us, length us, event | category | flops | bytes accessed | tf_op | source)
XLA Modules:
  0.0 158.0 jit_solution(2021780740295616714)
XLA Ops:
  0.0 5.2 %table.1 = (s32[128,128]{1,0:T(8,128)}, bf16[768,1024]{1,0:T(8,128)(2,1)}) custom-call(s32[256,512]{1,0:T(8,128)} %refs_0_.3, s32[1,256]{1,0:T(1,128)} %bitcast.13, bf16[1024,1024]{1,0:T(8,128)(2,1)} %refs_1_.1), custom_call_target="tpu_custom_call" | custom-call | flops 2147483648 | tf_op jit(solution)/shard_map/table/pallas_call | solution.py:435
  5.2 0.0 copy-start.2
  5.2 0.0 copy-start.3
  5.2 0.0 copy-start.4
  5.2 8.8 %all-to-all-start.1 = ((bf16[16,48,1024]{2,1,0:T(8,128)(2,1)}), bf16[16,48,1024]{2,1,0:T(8,128)(2,1)}, u32[]{:S(2)}, u32[]{:S(2)}) async-start(bf16[16,48,1024]{2,1,0:T(8,128)(2,1)} %bitcast.15), calls=%async_computation.1 | async-start | bytes 3145728 | tf_op jit(solution)/shard_map/all_to_all | solution.py:487
  14.0 0.0 copy-start
  14.0 5.3 %meta.1 = (s32[2,8,1024]{2,1,0:T(8,128)S(1)}, s32[1024,128]{1,0:T(8,128)}) custom-call(s32[256,512]{1,0:T(8,128)S(1)} %copy-done.2, s32[1,256]{1,0:T(1,128)S(1)} %bitcast.14, s32[1,256]{1,0:T(1,128)S(1)} %bitcast.12), custom_call_target="tpu_custom_call" | custom-call | flops 4294967296 | tf_op jit(solution)/shard_map/meta/pallas_call | solution.py:453
  19.3 0.9 rest.1.refs_0_
  20.2 1.3 collective-permute-start
  21.5 1.5 collective-permute-start.1
  22.9 0.6 compare_reduce_fusion
  24.2 9.7 %collective-permute-done.refs_1_ = bf16[256,1024]{1,0:T(8,128)(2,1)S(1)} collective-permute-done((bf16[256,1024]{1,0:T(8,128)(2,1)S(1)}, bf16[256,1024]{1,0:T(8,128)(2,1)S(1)}, u32[]{:S(2)}, u32[]{:S(2)}) %collective-permute-start) | collective-permute-done | bytes 524320 | tf_op jit(solution)/shard_map/ppermute | solution.py:470
  33.9 0.1 join.1.after
  34.1 2.9 %all-to-all-done.1 = bf16[16,48,1024]{2,1,0:T(8,128)(2,1)} async-done(((bf16[16,48,1024]{2,1,0:T(8,128)(2,1)}), bf16[16,48,1024]{2,1,0:T(8,128)(2,1)}, u32[]{:S(2)}, u32[]{:S(2)}) %all-to-all-start.1) | async-done | bytes 1572896 | tf_op jit(solution)/shard_map/all_to_all | solution.py:487
  36.9 48.8 %split.1 = (bf16[768,1024]{1,0:T(8,128)(2,1)}, bf16[512,1024]{1,0:T(8,128)(2,1)}, bf16[256,1024]{1,0:T(8,128)(2,1)}) custom-call(bf16[768,1024]{1,0:T(8,128)(2,1)} %bitcast.2.rows, bf16[16,48,1024]{2,1,0:T(8,128)(2,1)S(1)} %join.1.after, s32[1,1]{1,0:T(1,128)} %bitcast.4.also_after), custom_call_target="tpu_custom_call", output_to_operand_aliasing={{0}: (0, {})} | custom-call | tf_op jit(solution)/shard_map/split/pallas_call | solution.py:505
  85.7 2.6 %collective-permute-start.3 = (bf16[768,1024]{1,0:T(8,128)(2,1)}, bf16[768,1024]{1,0:T(8,128)(2,1)}, u32[]{:S(2)}, u32[]{:S(2)}) collective-permute-start(bf16[768,1024]{1,0:T(8,128)(2,1)} %get-tuple-element.32.own0), channel_id=1, source_target_pairs={{0,1},{1,0},{2,3},{3,2},{4,5},{5,4},{6,7},{7,6},{8,9},{9,8},{10,11... | collective-permute-start | bytes 4718600 | tf_op jit(solution)/shard_map/ppermute | solution.py:473
  88.3 1.2 collective-permute-start.2
  89.5 1.5 collective-permute-start.4
  91.0 1.3 collective-permute-start.5
  92.3 27.5 %conditional.1 = (bf16[16,48,1024]{2,1,0:T(8,128)(2,1)}, f32[8,1024]{1,0:T(8,128)S(1)}) conditional(s32[]{:T(128)} %convert_element_type.4, () %tuple.13, (bf16[16,48,1024]{2,1,0:T(8,128)(2,1)}, bf16[768,1024]{1,0:T(8,128)(2,1)}, bf16[768,1024]{1,0:T(8,128)(2,1)}, s32[2,8,1024]{2,1,0:T(8,128)S(1)}, s32[1024,128]{1,0:T(8,128)}) %tuple.17), branch_computations={%region_1.0_spmd, %region_2.0_spmd} | conditional | flops 1476395008 | bytes 4718640 | solution.py:540
  92.3 4.4 %all-to-all-start = ((bf16[16,48,1024]{2,1,0:T(8,128)(2,1)}), bf16[16,48,1024]{2,1,0:T(8,128)(2,1)}, u32[]{:S(2)}, u32[]{:S(2)}) async-start(bf16[16,48,1024]{2,1,0:T(8,128)(2,1)} %get-tuple-element.15), calls=%async_computation | async-start | bytes 3145728 | tf_op jit(solution)/shard_map/cond/branch_1_fun/all_to_all | solution.py:487
  96.7 4.1 %near.1 = f32[8,1024]{1,0:T(8,128)S(1)} custom-call(bf16[768,1024]{1,0:T(8,128)(2,1)} %get-tuple-element.16.own0, bf16[768,1024]{1,0:T(8,128)(2,1)} %get-tuple-element.17.sib0, s32[2,8,1024]{2,1,0:T(8,128)S(1)} %get-tuple-element.18.meta, s32[1024,128]{1,0:T(8,128)} %get-tuple-element.19.codes), custom_call_target="tpu_custom_call" | custom-call | flops 1476395008 | tf_op jit(solution)/shard_map/cond/branch_1_fun/near/pallas_call | solution.py:519
  100.8 18.9 %all-to-all-done = bf16[16,48,1024]{2,1,0:T(8,128)(2,1)} async-done(((bf16[16,48,1024]{2,1,0:T(8,128)(2,1)}), bf16[16,48,1024]{2,1,0:T(8,128)(2,1)}, u32[]{:S(2)}, u32[]{:S(2)}) %all-to-all-start) | async-done | bytes 1572896 | tf_op jit(solution)/shard_map/cond/branch_1_fun/all_to_all | solution.py:487
  119.8 2.4 %collective-permute-start.7 = (bf16[16,48,1024]{2,1,0:T(8,128)(2,1)}, bf16[16,48,1024]{2,1,0:T(8,128)(2,1)S(1)}, u32[]{:S(2)}, u32[]{:S(2)}) collective-permute-start(bf16[16,48,1024]{2,1,0:T(8,128)(2,1)} %get-tuple-element.34.arrived.refs_4_), channel_id=1, source_target_pairs={{0,1},{1,0},{2,3},{3,2},{4,5},{5,4},{6,7},{7,6},{8,9},{9,8},{10,11... | collective-permute-start | bytes 4718600 | tf_op jit(solution)/shard_map/ppermute | solution.py:473
  122.2 7.2 %middle.1.after.before = f32[8,1024]{1,0:T(8,128)S(1)} custom-call(bf16[768,1024]{1,0:T(8,128)(2,1)} %get-tuple-element.32.own0, bf16[16,48,1024]{2,1,0:T(8,128)(2,1)} %get-tuple-element.34.arrived.refs_4_, bf16[512,1024]{1,0:T(8,128)(2,1)S(1)} %collective-permute-done.4.high01.refs_1_, bf16[768,1024]{1,0:T(8,128)(2,1)} %collective-permute-done.3.sib0, ...), custom_call_target="tpu_custom_call" | custom-call | flops 3355443200 | tf_op jit(solution)/shard_map/middle/pallas_call | solution.py:519
  129.4 0.0 collective-permute-done.5.also_after.high2.refs_2_
  129.4 0.1 collective-permute-start.6
  129.5 0.9 copy-done.6
  130.4 7.5 %main.1.refs_7_ = f32[8,1024]{1,0:T(8,128)S(1)} custom-call(bf16[768,1024]{1,0:T(8,128)(2,1)} %get-tuple-element.32.own0, bf16[16,48,1024]{2,1,0:T(8,128)(2,1)} %get-tuple-element.34.arrived.refs_4_, bf16[256,1024]{1,0:T(8,128)(2,1)S(1)} %collective-permute-done.5.also_after.high2.refs_2_, bf16[768,1024]{1,0:T(8,128)(2,1)} %collective-permute-done.3.sib0, ...), custom_call_target="tpu_custom_call" | custom-call | flops 3087007744 | tf_op jit(solution)/shard_map/main/pallas_call | solution.py:519
  137.9 3.6 %last.1 = f32[128,64]{1,0:T(8,128)S(1)} custom-call(bf16[768,1024]{1,0:T(8,128)(2,1)S(1)} %collective-permute-done.6.refs_0_, bf16[512,1024]{1,0:T(8,128)(2,1)S(1)} %collective-permute-done.4.high01.refs_1_, bf16[256,1024]{1,0:T(8,128)(2,1)S(1)} %collective-permute-done.5.also_after.high2.refs_2_, ...), custom_call_target="tpu_custom_call" | custom-call | flops 1073741824 | tf_op jit(solution)/shard_map/last/pallas_call | solution.py:519
  141.5 15.0 %all_to_all.20 = f32[128,1,64]{2,1,0:T(1,128)S(1)} all-to-all(f32[128,1,64]{2,1,0:T(1,128)S(1)} %bitcast.10), channel_id=1, replica_groups=mesh['pool'=16,'grp'=8] {'pool','grp'}, dimensions={0} | all-to-all | bytes 65536 | tf_op jit(solution)/shard_map/all_to_all | solution.py:558
  156.6 1.4 score.1
  (16 shorter events, 0.0 us)
Async XLA Ops:
  5.2 8.8 %copy-start.2 = (s32[256,512]{1,0:T(8,128)S(1)}, s32[256,512]{1,0:T(8,128)}, u32[]{:S(2)}) copy-start(s32[256,512]{1,0:T(8,128)} %refs_0_.3) | copy-start | bytes 1572868
  5.2 8.8 %copy-start.3 = (s32[256]{0:T(256)S(1)}, s32[256]{0:T(256)}, u32[]{:S(2)}) copy-start(s32[256]{0:T(256)} %param.9) | copy-start | bytes 3076
  5.2 8.8 %copy-start.4 = (s32[256]{0:T(256)S(1)}, s32[256]{0:T(256)}, u32[]{:S(2)}) copy-start(s32[256]{0:T(256)} %param.8) | copy-start | bytes 3076
  5.2 31.7 %all-to-all-start.1 = ((bf16[16,48,1024]{2,1,0:T(8,128)(2,1)}), bf16[16,48,1024]{2,1,0:T(8,128)(2,1)}, u32[]{:S(2)}, u32[]{:S(2)}) async-start(bf16[16,48,1024]{2,1,0:T(8,128)(2,1)} %bitcast.15), calls=%async_computation.1 | async-start | bytes 3145728 | tf_op jit(solution)/shard_map/all_to_all | solution.py:487
  14.0 5.3 %copy-start = (bf16[1024,1024]{1,0:T(8,128)(2,1)S(1)}, bf16[1024,1024]{1,0:T(8,128)(2,1)}, u32[]{:S(2)}) copy-start(bf16[1024,1024]{1,0:T(8,128)(2,1)} %refs_1_.1) | copy-start | bytes 6291460
  14.0 5.3 %copy-start.1 = (s32[128,128]{1,0:T(8,128)S(1)}, s32[128,128]{1,0:T(8,128)}, u32[]{:S(2)}) copy-start(s32[128,128]{1,0:T(8,128)} %get-tuple-element.29.refs_0_) | copy-start | bytes 196612
  20.2 13.7 %collective-permute-start = (bf16[256,1024]{1,0:T(8,128)(2,1)S(1)}, bf16[256,1024]{1,0:T(8,128)(2,1)S(1)}, u32[]{:S(2)}, u32[]{:S(2)}) collective-permute-start(bf16[256,1024]{1,0:T(8,128)(2,1)S(1)} %rest.1.refs_0_), channel_id=1, source_target_pairs={{0,2},{1,3},{2,4},{3,5},{4,6},{5,7},{6,0},{7,1},{8,10},{9,11},{10,... | collective-permute-start | bytes 1572872 | tf_op jit(solution)/shard_map/ppermute | solution.py:470
  21.5 12.5 %collective-permute-start.1 = (bf16[256,1024]{1,0:T(8,128)(2,1)S(1)}, bf16[256,1024]{1,0:T(8,128)(2,1)S(1)}, u32[]{:S(2)}, u32[]{:S(2)}) collective-permute-start(bf16[256,1024]{1,0:T(8,128)(2,1)S(1)} %rest.1.refs_0_), channel_id=1, source_target_pairs={{0,6},{1,7},{2,0},{3,1},{4,2},{5,3},{6,4},{7,5},{8,14},{9,15},{10,... | collective-permute-start | bytes 1572872 | tf_op jit(solution)/shard_map/ppermute | solution.py:470
  34.0 51.6 %copy-start.5 = (bf16[16,48,1024]{2,1,0:T(8,128)(2,1)}, bf16[16,48,1024]{2,1,0:T(8,128)(2,1)S(1)}, u32[]{:S(2)}) copy-start(bf16[16,48,1024]{2,1,0:T(8,128)(2,1)S(1)} %join.1.after) | copy-start | bytes 4718596
  85.7 6.6 %collective-permute-start.3 = (bf16[768,1024]{1,0:T(8,128)(2,1)}, bf16[768,1024]{1,0:T(8,128)(2,1)}, u32[]{:S(2)}, u32[]{:S(2)}) collective-permute-start(bf16[768,1024]{1,0:T(8,128)(2,1)} %get-tuple-element.32.own0), channel_id=1, source_target_pairs={{0,1},{1,0},{2,3},{3,2},{4,5},{5,4},{6,7},{7,6},{8,9},{9,8},{10,11... | collective-permute-start | bytes 4718600 | tf_op jit(solution)/shard_map/ppermute | solution.py:473
  88.3 41.1 %collective-permute-start.2 = (bf16[768,1024]{1,0:T(8,128)(2,1)}, bf16[768,1024]{1,0:T(8,128)(2,1)S(1)}, u32[]{:S(2)}, u32[]{:S(2)}) collective-permute-start(bf16[768,1024]{1,0:T(8,128)(2,1)} %get-tuple-element.32.own0), channel_id=1, source_target_pairs={{0,2},{1,3},{2,4},{3,5},{4,6},{5,7},{6,0},{7,1},{8,10},{9,11},{10,... | collective-permute-start | bytes 4718600 | tf_op jit(solution)/shard_map/ppermute | solution.py:470
  89.5 32.6 %collective-permute-start.4 = (bf16[512,1024]{1,0:T(8,128)(2,1)}, bf16[512,1024]{1,0:T(8,128)(2,1)S(1)}, u32[]{:S(2)}, u32[]{:S(2)}) collective-permute-start(bf16[512,1024]{1,0:T(8,128)(2,1)} %get-tuple-element.35), channel_id=1, source_target_pairs={{0,6},{1,7},{2,0},{3,1},{4,2},{5,3},{6,4},{7,5},{8,14},{9,15},{10,... | collective-permute-start | bytes 3145736 | tf_op jit(solution)/shard_map/ppermute | solution.py:470
  91.0 38.4 %collective-permute-start.5 = (bf16[256,1024]{1,0:T(8,128)(2,1)}, bf16[256,1024]{1,0:T(8,128)(2,1)S(1)}, u32[]{:S(2)}, u32[]{:S(2)}) collective-permute-start(bf16[256,1024]{1,0:T(8,128)(2,1)} %get-tuple-element.37), channel_id=1, source_target_pairs={{0,6},{1,7},{2,0},{3,1},{4,2},{5,3},{6,4},{7,5},{8,14},{9,15},{10,... | collective-permute-start | bytes 1572872 | tf_op jit(solution)/shard_map/ppermute | solution.py:470
  92.3 27.5 %all-to-all-start = ((bf16[16,48,1024]{2,1,0:T(8,128)(2,1)}), bf16[16,48,1024]{2,1,0:T(8,128)(2,1)}, u32[]{:S(2)}, u32[]{:S(2)}) async-start(bf16[16,48,1024]{2,1,0:T(8,128)(2,1)} %get-tuple-element.15), calls=%async_computation | async-start | bytes 3145728 | tf_op jit(solution)/shard_map/cond/branch_1_fun/all_to_all | solution.py:487
  119.8 9.7 %collective-permute-start.7 = (bf16[16,48,1024]{2,1,0:T(8,128)(2,1)}, bf16[16,48,1024]{2,1,0:T(8,128)(2,1)S(1)}, u32[]{:S(2)}, u32[]{:S(2)}) collective-permute-start(bf16[16,48,1024]{2,1,0:T(8,128)(2,1)} %get-tuple-element.34.arrived.refs_4_), channel_id=1, source_target_pairs={{0,1},{1,0},{2,3},{3,2},{4,5},{5,4},{6,7},{7,6},{8,9},{9,8},{10,11... | collective-permute-start | bytes 4718600 | tf_op jit(solution)/shard_map/ppermute | solution.py:473
  129.4 1.0 copy-start.6
  129.4 8.5 %collective-permute-start.6 = (bf16[768,1024]{1,0:T(8,128)(2,1)S(1)}, bf16[768,1024]{1,0:T(8,128)(2,1)S(1)}, u32[]{:S(2)}, u32[]{:S(2)}) collective-permute-start(bf16[768,1024]{1,0:T(8,128)(2,1)S(1)} %follow.1.low0), channel_id=1, source_target_pairs={{0,1},{1,0},{2,3},{3,2},{4,5},{5,4},{6,7},{7,6},{8,9},{9,8},{10,11... | collective-permute-start | bytes 4718600 | tf_op jit(solution)/shard_map/ppermute | solution.py:473

commit v9 on v8

--- a/solution.py
+++ b/solution.py
@@ -375,15 +375,18 @@
 
 def last_kernel(
     pools, group, main, rest, lows0, high01, high2, swapped, arrived, meta, codes, before, out,
-    sims, rows, cols, every,
+    sims, rows, cols, every, upper, sem,
 ):
-    width = arrived.shape[1] // 3
+    width = swapped.shape[1] // 3
+    copy = pltpu.make_async_copy(arrived.at[:, pl.ds(2 * width, width), :], upper, sem)
+    copy.start()
     moves = [
         (LOWS, lows0, None, 0, 3), (LOWS, swapped, width, 3, 1), (HIGH, high01, None, 0, 2),
-        (HIGH, high2, None, 2, 1), (HIGH, arrived, 2 * width, 3, 1),
+        (HIGH, high2, None, 2, 1), (HIGH, upper, 0, 3, 1),
     ]
     tiles = Tiles(
         moves, meta, codes, rows, cols, (LOWS,), (HIGH,))
+    copy.wait()
     either(outer_chip(), lambda flip: run(tiles.matched(flip, LOWS, HIGH, ALL_PAIRS), sims))
     every[...] = jnp.zeros(every.shape, F32)
     for cls, place in enumerate(tiles.relatives):
@@ -506,7 +509,7 @@
         split_kernel,
         out_shape=tuple(sds((n * QUARTER, feature), BF16) for n in (3, 2, 1)),
         in_specs=[hbm] * 3,
-        out_specs=(hbm, hbm, hbm),
+        out_specs=(hbm, vmem, vmem),
         input_output_aliases={0: 0},
         scratch_shapes=[pltpu.SemaphoreType.DMA((2,))],
         compiler_params=PARAMS,
@@ -515,10 +518,11 @@
     low0, high01, high2 = shift(own0, 2), shift(own01, -2), shift(own2, -2)
     sib0 = swap(own0)
 
-    def tiles(kernel, name, squares, operands, small, out_shape=(8, rows_dev), more=()):
+    def tiles(kernel, name, squares, operands, small, out_shape=(8, rows_dev), more=(), specs=None):
         return pl.pallas_call(
             kernel,
             out_shape=sds(out_shape, F32),
+            in_specs=specs or [vmem] * (len(operands) + len(small)),
             scratch_shapes=[
                 pltpu.VMEM((2, 3 * QUARTER, QUARTER), F32),
                 pltpu.VMEM((4, rows_dev, 128), F32),
@@ -553,7 +557,12 @@
         lambda *refs: last_kernel(pools, group, group * (places - last), group * last, *refs),
         "last", 8, (swap(low0), high01, high2, swapped, arrived), (meta, codes, best),
         out_shape=(devices, group * places),
-        more=(pltpu.VMEM((group, rows_dev), F32),),
+        more=(
+            pltpu.VMEM((group, rows_dev), F32),
+            pltpu.VMEM((pools, QUARTER // pools, feature), BF16),
+            pltpu.SemaphoreType.DMA,
+        ),
+        specs=[vmem] * 4 + [hbm] + [vmem] * 3,
     )
     returned = lax.all_to_all(best, ("pool", "grp"), split_axis=0, concat_axis=0, tiled=True)
     scores = pl.pallas_call(

time: 158 us -> 112 us (0.71)
  Pallas kernels: 84 us -> 37.2 us
    pallas_call x1, Pallas kernels: 48.8 us -> 2.54 us  [body(): pl.pallas_call(split_kernel, out_shape=tuple((sds((n * QUARTER, feature),...]
  transfers between devices with their start and end apart: 10 -> 10, of which waited for: 3 -> 3; matrix products, arithmetic and copies ran while one was open for 0% -> 1% of each run, Pallas kernels for 16% -> 23%
where the time goes in v9:
time: 112 us; the launch traced here: 111 us
  Pallas kernels  37.2 us (33%)
  waiting for transfers between devices  31.5 us (28%)
  starting transfers between devices  25 us (22%)
  blocking collectives  15 us (13%)
    pallas_call x4, Pallas kernels, tiles(): pl.pallas_call(kernel, out_shape=sds(out_shape, F32), in_specs=specs or [...  21.9 us
    all_to_all x2, waiting for transfers between devices, to_pools(): return lax.all_to_all(rows, 'pool', split_axis=0, concat_axis=0, tiled=True)  21.8 us
    all_to_all x1, blocking collectives, body(): lax.all_to_all(best, ('pool', 'grp'), split_axis=0, concat_axis=0, tiled=...  15 us
    all_to_all x2, starting transfers between devices, to_pools(): return lax.all_to_all(rows, 'pool', split_axis=0, concat_axis=0, tiled=True)  13.2 us
    ppermute x5, waiting for transfers between devices, shift(): lax.ppermute(rows, 'grp', [(g, (g + by) % group) for g in range(group)])  9.73 us
    ppermute x5, starting transfers between devices, shift(): lax.ppermute(rows, 'grp', [(g, (g + by) % group) for g in range(group)])  6.7 us
    pallas_call x1, Pallas kernels, body(): pl.pallas_call(lambda *refs: meta_kernel(group, places, last, *refs), out...  5.26 us
    pallas_call x1, Pallas kernels, body(): pl.pallas_call(lambda *refs: table_kernel(pools, group, places, last, *re...  5.16 us
  transfers between devices with their start and end apart: 10, of which 3 were waited for; matrix products, arithmetic and copies ran while one was open for 1% of the time, Pallas kernels for 23%

profile of v9, /device:TPU:1, one launch (start us, length us, event | category | flops | bytes accessed | tf_op | source)
XLA Modules:
  0.0 111.1 jit_solution(3200348020120853035)
XLA Ops:
  0.0 5.2 %table.1 = (s32[128,128]{1,0:T(8,128)}, bf16[768,1024]{1,0:T(8,128)(2,1)}) custom-call(s32[256,512]{1,0:T(8,128)} %refs_0_.3, s32[1,256]{1,0:T(1,128)} %bitcast.13, bf16[1024,1024]{1,0:T(8,128)(2,1)} %refs_1_.1), custom_call_target="tpu_custom_call" | custom-call | flops 2147483648 | tf_op jit(solution)/shard_map/table/pallas_call | solution.py:438
  5.2 0.0 copy-start.2
  5.2 0.0 copy-start.3
  5.2 0.0 copy-start.4
  5.2 8.8 %all-to-all-start.1 = ((bf16[16,48,1024]{2,1,0:T(8,128)(2,1)}), bf16[16,48,1024]{2,1,0:T(8,128)(2,1)}, u32[]{:S(2)}, u32[]{:S(2)}) async-start(bf16[16,48,1024]{2,1,0:T(8,128)(2,1)} %bitcast.15), calls=%async_computation.1 | async-start | bytes 3145728 | tf_op jit(solution)/shard_map/all_to_all | solution.py:490
  14.0 0.0 copy-start
  14.0 5.3 %meta.1 = (s32[2,8,1024]{2,1,0:T(8,128)S(1)}, s32[1024,128]{1,0:T(8,128)}) custom-call(s32[256,512]{1,0:T(8,128)S(1)} %copy-done.2, s32[1,256]{1,0:T(1,128)S(1)} %bitcast.14, s32[1,256]{1,0:T(1,128)S(1)} %bitcast.12), custom_call_target="tpu_custom_call" | custom-call | flops 4294967296 | tf_op jit(solution)/shard_map/meta/pallas_call | solution.py:456
  19.3 0.9 rest.1.refs_0_
  20.2 1.3 %collective-permute-start = (bf16[256,1024]{1,0:T(8,128)(2,1)S(1)}, bf16[256,1024]{1,0:T(8,128)(2,1)S(1)}, u32[]{:S(2)}, u32[]{:S(2)}) collective-permute-start(bf16[256,1024]{1,0:T(8,128)(2,1)S(1)} %rest.1.refs_0_), channel_id=1, source_target_pairs={{0,2},{1,3},{2,4},{3,5},{4,6},{5,7},{6,0},{7,1},{8,10},{9,11},{10,... | collective-permute-start | bytes 1572872 | tf_op jit(solution)/shard_map/ppermute | solution.py:473
  21.5 1.5 %collective-permute-start.1 = (bf16[256,1024]{1,0:T(8,128)(2,1)S(1)}, bf16[256,1024]{1,0:T(8,128)(2,1)S(1)}, u32[]{:S(2)}, u32[]{:S(2)}) collective-permute-start(bf16[256,1024]{1,0:T(8,128)(2,1)S(1)} %rest.1.refs_0_), channel_id=1, source_target_pairs={{0,6},{1,7},{2,0},{3,1},{4,2},{5,3},{6,4},{7,5},{8,14},{9,15},{10,... | collective-permute-start | bytes 1572872 | tf_op jit(solution)/shard_map/ppermute | solution.py:473
  22.9 0.6 compare_reduce_fusion
  24.2 9.7 %collective-permute-done.refs_1_ = bf16[256,1024]{1,0:T(8,128)(2,1)S(1)} collective-permute-done((bf16[256,1024]{1,0:T(8,128)(2,1)S(1)}, bf16[256,1024]{1,0:T(8,128)(2,1)S(1)}, u32[]{:S(2)}, u32[]{:S(2)}) %collective-permute-start) | collective-permute-done | bytes 524320 | tf_op jit(solution)/shard_map/ppermute | solution.py:473
  33.9 0.1 join.1.after
  34.1 2.9 %all-to-all-done.1 = bf16[16,48,1024]{2,1,0:T(8,128)(2,1)} async-done(((bf16[16,48,1024]{2,1,0:T(8,128)(2,1)}), bf16[16,48,1024]{2,1,0:T(8,128)(2,1)}, u32[]{:S(2)}, u32[]{:S(2)}) %all-to-all-start.1) | async-done | bytes 1572896 | tf_op jit(solution)/shard_map/all_to_all | solution.py:490
  36.9 2.5 %split.1 = (bf16[768,1024]{1,0:T(8,128)(2,1)}, bf16[512,1024]{1,0:T(8,128)(2,1)}, bf16[256,1024]{1,0:T(8,128)(2,1)}) custom-call(bf16[768,1024]{1,0:T(8,128)(2,1)} %bitcast.2.rows, bf16[16,48,1024]{2,1,0:T(8,128)(2,1)S(1)} %join.1.after, s32[1,1]{1,0:T(1,128)} %bitcast.4.also_after), custom_call_target="tpu_custom_call", output_to_operand_aliasing={{0}: (0, {})} | custom-call | tf_op jit(solution)/shard_map/split/pallas_call | solution.py:508
  39.5 2.6 %collective-permute-start.3 = (bf16[768,1024]{1,0:T(8,128)(2,1)}, bf16[768,1024]{1,0:T(8,128)(2,1)}, u32[]{:S(2)}, u32[]{:S(2)}) collective-permute-start(bf16[768,1024]{1,0:T(8,128)(2,1)} %get-tuple-element.32.own0), channel_id=1, source_target_pairs={{0,1},{1,0},{2,3},{3,2},{4,5},{5,4},{6,7},{7,6},{8,9},{9,8},{10,11... | collective-permute-start | bytes 4718600 | tf_op jit(solution)/shard_map/ppermute | solution.py:476
  42.1 1.2 %collective-permute-start.2 = (bf16[768,1024]{1,0:T(8,128)(2,1)}, bf16[768,1024]{1,0:T(8,128)(2,1)S(1)}, u32[]{:S(2)}, u32[]{:S(2)}) collective-permute-start(bf16[768,1024]{1,0:T(8,128)(2,1)} %get-tuple-element.32.own0), channel_id=1, source_target_pairs={{0,2},{1,3},{2,4},{3,5},{4,6},{5,7},{6,0},{7,1},{8,10},{9,11},{10,... | collective-permute-start | bytes 4718600 | tf_op jit(solution)/shard_map/ppermute | solution.py:473
  43.3 1.5 %collective-permute-start.4 = (bf16[512,1024]{1,0:T(8,128)(2,1)}, bf16[512,1024]{1,0:T(8,128)(2,1)S(1)}, u32[]{:S(2)}, u32[]{:S(2)}) collective-permute-start(bf16[512,1024]{1,0:T(8,128)(2,1)} %get-tuple-element.35), channel_id=1, source_target_pairs={{0,6},{1,7},{2,0},{3,1},{4,2},{5,3},{6,4},{7,5},{8,14},{9,15},{10,... | collective-permute-start | bytes 3145736 | tf_op jit(solution)/shard_map/ppermute | solution.py:473
  44.8 1.3 %collective-permute-start.5 = (bf16[256,1024]{1,0:T(8,128)(2,1)}, bf16[256,1024]{1,0:T(8,128)(2,1)S(1)}, u32[]{:S(2)}, u32[]{:S(2)}) collective-permute-start(bf16[256,1024]{1,0:T(8,128)(2,1)} %get-tuple-element.37), channel_id=1, source_target_pairs={{0,6},{1,7},{2,0},{3,1},{4,2},{5,3},{6,4},{7,5},{8,14},{9,15},{10,... | collective-permute-start | bytes 1572872 | tf_op jit(solution)/shard_map/ppermute | solution.py:473
  46.1 0.0 collective-permute-done.3.sib0
  46.1 27.5 %conditional.1 = (bf16[16,48,1024]{2,1,0:T(8,128)(2,1)}, f32[8,1024]{1,0:T(8,128)S(1)}) conditional(s32[]{:T(128)} %convert_element_type.4, () %tuple.13, (bf16[16,48,1024]{2,1,0:T(8,128)(2,1)}, bf16[768,1024]{1,0:T(8,128)(2,1)}, bf16[768,1024]{1,0:T(8,128)(2,1)}, s32[2,8,1024]{2,1,0:T(8,128)S(1)}, s32[1024,128]{1,0:T(8,128)}) %tuple.17), branch_computations={%region_1.0_spmd, %region_2.0_spmd} | conditional | flops 1476395008 | bytes 4718640 | solution.py:544
  46.1 4.4 %all-to-all-start = ((bf16[16,48,1024]{2,1,0:T(8,128)(2,1)}), bf16[16,48,1024]{2,1,0:T(8,128)(2,1)}, u32[]{:S(2)}, u32[]{:S(2)}) async-start(bf16[16,48,1024]{2,1,0:T(8,128)(2,1)} %get-tuple-element.15), calls=%async_computation | async-start | bytes 3145728 | tf_op jit(solution)/shard_map/cond/branch_1_fun/all_to_all | solution.py:490
  50.5 4.1 %near.1 = f32[8,1024]{1,0:T(8,128)S(1)} custom-call(bf16[768,1024]{1,0:T(8,128)(2,1)} %get-tuple-element.16.own0, bf16[768,1024]{1,0:T(8,128)(2,1)} %get-tuple-element.17.sib0, s32[2,8,1024]{2,1,0:T(8,128)S(1)} %get-tuple-element.18.meta, s32[1024,128]{1,0:T(8,128)} %get-tuple-element.19.codes), custom_call_target="tpu_custom_call" | custom-call | flops 1476395008 | tf_op jit(solution)/shard_map/cond/branch_1_fun/near/pallas_call | solution.py:522
  54.6 18.9 %all-to-all-done = bf16[16,48,1024]{2,1,0:T(8,128)(2,1)} async-done(((bf16[16,48,1024]{2,1,0:T(8,128)(2,1)}), bf16[16,48,1024]{2,1,0:T(8,128)(2,1)}, u32[]{:S(2)}, u32[]{:S(2)}) %all-to-all-start) | async-done | bytes 1572896 | tf_op jit(solution)/shard_map/cond/branch_1_fun/all_to_all | solution.py:490
  73.5 2.4 %collective-permute-start.7 = (bf16[16,48,1024]{2,1,0:T(8,128)(2,1)}, bf16[16,48,1024]{2,1,0:T(8,128)(2,1)S(1)}, u32[]{:S(2)}, u32[]{:S(2)}) collective-permute-start(bf16[16,48,1024]{2,1,0:T(8,128)(2,1)} %get-tuple-element.34.arrived.refs_4_), channel_id=1, source_target_pairs={{0,1},{1,0},{2,3},{3,2},{4,5},{5,4},{6,7},{7,6},{8,9},{9,8},{10,11... | collective-permute-start | bytes 4718600 | tf_op jit(solution)/shard_map/ppermute | solution.py:476
  75.9 7.2 %middle.1.after.before = f32[8,1024]{1,0:T(8,128)S(1)} custom-call(bf16[768,1024]{1,0:T(8,128)(2,1)} %get-tuple-element.32.own0, bf16[16,48,1024]{2,1,0:T(8,128)(2,1)} %get-tuple-element.34.arrived.refs_4_, bf16[512,1024]{1,0:T(8,128)(2,1)S(1)} %collective-permute-done.4.high01.refs_1_, bf16[768,1024]{1,0:T(8,128)(2,1)} %collective-permute-done.3.sib0, ...), custom_call_target="tpu_custom_call" | custom-call | flops 3355443200 | tf_op jit(solution)/shard_map/middle/pallas_call | solution.py:522
  83.2 0.1 collective-permute-start.6
  83.3 0.9 copy-done.6
  84.2 7.5 %main.1.refs_7_ = f32[8,1024]{1,0:T(8,128)S(1)} custom-call(bf16[768,1024]{1,0:T(8,128)(2,1)} %get-tuple-element.32.own0, bf16[16,48,1024]{2,1,0:T(8,128)(2,1)} %get-tuple-element.34.arrived.refs_4_, bf16[256,1024]{1,0:T(8,128)(2,1)S(1)} %collective-permute-done.5.also_after.high2.refs_2_, bf16[768,1024]{1,0:T(8,128)(2,1)} %collective-permute-done.3.sib0, ...), custom_call_target="tpu_custom_call" | custom-call | flops 3087007744 | tf_op jit(solution)/shard_map/main/pallas_call | solution.py:522
  91.7 3.0 %last.1 = f32[128,64]{1,0:T(8,128)S(1)} custom-call(bf16[768,1024]{1,0:T(8,128)(2,1)S(1)} %collective-permute-done.6.refs_0_, bf16[512,1024]{1,0:T(8,128)(2,1)S(1)} %collective-permute-done.4.high01.refs_1_, bf16[256,1024]{1,0:T(8,128)(2,1)S(1)} %collective-permute-done.5.also_after.high2.refs_2_, ...), custom_call_target="tpu_custom_call" | custom-call | flops 1073741824 | tf_op jit(solution)/shard_map/last/pallas_call | solution.py:522
  94.7 15.0 %all_to_all.20 = f32[128,1,64]{2,1,0:T(1,128)S(1)} all-to-all(f32[128,1,64]{2,1,0:T(1,128)S(1)} %bitcast.10), channel_id=1, replica_groups=mesh['pool'=16,'grp'=8] {'pool','grp'}, dimensions={0} | all-to-all | bytes 65536 | tf_op jit(solution)/shard_map/all_to_all | solution.py:567
  109.7 1.4 %score.1 = f32[1,1024]{1,0:T(1,128)} custom-call(s32[128,128]{1,0:T(8,128)S(1)} %copy-done.1, f32[128,64]{1,0:T(8,128)S(1)} %bitcast.11), custom_call_target="tpu_custom_call" | custom-call | tf_op jit(solution)/shard_map/score/pallas_call | solution.py:568
  (16 shorter events, 0.0 us)
Async XLA Ops:
  5.2 8.8 %copy-start.2 = (s32[256,512]{1,0:T(8,128)S(1)}, s32[256,512]{1,0:T(8,128)}, u32[]{:S(2)}) copy-start(s32[256,512]{1,0:T(8,128)} %refs_0_.3) | copy-start | bytes 1572868
  5.2 8.8 %copy-start.3 = (s32[256]{0:T(256)S(1)}, s32[256]{0:T(256)}, u32[]{:S(2)}) copy-start(s32[256]{0:T(256)} %param.9) | copy-start | bytes 3076
  5.2 8.8 %copy-start.4 = (s32[256]{0:T(256)S(1)}, s32[256]{0:T(256)}, u32[]{:S(2)}) copy-start(s32[256]{0:T(256)} %param.8) | copy-start | bytes 3076
  5.2 31.7 %all-to-all-start.1 = ((bf16[16,48,1024]{2,1,0:T(8,128)(2,1)}), bf16[16,48,1024]{2,1,0:T(8,128)(2,1)}, u32[]{:S(2)}, u32[]{:S(2)}) async-start(bf16[16,48,1024]{2,1,0:T(8,128)(2,1)} %bitcast.15), calls=%async_computation.1 | async-start | bytes 3145728 | tf_op jit(solution)/shard_map/all_to_all | solution.py:490
  14.0 5.3 %copy-start = (bf16[1024,1024]{1,0:T(8,128)(2,1)S(1)}, bf16[1024,1024]{1,0:T(8,128)(2,1)}, u32[]{:S(2)}) copy-start(bf16[1024,1024]{1,0:T(8,128)(2,1)} %refs_1_.1) | copy-start | bytes 6291460
  14.0 5.3 %copy-start.1 = (s32[128,128]{1,0:T(8,128)S(1)}, s32[128,128]{1,0:T(8,128)}, u32[]{:S(2)}) copy-start(s32[128,128]{1,0:T(8,128)} %get-tuple-element.29.refs_0_) | copy-start | bytes 196612
  20.2 13.7 %collective-permute-start = (bf16[256,1024]{1,0:T(8,128)(2,1)S(1)}, bf16[256,1024]{1,0:T(8,128)(2,1)S(1)}, u32[]{:S(2)}, u32[]{:S(2)}) collective-permute-start(bf16[256,1024]{1,0:T(8,128)(2,1)S(1)} %rest.1.refs_0_), channel_id=1, source_target_pairs={{0,2},{1,3},{2,4},{3,5},{4,6},{5,7},{6,0},{7,1},{8,10},{9,11},{10,... | collective-permute-start | bytes 1572872 | tf_op jit(solution)/shard_map/ppermute | solution.py:473
  21.5 12.5 %collective-permute-start.1 = (bf16[256,1024]{1,0:T(8,128)(2,1)S(1)}, bf16[256,1024]{1,0:T(8,128)(2,1)S(1)}, u32[]{:S(2)}, u32[]{:S(2)}) collective-permute-start(bf16[256,1024]{1,0:T(8,128)(2,1)S(1)} %rest.1.refs_0_), channel_id=1, source_target_pairs={{0,6},{1,7},{2,0},{3,1},{4,2},{5,3},{6,4},{7,5},{8,14},{9,15},{10,... | collective-permute-start | bytes 1572872 | tf_op jit(solution)/shard_map/ppermute | solution.py:473
  34.0 5.4 %copy-start.5 = (bf16[16,48,1024]{2,1,0:T(8,128)(2,1)}, bf16[16,48,1024]{2,1,0:T(8,128)(2,1)S(1)}, u32[]{:S(2)}) copy-start(bf16[16,48,1024]{2,1,0:T(8,128)(2,1)S(1)} %join.1.after) | copy-start | bytes 4718596
  39.5 6.6 %collective-permute-start.3 = (bf16[768,1024]{1,0:T(8,128)(2,1)}, bf16[768,1024]{1,0:T(8,128)(2,1)}, u32[]{:S(2)}, u32[]{:S(2)}) collective-permute-start(bf16[768,1024]{1,0:T(8,128)(2,1)} %get-tuple-element.32.own0), channel_id=1, source_target_pairs={{0,1},{1,0},{2,3},{3,2},{4,5},{5,4},{6,7},{7,6},{8,9},{9,8},{10,11... | collective-permute-start | bytes 4718600 | tf_op jit(solution)/shard_map/ppermute | solution.py:476
  42.1 41.1 %collective-permute-start.2 = (bf16[768,1024]{1,0:T(8,128)(2,1)}, bf16[768,1024]{1,0:T(8,128)(2,1)S(1)}, u32[]{:S(2)}, u32[]{:S(2)}) collective-permute-start(bf16[768,1024]{1,0:T(8,128)(2,1)} %get-tuple-element.32.own0), channel_id=1, source_target_pairs={{0,2},{1,3},{2,4},{3,5},{4,6},{5,7},{6,0},{7,1},{8,10},{9,11},{10,... | collective-permute-start | bytes 4718600 | tf_op jit(solution)/shard_map/ppermute | solution.py:473
  43.3 32.6 %collective-permute-start.4 = (bf16[512,1024]{1,0:T(8,128)(2,1)}, bf16[512,1024]{1,0:T(8,128)(2,1)S(1)}, u32[]{:S(2)}, u32[]{:S(2)}) collective-permute-start(bf16[512,1024]{1,0:T(8,128)(2,1)} %get-tuple-element.35), channel_id=1, source_target_pairs={{0,6},{1,7},{2,0},{3,1},{4,2},{5,3},{6,4},{7,5},{8,14},{9,15},{10,... | collective-permute-start | bytes 3145736 | tf_op jit(solution)/shard_map/ppermute | solution.py:473
  44.8 38.4 %collective-permute-start.5 = (bf16[256,1024]{1,0:T(8,128)(2,1)}, bf16[256,1024]{1,0:T(8,128)(2,1)S(1)}, u32[]{:S(2)}, u32[]{:S(2)}) collective-permute-start(bf16[256,1024]{1,0:T(8,128)(2,1)} %get-tuple-element.37), channel_id=1, source_target_pairs={{0,6},{1,7},{2,0},{3,1},{4,2},{5,3},{6,4},{7,5},{8,14},{9,15},{10,... | collective-permute-start | bytes 1572872 | tf_op jit(solution)/shard_map/ppermute | solution.py:473
  46.1 27.5 %all-to-all-start = ((bf16[16,48,1024]{2,1,0:T(8,128)(2,1)}), bf16[16,48,1024]{2,1,0:T(8,128)(2,1)}, u32[]{:S(2)}, u32[]{:S(2)}) async-start(bf16[16,48,1024]{2,1,0:T(8,128)(2,1)} %get-tuple-element.15), calls=%async_computation | async-start | bytes 3145728 | tf_op jit(solution)/shard_map/cond/branch_1_fun/all_to_all | solution.py:490
  73.5 9.8 %collective-permute-start.7 = (bf16[16,48,1024]{2,1,0:T(8,128)(2,1)}, bf16[16,48,1024]{2,1,0:T(8,128)(2,1)S(1)}, u32[]{:S(2)}, u32[]{:S(2)}) collective-permute-start(bf16[16,48,1024]{2,1,0:T(8,128)(2,1)} %get-tuple-element.34.arrived.refs_4_), channel_id=1, source_target_pairs={{0,1},{1,0},{2,3},{3,2},{4,5},{5,4},{6,7},{7,6},{8,9},{9,8},{10,11... | collective-permute-start | bytes 4718600 | tf_op jit(solution)/shard_map/ppermute | solution.py:476
  83.2 1.0 copy-start.6
  83.2 8.5 %collective-permute-start.6 = (bf16[768,1024]{1,0:T(8,128)(2,1)S(1)}, bf16[768,1024]{1,0:T(8,128)(2,1)S(1)}, u32[]{:S(2)}, u32[]{:S(2)}) collective-permute-start(bf16[768,1024]{1,0:T(8,128)(2,1)S(1)} %follow.1.low0), channel_id=1, source_target_pairs={{0,1},{1,0},{2,3},{3,2},{4,5},{5,4},{6,7},{7,6},{8,9},{9,8},{10,11... | collective-permute-start | bytes 4718600 | tf_op jit(solution)/shard_map/ppermute | solution.py:476

commit v10 on v9

--- a/solution.py
+++ b/solution.py
@@ -298,19 +298,6 @@
     del rows, after, also_after, out
 
 
-def split_kernel(rows, after, also_after, out, first, third, sems):
-    del after, also_after, out
-    parts = ((first, 0, 2), (third, 2, 1))
-    copies = [
-        pltpu.make_async_copy(rows.at[pl.ds(at * QUARTER, n * QUARTER), :], part, sems.at[i])
-        for i, (part, at, n) in enumerate(parts)
-    ]
-    for copy in copies:
-        copy.start()
-    for copy in copies:
-        copy.wait()
-
-
 def join_kernel(pools, rest, low_rest, high_rest, out):
     width = QUARTER // pools
     for n, part in enumerate((rest, low_rest, high_rest)):
@@ -329,20 +316,16 @@
         out[cls : cls + 1, :] = tiles.result(cls)
 
 
-def middle_kernel(
-    own0, arrived, high01, sib0, meta, codes, near, out, sims, rows, cols
-):
+def middle_kernel(own0, arrived, sib0, meta, codes, near, out, sims, rows, cols):
     width = arrived.shape[1] // 3
     moves = [
-        (OWN, own0, None, 0, 3), (OWN, arrived, 0, 3, 1), (HIGH, high01, None, 0, 2),
-        (HIGH, arrived, 2 * width, 3, 1), (SIB, sib0, None, 0, 3),
+        (OWN, own0, None, 0, 3), (OWN, arrived, 0, 3, 1), (HIGH, arrived, 2 * width, 3, 1),
+        (SIB, sib0, None, 0, 3),
     ]
-    tiles = Tiles(
-        moves, meta, codes, rows, cols, (OWN, SIB), (OWN, HIGH))
+    tiles = Tiles(moves, meta, codes, rows, cols, (OWN, SIB), (OWN, HIGH))
     pieces = [tiles.piece(OWN, 0, 3, OWN, 3), tiles.piece(OWN, 3, 1, OWN, 3, same=0)]
-    for b in (0, 1, 3):
-        pieces += [tiles.piece(OWN, 0, 3, HIGH, b), tiles.piece(OWN, 3, 1, HIGH, b)]
-    pieces += [tiles.piece(SIB, 0, 3, HIGH, b) for b in (0, 1, 3)]
+    pieces += [tiles.piece(OWN, 0, 3, HIGH, 3), tiles.piece(OWN, 3, 1, HIGH, 3)]
+    pieces += [tiles.piece(SIB, 0, 3, HIGH, 3)]
     run(pieces, sims)
     out[...] = near[...]
     for cls in (OWN, SIB, HIGH):
@@ -350,21 +333,20 @@
 
 
 def main_kernel(
-    own0, arrived, high2, sib0, swapped, low0, high01, meta, codes, before, out,
-    sims, rows, cols,
+    own0, arrived, high0, sib0, swapped, low0, meta, codes, before, out, sims, rows, cols
 ):
     width = arrived.shape[1] // 3
     moves = [
-        (HIGH, high2, None, 2, 1), (OWN, own0, None, 0, 3), (OWN, arrived, 0, 3, 1),
-        (SIB, sib0, None, 0, 3), (SIB, swapped, 0, 3, 1), (HIGH, high01, None, 0, 2),
-        (HIGH, arrived, 2 * width, 3, 1), (LOW, low0, None, 0, 3), (LOW, arrived, width, 3, 1),
+        (HIGH, high0, None, 0, 3), (OWN, own0, None, 0, 3), (OWN, arrived, 0, 3, 1),
+        (SIB, sib0, None, 0, 3), (SIB, swapped, 0, 3, 1), (HIGH, arrived, 2 * width, 3, 1),
+        (LOW, low0, None, 0, 3), (LOW, arrived, width, 3, 1),
     ]
-    tiles = Tiles(
-        moves, meta, codes, rows, cols, (OWN, SIB, LOW), (SIB, HIGH)
-    )
-    pieces = [tiles.piece(cls, 0, 3, HIGH, 2) for cls in (OWN, SIB)]
-    pieces += [tiles.piece(OWN, 3, 1, HIGH, 2)]
-    pieces += [tiles.piece(SIB, 3, 1, HIGH, b) for b in range(4)]
+    tiles = Tiles(moves, meta, codes, rows, cols, (OWN, SIB, LOW), (SIB, HIGH))
+    pieces = []
+    for b in range(3):
+        for cls in (OWN, SIB):
+            pieces += [tiles.piece(cls, 0, 3, HIGH, b), tiles.piece(cls, 3, 1, HIGH, b)]
+    pieces += [tiles.piece(SIB, 3, 1, HIGH, 3)]
     run(pieces, sims)
     pairs = [(a, b) for a, b in ALL_PAIRS if 3 in (a, b)]
     either(second_core(), lambda flip: run(tiles.matched(flip, OWN, SIB, pairs), sims))
@@ -374,15 +356,15 @@
 
 
 def last_kernel(
-    pools, group, main, rest, lows0, high01, high2, swapped, arrived, meta, codes, before, out,
+    pools, group, main, rest, lows0, high0, swapped, arrived, meta, codes, before, out,
     sims, rows, cols, every, upper, sem,
 ):
     width = swapped.shape[1] // 3
     copy = pltpu.make_async_copy(arrived.at[:, pl.ds(2 * width, width), :], upper, sem)
     copy.start()
     moves = [
-        (LOWS, lows0, None, 0, 3), (LOWS, swapped, width, 3, 1), (HIGH, high01, None, 0, 2),
-        (HIGH, high2, None, 2, 1), (HIGH, upper, 0, 3, 1),
+        (LOWS, lows0, None, 0, 3), (LOWS, swapped, width, 3, 1), (HIGH, high0, None, 0, 3),
+        (HIGH, upper, 0, 3, 1),
     ]
     tiles = Tiles(
         moves, meta, codes, rows, cols, (LOWS,), (HIGH,))
@@ -505,17 +487,8 @@
         compiler_params=PARAMS,
         name="join",
     )(rest, low_rest, high_rest)
-    own0, own01, own2 = pl.pallas_call(
-        split_kernel,
-        out_shape=tuple(sds((n * QUARTER, feature), BF16) for n in (3, 2, 1)),
-        in_specs=[hbm] * 3,
-        out_specs=(hbm, vmem, vmem),
-        input_output_aliases={0: 0},
-        scratch_shapes=[pltpu.SemaphoreType.DMA((2,))],
-        compiler_params=PARAMS,
-        name="split",
-    )(own0, sent, some.astype(I32).reshape(1, 1))
-    low0, high01, high2 = shift(own0, 2), shift(own01, -2), shift(own2, -2)
+    own0 = follow(own0, sent, some.astype(I32).reshape(1, 1))
+    low0, high0 = shift(own0, 2), shift(own0, -2)
     sib0 = swap(own0)
 
     def tiles(kernel, name, squares, operands, small, out_shape=(8, rows_dev), more=(), specs=None):
@@ -545,24 +518,21 @@
         some, bring, bring_nothing, sent, own0, sib0, meta, codes
     )
     swapped = swap(arrived)
-    middle = tiles(
-        middle_kernel, "middle", 25, (own0, arrived, high01, sib0), (meta, codes, near)
-    )
-    low0 = follow(low0, middle, high2)
+    middle = tiles(middle_kernel, "middle", 11, (own0, arrived, sib0), (meta, codes, near))
+    low0 = follow(low0, middle, high0)
     best = tiles(
-        main_kernel, "main", 23, (own0, arrived, high2, sib0, swapped, low0, high01),
-        (meta, codes, middle),
+        main_kernel, "main", 37, (own0, arrived, high0, sib0, swapped, low0), (meta, codes, middle)
     )
     best = tiles(
         lambda *refs: last_kernel(pools, group, group * (places - last), group * last, *refs),
-        "last", 8, (swap(low0), high01, high2, swapped, arrived), (meta, codes, best),
+        "last", 8, (swap(low0), high0, swapped, arrived), (meta, codes, best),
         out_shape=(devices, group * places),
         more=(
             pltpu.VMEM((group, rows_dev), F32),
             pltpu.VMEM((pools, QUARTER // pools, feature), BF16),
             pltpu.SemaphoreType.DMA,
         ),
-        specs=[vmem] * 4 + [hbm] + [vmem] * 3,
+        specs=[vmem] * 3 + [hbm] + [vmem] * 3,
     )
     returned = lax.all_to_all(best, ("pool", "grp"), split_axis=0, concat_axis=0, tiled=True)
     scores = pl.pallas_call(

time: 112 us -> 109 us (0.973)
  waiting for transfers between devices: 31.5 us -> 35 us
  Pallas kernels: 37.2 us -> 34.6 us
  starting transfers between devices: 25 us -> 23.4 us
    pallas_call x1 -> x0, Pallas kernels: 2.54 us -> none  [body(): pl.pallas_call(split_kernel, out_shape=tuple((sds((n * QUARTER, feature),...]
    ppermute x5 -> x4, starting transfers between devices: 6.7 us -> 5.23 us  [shift(): lax.ppermute(rows, 'grp', [(g, (g + by) % group) for g in range(group)])]
    all_to_all x2, waiting for transfers between devices: 21.8 us -> 23.2 us  [to_pools(): return lax.all_to_all(rows, 'pool', split_axis=0, concat_axis=0, tiled=True)]
    ppermute x5 -> x4, waiting for transfers between devices: 9.73 us -> 10.9 us  [shift(): lax.ppermute(rows, 'grp', [(g, (g + by) % group) for g in range(group)])]
  transfers between devices with their start and end apart: 10 -> 9, of which waited for: 3 -> 5; matrix products, arithmetic and copies ran while one was open for 1% -> 1% of each run, Pallas kernels for 23% -> 23%
where the time goes in v10:
time: 109 us
  waiting for transfers between devices  35 us (32%)
  Pallas kernels  34.6 us (32%)
  starting transfers between devices  23.4 us (21%)
  blocking collectives  13.9 us (13%)
    all_to_all x2, waiting for transfers between devices, to_pools(): return lax.all_to_all(rows, 'pool', split_axis=0, concat_axis=0, tiled=True)  23.2 us
    pallas_call x4, Pallas kernels, tiles(): pl.pallas_call(kernel, out_shape=sds(out_shape, F32), in_specs=specs or [...  21.9 us
    all_to_all x1, blocking collectives, body(): lax.all_to_all(best, ('pool', 'grp'), split_axis=0, concat_axis=0, tiled=...  13.9 us
    all_to_all x2, starting transfers between devices, to_pools(): return lax.all_to_all(rows, 'pool', split_axis=0, concat_axis=0, tiled=True)  13.2 us
    ppermute x4, waiting for transfers between devices, shift(): lax.ppermute(rows, 'grp', [(g, (g + by) % group) for g in range(group)])  10.9 us
    pallas_call x1, Pallas kernels, body(): pl.pallas_call(lambda *refs: meta_kernel(group, places, last, *refs), out...  5.25 us
    ppermute x4, starting transfers between devices, shift(): lax.ppermute(rows, 'grp', [(g, (g + by) % group) for g in range(group)])  5.23 us
    pallas_call x1, Pallas kernels, body(): pl.pallas_call(lambda *refs: table_kernel(pools, group, places, last, *re...  5.16 us
  transfers between devices with their start and end apart: 9, of which 5 were waited for; matrix products, arithmetic and copies ran while one was open for 1% of the time, Pallas kernels for 23%

profile of v10, /device:TPU:1, one launch (start us, length us, event | category | flops | bytes accessed | tf_op | source)
XLA Modules:
  0.0 108.5 jit_solution(16289985196484339839)
XLA Ops:
  0.0 5.2 %table.1 = (s32[128,128]{1,0:T(8,128)}, bf16[768,1024]{1,0:T(8,128)(2,1)}) custom-call(s32[256,512]{1,0:T(8,128)} %refs_0_.3, s32[1,256]{1,0:T(1,128)} %bitcast.13, bf16[1024,1024]{1,0:T(8,128)(2,1)} %refs_1_.1), custom_call_target="tpu_custom_call" | custom-call | flops 2147483648 | tf_op jit(solution)/shard_map/table/pallas_call | solution.py:420
  5.2 0.0 copy-start.2
  5.2 0.0 copy-start.3
  5.2 0.0 copy-start.4
  5.2 8.8 %all-to-all-start.1 = ((bf16[16,48,1024]{2,1,0:T(8,128)(2,1)}), bf16[16,48,1024]{2,1,0:T(8,128)(2,1)}, u32[]{:S(2)}, u32[]{:S(2)}) async-start(bf16[16,48,1024]{2,1,0:T(8,128)(2,1)} %bitcast.15), calls=%async_computation.1 | async-start | bytes 3145728 | tf_op jit(solution)/shard_map/all_to_all | solution.py:472
  14.0 0.0 copy-start
  14.0 5.2 %meta.1 = (s32[2,8,1024]{2,1,0:T(8,128)S(1)}, s32[1024,128]{1,0:T(8,128)}) custom-call(s32[256,512]{1,0:T(8,128)S(1)} %copy-done.2, s32[1,256]{1,0:T(1,128)S(1)} %bitcast.14, s32[1,256]{1,0:T(1,128)S(1)} %bitcast.12), custom_call_target="tpu_custom_call" | custom-call | flops 4294967296 | tf_op jit(solution)/shard_map/meta/pallas_call | solution.py:438
  19.3 0.9 rest.1.refs_0_
  20.2 1.3 %collective-permute-start = (bf16[256,1024]{1,0:T(8,128)(2,1)S(1)}, bf16[256,1024]{1,0:T(8,128)(2,1)S(1)}, u32[]{:S(2)}, u32[]{:S(2)}) collective-permute-start(bf16[256,1024]{1,0:T(8,128)(2,1)S(1)} %rest.1.refs_0_), channel_id=1, source_target_pairs={{0,2},{1,3},{2,4},{3,5},{4,6},{5,7},{6,0},{7,1},{8,10},{9,11},{10,... | collective-permute-start | bytes 1572872 | tf_op jit(solution)/shard_map/ppermute | solution.py:455
  21.5 1.5 %collective-permute-start.1 = (bf16[256,1024]{1,0:T(8,128)(2,1)S(1)}, bf16[256,1024]{1,0:T(8,128)(2,1)S(1)}, u32[]{:S(2)}, u32[]{:S(2)}) collective-permute-start(bf16[256,1024]{1,0:T(8,128)(2,1)S(1)} %rest.1.refs_0_), channel_id=1, source_target_pairs={{0,6},{1,7},{2,0},{3,1},{4,2},{5,3},{6,4},{7,5},{8,14},{9,15},{10,... | collective-permute-start | bytes 1572872 | tf_op jit(solution)/shard_map/ppermute | solution.py:455
  22.9 0.6 compare_reduce_fusion
  24.2 9.7 %collective-permute-done.refs_1_ = bf16[256,1024]{1,0:T(8,128)(2,1)S(1)} collective-permute-done((bf16[256,1024]{1,0:T(8,128)(2,1)S(1)}, bf16[256,1024]{1,0:T(8,128)(2,1)S(1)}, u32[]{:S(2)}, u32[]{:S(2)}) %collective-permute-start) | collective-permute-done | bytes 524320 | tf_op jit(solution)/shard_map/ppermute | solution.py:455
  33.9 0.0 collective-permute-done.1.refs_2_
  33.9 0.1 join.1.after
  34.0 2.9 %all-to-all-done.1 = bf16[16,48,1024]{2,1,0:T(8,128)(2,1)} async-done(((bf16[16,48,1024]{2,1,0:T(8,128)(2,1)}), bf16[16,48,1024]{2,1,0:T(8,128)(2,1)}, u32[]{:S(2)}, u32[]{:S(2)}) %all-to-all-start.1) | async-done | bytes 1572896 | tf_op jit(solution)/shard_map/all_to_all | solution.py:472
  36.9 2.5 %collective-permute-start.3 = (bf16[768,1024]{1,0:T(8,128)(2,1)}, bf16[768,1024]{1,0:T(8,128)(2,1)}, u32[]{:S(2)}, u32[]{:S(2)}) collective-permute-start(bf16[768,1024]{1,0:T(8,128)(2,1)} %follow.2.own0), channel_id=1, source_target_pairs={{0,1},{1,0},{2,3},{3,2},{4,5},{5,4},{6,7},{7,6},{8,9},{9,8},{10,11... | collective-permute-start | bytes 4718600 | tf_op jit(solution)/shard_map/ppermute | solution.py:458
  39.5 2.5 %collective-permute-start.4 = (bf16[768,1024]{1,0:T(8,128)(2,1)}, bf16[768,1024]{1,0:T(8,128)(2,1)S(1)}, u32[]{:S(2)}, u32[]{:S(2)}) collective-permute-start(bf16[768,1024]{1,0:T(8,128)(2,1)} %follow.2.own0), channel_id=1, source_target_pairs={{0,6},{1,7},{2,0},{3,1},{4,2},{5,3},{6,4},{7,5},{8,14},{9,15},{10,... | collective-permute-start | bytes 4718600 | tf_op jit(solution)/shard_map/ppermute | solution.py:455
  41.9 0.0 collective-permute-start.2
  42.0 0.9 collective-permute-done.3.sib0
  42.8 28.9 %conditional.1 = (bf16[16,48,1024]{2,1,0:T(8,128)(2,1)}, f32[8,1024]{1,0:T(8,128)S(1)}) conditional(s32[]{:T(128)} %convert_element_type.4, () %tuple.13, (bf16[16,48,1024]{2,1,0:T(8,128)(2,1)}, bf16[768,1024]{1,0:T(8,128)(2,1)}, bf16[768,1024]{1,0:T(8,128)(2,1)}, s32[2,8,1024]{2,1,0:T(8,128)S(1)}, s32[1024,128]{1,0:T(8,128)}) %tuple.17), branch_computations={%region_1.0_spmd, %region_2.0_spmd} | conditional | flops 1476395008 | bytes 4718640 | solution.py:517
  42.8 4.4 %all-to-all-start = ((bf16[16,48,1024]{2,1,0:T(8,128)(2,1)}), bf16[16,48,1024]{2,1,0:T(8,128)(2,1)}, u32[]{:S(2)}, u32[]{:S(2)}) async-start(bf16[16,48,1024]{2,1,0:T(8,128)(2,1)} %get-tuple-element.15), calls=%async_computation | async-start | bytes 3145728 | tf_op jit(solution)/shard_map/cond/branch_1_fun/all_to_all | solution.py:472
  47.3 4.1 %near.1 = f32[8,1024]{1,0:T(8,128)S(1)} custom-call(bf16[768,1024]{1,0:T(8,128)(2,1)} %get-tuple-element.16.own0, bf16[768,1024]{1,0:T(8,128)(2,1)} %get-tuple-element.17.sib0, s32[2,8,1024]{2,1,0:T(8,128)S(1)} %get-tuple-element.18.meta, s32[1024,128]{1,0:T(8,128)} %get-tuple-element.19.codes), custom_call_target="tpu_custom_call" | custom-call | flops 1476395008 | tf_op jit(solution)/shard_map/cond/branch_1_fun/near/pallas_call | solution.py:495
  51.4 20.3 %all-to-all-done = bf16[16,48,1024]{2,1,0:T(8,128)(2,1)} async-done(((bf16[16,48,1024]{2,1,0:T(8,128)(2,1)}), bf16[16,48,1024]{2,1,0:T(8,128)(2,1)}, u32[]{:S(2)}, u32[]{:S(2)}) %all-to-all-start) | async-done | bytes 1572896 | tf_op jit(solution)/shard_map/cond/branch_1_fun/all_to_all | solution.py:472
  71.7 1.4 %collective-permute-start.6 = (bf16[16,48,1024]{2,1,0:T(8,128)(2,1)}, bf16[16,48,1024]{2,1,0:T(8,128)(2,1)S(1)}, u32[]{:S(2)}, u32[]{:S(2)}) collective-permute-start(bf16[16,48,1024]{2,1,0:T(8,128)(2,1)} %get-tuple-element.30.arrived.refs_3_), channel_id=1, source_target_pairs={{0,1},{1,0},{2,3},{3,2},{4,5},{5,4},{6,7},{7,6},{8,9},{9,8},{10,11... | collective-permute-start | bytes 4718600 | tf_op jit(solution)/shard_map/ppermute | solution.py:458
  73.1 4.7 %middle.1.after.before = f32[8,1024]{1,0:T(8,128)S(1)} custom-call(bf16[768,1024]{1,0:T(8,128)(2,1)} %follow.2.own0, bf16[16,48,1024]{2,1,0:T(8,128)(2,1)} %get-tuple-element.30.arrived.refs_3_, bf16[768,1024]{1,0:T(8,128)(2,1)} %collective-permute-done.3.sib0, s32[2,8,1024]{2,1,0:T(8,128)S(1)} %get-tuple-element.28.refs_2_.meta.refs_4_, ...), custom_call_target="tpu_custom_call" | custom-call | flops 1476395008 | tf_op jit(solution)/shard_map/middle/pallas_call | solution.py:495
  77.9 1.2 %collective-permute-done.2.rows = bf16[768,1024]{1,0:T(8,128)(2,1)S(1)} collective-permute-done((bf16[768,1024]{1,0:T(8,128)(2,1)}, bf16[768,1024]{1,0:T(8,128)(2,1)S(1)}, u32[]{:S(2)}, u32[]{:S(2)}) %collective-permute-start.2) | collective-permute-done | bytes 1572896 | tf_op jit(solution)/shard_map/ppermute | solution.py:455
  79.1 1.1 %collective-permute-start.5 = (bf16[768,1024]{1,0:T(8,128)(2,1)S(1)}, bf16[768,1024]{1,0:T(8,128)(2,1)S(1)}, u32[]{:S(2)}, u32[]{:S(2)}) collective-permute-start(bf16[768,1024]{1,0:T(8,128)(2,1)S(1)} %follow.3.low0), channel_id=1, source_target_pairs={{0,1},{1,0},{2,3},{3,2},{4,5},{5,4},{6,7},{7,6},{8,9},{9,8},{10,11... | collective-permute-start | bytes 4718600 | tf_op jit(solution)/shard_map/ppermute | solution.py:458
  80.2 0.0 collective-permute-done.6.swapped.refs_2_
  80.2 10.0 %main.1.refs_6_ = f32[8,1024]{1,0:T(8,128)S(1)} custom-call(bf16[768,1024]{1,0:T(8,128)(2,1)} %follow.2.own0, bf16[16,48,1024]{2,1,0:T(8,128)(2,1)} %get-tuple-element.30.arrived.refs_3_, bf16[768,1024]{1,0:T(8,128)(2,1)S(1)} %collective-permute-done.4.also_after.high0.refs_1_, bf16[768,1024]{1,0:T(8,128)(2,1)} %collective-permute-done.3.sib0, ...), custom_call_target="tpu_custom_call" | custom-call | flops 4966055936 | tf_op jit(solution)/shard_map/main/pallas_call | solution.py:495
  90.2 3.0 %last.1 = f32[128,64]{1,0:T(8,128)S(1)} custom-call(bf16[768,1024]{1,0:T(8,128)(2,1)S(1)} %collective-permute-done.5.refs_0_, bf16[768,1024]{1,0:T(8,128)(2,1)S(1)} %collective-permute-done.4.also_after.high0.refs_1_, bf16[16,48,1024]{2,1,0:T(8,128)(2,1)S(1)} %collective-permute-done.6.swapped.refs_2_, ...), custom_call_target="tpu_custom_call" | custom-call | flops 1073741824 | tf_op jit(solution)/shard_map/last/pallas_call | solution.py:495
  93.2 13.9 %all_to_all.20 = f32[128,1,64]{2,1,0:T(1,128)S(1)} all-to-all(f32[128,1,64]{2,1,0:T(1,128)S(1)} %bitcast.10), channel_id=1, replica_groups=mesh['pool'=16,'grp'=8] {'pool','grp'}, dimensions={0} | all-to-all | bytes 65536 | tf_op jit(solution)/shard_map/all_to_all | solution.py:537
  107.1 1.4 %score.1 = f32[1,1024]{1,0:T(1,128)} custom-call(s32[128,128]{1,0:T(8,128)S(1)} %copy-done.1, f32[128,64]{1,0:T(8,128)S(1)} %bitcast.11), custom_call_target="tpu_custom_call" | custom-call | tf_op jit(solution)/shard_map/score/pallas_call | solution.py:538
  (14 shorter events, 0.0 us)
Async XLA Ops:
  5.2 8.8 %copy-start.2 = (s32[256,512]{1,0:T(8,128)S(1)}, s32[256,512]{1,0:T(8,128)}, u32[]{:S(2)}) copy-start(s32[256,512]{1,0:T(8,128)} %refs_0_.3) | copy-start | bytes 1572868
  5.2 8.8 %copy-start.3 = (s32[256]{0:T(256)S(1)}, s32[256]{0:T(256)}, u32[]{:S(2)}) copy-start(s32[256]{0:T(256)} %param.9) | copy-start | bytes 3076
  5.2 8.8 %copy-start.4 = (s32[256]{0:T(256)S(1)}, s32[256]{0:T(256)}, u32[]{:S(2)}) copy-start(s32[256]{0:T(256)} %param.8) | copy-start | bytes 3076
  5.2 31.7 %all-to-all-start.1 = ((bf16[16,48,1024]{2,1,0:T(8,128)(2,1)}), bf16[16,48,1024]{2,1,0:T(8,128)(2,1)}, u32[]{:S(2)}, u32[]{:S(2)}) async-start(bf16[16,48,1024]{2,1,0:T(8,128)(2,1)} %bitcast.15), calls=%async_computation.1 | async-start | bytes 3145728 | tf_op jit(solution)/shard_map/all_to_all | solution.py:472
  14.0 5.3 %copy-start = (bf16[1024,1024]{1,0:T(8,128)(2,1)S(1)}, bf16[1024,1024]{1,0:T(8,128)(2,1)}, u32[]{:S(2)}) copy-start(bf16[1024,1024]{1,0:T(8,128)(2,1)} %refs_1_.1) | copy-start | bytes 6291460
  14.0 5.3 %copy-start.1 = (s32[128,128]{1,0:T(8,128)S(1)}, s32[128,128]{1,0:T(8,128)}, u32[]{:S(2)}) copy-start(s32[128,128]{1,0:T(8,128)} %get-tuple-element.26.refs_0_) | copy-start | bytes 196612
  20.2 13.7 %collective-permute-start = (bf16[256,1024]{1,0:T(8,128)(2,1)S(1)}, bf16[256,1024]{1,0:T(8,128)(2,1)S(1)}, u32[]{:S(2)}, u32[]{:S(2)}) collective-permute-start(bf16[256,1024]{1,0:T(8,128)(2,1)S(1)} %rest.1.refs_0_), channel_id=1, source_target_pairs={{0,2},{1,3},{2,4},{3,5},{4,6},{5,7},{6,0},{7,1},{8,10},{9,11},{10,... | collective-permute-start | bytes 1572872 | tf_op jit(solution)/shard_map/ppermute | solution.py:455
  21.5 12.5 %collective-permute-start.1 = (bf16[256,1024]{1,0:T(8,128)(2,1)S(1)}, bf16[256,1024]{1,0:T(8,128)(2,1)S(1)}, u32[]{:S(2)}, u32[]{:S(2)}) collective-permute-start(bf16[256,1024]{1,0:T(8,128)(2,1)S(1)} %rest.1.refs_0_), channel_id=1, source_target_pairs={{0,6},{1,7},{2,0},{3,1},{4,2},{5,3},{6,4},{7,5},{8,14},{9,15},{10,... | collective-permute-start | bytes 1572872 | tf_op jit(solution)/shard_map/ppermute | solution.py:455
  34.0 2.9 %copy-start.5 = (bf16[16,48,1024]{2,1,0:T(8,128)(2,1)}, bf16[16,48,1024]{2,1,0:T(8,128)(2,1)S(1)}, u32[]{:S(2)}) copy-start(bf16[16,48,1024]{2,1,0:T(8,128)(2,1)S(1)} %join.1.after) | copy-start | bytes 4718596
  36.9 5.9 %collective-permute-start.3 = (bf16[768,1024]{1,0:T(8,128)(2,1)}, bf16[768,1024]{1,0:T(8,128)(2,1)}, u32[]{:S(2)}, u32[]{:S(2)}) collective-permute-start(bf16[768,1024]{1,0:T(8,128)(2,1)} %follow.2.own0), channel_id=1, source_target_pairs={{0,1},{1,0},{2,3},{3,2},{4,5},{5,4},{6,7},{7,6},{8,9},{9,8},{10,11... | collective-permute-start | bytes 4718600 | tf_op jit(solution)/shard_map/ppermute | solution.py:458
  39.5 38.4 %collective-permute-start.4 = (bf16[768,1024]{1,0:T(8,128)(2,1)}, bf16[768,1024]{1,0:T(8,128)(2,1)S(1)}, u32[]{:S(2)}, u32[]{:S(2)}) collective-permute-start(bf16[768,1024]{1,0:T(8,128)(2,1)} %follow.2.own0), channel_id=1, source_target_pairs={{0,6},{1,7},{2,0},{3,1},{4,2},{5,3},{6,4},{7,5},{8,14},{9,15},{10,... | collective-permute-start | bytes 4718600 | tf_op jit(solution)/shard_map/ppermute | solution.py:455
  41.9 37.1 %collective-permute-start.2 = (bf16[768,1024]{1,0:T(8,128)(2,1)}, bf16[768,1024]{1,0:T(8,128)(2,1)S(1)}, u32[]{:S(2)}, u32[]{:S(2)}) collective-permute-start(bf16[768,1024]{1,0:T(8,128)(2,1)} %follow.2.own0), channel_id=1, source_target_pairs={{0,2},{1,3},{2,4},{3,5},{4,6},{5,7},{6,0},{7,1},{8,10},{9,11},{10,... | collective-permute-start | bytes 4718600 | tf_op jit(solution)/shard_map/ppermute | solution.py:455
  42.8 28.9 %all-to-all-start = ((bf16[16,48,1024]{2,1,0:T(8,128)(2,1)}), bf16[16,48,1024]{2,1,0:T(8,128)(2,1)}, u32[]{:S(2)}, u32[]{:S(2)}) async-start(bf16[16,48,1024]{2,1,0:T(8,128)(2,1)} %get-tuple-element.15), calls=%async_computation | async-start | bytes 3145728 | tf_op jit(solution)/shard_map/cond/branch_1_fun/all_to_all | solution.py:472
  71.7 8.5 %collective-permute-start.6 = (bf16[16,48,1024]{2,1,0:T(8,128)(2,1)}, bf16[16,48,1024]{2,1,0:T(8,128)(2,1)S(1)}, u32[]{:S(2)}, u32[]{:S(2)}) collective-permute-start(bf16[16,48,1024]{2,1,0:T(8,128)(2,1)} %get-tuple-element.30.arrived.refs_3_), channel_id=1, source_target_pairs={{0,1},{1,0},{2,3},{3,2},{4,5},{5,4},{6,7},{7,6},{8,9},{9,8},{10,11... | collective-permute-start | bytes 4718600 | tf_op jit(solution)/shard_map/ppermute | solution.py:458
  77.9 2.3 %copy-start.6 = (s32[1024,128]{1,0:T(8,128)S(1)}, s32[1024,128]{1,0:T(8,128)}, u32[]{:S(2)}) copy-start(s32[1024,128]{1,0:T(8,128)} %get-tuple-element.29.codes.refs_5_) | copy-start | bytes 1572868
  79.1 11.1 %collective-permute-start.5 = (bf16[768,1024]{1,0:T(8,128)(2,1)S(1)}, bf16[768,1024]{1,0:T(8,128)(2,1)S(1)}, u32[]{:S(2)}, u32[]{:S(2)}) collective-permute-start(bf16[768,1024]{1,0:T(8,128)(2,1)S(1)} %follow.3.low0), channel_id=1, source_target_pairs={{0,1},{1,0},{2,3},{3,2},{4,5},{5,4},{6,7},{7,6},{8,9},{9,8},{10,11... | collective-permute-start | bytes 4718600 | tf_op jit(solution)/shard_map/ppermute | solution.py:458

commit v11 on v10

--- a/solution.py
+++ b/solution.py
@@ -316,7 +316,9 @@
         out[cls : cls + 1, :] = tiles.result(cls)
 
 
-def middle_kernel(own0, arrived, sib0, meta, codes, near, out, sims, rows, cols):
+def middle_kernel(
+    own0, arrived, sib0, meta, codes, near, out, own_out, arrived_out, sib_out, sims, rows, cols
+):
     width = arrived.shape[1] // 3
     moves = [
         (OWN, own0, None, 0, 3), (OWN, arrived, 0, 3, 1), (HIGH, arrived, 2 * width, 3, 1),
@@ -327,6 +329,9 @@
     pieces += [tiles.piece(OWN, 0, 3, HIGH, 3), tiles.piece(OWN, 3, 1, HIGH, 3)]
     pieces += [tiles.piece(SIB, 0, 3, HIGH, 3)]
     run(pieces, sims)
+    own_out[...] = own0[...]
+    arrived_out[...] = arrived[...]
+    sib_out[...] = sib0[...]
     out[...] = near[...]
     for cls in (OWN, SIB, HIGH):
         out[cls : cls + 1, :] = jnp.maximum(near[cls : cls + 1, :], tiles.result(cls))
@@ -491,10 +496,10 @@
     low0, high0 = shift(own0, 2), shift(own0, -2)
     sib0 = swap(own0)
 
-    def tiles(kernel, name, squares, operands, small, out_shape=(8, rows_dev), more=(), specs=None):
+    def tiles(kernel, name, squares, operands, small, out_shape=(8, rows_dev), more=(), specs=None, kept=()):
         return pl.pallas_call(
             kernel,
-            out_shape=sds(out_shape, F32),
+            out_shape=(sds(out_shape, F32), *kept) if kept else sds(out_shape, F32),
             in_specs=specs or [vmem] * (len(operands) + len(small)),
             scratch_shapes=[
                 pltpu.VMEM((2, 3 * QUARTER, QUARTER), F32),
@@ -518,7 +523,10 @@
         some, bring, bring_nothing, sent, own0, sib0, meta, codes
     )
     swapped = swap(arrived)
-    middle = tiles(middle_kernel, "middle", 11, (own0, arrived, sib0), (meta, codes, near))
+    middle, own0, arrived, sib0 = tiles(
+        middle_kernel, "middle", 11, (own0, arrived, sib0), (meta, codes, near),
+        kept=[sds(kept.shape, BF16) for kept in (own0, arrived, sib0)],
+    )
     low0 = follow(low0, middle, high0)
     best = tiles(
         main_kernel, "main", 37, (own0, arrived, high0, sib0, swapped, low0), (meta, codes, middle)

time: 109 us -> 106 us (0.972)
  Pallas kernels: 34.6 us -> 31.8 us
    pallas_call x4, Pallas kernels: 21.9 us -> 19 us  [tiles(): pl.pallas_call(kernel, out_shape=(sds(out_shape, F32), *kept) if kept els...]
  transfers between devices with their start and end apart: 9 -> 9, of which waited for: 5 -> 5; matrix products, arithmetic and copies ran while one was open for 1% -> 1% of each run, Pallas kernels for 23% -> 22%
where the time goes in v11:
time: 106 us
  waiting for transfers between devices  34.9 us (33%)
  Pallas kernels  31.8 us (30%)
  starting transfers between devices  23.3 us (22%)
  blocking collectives  14.2 us (13%)
    all_to_all x2, waiting for transfers between devices, to_pools(): return lax.all_to_all(rows, 'pool', split_axis=0, concat_axis=0, tiled=True)  23.9 us
    pallas_call x4, Pallas kernels, tiles(): pl.pallas_call(kernel, out_shape=(sds(out_shape, F32), *kept) if kept els...  19 us
    all_to_all x1, blocking collectives, body(): lax.all_to_all(best, ('pool', 'grp'), split_axis=0, concat_axis=0, tiled=...  14.2 us
    all_to_all x2, starting transfers between devices, to_pools(): return lax.all_to_all(rows, 'pool', split_axis=0, concat_axis=0, tiled=True)  13.2 us
    ppermute x4, waiting for transfers between devices, shift(): lax.ppermute(rows, 'grp', [(g, (g + by) % group) for g in range(group)])  10.2 us
    pallas_call x1, Pallas kernels, body(): pl.pallas_call(lambda *refs: meta_kernel(group, places, last, *refs), out...  5.24 us
    ppermute x4, starting transfers between devices, shift(): lax.ppermute(rows, 'grp', [(g, (g + by) % group) for g in range(group)])  5.23 us
    pallas_call x1, Pallas kernels, body(): pl.pallas_call(lambda *refs: table_kernel(pools, group, places, last, *re...  5.16 us
  transfers between devices with their start and end apart: 9, of which 5 were waited for; matrix products, arithmetic and copies ran while one was open for 1% of the time, Pallas kernels for 22%

profile of v11, /device:TPU:1, one launch (start us, length us, event | category | flops | bytes accessed | tf_op | source)
XLA Modules:
  0.0 105.7 jit_solution(7779930627776694132)
XLA Ops:
  0.0 5.2 %table.1 = (s32[128,128]{1,0:T(8,128)}, bf16[768,1024]{1,0:T(8,128)(2,1)}) custom-call(s32[256,512]{1,0:T(8,128)} %refs_0_.3, s32[1,256]{1,0:T(1,128)} %bitcast.13, bf16[1024,1024]{1,0:T(8,128)(2,1)} %refs_1_.1), custom_call_target="tpu_custom_call" | custom-call | flops 2147483648 | tf_op jit(solution)/shard_map/table/pallas_call | solution.py:425
  5.2 0.0 copy-start.2
  5.2 0.0 copy-start.3
  5.2 0.0 copy-start.4
  5.2 8.8 %all-to-all-start.1 = ((bf16[16,48,1024]{2,1,0:T(8,128)(2,1)}), bf16[16,48,1024]{2,1,0:T(8,128)(2,1)}, u32[]{:S(2)}, u32[]{:S(2)}) async-start(bf16[16,48,1024]{2,1,0:T(8,128)(2,1)} %bitcast.15), calls=%async_computation.1 | async-start | bytes 3145728 | tf_op jit(solution)/shard_map/all_to_all | solution.py:477
  14.0 0.0 copy-start
  14.0 5.2 %meta.1 = (s32[2,8,1024]{2,1,0:T(8,128)S(1)}, s32[1024,128]{1,0:T(8,128)}) custom-call(s32[256,512]{1,0:T(8,128)S(1)} %copy-done.2, s32[1,256]{1,0:T(1,128)S(1)} %bitcast.14, s32[1,256]{1,0:T(1,128)S(1)} %bitcast.12), custom_call_target="tpu_custom_call" | custom-call | flops 4294967296 | tf_op jit(solution)/shard_map/meta/pallas_call | solution.py:443
  19.3 0.9 rest.1.refs_0_
  20.2 1.3 %collective-permute-start = (bf16[256,1024]{1,0:T(8,128)(2,1)S(1)}, bf16[256,1024]{1,0:T(8,128)(2,1)S(1)}, u32[]{:S(2)}, u32[]{:S(2)}) collective-permute-start(bf16[256,1024]{1,0:T(8,128)(2,1)S(1)} %rest.1.refs_0_), channel_id=1, source_target_pairs={{0,2},{1,3},{2,4},{3,5},{4,6},{5,7},{6,0},{7,1},{8,10},{9,11},{10,... | collective-permute-start | bytes 1572872 | tf_op jit(solution)/shard_map/ppermute | solution.py:460
  21.5 1.5 %collective-permute-start.1 = (bf16[256,1024]{1,0:T(8,128)(2,1)S(1)}, bf16[256,1024]{1,0:T(8,128)(2,1)S(1)}, u32[]{:S(2)}, u32[]{:S(2)}) collective-permute-start(bf16[256,1024]{1,0:T(8,128)(2,1)S(1)} %rest.1.refs_0_), channel_id=1, source_target_pairs={{0,6},{1,7},{2,0},{3,1},{4,2},{5,3},{6,4},{7,5},{8,14},{9,15},{10,... | collective-permute-start | bytes 1572872 | tf_op jit(solution)/shard_map/ppermute | solution.py:460
  22.9 0.6 compare_reduce_fusion
  24.2 9.7 %collective-permute-done.refs_1_ = bf16[256,1024]{1,0:T(8,128)(2,1)S(1)} collective-permute-done((bf16[256,1024]{1,0:T(8,128)(2,1)S(1)}, bf16[256,1024]{1,0:T(8,128)(2,1)S(1)}, u32[]{:S(2)}, u32[]{:S(2)}) %collective-permute-start) | collective-permute-done | bytes 524320 | tf_op jit(solution)/shard_map/ppermute | solution.py:460
  33.9 0.0 collective-permute-done.1.refs_2_
  33.9 0.1 join.1.after
  34.1 2.9 %all-to-all-done.1 = bf16[16,48,1024]{2,1,0:T(8,128)(2,1)} async-done(((bf16[16,48,1024]{2,1,0:T(8,128)(2,1)}), bf16[16,48,1024]{2,1,0:T(8,128)(2,1)}, u32[]{:S(2)}, u32[]{:S(2)}) %all-to-all-start.1) | async-done | bytes 1572896 | tf_op jit(solution)/shard_map/all_to_all | solution.py:477
  36.9 2.5 %collective-permute-start.3 = (bf16[768,1024]{1,0:T(8,128)(2,1)}, bf16[768,1024]{1,0:T(8,128)(2,1)}, u32[]{:S(2)}, u32[]{:S(2)}) collective-permute-start(bf16[768,1024]{1,0:T(8,128)(2,1)} %follow.2.own0), channel_id=1, source_target_pairs={{0,1},{1,0},{2,3},{3,2},{4,5},{5,4},{6,7},{7,6},{8,9},{9,8},{10,11... | collective-permute-start | bytes 4718600 | tf_op jit(solution)/shard_map/ppermute | solution.py:463
  39.5 2.5 %collective-permute-start.4 = (bf16[768,1024]{1,0:T(8,128)(2,1)}, bf16[768,1024]{1,0:T(8,128)(2,1)S(1)}, u32[]{:S(2)}, u32[]{:S(2)}) collective-permute-start(bf16[768,1024]{1,0:T(8,128)(2,1)} %follow.2.own0), channel_id=1, source_target_pairs={{0,6},{1,7},{2,0},{3,1},{4,2},{5,3},{6,4},{7,5},{8,14},{9,15},{10,... | collective-permute-start | bytes 4718600 | tf_op jit(solution)/shard_map/ppermute | solution.py:460
  42.0 0.9 collective-permute-done.3.sib0
  42.9 29.6 %conditional.1 = (bf16[16,48,1024]{2,1,0:T(8,128)(2,1)}, f32[8,1024]{1,0:T(8,128)S(1)}) conditional(s32[]{:T(128)} %convert_element_type.4, () %tuple.13, (bf16[16,48,1024]{2,1,0:T(8,128)(2,1)}, bf16[768,1024]{1,0:T(8,128)(2,1)}, bf16[768,1024]{1,0:T(8,128)(2,1)}, s32[2,8,1024]{2,1,0:T(8,128)S(1)}, s32[1024,128]{1,0:T(8,128)}) %tuple.17), branch_computations={%region_1.0_spmd, %region_2.0_spmd} | conditional | flops 1476395008 | bytes 4718640 | solution.py:522
  42.9 4.4 %all-to-all-start = ((bf16[16,48,1024]{2,1,0:T(8,128)(2,1)}), bf16[16,48,1024]{2,1,0:T(8,128)(2,1)}, u32[]{:S(2)}, u32[]{:S(2)}) async-start(bf16[16,48,1024]{2,1,0:T(8,128)(2,1)} %get-tuple-element.15), calls=%async_computation | async-start | bytes 3145728 | tf_op jit(solution)/shard_map/cond/branch_1_fun/all_to_all | solution.py:477
  47.3 4.1 %near.1 = f32[8,1024]{1,0:T(8,128)S(1)} custom-call(bf16[768,1024]{1,0:T(8,128)(2,1)} %get-tuple-element.16.own0, bf16[768,1024]{1,0:T(8,128)(2,1)} %get-tuple-element.17.sib0, s32[2,8,1024]{2,1,0:T(8,128)S(1)} %get-tuple-element.18.meta, s32[1024,128]{1,0:T(8,128)} %get-tuple-element.19.codes), custom_call_target="tpu_custom_call" | custom-call | flops 1476395008 | tf_op jit(solution)/shard_map/cond/branch_1_fun/near/pallas_call | solution.py:500
  51.4 21.0 %all-to-all-done = bf16[16,48,1024]{2,1,0:T(8,128)(2,1)} async-done(((bf16[16,48,1024]{2,1,0:T(8,128)(2,1)}), bf16[16,48,1024]{2,1,0:T(8,128)(2,1)}, u32[]{:S(2)}, u32[]{:S(2)}) %all-to-all-start) | async-done | bytes 1572896 | tf_op jit(solution)/shard_map/cond/branch_1_fun/all_to_all | solution.py:477
  72.4 1.2 %collective-permute-start.6 = (bf16[16,48,1024]{2,1,0:T(8,128)(2,1)}, bf16[16,48,1024]{2,1,0:T(8,128)(2,1)S(1)}, u32[]{:S(2)}, u32[]{:S(2)}) collective-permute-start(bf16[16,48,1024]{2,1,0:T(8,128)(2,1)} %get-tuple-element.34.arrived), channel_id=1, source_target_pairs={{0,1},{1,0},{2,3},{3,2},{4,5},{5,4},{6,7},{7,6},{8,9},{9,8},{10,11... | collective-permute-start | bytes 4718600 | tf_op jit(solution)/shard_map/ppermute | solution.py:463
  73.6 5.0 %middle.1 = (f32[8,1024]{1,0:T(8,128)S(1)}, bf16[768,1024]{1,0:T(8,128)(2,1)S(1)}, bf16[16,48,1024]{2,1,0:T(8,128)(2,1)S(1)}, bf16[768,1024]{1,0:T(8,128)(2,1)S(1)}) custom-call(bf16[768,1024]{1,0:T(8,128)(2,1)} %follow.2.own0, bf16[16,48,1024]{2,1,0:T(8,128)(2,1)} %get-tuple-element.34.arrived, bf16[768,1024]{1,0:T(8,128)(2,1)} %collective-permute-done.3.sib0, ...), custom_call_target="tpu_custom_call" | custom-call | flops 1476395008 | tf_op jit(solution)/shard_map/middle/pallas_call | solution.py:500
  78.6 0.0 collective-permute-done.4.also_after.high0.refs_1_
  78.7 0.4 collective-permute-done.2.rows
  79.1 1.1 %collective-permute-start.5 = (bf16[768,1024]{1,0:T(8,128)(2,1)S(1)}, bf16[768,1024]{1,0:T(8,128)(2,1)S(1)}, u32[]{:S(2)}, u32[]{:S(2)}) collective-permute-start(bf16[768,1024]{1,0:T(8,128)(2,1)S(1)} %follow.3.low0), channel_id=1, source_target_pairs={{0,1},{1,0},{2,3},{3,2},{4,5},{5,4},{6,7},{7,6},{8,9},{9,8},{10,11... | collective-permute-start | bytes 4718600 | tf_op jit(solution)/shard_map/ppermute | solution.py:463
  80.2 7.6 %main.1.refs_6_ = f32[8,1024]{1,0:T(8,128)S(1)} custom-call(bf16[768,1024]{1,0:T(8,128)(2,1)S(1)} %get-tuple-element.38.own0, bf16[16,48,1024]{2,1,0:T(8,128)(2,1)S(1)} %get-tuple-element.37.arrived.refs_3_, bf16[768,1024]{1,0:T(8,128)(2,1)S(1)} %collective-permute-done.4.also_after.high0.refs_1_, bf16[768,1024]{1,0:T(8,128)(2,1)S(1)} %get-tuple-element.39.sib0, ...), custom_call_target="tpu_custom_call" | custom-call | flops 4966055936 | tf_op jit(solution)/shard_map/main/pallas_call | solution.py:500
  87.8 0.0 collective-permute-done.5.refs_0_
  87.8 2.3 %last.1 = f32[128,64]{1,0:T(8,128)S(1)} custom-call(bf16[768,1024]{1,0:T(8,128)(2,1)S(1)} %collective-permute-done.5.refs_0_, bf16[768,1024]{1,0:T(8,128)(2,1)S(1)} %collective-permute-done.4.also_after.high0.refs_1_, bf16[16,48,1024]{2,1,0:T(8,128)(2,1)S(1)} %collective-permute-done.6.swapped.refs_2_, ...), custom_call_target="tpu_custom_call" | custom-call | flops 1073741824 | tf_op jit(solution)/shard_map/last/pallas_call | solution.py:500
  90.1 14.2 %all_to_all.20 = f32[128,1,64]{2,1,0:T(1,128)S(1)} all-to-all(f32[128,1,64]{2,1,0:T(1,128)S(1)} %bitcast.10), channel_id=1, replica_groups=mesh['pool'=16,'grp'=8] {'pool','grp'}, dimensions={0} | all-to-all | bytes 65536 | tf_op jit(solution)/shard_map/all_to_all | solution.py:545
  104.3 1.4 %score.1 = f32[1,1024]{1,0:T(1,128)} custom-call(s32[128,128]{1,0:T(8,128)S(1)} %copy-done.1, f32[128,64]{1,0:T(8,128)S(1)} %bitcast.11), custom_call_target="tpu_custom_call" | custom-call | tf_op jit(solution)/shard_map/score/pallas_call | solution.py:546
  (14 shorter events, 0.0 us)
Async XLA Ops:
  5.2 8.8 %copy-start.2 = (s32[256,512]{1,0:T(8,128)S(1)}, s32[256,512]{1,0:T(8,128)}, u32[]{:S(2)}) copy-start(s32[256,512]{1,0:T(8,128)} %refs_0_.3) | copy-start | bytes 1572868
  5.2 8.8 %copy-start.3 = (s32[256]{0:T(256)S(1)}, s32[256]{0:T(256)}, u32[]{:S(2)}) copy-start(s32[256]{0:T(256)} %param.9) | copy-start | bytes 3076
  5.2 8.8 %copy-start.4 = (s32[256]{0:T(256)S(1)}, s32[256]{0:T(256)}, u32[]{:S(2)}) copy-start(s32[256]{0:T(256)} %param.8) | copy-start | bytes 3076
  5.2 31.7 %all-to-all-start.1 = ((bf16[16,48,1024]{2,1,0:T(8,128)(2,1)}), bf16[16,48,1024]{2,1,0:T(8,128)(2,1)}, u32[]{:S(2)}, u32[]{:S(2)}) async-start(bf16[16,48,1024]{2,1,0:T(8,128)(2,1)} %bitcast.15), calls=%async_computation.1 | async-start | bytes 3145728 | tf_op jit(solution)/shard_map/all_to_all | solution.py:477
  14.0 5.3 %copy-start = (bf16[1024,1024]{1,0:T(8,128)(2,1)S(1)}, bf16[1024,1024]{1,0:T(8,128)(2,1)}, u32[]{:S(2)}) copy-start(bf16[1024,1024]{1,0:T(8,128)(2,1)} %refs_1_.1) | copy-start | bytes 6291460
  14.0 5.3 %copy-start.1 = (s32[128,128]{1,0:T(8,128)S(1)}, s32[128,128]{1,0:T(8,128)}, u32[]{:S(2)}) copy-start(s32[128,128]{1,0:T(8,128)} %get-tuple-element.30.refs_0_) | copy-start | bytes 196612
  20.2 13.7 %collective-permute-start = (bf16[256,1024]{1,0:T(8,128)(2,1)S(1)}, bf16[256,1024]{1,0:T(8,128)(2,1)S(1)}, u32[]{:S(2)}, u32[]{:S(2)}) collective-permute-start(bf16[256,1024]{1,0:T(8,128)(2,1)S(1)} %rest.1.refs_0_), channel_id=1, source_target_pairs={{0,2},{1,3},{2,4},{3,5},{4,6},{5,7},{6,0},{7,1},{8,10},{9,11},{10,... | collective-permute-start | bytes 1572872 | tf_op jit(solution)/shard_map/ppermute | solution.py:460
  21.5 12.5 %collective-permute-start.1 = (bf16[256,1024]{1,0:T(8,128)(2,1)S(1)}, bf16[256,1024]{1,0:T(8,128)(2,1)S(1)}, u32[]{:S(2)}, u32[]{:S(2)}) collective-permute-start(bf16[256,1024]{1,0:T(8,128)(2,1)S(1)} %rest.1.refs_0_), channel_id=1, source_target_pairs={{0,6},{1,7},{2,0},{3,1},{4,2},{5,3},{6,4},{7,5},{8,14},{9,15},{10,... | collective-permute-start | bytes 1572872 | tf_op jit(solution)/shard_map/ppermute | solution.py:460
  34.0 5.4 %copy-start.5 = (bf16[16,48,1024]{2,1,0:T(8,128)(2,1)}, bf16[16,48,1024]{2,1,0:T(8,128)(2,1)S(1)}, u32[]{:S(2)}) copy-start(bf16[16,48,1024]{2,1,0:T(8,128)(2,1)S(1)} %join.1.after) | copy-start | bytes 4718596
  36.9 5.9 %collective-permute-start.3 = (bf16[768,1024]{1,0:T(8,128)(2,1)}, bf16[768,1024]{1,0:T(8,128)(2,1)}, u32[]{:S(2)}, u32[]{:S(2)}) collective-permute-start(bf16[768,1024]{1,0:T(8,128)(2,1)} %follow.2.own0), channel_id=1, source_target_pairs={{0,1},{1,0},{2,3},{3,2},{4,5},{5,4},{6,7},{7,6},{8,9},{9,8},{10,11... | collective-permute-start | bytes 4718600 | tf_op jit(solution)/shard_map/ppermute | solution.py:463
  39.5 39.2 %collective-permute-start.4 = (bf16[768,1024]{1,0:T(8,128)(2,1)}, bf16[768,1024]{1,0:T(8,128)(2,1)S(1)}, u32[]{:S(2)}, u32[]{:S(2)}) collective-permute-start(bf16[768,1024]{1,0:T(8,128)(2,1)} %follow.2.own0), channel_id=1, source_target_pairs={{0,6},{1,7},{2,0},{3,1},{4,2},{5,3},{6,4},{7,5},{8,14},{9,15},{10,... | collective-permute-start | bytes 4718600 | tf_op jit(solution)/shard_map/ppermute | solution.py:460
  42.0 37.1 %collective-permute-start.2 = (bf16[768,1024]{1,0:T(8,128)(2,1)}, bf16[768,1024]{1,0:T(8,128)(2,1)S(1)}, u32[]{:S(2)}, u32[]{:S(2)}) collective-permute-start(bf16[768,1024]{1,0:T(8,128)(2,1)} %follow.2.own0), channel_id=1, source_target_pairs={{0,2},{1,3},{2,4},{3,5},{4,6},{5,7},{6,0},{7,1},{8,10},{9,11},{10,... | collective-permute-start | bytes 4718600 | tf_op jit(solution)/shard_map/ppermute | solution.py:460
  42.9 29.6 %all-to-all-start = ((bf16[16,48,1024]{2,1,0:T(8,128)(2,1)}), bf16[16,48,1024]{2,1,0:T(8,128)(2,1)}, u32[]{:S(2)}, u32[]{:S(2)}) async-start(bf16[16,48,1024]{2,1,0:T(8,128)(2,1)} %get-tuple-element.15), calls=%async_computation | async-start | bytes 3145728 | tf_op jit(solution)/shard_map/cond/branch_1_fun/all_to_all | solution.py:477
  72.4 7.8 %collective-permute-start.6 = (bf16[16,48,1024]{2,1,0:T(8,128)(2,1)}, bf16[16,48,1024]{2,1,0:T(8,128)(2,1)S(1)}, u32[]{:S(2)}, u32[]{:S(2)}) collective-permute-start(bf16[16,48,1024]{2,1,0:T(8,128)(2,1)} %get-tuple-element.34.arrived), channel_id=1, source_target_pairs={{0,1},{1,0},{2,3},{3,2},{4,5},{5,4},{6,7},{7,6},{8,9},{9,8},{10,11... | collective-permute-start | bytes 4718600 | tf_op jit(solution)/shard_map/ppermute | solution.py:463
  79.1 1.1 %copy-start.6 = (s32[1024,128]{1,0:T(8,128)S(1)}, s32[1024,128]{1,0:T(8,128)}, u32[]{:S(2)}) copy-start(s32[1024,128]{1,0:T(8,128)} %get-tuple-element.33.codes.refs_5_) | copy-start | bytes 1572868
  79.1 8.7 %collective-permute-start.5 = (bf16[768,1024]{1,0:T(8,128)(2,1)S(1)}, bf16[768,1024]{1,0:T(8,128)(2,1)S(1)}, u32[]{:S(2)}, u32[]{:S(2)}) collective-permute-start(bf16[768,1024]{1,0:T(8,128)(2,1)S(1)} %follow.3.low0), channel_id=1, source_target_pairs={{0,1},{1,0},{2,3},{3,2},{4,5},{5,4},{6,7},{7,6},{8,9},{9,8},{10,11... | collective-permute-start | bytes 4718600 | tf_op jit(solution)/shard_map/ppermute | solution.py:463

commit v12 on v11

--- a/solution.py
+++ b/solution.py
@@ -75,7 +75,10 @@
     table = pair.astype(I32) - 1
     table_ref[...] = table
     copies[2].wait()
-    main_ref[...] = picked_rows(table, emb_ref[...], 0, places - last, pools)
+    for first in range(0, places - last, last):
+        part = picked_rows(table, emb_ref[...], first, last, pools)
+        part = part.reshape(pools, last * group, -1)
+        main_ref[:, first * group : (first + last) * group, :] = part
 
 
 def rest_kernel(pools, places, last, table_ref, emb_ref, after, out):
@@ -317,7 +320,8 @@
 
 
 def middle_kernel(
-    own0, arrived, sib0, meta, codes, near, out, own_out, arrived_out, sib_out, sims, rows, cols
+    own0, arrived, sib0, meta, codes, near, out, own_out, arrived_out, sib_out, codes_out,
+    sims, rows, cols
 ):
     width = arrived.shape[1] // 3
     moves = [
@@ -332,6 +336,7 @@
     own_out[...] = own0[...]
     arrived_out[...] = arrived[...]
     sib_out[...] = sib0[...]
+    codes_out[...] = codes[...]
     out[...] = near[...]
     for cls in (OWN, SIB, HIGH):
         out[cls : cls + 1, :] = jnp.maximum(near[cls : cls + 1, :], tiles.result(cls))
@@ -426,7 +431,7 @@
         lambda *refs: table_kernel(pools, group, places, last, *refs),
         out_shape=(
             sds((devices, 128), I32),
-            sds((3 * QUARTER, feature), BF16),
+            sds((pools, 3 * QUARTER // pools, feature), BF16),
         ),
         in_specs=[hbm] * 3,
         scratch_shapes=[
@@ -485,7 +490,7 @@
         name="rest",
     )(table, embeddings, meta)
     low_rest, high_rest = shift(rest, 2), shift(rest, -2)
-    own0 = to_pools(main.reshape(pools, -1, feature)).reshape(-1, feature)
+    own0 = to_pools(main).reshape(-1, feature)
     sent = pl.pallas_call(
         lambda *refs: join_kernel(pools, *refs),
         out_shape=sds((pools, 3 * QUARTER // pools, feature), BF16),
@@ -523,9 +528,9 @@
         some, bring, bring_nothing, sent, own0, sib0, meta, codes
     )
     swapped = swap(arrived)
-    middle, own0, arrived, sib0 = tiles(
+    middle, own0, arrived, sib0, codes = tiles(
         middle_kernel, "middle", 11, (own0, arrived, sib0), (meta, codes, near),
-        kept=[sds(kept.shape, BF16) for kept in (own0, arrived, sib0)],
+        kept=[sds(kept.shape, kept.dtype) for kept in (own0, arrived, sib0, codes)],
     )
     low0 = follow(low0, middle, high0)
     best = tiles(

time: 106 us -> 105 us (level)
  no operation moved by 1% of the time
where the time goes in v12:
time: 105 us
  waiting for transfers between devices  34.9 us (33%)
  Pallas kernels  31.8 us (30%)
  starting transfers between devices  23.3 us (22%)
  blocking collectives  13.6 us (13%)
    all_to_all x2, waiting for transfers between devices, to_pools(): return lax.all_to_all(rows, 'pool', split_axis=0, concat_axis=0, tiled=True)  23.9 us
    pallas_call x4, Pallas kernels, tiles(): pl.pallas_call(kernel, out_shape=(sds(out_shape, F32), *kept) if kept els...  19.1 us
    all_to_all x1, blocking collectives, body(): lax.all_to_all(best, ('pool', 'grp'), split_axis=0, concat_axis=0, tiled=...  13.6 us
    all_to_all x2, starting transfers between devices, to_pools(): return lax.all_to_all(rows, 'pool', split_axis=0, concat_axis=0, tiled=True)  13.2 us
    ppermute x4, waiting for transfers between devices, shift(): lax.ppermute(rows, 'grp', [(g, (g + by) % group) for g in range(group)])  10.1 us
    pallas_call x1, Pallas kernels, body(): pl.pallas_call(lambda *refs: meta_kernel(group, places, last, *refs), out...  5.25 us
    ppermute x4, starting transfers between devices, shift(): lax.ppermute(rows, 'grp', [(g, (g + by) % group) for g in range(group)])  5.23 us
    pallas_call x1, Pallas kernels, body(): pl.pallas_call(lambda *refs: table_kernel(pools, group, places, last, *re...  5.14 us
  transfers between devices with their start and end apart: 9, of which 5 were waited for; matrix products, arithmetic and copies ran while one was open for 1% of the time, Pallas kernels for 22%

profile of v12, /device:TPU:1, one launch (start us, length us, event | category | flops | bytes accessed | tf_op | source)
XLA Modules:
  0.0 105.0 jit_solution(3776020799688117230)
XLA Ops:
  0.0 5.1 %table.1 = (s32[128,128]{1,0:T(8,128)}, bf16[16,48,1024]{2,1,0:T(8,128)(2,1)}) custom-call(s32[256,512]{1,0:T(8,128)} %refs_0_.3, s32[1,256]{1,0:T(1,128)} %bitcast.12, bf16[1024,1024]{1,0:T(8,128)(2,1)} %refs_1_.1), custom_call_target="tpu_custom_call" | custom-call | flops 2147483648 | tf_op jit(solution)/shard_map/table/pallas_call | solution.py:430
  5.2 0.0 copy-start.2
  5.2 0.0 copy-start.3
  5.2 0.0 copy-start.4
  5.2 8.8 %all-to-all-start.1 = ((bf16[16,48,1024]{2,1,0:T(8,128)(2,1)}), bf16[16,48,1024]{2,1,0:T(8,128)(2,1)}, u32[]{:S(2)}, u32[]{:S(2)}) async-start(bf16[16,48,1024]{2,1,0:T(8,128)(2,1)} %get-tuple-element.32), calls=%async_computation.1 | async-start | bytes 3145728 | tf_op jit(solution)/shard_map/all_to_all | solution.py:482
  14.0 0.0 copy-start
  14.0 5.2 %meta.1 = (s32[2,8,1024]{2,1,0:T(8,128)S(1)}, s32[1024,128]{1,0:T(8,128)}) custom-call(s32[256,512]{1,0:T(8,128)S(1)} %copy-done.2, s32[1,256]{1,0:T(1,128)S(1)} %bitcast.13, s32[1,256]{1,0:T(1,128)S(1)} %bitcast.11), custom_call_target="tpu_custom_call" | custom-call | flops 4294967296 | tf_op jit(solution)/shard_map/meta/pallas_call | solution.py:448
  19.3 0.9 rest.1.refs_0_
  20.2 1.3 %collective-permute-start = (bf16[256,1024]{1,0:T(8,128)(2,1)S(1)}, bf16[256,1024]{1,0:T(8,128)(2,1)S(1)}, u32[]{:S(2)}, u32[]{:S(2)}) collective-permute-start(bf16[256,1024]{1,0:T(8,128)(2,1)S(1)} %rest.1.refs_0_), channel_id=1, source_target_pairs={{0,2},{1,3},{2,4},{3,5},{4,6},{5,7},{6,0},{7,1},{8,10},{9,11},{10,... | collective-permute-start | bytes 1572872 | tf_op jit(solution)/shard_map/ppermute | solution.py:465
  21.4 1.5 %collective-permute-start.1 = (bf16[256,1024]{1,0:T(8,128)(2,1)S(1)}, bf16[256,1024]{1,0:T(8,128)(2,1)S(1)}, u32[]{:S(2)}, u32[]{:S(2)}) collective-permute-start(bf16[256,1024]{1,0:T(8,128)(2,1)S(1)} %rest.1.refs_0_), channel_id=1, source_target_pairs={{0,6},{1,7},{2,0},{3,1},{4,2},{5,3},{6,4},{7,5},{8,14},{9,15},{10,... | collective-permute-start | bytes 1572872 | tf_op jit(solution)/shard_map/ppermute | solution.py:465
  22.9 0.6 compare_reduce_fusion
  24.2 9.7 %collective-permute-done.refs_1_ = bf16[256,1024]{1,0:T(8,128)(2,1)S(1)} collective-permute-done((bf16[256,1024]{1,0:T(8,128)(2,1)S(1)}, bf16[256,1024]{1,0:T(8,128)(2,1)S(1)}, u32[]{:S(2)}, u32[]{:S(2)}) %collective-permute-start) | collective-permute-done | bytes 524320 | tf_op jit(solution)/shard_map/ppermute | solution.py:465
  33.9 0.1 join.1.after
  34.0 2.9 %all-to-all-done.1 = bf16[16,48,1024]{2,1,0:T(8,128)(2,1)} async-done(((bf16[16,48,1024]{2,1,0:T(8,128)(2,1)}), bf16[16,48,1024]{2,1,0:T(8,128)(2,1)}, u32[]{:S(2)}, u32[]{:S(2)}) %all-to-all-start.1) | async-done | bytes 1572896 | tf_op jit(solution)/shard_map/all_to_all | solution.py:482
  36.9 2.6 %collective-permute-start.3 = (bf16[768,1024]{1,0:T(8,128)(2,1)}, bf16[768,1024]{1,0:T(8,128)(2,1)}, u32[]{:S(2)}, u32[]{:S(2)}) collective-permute-start(bf16[768,1024]{1,0:T(8,128)(2,1)} %follow.2.own0), channel_id=1, source_target_pairs={{0,1},{1,0},{2,3},{3,2},{4,5},{5,4},{6,7},{7,6},{8,9},{9,8},{10,11... | collective-permute-start | bytes 4718600 | tf_op jit(solution)/shard_map/ppermute | solution.py:468
  39.5 2.5 %collective-permute-start.4 = (bf16[768,1024]{1,0:T(8,128)(2,1)}, bf16[768,1024]{1,0:T(8,128)(2,1)S(1)}, u32[]{:S(2)}, u32[]{:S(2)}) collective-permute-start(bf16[768,1024]{1,0:T(8,128)(2,1)} %follow.2.own0), channel_id=1, source_target_pairs={{0,6},{1,7},{2,0},{3,1},{4,2},{5,3},{6,4},{7,5},{8,14},{9,15},{10,... | collective-permute-start | bytes 4718600 | tf_op jit(solution)/shard_map/ppermute | solution.py:465
  41.9 0.0 collective-permute-start.2
  41.9 0.9 collective-permute-done.3.sib0
  42.8 29.5 %conditional.1 = (bf16[16,48,1024]{2,1,0:T(8,128)(2,1)}, f32[8,1024]{1,0:T(8,128)S(1)}) conditional(s32[]{:T(128)} %convert_element_type.4, () %tuple.13, (bf16[16,48,1024]{2,1,0:T(8,128)(2,1)}, bf16[768,1024]{1,0:T(8,128)(2,1)}, bf16[768,1024]{1,0:T(8,128)(2,1)}, s32[2,8,1024]{2,1,0:T(8,128)S(1)}, s32[1024,128]{1,0:T(8,128)}) %tuple.17), branch_computations={%region_1.0_spmd, %region_2.0_spmd} | conditional | flops 1476395008 | bytes 4718640 | solution.py:527
  42.8 4.4 %all-to-all-start = ((bf16[16,48,1024]{2,1,0:T(8,128)(2,1)}), bf16[16,48,1024]{2,1,0:T(8,128)(2,1)}, u32[]{:S(2)}, u32[]{:S(2)}) async-start(bf16[16,48,1024]{2,1,0:T(8,128)(2,1)} %get-tuple-element.15), calls=%async_computation | async-start | bytes 3145728 | tf_op jit(solution)/shard_map/cond/branch_1_fun/all_to_all | solution.py:482
  47.2 4.1 %near.1 = f32[8,1024]{1,0:T(8,128)S(1)} custom-call(bf16[768,1024]{1,0:T(8,128)(2,1)} %get-tuple-element.16.own0, bf16[768,1024]{1,0:T(8,128)(2,1)} %get-tuple-element.17.sib0, s32[2,8,1024]{2,1,0:T(8,128)S(1)} %get-tuple-element.18.meta, s32[1024,128]{1,0:T(8,128)} %get-tuple-element.19.codes), custom_call_target="tpu_custom_call" | custom-call | flops 1476395008 | tf_op jit(solution)/shard_map/cond/branch_1_fun/near/pallas_call | solution.py:505
  51.4 21.0 %all-to-all-done = bf16[16,48,1024]{2,1,0:T(8,128)(2,1)} async-done(((bf16[16,48,1024]{2,1,0:T(8,128)(2,1)}), bf16[16,48,1024]{2,1,0:T(8,128)(2,1)}, u32[]{:S(2)}, u32[]{:S(2)}) %all-to-all-start) | async-done | bytes 1572896 | tf_op jit(solution)/shard_map/cond/branch_1_fun/all_to_all | solution.py:482
  72.4 1.2 %collective-permute-start.6 = (bf16[16,48,1024]{2,1,0:T(8,128)(2,1)}, bf16[16,48,1024]{2,1,0:T(8,128)(2,1)S(1)}, u32[]{:S(2)}, u32[]{:S(2)}) collective-permute-start(bf16[16,48,1024]{2,1,0:T(8,128)(2,1)} %get-tuple-element.35.arrived), channel_id=1, source_target_pairs={{0,1},{1,0},{2,3},{3,2},{4,5},{5,4},{6,7},{7,6},{8,9},{9,8},{10,11... | collective-permute-start | bytes 4718600 | tf_op jit(solution)/shard_map/ppermute | solution.py:468
  73.6 5.1 %middle.1 = (f32[8,1024]{1,0:T(8,128)S(1)}, bf16[768,1024]{1,0:T(8,128)(2,1)S(1)}, bf16[16,48,1024]{2,1,0:T(8,128)(2,1)S(1)}, bf16[768,1024]{1,0:T(8,128)(2,1)S(1)}, s32[1024,128]{1,0:T(8,128)S(1)}) custom-call(bf16[768,1024]{1,0:T(8,128)(2,1)} %follow.2.own0, bf16[16,48,1024]{2,1,0:T(8,128)(2,1)} %get-tuple-element.35.arrived, ...), custom_call_target="tpu_custom_call" | custom-call | flops 1476395008 | tf_op jit(solution)/shard_map/middle/pallas_call | solution.py:505
  78.7 0.4 collective-permute-done.2.rows
  79.1 1.1 %collective-permute-start.5 = (bf16[768,1024]{1,0:T(8,128)(2,1)S(1)}, bf16[768,1024]{1,0:T(8,128)(2,1)S(1)}, u32[]{:S(2)}, u32[]{:S(2)}) collective-permute-start(bf16[768,1024]{1,0:T(8,128)(2,1)S(1)} %follow.3.low0), channel_id=1, source_target_pairs={{0,1},{1,0},{2,3},{3,2},{4,5},{5,4},{6,7},{7,6},{8,9},{9,8},{10,11... | collective-permute-start | bytes 4718600 | tf_op jit(solution)/shard_map/ppermute | solution.py:468
  80.2 0.0 collective-permute-done.6.swapped.refs_2_
  80.2 7.6 %main.1.refs_6_ = f32[8,1024]{1,0:T(8,128)S(1)} custom-call(bf16[768,1024]{1,0:T(8,128)(2,1)S(1)} %get-tuple-element.40.own0, bf16[16,48,1024]{2,1,0:T(8,128)(2,1)S(1)} %get-tuple-element.38.arrived.refs_3_, bf16[768,1024]{1,0:T(8,128)(2,1)S(1)} %collective-permute-done.4.also_after.high0.refs_1_, bf16[768,1024]{1,0:T(8,128)(2,1)S(1)} %get-tuple-element.41.sib0, ...), custom_call_target="tpu_custom_call" | custom-call | flops 4966055936 | tf_op jit(solution)/shard_map/main/pallas_call | solution.py:505
  87.8 0.0 collective-permute-done.5.refs_0_
  87.8 2.3 %last.1 = f32[128,64]{1,0:T(8,128)S(1)} custom-call(bf16[768,1024]{1,0:T(8,128)(2,1)S(1)} %collective-permute-done.5.refs_0_, bf16[768,1024]{1,0:T(8,128)(2,1)S(1)} %collective-permute-done.4.also_after.high0.refs_1_, bf16[16,48,1024]{2,1,0:T(8,128)(2,1)S(1)} %collective-permute-done.6.swapped.refs_2_, ...), custom_call_target="tpu_custom_call" | custom-call | flops 1073741824 | tf_op jit(solution)/shard_map/last/pallas_call | solution.py:505
  90.1 13.6 %all_to_all.20 = f32[128,1,64]{2,1,0:T(1,128)S(1)} all-to-all(f32[128,1,64]{2,1,0:T(1,128)S(1)} %bitcast.9), channel_id=1, replica_groups=mesh['pool'=16,'grp'=8] {'pool','grp'}, dimensions={0} | all-to-all | bytes 65536 | tf_op jit(solution)/shard_map/all_to_all | solution.py:550
  103.6 1.4 %score.1 = f32[1,1024]{1,0:T(1,128)} custom-call(s32[128,128]{1,0:T(8,128)S(1)} %copy-done.1, f32[128,64]{1,0:T(8,128)S(1)} %bitcast.10), custom_call_target="tpu_custom_call" | custom-call | tf_op jit(solution)/shard_map/score/pallas_call | solution.py:551
  (12 shorter events, 0.0 us)
Async XLA Ops:
  5.2 8.8 %copy-start.2 = (s32[256,512]{1,0:T(8,128)S(1)}, s32[256,512]{1,0:T(8,128)}, u32[]{:S(2)}) copy-start(s32[256,512]{1,0:T(8,128)} %refs_0_.3) | copy-start | bytes 1572868
  5.2 8.8 %copy-start.3 = (s32[256]{0:T(256)S(1)}, s32[256]{0:T(256)}, u32[]{:S(2)}) copy-start(s32[256]{0:T(256)} %param.9) | copy-start | bytes 3076
  5.2 8.8 %copy-start.4 = (s32[256]{0:T(256)S(1)}, s32[256]{0:T(256)}, u32[]{:S(2)}) copy-start(s32[256]{0:T(256)} %param.8) | copy-start | bytes 3076
  5.2 31.7 %all-to-all-start.1 = ((bf16[16,48,1024]{2,1,0:T(8,128)(2,1)}), bf16[16,48,1024]{2,1,0:T(8,128)(2,1)}, u32[]{:S(2)}, u32[]{:S(2)}) async-start(bf16[16,48,1024]{2,1,0:T(8,128)(2,1)} %get-tuple-element.32), calls=%async_computation.1 | async-start | bytes 3145728 | tf_op jit(solution)/shard_map/all_to_all | solution.py:482
  14.0 5.3 %copy-start = (bf16[1024,1024]{1,0:T(8,128)(2,1)S(1)}, bf16[1024,1024]{1,0:T(8,128)(2,1)}, u32[]{:S(2)}) copy-start(bf16[1024,1024]{1,0:T(8,128)(2,1)} %refs_1_.1) | copy-start | bytes 6291460
  14.0 5.3 %copy-start.1 = (s32[128,128]{1,0:T(8,128)S(1)}, s32[128,128]{1,0:T(8,128)}, u32[]{:S(2)}) copy-start(s32[128,128]{1,0:T(8,128)} %get-tuple-element.31.refs_0_) | copy-start | bytes 196612
  20.2 13.7 %collective-permute-start = (bf16[256,1024]{1,0:T(8,128)(2,1)S(1)}, bf16[256,1024]{1,0:T(8,128)(2,1)S(1)}, u32[]{:S(2)}, u32[]{:S(2)}) collective-permute-start(bf16[256,1024]{1,0:T(8,128)(2,1)S(1)} %rest.1.refs_0_), channel_id=1, source_target_pairs={{0,2},{1,3},{2,4},{3,5},{4,6},{5,7},{6,0},{7,1},{8,10},{9,11},{10,... | collective-permute-start | bytes 1572872 | tf_op jit(solution)/shard_map/ppermute | solution.py:465
  21.4 12.5 %collective-permute-start.1 = (bf16[256,1024]{1,0:T(8,128)(2,1)S(1)}, bf16[256,1024]{1,0:T(8,128)(2,1)S(1)}, u32[]{:S(2)}, u32[]{:S(2)}) collective-permute-start(bf16[256,1024]{1,0:T(8,128)(2,1)S(1)} %rest.1.refs_0_), channel_id=1, source_target_pairs={{0,6},{1,7},{2,0},{3,1},{4,2},{5,3},{6,4},{7,5},{8,14},{9,15},{10,... | collective-permute-start | bytes 1572872 | tf_op jit(solution)/shard_map/ppermute | solution.py:465
  34.0 5.4 %copy-start.5 = (bf16[16,48,1024]{2,1,0:T(8,128)(2,1)}, bf16[16,48,1024]{2,1,0:T(8,128)(2,1)S(1)}, u32[]{:S(2)}) copy-start(bf16[16,48,1024]{2,1,0:T(8,128)(2,1)S(1)} %join.1.after) | copy-start | bytes 4718596
  36.9 5.9 %collective-permute-start.3 = (bf16[768,1024]{1,0:T(8,128)(2,1)}, bf16[768,1024]{1,0:T(8,128)(2,1)}, u32[]{:S(2)}, u32[]{:S(2)}) collective-permute-start(bf16[768,1024]{1,0:T(8,128)(2,1)} %follow.2.own0), channel_id=1, source_target_pairs={{0,1},{1,0},{2,3},{3,2},{4,5},{5,4},{6,7},{7,6},{8,9},{9,8},{10,11... | collective-permute-start | bytes 4718600 | tf_op jit(solution)/shard_map/ppermute | solution.py:468
  39.5 39.2 %collective-permute-start.4 = (bf16[768,1024]{1,0:T(8,128)(2,1)}, bf16[768,1024]{1,0:T(8,128)(2,1)S(1)}, u32[]{:S(2)}, u32[]{:S(2)}) collective-permute-start(bf16[768,1024]{1,0:T(8,128)(2,1)} %follow.2.own0), channel_id=1, source_target_pairs={{0,6},{1,7},{2,0},{3,1},{4,2},{5,3},{6,4},{7,5},{8,14},{9,15},{10,... | collective-permute-start | bytes 4718600 | tf_op jit(solution)/shard_map/ppermute | solution.py:465
  41.9 37.1 %collective-permute-start.2 = (bf16[768,1024]{1,0:T(8,128)(2,1)}, bf16[768,1024]{1,0:T(8,128)(2,1)S(1)}, u32[]{:S(2)}, u32[]{:S(2)}) collective-permute-start(bf16[768,1024]{1,0:T(8,128)(2,1)} %follow.2.own0), channel_id=1, source_target_pairs={{0,2},{1,3},{2,4},{3,5},{4,6},{5,7},{6,0},{7,1},{8,10},{9,11},{10,... | collective-permute-start | bytes 4718600 | tf_op jit(solution)/shard_map/ppermute | solution.py:465
  42.8 29.5 %all-to-all-start = ((bf16[16,48,1024]{2,1,0:T(8,128)(2,1)}), bf16[16,48,1024]{2,1,0:T(8,128)(2,1)}, u32[]{:S(2)}, u32[]{:S(2)}) async-start(bf16[16,48,1024]{2,1,0:T(8,128)(2,1)} %get-tuple-element.15), calls=%async_computation | async-start | bytes 3145728 | tf_op jit(solution)/shard_map/cond/branch_1_fun/all_to_all | solution.py:482
  72.4 7.8 %collective-permute-start.6 = (bf16[16,48,1024]{2,1,0:T(8,128)(2,1)}, bf16[16,48,1024]{2,1,0:T(8,128)(2,1)S(1)}, u32[]{:S(2)}, u32[]{:S(2)}) collective-permute-start(bf16[16,48,1024]{2,1,0:T(8,128)(2,1)} %get-tuple-element.35.arrived), channel_id=1, source_target_pairs={{0,1},{1,0},{2,3},{3,2},{4,5},{5,4},{6,7},{7,6},{8,9},{9,8},{10,11... | collective-permute-start | bytes 4718600 | tf_op jit(solution)/shard_map/ppermute | solution.py:468
  79.1 8.7 %collective-permute-start.5 = (bf16[768,1024]{1,0:T(8,128)(2,1)S(1)}, bf16[768,1024]{1,0:T(8,128)(2,1)S(1)}, u32[]{:S(2)}, u32[]{:S(2)}) collective-permute-start(bf16[768,1024]{1,0:T(8,128)(2,1)S(1)} %follow.3.low0), channel_id=1, source_target_pairs={{0,1},{1,0},{2,3},{3,2},{4,5},{5,4},{6,7},{7,6},{8,9},{9,8},{10,11... | collective-permute-start | bytes 4718600 | tf_op jit(solution)/shard_map/ppermute | solution.py:468

commit v13 on v12

--- a/solution.py
+++ b/solution.py
@@ -81,8 +81,7 @@
         main_ref[:, first * group : (first + last) * group, :] = part
 
 
-def rest_kernel(pools, places, last, table_ref, emb_ref, after, out):
-    del after
+def rest_kernel(pools, places, last, table_ref, emb_ref, out):
     out[...] = picked_rows(table_ref[...], emb_ref[...], places - last, last, pools)
 
 
@@ -301,7 +300,8 @@
     del rows, after, also_after, out
 
 
-def join_kernel(pools, rest, low_rest, high_rest, out):
+def join_kernel(pools, rest, low_rest, high_rest, after, out):
+    del after
     width = QUARTER // pools
     for n, part in enumerate((rest, low_rest, high_rest)):
         out[:, n * width : (n + 1) * width, :] = part[...].reshape(pools, width, -1)
@@ -485,18 +485,18 @@
     rest = pl.pallas_call(
         lambda *refs: rest_kernel(pools, places, last, *refs),
         out_shape=sds((QUARTER, feature), BF16),
-        in_specs=[vmem, vmem, hbm],
         compiler_params=PARAMS,
         name="rest",
-    )(table, embeddings, meta)
+    )(table, embeddings)
     low_rest, high_rest = shift(rest, 2), shift(rest, -2)
     own0 = to_pools(main).reshape(-1, feature)
     sent = pl.pallas_call(
         lambda *refs: join_kernel(pools, *refs),
         out_shape=sds((pools, 3 * QUARTER // pools, feature), BF16),
+        in_specs=[vmem] * 3 + [hbm],
         compiler_params=PARAMS,
         name="join",
-    )(rest, low_rest, high_rest)
+    )(rest, low_rest, high_rest, meta)
     own0 = follow(own0, sent, some.astype(I32).reshape(1, 1))
     low0, high0 = shift(own0, 2), shift(own0, -2)
     sib0 = swap(own0)

time: 105 us -> 105 us (level)
  Pallas kernels: 31.8 us -> 33 us
  waiting for transfers between devices: 34.9 us -> 33.7 us
    ppermute x4, waiting for transfers between devices: 10.1 us -> 4.95 us  [shift(): lax.ppermute(rows, 'grp', [(g, (g + by) % group) for g in range(group)])]
    all_to_all x2, waiting for transfers between devices: 23.9 us -> 27.9 us  [to_pools(): return lax.all_to_all(rows, 'pool', split_axis=0, concat_axis=0, tiled=True)]
    pallas_call x1, Pallas kernels: 0.1 us -> 1.27 us  [body(): pl.pallas_call(lambda *refs: join_kernel(pools, *refs), out_shape=sds((po...]
  transfers between devices with their start and end apart: 9 -> 9, of which waited for: 5 -> 5; matrix products, arithmetic and copies ran while one was open for 1% -> 1% of each run, Pallas kernels for 22% -> 23%
where the time goes in v13:
time: 105 us
  waiting for transfers between devices  33.7 us (32%)
  Pallas kernels  33 us (31%)
  starting transfers between devices  23.3 us (22%)
  blocking collectives  13.6 us (13%)
    all_to_all x2, waiting for transfers between devices, to_pools(): return lax.all_to_all(rows, 'pool', split_axis=0, concat_axis=0, tiled=True)  27.9 us
    pallas_call x4, Pallas kernels, tiles(): pl.pallas_call(kernel, out_shape=(sds(out_shape, F32), *kept) if kept els...  19.1 us
    all_to_all x1, blocking collectives, body(): lax.all_to_all(best, ('pool', 'grp'), split_axis=0, concat_axis=0, tiled=...  13.6 us
    all_to_all x2, starting transfers between devices, to_pools(): return lax.all_to_all(rows, 'pool', split_axis=0, concat_axis=0, tiled=True)  13.2 us
    pallas_call x1, Pallas kernels, body(): pl.pallas_call(lambda *refs: meta_kernel(group, places, last, *refs), out...  5.25 us
    ppermute x4, starting transfers between devices, shift(): lax.ppermute(rows, 'grp', [(g, (g + by) % group) for g in range(group)])  5.23 us
    pallas_call x1, Pallas kernels, body(): pl.pallas_call(lambda *refs: table_kernel(pools, group, places, last, *re...  5.15 us
    ppermute x4, waiting for transfers between devices, shift(): lax.ppermute(rows, 'grp', [(g, (g + by) % group) for g in range(group)])  4.95 us
  transfers between devices with their start and end apart: 9, of which 5 were waited for; matrix products, arithmetic and copies ran while one was open for 1% of the time, Pallas kernels for 23%

profile of v13, /device:TPU:1, one launch (start us, length us, event | category | flops | bytes accessed | tf_op | source)
XLA Modules:
  0.0 105.0 jit_solution(6480835916731767482)
XLA Ops:
  0.0 5.1 %table.1 = (s32[128,128]{1,0:T(8,128)}, bf16[16,48,1024]{2,1,0:T(8,128)(2,1)}) custom-call(s32[256,512]{1,0:T(8,128)} %refs_0_.3, s32[1,256]{1,0:T(1,128)} %bitcast.11, bf16[1024,1024]{1,0:T(8,128)(2,1)} %refs_1_.1), custom_call_target="tpu_custom_call" | custom-call | flops 2147483648 | tf_op jit(solution)/shard_map/table/pallas_call | solution.py:430
  5.2 0.0 copy-start
  5.2 8.8 %all-to-all-start.1 = ((bf16[16,48,1024]{2,1,0:T(8,128)(2,1)}), bf16[16,48,1024]{2,1,0:T(8,128)(2,1)}, u32[]{:S(2)}, u32[]{:S(2)}) async-start(bf16[16,48,1024]{2,1,0:T(8,128)(2,1)} %get-tuple-element.32), calls=%async_computation.1 | async-start | bytes 3145728 | tf_op jit(solution)/shard_map/all_to_all | solution.py:482
  14.0 0.0 copy-start.3
  14.0 0.0 copy-start.2
  14.0 0.0 copy-start.4
  14.0 0.9 rest.1.refs_0_
  14.9 1.3 %collective-permute-start = (bf16[256,1024]{1,0:T(8,128)(2,1)S(1)}, bf16[256,1024]{1,0:T(8,128)(2,1)S(1)}, u32[]{:S(2)}, u32[]{:S(2)}) collective-permute-start(bf16[256,1024]{1,0:T(8,128)(2,1)S(1)} %rest.1.refs_0_), channel_id=1, source_target_pairs={{0,2},{1,3},{2,4},{3,5},{4,6},{5,7},{6,0},{7,1},{8,10},{9,11},{10,... | collective-permute-start | bytes 1572872 | tf_op jit(solution)/shard_map/ppermute | solution.py:465
  16.2 1.5 %collective-permute-start.1 = (bf16[256,1024]{1,0:T(8,128)(2,1)S(1)}, bf16[256,1024]{1,0:T(8,128)(2,1)S(1)}, u32[]{:S(2)}, u32[]{:S(2)}) collective-permute-start(bf16[256,1024]{1,0:T(8,128)(2,1)S(1)} %rest.1.refs_0_), channel_id=1, source_target_pairs={{0,6},{1,7},{2,0},{3,1},{4,2},{5,3},{6,4},{7,5},{8,14},{9,15},{10,... | collective-permute-start | bytes 1572872 | tf_op jit(solution)/shard_map/ppermute | solution.py:465
  17.6 0.6 compare_reduce_fusion
  18.9 5.2 %meta.1 = (s32[2,8,1024]{2,1,0:T(8,128)S(1)}, s32[1024,128]{1,0:T(8,128)}) custom-call(s32[256,512]{1,0:T(8,128)S(1)} %copy-done.2, s32[1,256]{1,0:T(1,128)S(1)} %bitcast.12, s32[1,256]{1,0:T(1,128)S(1)} %bitcast.13), custom_call_target="tpu_custom_call" | custom-call | flops 4294967296 | tf_op jit(solution)/shard_map/meta/pallas_call | solution.py:448
  24.2 4.5 %collective-permute-done.refs_1_ = bf16[256,1024]{1,0:T(8,128)(2,1)S(1)} collective-permute-done((bf16[256,1024]{1,0:T(8,128)(2,1)S(1)}, bf16[256,1024]{1,0:T(8,128)(2,1)S(1)}, u32[]{:S(2)}, u32[]{:S(2)}) %collective-permute-start) | collective-permute-done | bytes 524320 | tf_op jit(solution)/shard_map/ppermute | solution.py:465
  28.7 0.0 collective-permute-done.1.refs_2_
  28.7 1.3 %join.1.after = bf16[16,48,1024]{2,1,0:T(8,128)(2,1)} custom-call(bf16[256,1024]{1,0:T(8,128)(2,1)S(1)} %rest.1.refs_0_, bf16[256,1024]{1,0:T(8,128)(2,1)S(1)} %collective-permute-done.refs_1_, bf16[256,1024]{1,0:T(8,128)(2,1)S(1)} %collective-permute-done.1.refs_2_, s32[2,8,1024]{2,1,0:T(8,128)S(1)} %get-tuple-element.33.refs_3_.meta.refs_4_), custom_call_target="tpu_custom_call" | custom-call | tf_op jit(solution)/shard_map/join/pallas_call | solution.py:493
  30.0 6.9 %all-to-all-done.1 = bf16[16,48,1024]{2,1,0:T(8,128)(2,1)} async-done(((bf16[16,48,1024]{2,1,0:T(8,128)(2,1)}), bf16[16,48,1024]{2,1,0:T(8,128)(2,1)}, u32[]{:S(2)}, u32[]{:S(2)}) %all-to-all-start.1) | async-done | bytes 1572896 | tf_op jit(solution)/shard_map/all_to_all | solution.py:482
  36.9 2.6 %collective-permute-start.3 = (bf16[768,1024]{1,0:T(8,128)(2,1)}, bf16[768,1024]{1,0:T(8,128)(2,1)}, u32[]{:S(2)}, u32[]{:S(2)}) collective-permute-start(bf16[768,1024]{1,0:T(8,128)(2,1)} %follow.2.own0), channel_id=1, source_target_pairs={{0,1},{1,0},{2,3},{3,2},{4,5},{5,4},{6,7},{7,6},{8,9},{9,8},{10,11... | collective-permute-start | bytes 4718600 | tf_op jit(solution)/shard_map/ppermute | solution.py:468
  39.4 2.5 %collective-permute-start.4 = (bf16[768,1024]{1,0:T(8,128)(2,1)}, bf16[768,1024]{1,0:T(8,128)(2,1)S(1)}, u32[]{:S(2)}, u32[]{:S(2)}) collective-permute-start(bf16[768,1024]{1,0:T(8,128)(2,1)} %follow.2.own0), channel_id=1, source_target_pairs={{0,6},{1,7},{2,0},{3,1},{4,2},{5,3},{6,4},{7,5},{8,14},{9,15},{10,... | collective-permute-start | bytes 4718600 | tf_op jit(solution)/shard_map/ppermute | solution.py:465
  41.9 0.0 collective-permute-start.2
  41.9 0.9 collective-permute-done.3.sib0
  42.8 29.5 %conditional.1 = (bf16[16,48,1024]{2,1,0:T(8,128)(2,1)}, f32[8,1024]{1,0:T(8,128)S(1)}) conditional(s32[]{:T(128)} %convert_element_type.4, () %tuple.13, (bf16[16,48,1024]{2,1,0:T(8,128)(2,1)}, bf16[768,1024]{1,0:T(8,128)(2,1)}, bf16[768,1024]{1,0:T(8,128)(2,1)}, s32[2,8,1024]{2,1,0:T(8,128)S(1)}, s32[1024,128]{1,0:T(8,128)}) %tuple.14), branch_computations={%region_1.0_spmd, %region_2.0_spmd} | conditional | flops 1476395008 | bytes 4718640 | solution.py:527
  42.8 4.4 %all-to-all-start = ((bf16[16,48,1024]{2,1,0:T(8,128)(2,1)}), bf16[16,48,1024]{2,1,0:T(8,128)(2,1)}, u32[]{:S(2)}, u32[]{:S(2)}) async-start(bf16[16,48,1024]{2,1,0:T(8,128)(2,1)} %get-tuple-element.15), calls=%async_computation | async-start | bytes 3145728 | tf_op jit(solution)/shard_map/cond/branch_1_fun/all_to_all | solution.py:482
  47.2 4.1 %near.1 = f32[8,1024]{1,0:T(8,128)S(1)} custom-call(bf16[768,1024]{1,0:T(8,128)(2,1)} %get-tuple-element.16.own0, bf16[768,1024]{1,0:T(8,128)(2,1)} %get-tuple-element.17.sib0, s32[2,8,1024]{2,1,0:T(8,128)S(1)} %get-tuple-element.18.meta, s32[1024,128]{1,0:T(8,128)} %get-tuple-element.19.codes), custom_call_target="tpu_custom_call" | custom-call | flops 1476395008 | tf_op jit(solution)/shard_map/cond/branch_1_fun/near/pallas_call | solution.py:505
  51.4 21.0 %all-to-all-done = bf16[16,48,1024]{2,1,0:T(8,128)(2,1)} async-done(((bf16[16,48,1024]{2,1,0:T(8,128)(2,1)}), bf16[16,48,1024]{2,1,0:T(8,128)(2,1)}, u32[]{:S(2)}, u32[]{:S(2)}) %all-to-all-start) | async-done | bytes 1572896 | tf_op jit(solution)/shard_map/cond/branch_1_fun/all_to_all | solution.py:482
  72.4 1.2 %collective-permute-start.6 = (bf16[16,48,1024]{2,1,0:T(8,128)(2,1)}, bf16[16,48,1024]{2,1,0:T(8,128)(2,1)S(1)}, u32[]{:S(2)}, u32[]{:S(2)}) collective-permute-start(bf16[16,48,1024]{2,1,0:T(8,128)(2,1)} %get-tuple-element.35.arrived), channel_id=1, source_target_pairs={{0,1},{1,0},{2,3},{3,2},{4,5},{5,4},{6,7},{7,6},{8,9},{9,8},{10,11... | collective-permute-start | bytes 4718600 | tf_op jit(solution)/shard_map/ppermute | solution.py:468
  73.6 5.1 %middle.1 = (f32[8,1024]{1,0:T(8,128)S(1)}, bf16[768,1024]{1,0:T(8,128)(2,1)S(1)}, bf16[16,48,1024]{2,1,0:T(8,128)(2,1)S(1)}, bf16[768,1024]{1,0:T(8,128)(2,1)S(1)}, s32[1024,128]{1,0:T(8,128)S(1)}) custom-call(bf16[768,1024]{1,0:T(8,128)(2,1)} %follow.2.own0, bf16[16,48,1024]{2,1,0:T(8,128)(2,1)} %get-tuple-element.35.arrived, ...), custom_call_target="tpu_custom_call" | custom-call | flops 1476395008 | tf_op jit(solution)/shard_map/middle/pallas_call | solution.py:505
  78.6 0.0 collective-permute-done.4.also_after.high0.refs_1_
  78.7 0.4 collective-permute-done.2.rows
  79.1 1.1 %collective-permute-start.5 = (bf16[768,1024]{1,0:T(8,128)(2,1)S(1)}, bf16[768,1024]{1,0:T(8,128)(2,1)S(1)}, u32[]{:S(2)}, u32[]{:S(2)}) collective-permute-start(bf16[768,1024]{1,0:T(8,128)(2,1)S(1)} %follow.3.low0), channel_id=1, source_target_pairs={{0,1},{1,0},{2,3},{3,2},{4,5},{5,4},{6,7},{7,6},{8,9},{9,8},{10,11... | collective-permute-start | bytes 4718600 | tf_op jit(solution)/shard_map/ppermute | solution.py:468
  80.2 7.6 %main.1.refs_6_ = f32[8,1024]{1,0:T(8,128)S(1)} custom-call(bf16[768,1024]{1,0:T(8,128)(2,1)S(1)} %get-tuple-element.40.own0, bf16[16,48,1024]{2,1,0:T(8,128)(2,1)S(1)} %get-tuple-element.38.arrived.refs_3_, bf16[768,1024]{1,0:T(8,128)(2,1)S(1)} %collective-permute-done.4.also_after.high0.refs_1_, bf16[768,1024]{1,0:T(8,128)(2,1)S(1)} %get-tuple-element.41.sib0, ...), custom_call_target="tpu_custom_call" | custom-call | flops 4966055936 | tf_op jit(solution)/shard_map/main/pallas_call | solution.py:505
  87.8 2.3 %last.1 = f32[128,64]{1,0:T(8,128)S(1)} custom-call(bf16[768,1024]{1,0:T(8,128)(2,1)S(1)} %collective-permute-done.5.refs_0_, bf16[768,1024]{1,0:T(8,128)(2,1)S(1)} %collective-permute-done.4.also_after.high0.refs_1_, bf16[16,48,1024]{2,1,0:T(8,128)(2,1)S(1)} %collective-permute-done.6.swapped.refs_2_, ...), custom_call_target="tpu_custom_call" | custom-call | flops 1073741824 | tf_op jit(solution)/shard_map/last/pallas_call | solution.py:505
  90.1 13.6 %all_to_all.20 = f32[128,1,64]{2,1,0:T(1,128)S(1)} all-to-all(f32[128,1,64]{2,1,0:T(1,128)S(1)} %bitcast.9), channel_id=1, replica_groups=mesh['pool'=16,'grp'=8] {'pool','grp'}, dimensions={0} | all-to-all | bytes 65536 | tf_op jit(solution)/shard_map/all_to_all | solution.py:550
  103.6 1.4 %score.1 = f32[1,1024]{1,0:T(1,128)} custom-call(s32[128,128]{1,0:T(8,128)S(1)} %copy-done.1, f32[128,64]{1,0:T(8,128)S(1)} %bitcast.10), custom_call_target="tpu_custom_call" | custom-call | tf_op jit(solution)/shard_map/score/pallas_call | solution.py:551
  (10 shorter events, 0.0 us)
Async XLA Ops:
  5.2 8.8 %copy-start = (bf16[1024,1024]{1,0:T(8,128)(2,1)S(1)}, bf16[1024,1024]{1,0:T(8,128)(2,1)}, u32[]{:S(2)}) copy-start(bf16[1024,1024]{1,0:T(8,128)(2,1)} %refs_1_.1) | copy-start | bytes 6291460
  5.2 8.8 %copy-start.1 = (s32[128,128]{1,0:T(8,128)S(1)}, s32[128,128]{1,0:T(8,128)}, u32[]{:S(2)}) copy-start(s32[128,128]{1,0:T(8,128)} %get-tuple-element.31.refs_0_) | copy-start | bytes 196612
  5.2 31.7 %all-to-all-start.1 = ((bf16[16,48,1024]{2,1,0:T(8,128)(2,1)}), bf16[16,48,1024]{2,1,0:T(8,128)(2,1)}, u32[]{:S(2)}, u32[]{:S(2)}) async-start(bf16[16,48,1024]{2,1,0:T(8,128)(2,1)} %get-tuple-element.32), calls=%async_computation.1 | async-start | bytes 3145728 | tf_op jit(solution)/shard_map/all_to_all | solution.py:482
  14.0 3.7 %copy-start.3 = (s32[256]{0:T(256)S(1)}, s32[256]{0:T(256)}, u32[]{:S(2)}) copy-start(s32[256]{0:T(256)} %param.8) | copy-start | bytes 3076
  14.0 5.0 %copy-start.2 = (s32[256,512]{1,0:T(8,128)S(1)}, s32[256,512]{1,0:T(8,128)}, u32[]{:S(2)}) copy-start(s32[256,512]{1,0:T(8,128)} %refs_0_.3) | copy-start | bytes 1572868
  14.0 5.0 %copy-start.4 = (s32[256]{0:T(256)S(1)}, s32[256]{0:T(256)}, u32[]{:S(2)}) copy-start(s32[256]{0:T(256)} %param.9) | copy-start | bytes 3076
  14.9 13.9 %collective-permute-start = (bf16[256,1024]{1,0:T(8,128)(2,1)S(1)}, bf16[256,1024]{1,0:T(8,128)(2,1)S(1)}, u32[]{:S(2)}, u32[]{:S(2)}) collective-permute-start(bf16[256,1024]{1,0:T(8,128)(2,1)S(1)} %rest.1.refs_0_), channel_id=1, source_target_pairs={{0,2},{1,3},{2,4},{3,5},{4,6},{5,7},{6,0},{7,1},{8,10},{9,11},{10,... | collective-permute-start | bytes 1572872 | tf_op jit(solution)/shard_map/ppermute | solution.py:465
  16.2 12.6 %collective-permute-start.1 = (bf16[256,1024]{1,0:T(8,128)(2,1)S(1)}, bf16[256,1024]{1,0:T(8,128)(2,1)S(1)}, u32[]{:S(2)}, u32[]{:S(2)}) collective-permute-start(bf16[256,1024]{1,0:T(8,128)(2,1)S(1)} %rest.1.refs_0_), channel_id=1, source_target_pairs={{0,6},{1,7},{2,0},{3,1},{4,2},{5,3},{6,4},{7,5},{8,14},{9,15},{10,... | collective-permute-start | bytes 1572872 | tf_op jit(solution)/shard_map/ppermute | solution.py:465
  36.9 5.9 %collective-permute-start.3 = (bf16[768,1024]{1,0:T(8,128)(2,1)}, bf16[768,1024]{1,0:T(8,128)(2,1)}, u32[]{:S(2)}, u32[]{:S(2)}) collective-permute-start(bf16[768,1024]{1,0:T(8,128)(2,1)} %follow.2.own0), channel_id=1, source_target_pairs={{0,1},{1,0},{2,3},{3,2},{4,5},{5,4},{6,7},{7,6},{8,9},{9,8},{10,11... | collective-permute-start | bytes 4718600 | tf_op jit(solution)/shard_map/ppermute | solution.py:468
  39.4 39.2 %collective-permute-start.4 = (bf16[768,1024]{1,0:T(8,128)(2,1)}, bf16[768,1024]{1,0:T(8,128)(2,1)S(1)}, u32[]{:S(2)}, u32[]{:S(2)}) collective-permute-start(bf16[768,1024]{1,0:T(8,128)(2,1)} %follow.2.own0), channel_id=1, source_target_pairs={{0,6},{1,7},{2,0},{3,1},{4,2},{5,3},{6,4},{7,5},{8,14},{9,15},{10,... | collective-permute-start | bytes 4718600 | tf_op jit(solution)/shard_map/ppermute | solution.py:465
  41.9 37.1 %collective-permute-start.2 = (bf16[768,1024]{1,0:T(8,128)(2,1)}, bf16[768,1024]{1,0:T(8,128)(2,1)S(1)}, u32[]{:S(2)}, u32[]{:S(2)}) collective-permute-start(bf16[768,1024]{1,0:T(8,128)(2,1)} %follow.2.own0), channel_id=1, source_target_pairs={{0,2},{1,3},{2,4},{3,5},{4,6},{5,7},{6,0},{7,1},{8,10},{9,11},{10,... | collective-permute-start | bytes 4718600 | tf_op jit(solution)/shard_map/ppermute | solution.py:465
  42.8 29.5 %all-to-all-start = ((bf16[16,48,1024]{2,1,0:T(8,128)(2,1)}), bf16[16,48,1024]{2,1,0:T(8,128)(2,1)}, u32[]{:S(2)}, u32[]{:S(2)}) async-start(bf16[16,48,1024]{2,1,0:T(8,128)(2,1)} %get-tuple-element.15), calls=%async_computation | async-start | bytes 3145728 | tf_op jit(solution)/shard_map/cond/branch_1_fun/all_to_all | solution.py:482
  72.4 7.8 %collective-permute-start.6 = (bf16[16,48,1024]{2,1,0:T(8,128)(2,1)}, bf16[16,48,1024]{2,1,0:T(8,128)(2,1)S(1)}, u32[]{:S(2)}, u32[]{:S(2)}) collective-permute-start(bf16[16,48,1024]{2,1,0:T(8,128)(2,1)} %get-tuple-element.35.arrived), channel_id=1, source_target_pairs={{0,1},{1,0},{2,3},{3,2},{4,5},{5,4},{6,7},{7,6},{8,9},{9,8},{10,11... | collective-permute-start | bytes 4718600 | tf_op jit(solution)/shard_map/ppermute | solution.py:468
  79.1 8.7 %collective-permute-start.5 = (bf16[768,1024]{1,0:T(8,128)(2,1)S(1)}, bf16[768,1024]{1,0:T(8,128)(2,1)S(1)}, u32[]{:S(2)}, u32[]{:S(2)}) collective-permute-start(bf16[768,1024]{1,0:T(8,128)(2,1)S(1)} %follow.3.low0), channel_id=1, source_target_pairs={{0,1},{1,0},{2,3},{3,2},{4,5},{5,4},{6,7},{7,6},{8,9},{9,8},{10,11... | collective-permute-start | bytes 4718600 | tf_op jit(solution)/shard_map/ppermute | solution.py:468

commit v14 on v13

--- a/solution.py
+++ b/solution.py
@@ -494,7 +494,7 @@
         lambda *refs: join_kernel(pools, *refs),
         out_shape=sds((pools, 3 * QUARTER // pools, feature), BF16),
         in_specs=[vmem] * 3 + [hbm],
-        compiler_params=PARAMS,
+        compiler_params=TABLE_PARAMS,
         name="join",
     )(rest, low_rest, high_rest, meta)
     own0 = follow(own0, sent, some.astype(I32).reshape(1, 1))

time: 105 us -> 105 us (level)
  waiting for transfers between devices: 33.7 us -> 31.9 us
  local copies, waits for them, and re-layouts: 0.03 us -> 1.64 us
    all_to_all x2, waiting for transfers between devices: 27.9 us -> 26.1 us  [to_pools(): return lax.all_to_all(rows, 'pool', split_axis=0, concat_axis=0, tiled=True)]
    unnamed x10 -> x18, local copies, waits for them, and re-layouts: 0.03 us -> 1.64 us
where the time goes in v14:
time: 105 us
  Pallas kernels  33.2 us (32%)
  waiting for transfers between devices  31.9 us (30%)
  starting transfers between devices  23.3 us (22%)
  blocking collectives  13.6 us (13%)
  local copies, waits for them, and re-layouts  1.64 us (2%)
    all_to_all x2, waiting for transfers between devices, to_pools(): return lax.all_to_all(rows, 'pool', split_axis=0, concat_axis=0, tiled=True)  26.1 us
    pallas_call x4, Pallas kernels, tiles(): pl.pallas_call(kernel, out_shape=(sds(out_shape, F32), *kept) if kept els...  19.1 us
    all_to_all x1, blocking collectives, body(): lax.all_to_all(best, ('pool', 'grp'), split_axis=0, concat_axis=0, tiled=...  13.6 us
    all_to_all x2, starting transfers between devices, to_pools(): return lax.all_to_all(rows, 'pool', split_axis=0, concat_axis=0, tiled=True)  13.2 us
    pallas_call x1, Pallas kernels, body(): pl.pallas_call(lambda *refs: meta_kernel(group, places, last, *refs), out...  5.25 us
    ppermute x4, starting transfers between devices, shift(): lax.ppermute(rows, 'grp', [(g, (g + by) % group) for g in range(group)])  5.23 us
    pallas_call x1, Pallas kernels, body(): pl.pallas_call(lambda *refs: table_kernel(pools, group, places, last, *re...  5.15 us
    ppermute x4, waiting for transfers between devices, shift(): lax.ppermute(rows, 'grp', [(g, (g + by) % group) for g in range(group)])  4.91 us
  transfers between devices with their start and end apart: 9, of which 5 were waited for; matrix products, arithmetic and copies ran while one was open for 1% of the time, Pallas kernels for 23%

profile of v14, /device:TPU:1, one launch (start us, length us, event | category | flops | bytes accessed | tf_op | source)
XLA Modules:
  0.0 105.1 jit_solution(8943625674229306099)
XLA Ops:
  0.0 5.2 %table.1 = (s32[128,128]{1,0:T(8,128)}, bf16[16,48,1024]{2,1,0:T(8,128)(2,1)}) custom-call(s32[256,512]{1,0:T(8,128)} %refs_0_.3, s32[1,256]{1,0:T(1,128)} %bitcast.11, bf16[1024,1024]{1,0:T(8,128)(2,1)} %refs_1_.1), custom_call_target="tpu_custom_call" | custom-call | flops 2147483648 | tf_op jit(solution)/shard_map/table/pallas_call | solution.py:430
  5.2 0.0 copy-start
  5.2 8.8 %all-to-all-start.1 = ((bf16[16,48,1024]{2,1,0:T(8,128)(2,1)}), bf16[16,48,1024]{2,1,0:T(8,128)(2,1)}, u32[]{:S(2)}, u32[]{:S(2)}) async-start(bf16[16,48,1024]{2,1,0:T(8,128)(2,1)} %get-tuple-element.32), calls=%async_computation.1 | async-start | bytes 3145728 | tf_op jit(solution)/shard_map/all_to_all | solution.py:482
  14.0 0.0 copy-start.4
  14.0 0.0 copy-start.3
  14.0 0.0 copy-start.5
  14.0 0.9 rest.1.refs_0_
  14.9 1.3 %collective-permute-start = (bf16[256,1024]{1,0:T(8,128)(2,1)S(1)}, bf16[256,1024]{1,0:T(8,128)(2,1)S(1)}, u32[]{:S(2)}, u32[]{:S(2)}) collective-permute-start(bf16[256,1024]{1,0:T(8,128)(2,1)S(1)} %rest.1.refs_0_), channel_id=1, source_target_pairs={{0,2},{1,3},{2,4},{3,5},{4,6},{5,7},{6,0},{7,1},{8,10},{9,11},{10,... | collective-permute-start | bytes 1572872 | tf_op jit(solution)/shard_map/ppermute | solution.py:465
  16.2 1.5 %collective-permute-start.1 = (bf16[256,1024]{1,0:T(8,128)(2,1)S(1)}, bf16[256,1024]{1,0:T(8,128)(2,1)S(1)}, u32[]{:S(2)}, u32[]{:S(2)}) collective-permute-start(bf16[256,1024]{1,0:T(8,128)(2,1)S(1)} %rest.1.refs_0_), channel_id=1, source_target_pairs={{0,6},{1,7},{2,0},{3,1},{4,2},{5,3},{6,4},{7,5},{8,14},{9,15},{10,... | collective-permute-start | bytes 1572872 | tf_op jit(solution)/shard_map/ppermute | solution.py:465
  17.6 0.6 compare_reduce_fusion
  19.0 5.2 %meta.1 = (s32[2,8,1024]{2,1,0:T(8,128)S(1)}, s32[1024,128]{1,0:T(8,128)}) custom-call(s32[256,512]{1,0:T(8,128)S(1)} %copy-done.3, s32[1,256]{1,0:T(1,128)S(1)} %bitcast.12, s32[1,256]{1,0:T(1,128)S(1)} %bitcast.13), custom_call_target="tpu_custom_call" | custom-call | flops 4294967296 | tf_op jit(solution)/shard_map/meta/pallas_call | solution.py:448
  24.2 4.5 %collective-permute-done.refs_1_ = bf16[256,1024]{1,0:T(8,128)(2,1)S(1)} collective-permute-done((bf16[256,1024]{1,0:T(8,128)(2,1)S(1)}, bf16[256,1024]{1,0:T(8,128)(2,1)S(1)}, u32[]{:S(2)}, u32[]{:S(2)}) %collective-permute-start) | collective-permute-done | bytes 524320 | tf_op jit(solution)/shard_map/ppermute | solution.py:465
  28.7 0.0 collective-permute-done.1.refs_2_
  28.7 0.8 copy-done.7
  29.5 0.8 copy-done.8
  30.3 1.5 %join.1.after = bf16[16,48,1024]{2,1,0:T(8,128)(2,1)S(1)} custom-call(bf16[256,1024]{1,0:T(8,128)(2,1)} %copy-done.1, bf16[256,1024]{1,0:T(8,128)(2,1)} %copy-done.7, bf16[256,1024]{1,0:T(8,128)(2,1)} %copy-done.8, s32[2,8,1024]{2,1,0:T(8,128)S(1)} %get-tuple-element.33.refs_3_.meta.refs_4_), custom_call_target="tpu_custom_call" | custom-call | tf_op jit(solution)/shard_map/join/pallas_call | solution.py:493
  31.8 5.1 %all-to-all-done.1 = bf16[16,48,1024]{2,1,0:T(8,128)(2,1)} async-done(((bf16[16,48,1024]{2,1,0:T(8,128)(2,1)}), bf16[16,48,1024]{2,1,0:T(8,128)(2,1)}, u32[]{:S(2)}, u32[]{:S(2)}) %all-to-all-start.1) | async-done | bytes 1572896 | tf_op jit(solution)/shard_map/all_to_all | solution.py:482
  36.9 2.6 %collective-permute-start.3 = (bf16[768,1024]{1,0:T(8,128)(2,1)}, bf16[768,1024]{1,0:T(8,128)(2,1)}, u32[]{:S(2)}, u32[]{:S(2)}) collective-permute-start(bf16[768,1024]{1,0:T(8,128)(2,1)} %follow.2.own0), channel_id=1, source_target_pairs={{0,1},{1,0},{2,3},{3,2},{4,5},{5,4},{6,7},{7,6},{8,9},{9,8},{10,11... | collective-permute-start | bytes 4718600 | tf_op jit(solution)/shard_map/ppermute | solution.py:468
  39.4 2.5 %collective-permute-start.4 = (bf16[768,1024]{1,0:T(8,128)(2,1)}, bf16[768,1024]{1,0:T(8,128)(2,1)S(1)}, u32[]{:S(2)}, u32[]{:S(2)}) collective-permute-start(bf16[768,1024]{1,0:T(8,128)(2,1)} %follow.2.own0), channel_id=1, source_target_pairs={{0,6},{1,7},{2,0},{3,1},{4,2},{5,3},{6,4},{7,5},{8,14},{9,15},{10,... | collective-permute-start | bytes 4718600 | tf_op jit(solution)/shard_map/ppermute | solution.py:465
  41.9 0.9 collective-permute-done.3.sib0
  42.8 29.6 %conditional.1 = (bf16[16,48,1024]{2,1,0:T(8,128)(2,1)}, f32[8,1024]{1,0:T(8,128)S(1)}) conditional(s32[]{:T(128)} %convert_element_type.4, () %tuple.13, (bf16[16,48,1024]{2,1,0:T(8,128)(2,1)}, bf16[768,1024]{1,0:T(8,128)(2,1)}, bf16[768,1024]{1,0:T(8,128)(2,1)}, s32[2,8,1024]{2,1,0:T(8,128)S(1)}, s32[1024,128]{1,0:T(8,128)}) %tuple.17), branch_computations={%region_1.0_spmd, %region_2.0_spmd} | conditional | flops 1476395008 | bytes 4718640 | solution.py:527
  42.8 4.4 %all-to-all-start = ((bf16[16,48,1024]{2,1,0:T(8,128)(2,1)}), bf16[16,48,1024]{2,1,0:T(8,128)(2,1)}, u32[]{:S(2)}, u32[]{:S(2)}) async-start(bf16[16,48,1024]{2,1,0:T(8,128)(2,1)} %get-tuple-element.15), calls=%async_computation | async-start | bytes 3145728 | tf_op jit(solution)/shard_map/cond/branch_1_fun/all_to_all | solution.py:482
  47.2 4.1 %near.1 = f32[8,1024]{1,0:T(8,128)S(1)} custom-call(bf16[768,1024]{1,0:T(8,128)(2,1)} %get-tuple-element.16.own0, bf16[768,1024]{1,0:T(8,128)(2,1)} %get-tuple-element.17.sib0, s32[2,8,1024]{2,1,0:T(8,128)S(1)} %get-tuple-element.18.meta, s32[1024,128]{1,0:T(8,128)} %get-tuple-element.19.codes), custom_call_target="tpu_custom_call" | custom-call | flops 1476395008 | tf_op jit(solution)/shard_map/cond/branch_1_fun/near/pallas_call | solution.py:505
  51.4 21.0 %all-to-all-done = bf16[16,48,1024]{2,1,0:T(8,128)(2,1)} async-done(((bf16[16,48,1024]{2,1,0:T(8,128)(2,1)}), bf16[16,48,1024]{2,1,0:T(8,128)(2,1)}, u32[]{:S(2)}, u32[]{:S(2)}) %all-to-all-start) | async-done | bytes 1572896 | tf_op jit(solution)/shard_map/cond/branch_1_fun/all_to_all | solution.py:482
  72.4 1.2 %collective-permute-start.6 = (bf16[16,48,1024]{2,1,0:T(8,128)(2,1)}, bf16[16,48,1024]{2,1,0:T(8,128)(2,1)S(1)}, u32[]{:S(2)}, u32[]{:S(2)}) collective-permute-start(bf16[16,48,1024]{2,1,0:T(8,128)(2,1)} %get-tuple-element.35.arrived), channel_id=1, source_target_pairs={{0,1},{1,0},{2,3},{3,2},{4,5},{5,4},{6,7},{7,6},{8,9},{9,8},{10,11... | collective-permute-start | bytes 4718600 | tf_op jit(solution)/shard_map/ppermute | solution.py:468
  73.6 5.1 %middle.1 = (f32[8,1024]{1,0:T(8,128)S(1)}, bf16[768,1024]{1,0:T(8,128)(2,1)S(1)}, bf16[16,48,1024]{2,1,0:T(8,128)(2,1)S(1)}, bf16[768,1024]{1,0:T(8,128)(2,1)S(1)}, s32[1024,128]{1,0:T(8,128)S(1)}) custom-call(bf16[768,1024]{1,0:T(8,128)(2,1)} %follow.2.own0, bf16[16,48,1024]{2,1,0:T(8,128)(2,1)} %get-tuple-element.35.arrived, ...), custom_call_target="tpu_custom_call" | custom-call | flops 1476395008 | tf_op jit(solution)/shard_map/middle/pallas_call | solution.py:505
  78.7 0.4 collective-permute-done.2.rows
  79.1 1.1 %collective-permute-start.5 = (bf16[768,1024]{1,0:T(8,128)(2,1)S(1)}, bf16[768,1024]{1,0:T(8,128)(2,1)S(1)}, u32[]{:S(2)}, u32[]{:S(2)}) collective-permute-start(bf16[768,1024]{1,0:T(8,128)(2,1)S(1)} %follow.3.low0), channel_id=1, source_target_pairs={{0,1},{1,0},{2,3},{3,2},{4,5},{5,4},{6,7},{7,6},{8,9},{9,8},{10,11... | collective-permute-start | bytes 4718600 | tf_op jit(solution)/shard_map/ppermute | solution.py:468
  80.2 7.6 %main.1.refs_6_ = f32[8,1024]{1,0:T(8,128)S(1)} custom-call(bf16[768,1024]{1,0:T(8,128)(2,1)S(1)} %get-tuple-element.40.own0, bf16[16,48,1024]{2,1,0:T(8,128)(2,1)S(1)} %get-tuple-element.38.arrived.refs_3_, bf16[768,1024]{1,0:T(8,128)(2,1)S(1)} %collective-permute-done.4.also_after.high0.refs_1_, bf16[768,1024]{1,0:T(8,128)(2,1)S(1)} %get-tuple-element.41.sib0, ...), custom_call_target="tpu_custom_call" | custom-call | flops 4966055936 | tf_op jit(solution)/shard_map/main/pallas_call | solution.py:505
  87.8 2.3 %last.1 = f32[128,64]{1,0:T(8,128)S(1)} custom-call(bf16[768,1024]{1,0:T(8,128)(2,1)S(1)} %collective-permute-done.5.refs_0_, bf16[768,1024]{1,0:T(8,128)(2,1)S(1)} %collective-permute-done.4.also_after.high0.refs_1_, bf16[16,48,1024]{2,1,0:T(8,128)(2,1)S(1)} %collective-permute-done.6.swapped.refs_2_, ...), custom_call_target="tpu_custom_call" | custom-call | flops 1073741824 | tf_op jit(solution)/shard_map/last/pallas_call | solution.py:505
  90.1 13.6 %all_to_all.20 = f32[128,1,64]{2,1,0:T(1,128)S(1)} all-to-all(f32[128,1,64]{2,1,0:T(1,128)S(1)} %bitcast.9), channel_id=1, replica_groups=mesh['pool'=16,'grp'=8] {'pool','grp'}, dimensions={0} | all-to-all | bytes 65536 | tf_op jit(solution)/shard_map/all_to_all | solution.py:550
  103.7 1.4 %score.1 = f32[1,1024]{1,0:T(1,128)} custom-call(s32[128,128]{1,0:T(8,128)S(1)} %copy-done.2, f32[128,64]{1,0:T(8,128)S(1)} %bitcast.10), custom_call_target="tpu_custom_call" | custom-call | tf_op jit(solution)/shard_map/score/pallas_call | solution.py:551
  (18 shorter events, 0.0 us)
Async XLA Ops:
  5.2 8.8 %copy-start = (bf16[1024,1024]{1,0:T(8,128)(2,1)S(1)}, bf16[1024,1024]{1,0:T(8,128)(2,1)}, u32[]{:S(2)}) copy-start(bf16[1024,1024]{1,0:T(8,128)(2,1)} %refs_1_.1) | copy-start | bytes 6291460
  5.2 8.8 %copy-start.2 = (s32[128,128]{1,0:T(8,128)S(1)}, s32[128,128]{1,0:T(8,128)}, u32[]{:S(2)}) copy-start(s32[128,128]{1,0:T(8,128)} %get-tuple-element.31.refs_0_) | copy-start | bytes 196612
  5.2 31.7 %all-to-all-start.1 = ((bf16[16,48,1024]{2,1,0:T(8,128)(2,1)}), bf16[16,48,1024]{2,1,0:T(8,128)(2,1)}, u32[]{:S(2)}, u32[]{:S(2)}) async-start(bf16[16,48,1024]{2,1,0:T(8,128)(2,1)} %get-tuple-element.32), calls=%async_computation.1 | async-start | bytes 3145728 | tf_op jit(solution)/shard_map/all_to_all | solution.py:482
  14.0 3.7 %copy-start.4 = (s32[256]{0:T(256)S(1)}, s32[256]{0:T(256)}, u32[]{:S(2)}) copy-start(s32[256]{0:T(256)} %param.8) | copy-start | bytes 3076
  14.0 5.0 %copy-start.3 = (s32[256,512]{1,0:T(8,128)S(1)}, s32[256,512]{1,0:T(8,128)}, u32[]{:S(2)}) copy-start(s32[256,512]{1,0:T(8,128)} %refs_0_.3) | copy-start | bytes 1572868
  14.0 5.0 %copy-start.5 = (s32[256]{0:T(256)S(1)}, s32[256]{0:T(256)}, u32[]{:S(2)}) copy-start(s32[256]{0:T(256)} %param.9) | copy-start | bytes 3076
  14.9 9.3 %copy-start.1 = (bf16[256,1024]{1,0:T(8,128)(2,1)}, bf16[256,1024]{1,0:T(8,128)(2,1)S(1)}, u32[]{:S(2)}) copy-start(bf16[256,1024]{1,0:T(8,128)(2,1)S(1)} %rest.1.refs_0_) | copy-start | bytes 1572868
  14.9 13.8 %collective-permute-start = (bf16[256,1024]{1,0:T(8,128)(2,1)S(1)}, bf16[256,1024]{1,0:T(8,128)(2,1)S(1)}, u32[]{:S(2)}, u32[]{:S(2)}) collective-permute-start(bf16[256,1024]{1,0:T(8,128)(2,1)S(1)} %rest.1.refs_0_), channel_id=1, source_target_pairs={{0,2},{1,3},{2,4},{3,5},{4,6},{5,7},{6,0},{7,1},{8,10},{9,11},{10,... | collective-permute-start | bytes 1572872 | tf_op jit(solution)/shard_map/ppermute | solution.py:465
  16.2 12.6 %collective-permute-start.1 = (bf16[256,1024]{1,0:T(8,128)(2,1)S(1)}, bf16[256,1024]{1,0:T(8,128)(2,1)S(1)}, u32[]{:S(2)}, u32[]{:S(2)}) collective-permute-start(bf16[256,1024]{1,0:T(8,128)(2,1)S(1)} %rest.1.refs_0_), channel_id=1, source_target_pairs={{0,6},{1,7},{2,0},{3,1},{4,2},{5,3},{6,4},{7,5},{8,14},{9,15},{10,... | collective-permute-start | bytes 1572872 | tf_op jit(solution)/shard_map/ppermute | solution.py:465
  28.7 0.8 copy-start.7
  29.5 0.8 copy-start.8
  31.8 5.1 %copy-start.6 = (bf16[16,48,1024]{2,1,0:T(8,128)(2,1)}, bf16[16,48,1024]{2,1,0:T(8,128)(2,1)S(1)}, u32[]{:S(2)}) copy-start(bf16[16,48,1024]{2,1,0:T(8,128)(2,1)S(1)} %join.1.after) | copy-start | bytes 4718596
  36.9 5.9 %collective-permute-start.3 = (bf16[768,1024]{1,0:T(8,128)(2,1)}, bf16[768,1024]{1,0:T(8,128)(2,1)}, u32[]{:S(2)}, u32[]{:S(2)}) collective-permute-start(bf16[768,1024]{1,0:T(8,128)(2,1)} %follow.2.own0), channel_id=1, source_target_pairs={{0,1},{1,0},{2,3},{3,2},{4,5},{5,4},{6,7},{7,6},{8,9},{9,8},{10,11... | collective-permute-start | bytes 4718600 | tf_op jit(solution)/shard_map/ppermute | solution.py:468
  39.4 39.2 %collective-permute-start.4 = (bf16[768,1024]{1,0:T(8,128)(2,1)}, bf16[768,1024]{1,0:T(8,128)(2,1)S(1)}, u32[]{:S(2)}, u32[]{:S(2)}) collective-permute-start(bf16[768,1024]{1,0:T(8,128)(2,1)} %follow.2.own0), channel_id=1, source_target_pairs={{0,6},{1,7},{2,0},{3,1},{4,2},{5,3},{6,4},{7,5},{8,14},{9,15},{10,... | collective-permute-start | bytes 4718600 | tf_op jit(solution)/shard_map/ppermute | solution.py:465
  41.9 37.1 %collective-permute-start.2 = (bf16[768,1024]{1,0:T(8,128)(2,1)}, bf16[768,1024]{1,0:T(8,128)(2,1)S(1)}, u32[]{:S(2)}, u32[]{:S(2)}) collective-permute-start(bf16[768,1024]{1,0:T(8,128)(2,1)} %follow.2.own0), channel_id=1, source_target_pairs={{0,2},{1,3},{2,4},{3,5},{4,6},{5,7},{6,0},{7,1},{8,10},{9,11},{10,... | collective-permute-start | bytes 4718600 | tf_op jit(solution)/shard_map/ppermute | solution.py:465
  42.8 29.6 %all-to-all-start = ((bf16[16,48,1024]{2,1,0:T(8,128)(2,1)}), bf16[16,48,1024]{2,1,0:T(8,128)(2,1)}, u32[]{:S(2)}, u32[]{:S(2)}) async-start(bf16[16,48,1024]{2,1,0:T(8,128)(2,1)} %get-tuple-element.15), calls=%async_computation | async-start | bytes 3145728 | tf_op jit(solution)/shard_map/cond/branch_1_fun/all_to_all | solution.py:482
  72.4 7.8 %collective-permute-start.6 = (bf16[16,48,1024]{2,1,0:T(8,128)(2,1)}, bf16[16,48,1024]{2,1,0:T(8,128)(2,1)S(1)}, u32[]{:S(2)}, u32[]{:S(2)}) collective-permute-start(bf16[16,48,1024]{2,1,0:T(8,128)(2,1)} %get-tuple-element.35.arrived), channel_id=1, source_target_pairs={{0,1},{1,0},{2,3},{3,2},{4,5},{5,4},{6,7},{7,6},{8,9},{9,8},{10,11... | collective-permute-start | bytes 4718600 | tf_op jit(solution)/shard_map/ppermute | solution.py:468
  79.1 8.7 %collective-permute-start.5 = (bf16[768,1024]{1,0:T(8,128)(2,1)S(1)}, bf16[768,1024]{1,0:T(8,128)(2,1)S(1)}, u32[]{:S(2)}, u32[]{:S(2)}) collective-permute-start(bf16[768,1024]{1,0:T(8,128)(2,1)S(1)} %follow.3.low0), channel_id=1, source_target_pairs={{0,1},{1,0},{2,3},{3,2},{4,5},{5,4},{6,7},{7,6},{8,9},{9,8},{10,11... | collective-permute-start | bytes 4718600 | tf_op jit(solution)/shard_map/ppermute | solution.py:468
